TPU v7x, 32 devices: a whole 2x2x4 slice. The times are simulated.
32 devices in a mesh: ctx: 8 (over z, core), ch: 4 (over y, x).
Axes of the slice: x: 2, y: 2, z: 4, core: 2. Of those that a mesh axis runs over, the one named last changes fastest.
Arguments:
- query_in: bfloat16 [2048, 4096], P('ctx', 'ch'), may hold values from -63 to 63
- key_in: bfloat16 [2048, 4096], P('ctx', 'ch'), may hold values from -4 to 4
- value_in: bfloat16 [2048, 4096], P('ctx', 'ch'), may hold values from -4 to 4
- short_taps: float32 [7, 3, 4096], P(None, None, 'ch'), may hold values from -2 to 2
- residues: float32 [4096, 16], P('ch'), may hold values from -1.5 to 1.5
- decays: float32 [4096, 16], P('ch'), may hold values from 2.4414063e-05 to 0.02
- out_weight: bfloat16 [4096, 4096], P('ch'), may hold values from -0.125 to 0.125
- out_grad: bfloat16 [2048, 4096], P('ctx', 'ch'), may hold values from -6 to 6
Outputs:
- projected: bfloat16 [2048, 4096], P('ctx', 'ch')
- grad_query: bfloat16 [2048, 4096], P('ctx', 'ch')
- grad_key: bfloat16 [2048, 4096], P('ctx', 'ch')
- grad_value: bfloat16 [2048, 4096], P('ctx', 'ch')
All inputs are finite; a program needn't handle non-finite values.
Results may differ from a plain program's by a relative error of at most 0.0058.
Values may be sent and summed in bfloat16 or wider, within the bound.
No kernel may reach another device: no remote copies, remote signals or barrier semaphores. Data moves between devices by JAX's collectives and lax.ppermute only.
A program may use at most 128 MiB of HBM per device.

v0:
```python
import functools

import jax
import jax.numpy as jnp
from jax import lax
from jax.experimental import pallas as pl
from jax.experimental.pallas import tpu as pltpu
from jax.sharding import PartitionSpec as P

SUB = 8
LANES = 128
STEP = 8
F32 = jnp.float32
BF16 = jnp.bfloat16
VMEM_LIMIT = 48 * 1024 * 1024


def as_tiles(rows):
    return rows.reshape(rows.shape[0] // SUB, SUB, LANES)


def as_rows(tiles):
    return tiles.reshape(tiles.shape[0] * SUB, LANES)


def tile(ref, token):
    return ref[pl.ds(pl.multiple_of(token * SUB, SUB), SUB), :]


def tree_sum(terms):
    while len(terms) > 1:
        terms = [
            terms[i] + terms[i + 1] if i + 1 < len(terms) else terms[i]
            for i in range(0, len(terms), 2)
        ]
    return terms[0]


def round16(value):
    return value.astype(BF16).astype(F32)


def scatter_tokens(ref, value, first_token):
    tokens, channels = value.shape
    for group in range(channels // LANES):
        ref[pl.ds(first_token * SUB + group, tokens, stride=SUB), :] = value[
            :, group * LANES : (group + 1) * LANES
        ]


def gather_tokens(ref, out_ref):
    tokens, channels = out_ref.shape
    for group in range(channels // LANES):
        out_ref[:, group * LANES : (group + 1) * LANES] = ref[
            pl.ds(group, tokens, stride=SUB), :
        ].astype(out_ref.dtype)


def end_state(signal_ref, decay_ref, state_ref, reverse):
    modes = decay_ref.shape[0]
    tokens = signal_ref.shape[0] // SUB
    factors = [jnp.exp(-decay_ref[n]) for n in range(modes)]

    def body(step, states):
        for inner in range(STEP):
            token = step * STEP + inner
            u = tile(signal_ref, tokens - 1 - token if reverse else token)
            states = [factors[n] * states[n] + u for n in range(modes)]
        return states

    zeros = [jnp.zeros((SUB, LANES), F32) for _ in range(modes)]
    states = lax.fori_loop(0, tokens // STEP, body, zeros)
    for n in range(modes):
        state_ref[n] = states[n]


def featurize_kernel(
    q_ref, k_ref, v_ref, halo_ref, taps_ref, decay_ref,
    qf_ref, kf_ref, vf_ref, mixed_ref, state_ref, wide_ref,
):
    tokens = q_ref.shape[0]
    taps = taps_ref.shape[0]
    rim = taps - 1
    halo = halo_ref[...].astype(F32)
    for stream, source in enumerate((q_ref, k_ref, v_ref)):
        wide = wide_ref.at[stream]
        scatter_tokens(wide, halo[stream * rim : (stream + 1) * rim], 0)
        scatter_tokens(wide, source[...].astype(F32), rim)

    def body(step, carry):
        first = pl.multiple_of(step * STEP * SUB, SUB)
        feats = []
        for stream, feat_ref in enumerate((qf_ref, kf_ref, vf_ref)):
            window = as_tiles(wide_ref[stream, pl.ds(first, (STEP + rim) * SUB), :])
            total = taps_ref[0, stream] * window[rim : rim + STEP]
            for tap in range(1, taps):
                total = total + taps_ref[tap, stream] * window[rim - tap : rim - tap + STEP]
            feat_ref[pl.ds(first, STEP * SUB), :] = as_rows(total)
            feats.append(total)
        mixed_ref[pl.ds(first, STEP * SUB), :] = as_rows(round16(feats[1] * feats[2]))
        return carry

    lax.fori_loop(0, tokens // STEP, body, 0)
    end_state(mixed_ref, decay_ref, state_ref, False)


def local_conv_kernel(signal_ref, decay_ref, scale_ref, out_ref, *, reverse):
    modes = decay_ref.shape[0]
    tokens = signal_ref.shape[0] // SUB
    factors = [jnp.exp(-decay_ref[n]) for n in range(modes)]
    scales = [scale_ref[n] for n in range(modes)]

    def body(step, states):
        for inner in range(STEP):
            token = step * STEP + inner
            token = tokens - 1 - token if reverse else token
            u = tile(signal_ref, token)
            states = [factors[n] * states[n] + u for n in range(modes)]
            out_ref[pl.ds(pl.multiple_of(token * SUB, SUB), SUB), :] = tree_sum(
                [scales[n] * states[n] for n in range(modes)]
            )
        return states

    zeros = [jnp.zeros((SUB, LANES), F32) for _ in range(modes)]
    lax.fori_loop(0, tokens // STEP, body, zeros)


def carried_states(message_refs, decay_ref, powers):
    states = []
    for n in range(decay_ref.shape[0]):
        terms = [
            ref[n] if power == 0 else ref[n] * jnp.exp(-decay_ref[n] * float(power))
            for ref, power in zip(message_refs, powers)
        ]
        states.append(tree_sum(terms))
    return states


def add_carried(local_ref, out_ref, states, decay_ref, scale_ref, reverse):
    modes = decay_ref.shape[0]
    tokens = local_ref.shape[0] // SUB
    factors = [jnp.exp(-decay_ref[n]) for n in range(modes)]
    scaled = [scale_ref[n] * states[n] for n in range(modes)]

    def body(step, scaled):
        for inner in range(STEP):
            token = step * STEP + inner
            token = tokens - 1 - token if reverse else token
            scaled = [factors[n] * scaled[n] for n in range(modes)]
            rows = pl.ds(pl.multiple_of(token * SUB, SUB), SUB)
            out_ref[rows, :] = local_ref[rows, :] + tree_sum(list(scaled))
        return scaled

    lax.fori_loop(0, tokens // STEP, body, scaled)


def project_kernel(*refs, powers, order):
    count = len(powers)
    messages = refs[:count]
    (
        local_ref, decay_ref, scale_ref, qf_ref, weight_ref,
        conv_ref, out_ref, rows_ref, gated_ref, held_ref, sems,
    ) = refs[count:]
    parts, _, width = out_ref.shape
    copies = [
        pltpu.make_async_copy(
            weight_ref.at[:, pl.ds(part * width, width)], held_ref.at[part], sems.at[part]
        )
        for part in range(parts)
    ]
    for part in order:
        copies[part].start()
    states = carried_states(messages, decay_ref, powers)
    add_carried(local_ref, conv_ref, states, decay_ref, scale_ref, False)
    rows_ref[...] = qf_ref[...] * conv_ref[...]
    gather_tokens(rows_ref, gated_ref)
    block = min(width, 256)
    for part in order:
        copies[part].wait()

        def body(step, carry):
            columns = pl.ds(pl.multiple_of(step * block, block), block)
            out_ref[part, :, columns] = jnp.dot(
                gated_ref[...], held_ref[part, :, columns], preferred_element_type=F32
            ).astype(out_ref.dtype)
            return carry

        lax.fori_loop(0, width // block, body, 0)


def back_products(index_ref, piece_refs, weight_ref, held_ref, sems, total_ref, base_ref):
    channels = total_ref.shape[1]
    copies, parts = [], []
    for ref in piece_refs:
        for inner in range(ref.shape[0]):
            parts.append((ref, inner))
    width = piece_refs[0].shape[2]
    for number in range(len(parts)):
        first = pl.multiple_of(index_ref[number] * width, width)
        copies.append(
            pltpu.make_async_copy(
                weight_ref.at[:, pl.ds(first, width)], held_ref.at[number], sems.at[number]
            )
        )
    for copy in copies:
        copy.start()
    block = min(channels, 256)
    for number, (ref, inner) in enumerate(parts):
        copies[number].wait()

        def body(step, carry):
            columns = pl.ds(pl.multiple_of(step * block, block), block)
            product = lax.dot_general(
                ref[inner], held_ref[number, columns, :],
                (((1,), (1,)), ((), ())), preferred_element_type=F32,
            )
            before = base_ref if number == 0 else total_ref
            total_ref[:, columns] = product if before is None else before[:, columns] + product
            return carry

        lax.fori_loop(0, channels // block, body, 0)


def back_part_kernel(*refs):
    index_ref, *pieces, weight_ref, total_ref, held_ref, sems = refs
    back_products(index_ref, pieces, weight_ref, held_ref, sems, total_ref, None)


def back_last_kernel(*refs, has_base):
    index_ref, *rest = refs
    (
        weight_ref, qf_ref, decay_ref,
        grad_ref, mixed_ref, state_ref, total_ref, held_ref, sems,
    ) = rest[-9:]
    pieces = rest[:-9]
    base_ref = None
    if has_base:
        base_ref, *pieces = pieces
    back_products(index_ref, pieces, weight_ref, held_ref, sems, total_ref, base_ref)
    scatter_tokens(grad_ref, total_ref[...], 0)
    mixed_ref[...] = round16(grad_ref[...] * qf_ref[...])
    end_state(mixed_ref, decay_ref, state_ref, True)


def finish_kernel(*refs, powers):
    count = len(powers)
    messages = refs[:count]
    (
        local_ref, decay_ref, scale_ref, kf_ref, vf_ref, grad_ref, conv_ref, halo_ref, taps_ref,
        gq_ref, gk_ref, gv_ref, total_ref, wide_ref, rows_ref,
    ) = refs[count:]
    modes = decay_ref.shape[0]
    taps = taps_ref.shape[0]
    rim = taps - 1
    tokens = gq_ref.shape[0]
    states = carried_states(messages, decay_ref, powers)
    add_carried(local_ref, total_ref, states, decay_ref, scale_ref, True)

    def body(step, carry):
        rows = pl.ds(pl.multiple_of(step * STEP * SUB, SUB), STEP * SUB)
        wide_ref[0, rows, :] = round16(grad_ref[rows, :] * conv_ref[rows, :])
        wide_ref[1, rows, :] = round16(total_ref[rows, :] * vf_ref[rows, :])
        wide_ref[2, rows, :] = round16(total_ref[rows, :] * kf_ref[rows, :])
        return carry

    lax.fori_loop(0, tokens // STEP, body, 0)
    growth = [jnp.exp(decay_ref[n]) for n in range(modes)]
    for ahead in range(rim):
        rows = pl.ds((tokens + ahead) * SUB, SUB)
        grad_conv = tree_sum([scale_ref[n] * states[n] for n in range(modes)])
        wide_ref[0, rows, :] = halo_ref[0, pl.ds(ahead * SUB, SUB), :]
        wide_ref[1, rows, :] = round16(grad_conv * halo_ref[3, pl.ds(ahead * SUB, SUB), :])
        wide_ref[2, rows, :] = round16(grad_conv * halo_ref[2, pl.ds(ahead * SUB, SUB), :])
        arrived = halo_ref[1, pl.ds(ahead * SUB, SUB), :]
        states = [(states[n] - arrived) * growth[n] for n in range(modes)]

    def spread(step, carry):
        first = pl.multiple_of(step * STEP * SUB, SUB)
        for stream in range(3):
            window = as_tiles(wide_ref[stream, pl.ds(first, (STEP + rim) * SUB), :])
            total = taps_ref[0, stream] * window[:STEP]
            for tap in range(1, taps):
                total = total + taps_ref[tap, stream] * window[tap : tap + STEP]
            rows_ref[stream, pl.ds(first, STEP * SUB), :] = as_rows(total)
        return carry

    lax.fori_loop(0, tokens // STEP, spread, 0)
    for stream, out_ref in enumerate((gq_ref, gk_ref, gv_ref)):
        gather_tokens(rows_ref.at[stream], out_ref)


IN_VMEM = pl.BlockSpec(memory_space=pltpu.VMEM)
IN_SMEM = pl.BlockSpec(memory_space=pltpu.SMEM)
ANYWHERE = pl.BlockSpec(memory_space=pl.ANY)


def call(kernel, outs, args, specs, scratch, name, flops, moved):
    return pl.pallas_call(
        kernel,
        out_shape=[jax.ShapeDtypeStruct(shape, kind) for shape, kind in outs],
        in_specs=specs,
        out_specs=[IN_VMEM] * len(outs),
        scratch_shapes=scratch,
        compiler_params=pltpu.CompilerParams(vmem_limit_bytes=VMEM_LIMIT),
        cost_estimate=pl.CostEstimate(flops=flops, bytes_accessed=moved, transcendentals=0),
        name=name,
    )(*args)


def shift(value, axis, steps):
    count = lax.axis_size(axis)
    pairs = [(s, s + steps) for s in range(count) if 0 <= s + steps < count]
    return lax.ppermute(value, axis, pairs)


def exchange(value, axis, mask):
    count = lax.axis_size(axis)
    return lax.ppermute(value, axis, [(s, s ^ mask) for s in range(count)])


def windowed(state, decays, tokens, direction, radix):
    count = lax.axis_size("ctx")
    window = 1
    while window * radix < count - 1 and window < radix:
        terms = [state]
        for step in range(1, radix):
            faded = jnp.exp(-decays * float(tokens * window * step))
            terms.append(faded * shift(state, "ctx", direction * window * step))
        state = tree_sum(terms)
        window *= radix
    messages, powers = [], []
    offset = 0
    while 1 + offset < count:
        messages.append(shift(state, "ctx", direction * (1 + offset)))
        powers.append(offset * tokens)
        offset += window
    return messages, powers


def gathered_state(state, decays, tokens, direction):
    count = lax.axis_size("ctx")
    everyone = lax.all_gather(state, "ctx", axis=0, tiled=False)
    gap = direction * (lax.axis_index("ctx") - jnp.arange(count)) - 1
    gap = gap[:, None, None, None]
    faded = jnp.exp(-decays[None] * (jnp.maximum(gap, 0) * tokens).astype(F32))
    return [jnp.sum(jnp.where(gap >= 0, faded * everyone, 0.0), axis=0)], [0]


def tiled_channels(value):
    groups = value.shape[-1] // LANES
    value = value.reshape(value.shape[:-1] + (groups, LANES))
    return jnp.pad(value, [(0, 0)] * (value.ndim - 2) + [(0, SUB - groups), (0, 0)])


def shards(query_in, key_in, value_in, short_taps, residues, decays, out_weight, out_grad):
    tokens, channels = query_in.shape
    taps = short_taps.shape[0]
    rim = taps - 1
    modes = decays.shape[1]
    fans = lax.axis_size("ch")
    mine = lax.axis_index("ch")
    rows = tokens * SUB
    size = rows * LANES * 4
    matmul = 2 * tokens * channels * channels
    tile_shape = (rows, LANES)
    state_shape = (modes, SUB, LANES)

    halo = jnp.concatenate([x[tokens - rim :] for x in (query_in, key_in, value_in)], axis=0)
    halo = shift(halo, "ctx", 1)
    tap_tiles = tiled_channels(short_taps)
    scale_tiles = tiled_channels((residues * jnp.sqrt(decays)).T)
    decay_tiles = tiled_channels(decays.T)

    query_feat, key_feat, value_feat, mixed, state = call(
        featurize_kernel,
        [(tile_shape, F32)] * 4 + [(state_shape, F32)],
        (query_in, key_in, value_in, halo, tap_tiles, decay_tiles),
        [IN_VMEM] * 6,
        [pltpu.VMEM((3, (tokens + rim) * SUB, LANES), F32)],
        "featurize", 20 * size, 5 * size,
    )
    messages, powers = windowed(state, decay_tiles, tokens, 1, 3)
    (local,) = call(
        functools.partial(local_conv_kernel, reverse=False),
        [(tile_shape, F32)], (mixed, decay_tiles, scale_tiles), [IN_VMEM] * 3, [],
        "local_conv", 16 * size, 2 * size,
    )
    conv_out, partial_sums = call(
        functools.partial(project_kernel, powers=tuple(powers), order=tuple(range(fans))),
        [(tile_shape, F32), ((fans, tokens, channels), BF16)],
        (*messages, local, decay_tiles, scale_tiles, query_feat, out_weight),
        [IN_VMEM] * (len(messages) + 4) + [ANYWHERE],
        [
            pltpu.VMEM(tile_shape, F32),
            pltpu.VMEM((tokens, channels), BF16),
            pltpu.VMEM((fans, channels, channels), BF16),
            pltpu.SemaphoreType.DMA((fans,)),
        ],
        "project", fans * matmul, fans * channels * channels * 2,
    )
    arrived = lax.all_to_all(partial_sums, "ch", split_axis=0, concat_axis=0, tiled=True)
    projected = jnp.sum(arrived.astype(F32), axis=0).astype(BF16)

    def scratch_for(count):
        return [
            pltpu.VMEM((count, channels, channels), BF16),
            pltpu.SemaphoreType.DMA((count,)),
        ]

    own = out_grad[None]
    if fans == 4:
        near = exchange(own, "ch", 1)
        far = exchange(own, "ch", 2)
        half = tokens // 2
        top = exchange(far[:, :half], "ch", 1)
        bottom = exchange(near[:, half:], "ch", 2)
        across = jnp.concatenate([top, bottom], axis=1)
        first_index = jnp.stack([mine, mine ^ 1, mine ^ 2]).astype(jnp.int32)
        (base,) = call(
            back_part_kernel,
            [((tokens, channels), F32)],
            (first_index, own, near, far, out_weight),
            [IN_SMEM] + [IN_VMEM] * 3 + [ANYWHERE],
            scratch_for(3), "back_part", 3 * matmul, 3 * channels * channels * 2,
        )
        pieces, bases, count = [across], [base], 1
        last_index = (mine ^ 3)[None].astype(jnp.int32)
    else:
        pieces, bases, count = [lax.all_gather(out_grad, "ch", axis=0, tiled=False)], [], fans
        last_index = jnp.arange(fans, dtype=jnp.int32)
    grad_gated, grad_mixed, back_state = call(
        functools.partial(back_last_kernel, has_base=bool(bases)),
        [(tile_shape, F32), (tile_shape, F32), (state_shape, F32)],
        (last_index, *bases, *pieces, out_weight, query_feat, decay_tiles),
        [IN_SMEM] + [IN_VMEM] * (len(bases) + len(pieces)) + [ANYWHERE] + [IN_VMEM] * 2,
        [pltpu.VMEM((tokens, channels), F32)] + scratch_for(count),
        "back_last", count * matmul, 4 * size,
    )
    back_messages, back_powers = gathered_state(back_state, decay_tiles, tokens, -1)
    (back_local,) = call(
        functools.partial(local_conv_kernel, reverse=True),
        [(tile_shape, F32)], (grad_mixed, decay_tiles, scale_tiles), [IN_VMEM] * 3, [],
        "back_local_conv", 16 * size, 2 * size,
    )
    head = slice(0, rim * SUB)
    grad_query_head = (grad_gated[head] * conv_out[head]).astype(BF16).astype(F32)
    ahead = shift(
        jnp.stack([grad_query_head, grad_mixed[head], key_feat[head], value_feat[head]]), "ctx", -1
    )
    grad_query, grad_key, grad_value = call(
        functools.partial(finish_kernel, powers=tuple(back_powers)),
        [((tokens, channels), BF16)] * 3,
        (
            *back_messages, back_local, decay_tiles, scale_tiles, key_feat, value_feat,
            grad_gated, conv_out, ahead, tap_tiles,
        ),
        [IN_VMEM] * (len(back_messages) + 9),
        [
            pltpu.VMEM(tile_shape, F32),
            pltpu.VMEM((3, (tokens + rim) * SUB, LANES), F32),
            pltpu.VMEM((3,) + tile_shape, F32),
        ],
        "finish", 20 * size, 8 * size,
    )
    return (projected, grad_query, grad_key, grad_value)


def solution(mesh):
    in_specs = (
        P("ctx", "ch"),
        P("ctx", "ch"),
        P("ctx", "ch"),
        P(None, None, "ch"),
        P("ch", None),
        P("ch", None),
        P("ch", None),
        P("ctx", "ch"),
    )
    out_specs = (P("ctx", "ch"), P("ctx", "ch"), P("ctx", "ch"), P("ctx", "ch"))
    return jax.shard_map(shards, mesh=mesh, in_specs=in_specs, out_specs=out_specs, check_vma=False)
```

profile of v0, /device:TPU:0, one launch (start us, length us, event | category | flops | bytes accessed | tf_op | source)
XLA Modules:
  0.0 114.7 jit_solution(9749745497499970188)
XLA Ops:
  0.6 3.0 %collective-permute-start.6 = (bf16[1,256,1024]{2,1,0:T(8,128)(2,1)}, bf16[1,256,1024]{2,1,0:T(8,128)(2,1)S(1)}, u32[]{:S(2)}, u32[]{:S(2)}) collective-permute-start(bf16[1,256,1024]{2,1,0:T(8,128)(2,1)} %bitcast.39), channel_id=1, source_target_pairs={{0,1},{1,0},{2,3},{3,2},{4,5},{5,4},{6,7},{7,6},{8,9},{9,8},{10,11... | collective-permute-start | bytes 1572872 | tf_op jit(solution)/shard_map/ppermute | solution.py:318
  3.6 1.5 %collective-permute-start.7 = (bf16[1,256,1024]{2,1,0:T(8,128)(2,1)}, bf16[1,256,1024]{2,1,0:T(8,128)(2,1)S(1)}, u32[]{:S(2)}, u32[]{:S(2)}) collective-permute-start(bf16[1,256,1024]{2,1,0:T(8,128)(2,1)} %bitcast.40), channel_id=1, source_target_pairs={{0,2},{1,3},{2,0},{3,1},{4,6},{5,7},{6,4},{7,5},{8,10},{9,11},{10,... | collective-permute-start | bytes 1572872 | tf_op jit(solution)/shard_map/ppermute | solution.py:318
  5.2 0.7 slice.32
  5.9 0.7 slice.31
  6.6 0.7 slice.30
  7.4 1.3 %collective-permute-start = (bf16[18,1024]{1,0:T(8,128)(2,1)S(1)}, bf16[18,1024]{1,0:T(8,128)(2,1)S(1)}, u32[]{:S(2)}, u32[]{:S(2)}) collective-permute-start(bf16[18,1024]{1,0:T(8,128)(2,1)S(1)} %pad_maximum_fusion.2), channel_id=1, source_target_pairs={{0,4},{4,8},{8,12},{12,16},{16,20},{20,24},{24,28},{1,5},{5,9},{9,... | collective-permute-start | bytes 110600 | tf_op jit(solution)/shard_map/ppermute | solution.py:313
  8.7 0.9 multiply_bitcast_fusion
  9.6 0.9 copy.17
  10.4 0.9 reshape.41
  11.4 0.0 collective-permute-done.halo_ref
  11.4 0.0 copy-start.4
  11.4 1.0 copy-done.4
  12.4 1.0 copy-done.5
  13.5 1.0 copy-done.6
  14.5 3.6 %featurize.1 = (f32[2048,128]{1,0:T(8,128)S(1)}, f32[2048,128]{1,0:T(8,128)S(1)}, f32[2048,128]{1,0:T(8,128)S(1)}, f32[2048,128]{1,0:T(8,128)S(1)}, f32[16,8,128]{2,1,0:T(8,128)S(1)}) custom-call(bf16[256,1024]{1,0:T(8,128)(2,1)S(1)} %copy-done.4, bf16[256,1024]{1,0:T(8,128)(2,1)S(1)} %copy-done.5, bf16[256,1024]{1,0:T(8,128)(2,1)S(1)} %copy-done.6, ...), custom_call_target="tpu_custom_call" | custom-call | flops 20971520 | bytes 5242880 | tf_op jit(solution)/shard_map/featurize/pallas_call | solution.py:298
  18.2 1.0 copy-done
  19.1 4.8 %collective-permute-start.2 = (f32[16,8,128]{2,1,0:T(8,128)S(1)}, f32[16,8,128]{2,1,0:T(8,128)S(1)}, u32[]{:S(2)}, u32[]{:S(2)}) collective-permute-start(f32[16,8,128]{2,1,0:T(8,128)S(1)} %get-tuple-element.17), channel_id=1, source_target_pairs={{0,8},{4,12},{8,16},{12,20},{16,24},{20,28},{1,9},{5,13},{9,17},{1... | collective-permute-start | bytes 196616 | tf_op jit(solution)/shard_map/ppermute | solution.py:313
  24.0 2.6 %collective-permute-start.1 = (f32[16,8,128]{2,1,0:T(8,128)S(1)}, f32[16,8,128]{2,1,0:T(8,128)S(1)}, u32[]{:S(2)}, u32[]{:S(2)}) collective-permute-start(f32[16,8,128]{2,1,0:T(8,128)S(1)} %get-tuple-element.17), channel_id=1, source_target_pairs={{0,4},{4,8},{8,12},{12,16},{16,20},{20,24},{24,28},{1,5},{5,9},{9,... | collective-permute-start | bytes 196616 | tf_op jit(solution)/shard_map/ppermute | solution.py:313
  26.6 0.0 collective-permute-done.2
  26.6 0.9 collective-permute-done.1
  27.5 3.4 %collective-permute-start.3 = (f32[16,8,128]{2,1,0:T(8,128)S(1)}, f32[16,8,128]{2,1,0:T(8,128)S(1)}, u32[]{:S(2)}, u32[]{:S(2)}) collective-permute-start(f32[16,8,128]{2,1,0:T(8,128)S(1)} %get-tuple-element.31), channel_id=1, source_target_pairs={{0,4},{4,8},{8,12},{12,16},{16,20},{20,24},{24,28},{1,5},{5,9},{9,... | collective-permute-start | bytes 196616 | tf_op jit(solution)/shard_map/ppermute | solution.py:313
  30.9 5.2 %collective-permute-start.4 = (f32[16,8,128]{2,1,0:T(8,128)S(1)}, f32[16,8,128]{2,1,0:T(8,128)S(1)}, u32[]{:S(2)}, u32[]{:S(2)}) collective-permute-start(f32[16,8,128]{2,1,0:T(8,128)S(1)} %get-tuple-element.31), channel_id=1, source_target_pairs={{0,16},{4,20},{8,24},{12,28},{1,17},{5,21},{9,25},{13,29},{2,18},{... | collective-permute-start | bytes 196616 | tf_op jit(solution)/shard_map/ppermute | solution.py:313
  36.1 1.3 %collective-permute-start.5 = (f32[16,8,128]{2,1,0:T(8,128)S(1)}, f32[16,8,128]{2,1,0:T(8,128)S(1)}, u32[]{:S(2)}, u32[]{:S(2)}) collective-permute-start(f32[16,8,128]{2,1,0:T(8,128)S(1)} %get-tuple-element.31), channel_id=1, source_target_pairs={{0,28},{1,29},{2,30},{3,31}} | collective-permute-start | bytes 196616 | tf_op jit(solution)/shard_map/ppermute | solution.py:313
  37.4 2.3 %local_conv.1.refs_3_ = f32[2048,128]{1,0:T(8,128)S(1)} custom-call(f32[2048,128]{1,0:T(8,128)S(1)} %get-tuple-element.18.signal_ref, f32[16,8,128]{2,1,0:T(8,128)S(1)} %bitcast.30, f32[16,8,128]{2,1,0:T(8,128)S(1)} %bitcast.35), custom_call_target="tpu_custom_call" | custom-call | flops 16777216 | bytes 2097152 | tf_op jit(solution)/shard_map/local_conv/pallas_call | solution.py:298
  39.7 0.0 collective-permute-done.3.refs_0_
  39.7 0.0 collective-permute-done.4.refs_1_
  39.7 0.0 collective-permute-done.5.refs_2_
  39.7 8.1 %project.1 = (f32[2048,128]{1,0:T(8,128)S(1)}, bf16[4,256,1024]{2,1,0:T(8,128)(2,1)}) custom-call(f32[16,8,128]{2,1,0:T(8,128)S(1)} %collective-permute-done.3.refs_0_, f32[16,8,128]{2,1,0:T(8,128)S(1)} %collective-permute-done.4.refs_1_, f32[16,8,128]{2,1,0:T(8,128)S(1)} %collective-permute-done.5.refs_2_, f32[2048,128]{1,0:T(8,128)S(1)} %local_conv.1.refs_3_, ...), custom_call_target="tpu_custom_call" | custom-call | flops 2147483648 | bytes 8388608 | tf_op jit(solution)/shard_map/project/pallas_call | solution.py:298
  47.8 1.0 copy-done.2
  48.8 4.4 %all-to-all-start = ((bf16[4,256,1024]{2,1,0:T(8,128)(2,1)}), bf16[4,256,1024]{2,1,0:T(8,128)(2,1)}, u32[]{:S(2)}, u32[]{:S(2)}) async-start(bf16[4,256,1024]{2,1,0:T(8,128)(2,1)} %get-tuple-element.20), calls=%async_computation | async-start | bytes 4194304 | tf_op jit(solution)/shard_map/all_to_all | solution.py:401
  53.2 0.1 pad_add_fusion.refs_0_
  53.3 0.0 collective-permute-done.6.refs_2_
  53.3 2.0 %collective-permute-start.9 = (bf16[1,128,1024]{2,1,0:T(8,128)(2,1)S(1)}, bf16[1,128,1024]{2,1,0:T(8,128)(2,1)S(1)}, u32[]{:S(2)}, u32[]{:S(2)}) collective-permute-start(bf16[1,128,1024]{2,1,0:T(8,128)(2,1)S(1)} %slice.41), channel_id=1, source_target_pairs={{0,2},{1,3},{2,0},{3,1},{4,6},{5,7},{6,4},{7,5},{8,10},{9,11},{10,... | collective-permute-start | bytes 786440 | tf_op jit(solution)/shard_map/ppermute | solution.py:318
  55.4 0.0 collective-permute-done.7.refs_3_
  55.4 1.5 %collective-permute-start.8 = (bf16[1,128,1024]{2,1,0:T(8,128)(2,1)S(1)}, bf16[1,128,1024]{2,1,0:T(8,128)(2,1)S(1)}, u32[]{:S(2)}, u32[]{:S(2)}) collective-permute-start(bf16[1,128,1024]{2,1,0:T(8,128)(2,1)S(1)} %slice.40), channel_id=1, source_target_pairs={{0,1},{1,0},{2,3},{3,2},{4,5},{5,4},{6,7},{7,6},{8,9},{9,8},{10,11... | collective-permute-start | bytes 786440 | tf_op jit(solution)/shard_map/ppermute | solution.py:318
  56.9 0.7 slice_bitcast_fusion
  57.7 1.0 copy-done.7
  58.7 6.2 %back_part.1.refs_1_ = f32[256,1024]{1,0:T(8,128)S(1)} custom-call(s32[3]{0:T(128)S(1)} %pad_add_fusion.refs_0_, bf16[1,256,1024]{2,1,0:T(8,128)(2,1)S(1)} %bitcast.41, bf16[1,256,1024]{2,1,0:T(8,128)(2,1)S(1)} %collective-permute-done.6.refs_2_, bf16[1,256,1024]{2,1,0:T(8,128)(2,1)S(1)} %collective-permute-done.7.refs_3_, bf16[1024,4096]{1,0:T(8,128)(2,1)} %refs_3_.1), custom_call_target="tpu_custom_call" | custom-call | flops 1610612736 | bytes 6291456 | tf_op jit(solution)/shard_map/back_part/pallas_call | solution.py:298
  64.9 17.7 %collective-permute-done.9 = bf16[1,128,1024]{2,1,0:T(8,128)(2,1)S(1)} collective-permute-done((bf16[1,128,1024]{2,1,0:T(8,128)(2,1)S(1)}, bf16[1,128,1024]{2,1,0:T(8,128)(2,1)S(1)}, u32[]{:S(2)}, u32[]{:S(2)}) %collective-permute-start.9) | collective-permute-done | bytes 262176 | tf_op jit(solution)/shard_map/ppermute | solution.py:318
  82.6 0.0 collective-permute-done.8
  82.7 4.6 %back_last.1 = (f32[2048,128]{1,0:T(8,128)S(1)}, f32[2048,128]{1,0:T(8,128)S(1)}, f32[16,8,128]{2,1,0:T(8,128)S(1)}) custom-call(s32[1]{0:T(128)} %bitcast.2.refs_0_, f32[256,1024]{1,0:T(8,128)S(1)} %back_part.1.refs_1_, bf16[1,256,1024]{2,1,0:T(8,128)(2,1)S(1)} %pad_maximum_fusion.refs_2_, bf16[1024,4096]{1,0:T(8,128)(2,1)} %refs_3_.1, ...), custom_call_target="tpu_custom_call" | custom-call | flops 536870912 | bytes 4194304 | tf_op jit(solution)/shard_map/back_last/pallas_call | solution.py:298
  87.4 1.4 %collective-permute-start.10 = (f32[4,48,128]{2,1,0:T(8,128)S(1)}, f32[4,48,128]{2,1,0:T(8,128)S(1)}, u32[]{:S(2)}, u32[]{:S(2)}) collective-permute-start(f32[4,48,128]{2,1,0:T(8,128)S(1)} %pad_maximum_fusion.1), channel_id=1, source_target_pairs={{4,0},{8,4},{12,8},{16,12},{20,16},{24,20},{28,24},{5,1},{9,5},{13... | collective-permute-start | bytes 294920 | tf_op jit(solution)/shard_map/ppermute | solution.py:313
  88.8 2.3 %back_local_conv.1.refs_1_ = f32[2048,128]{1,0:T(8,128)S(1)} custom-call(f32[2048,128]{1,0:T(8,128)S(1)} %get-tuple-element.22.signal_ref, f32[16,8,128]{2,1,0:T(8,128)S(1)} %bitcast.33, f32[16,8,128]{2,1,0:T(8,128)S(1)} %bitcast.37), custom_call_target="tpu_custom_call" | custom-call | flops 16777216 | bytes 2097152 | tf_op jit(solution)/shard_map/back_local_conv/pallas_call | solution.py:298
  91.1 15.5 %all-gather = f32[128,8,128]{2,1,0:T(8,128)S(1)} all-gather(f32[16,8,128]{2,1,0:T(8,128)S(1)} %get-tuple-element.21), channel_id=2, replica_groups=mesh['ctx'=8,'ch'=4] {'ctx'}, dimensions={0}, use_global_device_ids=true | all-gather | bytes 589824 | tf_op jit(solution)/shard_map/all_gather | solution.py:342
  106.6 0.2 select_reduce_fusion.refs_0_
  106.8 0.0 collective-permute-done.10.refs_8_
  106.8 5.0 %finish.1 = (bf16[256,1024]{1,0:T(8,128)(2,1)}, bf16[256,1024]{1,0:T(8,128)(2,1)}, bf16[256,1024]{1,0:T(8,128)(2,1)}) custom-call(f32[16,8,128]{2,1,0:T(8,128)S(1)} %select_reduce_fusion.refs_0_, f32[2048,128]{1,0:T(8,128)S(1)} %back_local_conv.1.refs_1_, f32[16,8,128]{2,1,0:T(8,128)S(1)} %bitcast.34, f32[16,8,128]{2,1,0:T(8,128)S(1)} %bitcast.38, ...), custom_call_target="tpu_custom_call" | custom-call | flops 20971520 | bytes 8388608 | tf_op jit(solution)/shard_map/finish/pallas_call | solution.py:298
  111.8 2.9 %reduce_sum.21 = bf16[256,1024]{1,0:T(8,128)(2,1)} reduce(bf16[4,256,1024]{2,1,0:T(8,128)(2,1)} %all-to-all-done, bf16[]{:T(256)} %constant.6.clone.1), dimensions={0}, to_apply=%region_0.1 | reduce | flops 786432 | bytes 2621442 | tf_op jit(solution)/shard_map/reduce_sum | solution.py:402
  (22 shorter events, 0.2 us)
Async XLA Ops:
  0.6 52.7 %collective-permute-start.6 = (bf16[1,256,1024]{2,1,0:T(8,128)(2,1)}, bf16[1,256,1024]{2,1,0:T(8,128)(2,1)S(1)}, u32[]{:S(2)}, u32[]{:S(2)}) collective-permute-start(bf16[1,256,1024]{2,1,0:T(8,128)(2,1)} %bitcast.39), channel_id=1, source_target_pairs={{0,1},{1,0},{2,3},{3,2},{4,5},{5,4},{6,7},{7,6},{8,9},{9,8},{10,11... | collective-permute-start | bytes 1572872 | tf_op jit(solution)/shard_map/ppermute | solution.py:318
  3.6 51.7 %collective-permute-start.7 = (bf16[1,256,1024]{2,1,0:T(8,128)(2,1)}, bf16[1,256,1024]{2,1,0:T(8,128)(2,1)S(1)}, u32[]{:S(2)}, u32[]{:S(2)}) collective-permute-start(bf16[1,256,1024]{2,1,0:T(8,128)(2,1)} %bitcast.40), channel_id=1, source_target_pairs={{0,2},{1,3},{2,0},{3,1},{4,6},{5,7},{6,4},{7,5},{8,10},{9,11},{10,... | collective-permute-start | bytes 1572872 | tf_op jit(solution)/shard_map/ppermute | solution.py:318
  7.4 4.0 %collective-permute-start = (bf16[18,1024]{1,0:T(8,128)(2,1)S(1)}, bf16[18,1024]{1,0:T(8,128)(2,1)S(1)}, u32[]{:S(2)}, u32[]{:S(2)}) collective-permute-start(bf16[18,1024]{1,0:T(8,128)(2,1)S(1)} %pad_maximum_fusion.2), channel_id=1, source_target_pairs={{0,4},{4,8},{8,12},{12,16},{16,20},{20,24},{24,28},{1,5},{5,9},{9,... | collective-permute-start | bytes 110600 | tf_op jit(solution)/shard_map/ppermute | solution.py:313
  11.4 1.0 copy-start.4
  12.4 1.0 copy-start.5
  13.5 1.0 copy-start.6
  18.2 1.0 copy-start
  19.1 7.4 %collective-permute-start.2 = (f32[16,8,128]{2,1,0:T(8,128)S(1)}, f32[16,8,128]{2,1,0:T(8,128)S(1)}, u32[]{:S(2)}, u32[]{:S(2)}) collective-permute-start(f32[16,8,128]{2,1,0:T(8,128)S(1)} %get-tuple-element.17), channel_id=1, source_target_pairs={{0,8},{4,12},{8,16},{12,20},{16,24},{20,28},{1,9},{5,13},{9,17},{1... | collective-permute-start | bytes 196616 | tf_op jit(solution)/shard_map/ppermute | solution.py:313
  24.0 3.4 %collective-permute-start.1 = (f32[16,8,128]{2,1,0:T(8,128)S(1)}, f32[16,8,128]{2,1,0:T(8,128)S(1)}, u32[]{:S(2)}, u32[]{:S(2)}) collective-permute-start(f32[16,8,128]{2,1,0:T(8,128)S(1)} %get-tuple-element.17), channel_id=1, source_target_pairs={{0,4},{4,8},{8,12},{12,16},{16,20},{20,24},{24,28},{1,5},{5,9},{9,... | collective-permute-start | bytes 196616 | tf_op jit(solution)/shard_map/ppermute | solution.py:313
  27.5 12.2 %collective-permute-start.3 = (f32[16,8,128]{2,1,0:T(8,128)S(1)}, f32[16,8,128]{2,1,0:T(8,128)S(1)}, u32[]{:S(2)}, u32[]{:S(2)}) collective-permute-start(f32[16,8,128]{2,1,0:T(8,128)S(1)} %get-tuple-element.31), channel_id=1, source_target_pairs={{0,4},{4,8},{8,12},{12,16},{16,20},{20,24},{24,28},{1,5},{5,9},{9,... | collective-permute-start | bytes 196616 | tf_op jit(solution)/shard_map/ppermute | solution.py:313
  30.9 8.8 %collective-permute-start.4 = (f32[16,8,128]{2,1,0:T(8,128)S(1)}, f32[16,8,128]{2,1,0:T(8,128)S(1)}, u32[]{:S(2)}, u32[]{:S(2)}) collective-permute-start(f32[16,8,128]{2,1,0:T(8,128)S(1)} %get-tuple-element.31), channel_id=1, source_target_pairs={{0,16},{4,20},{8,24},{12,28},{1,17},{5,21},{9,25},{13,29},{2,18},{... | collective-permute-start | bytes 196616 | tf_op jit(solution)/shard_map/ppermute | solution.py:313
  36.1 3.6 %collective-permute-start.5 = (f32[16,8,128]{2,1,0:T(8,128)S(1)}, f32[16,8,128]{2,1,0:T(8,128)S(1)}, u32[]{:S(2)}, u32[]{:S(2)}) collective-permute-start(f32[16,8,128]{2,1,0:T(8,128)S(1)} %get-tuple-element.31), channel_id=1, source_target_pairs={{0,28},{1,29},{2,30},{3,31}} | collective-permute-start | bytes 196616 | tf_op jit(solution)/shard_map/ppermute | solution.py:313
  47.8 1.0 copy-start.2
  48.8 63.0 %all-to-all-start = ((bf16[4,256,1024]{2,1,0:T(8,128)(2,1)}), bf16[4,256,1024]{2,1,0:T(8,128)(2,1)}, u32[]{:S(2)}, u32[]{:S(2)}) async-start(bf16[4,256,1024]{2,1,0:T(8,128)(2,1)} %get-tuple-element.20), calls=%async_computation | async-start | bytes 4194304 | tf_op jit(solution)/shard_map/all_to_all | solution.py:401
  53.3 29.3 %collective-permute-start.9 = (bf16[1,128,1024]{2,1,0:T(8,128)(2,1)S(1)}, bf16[1,128,1024]{2,1,0:T(8,128)(2,1)S(1)}, u32[]{:S(2)}, u32[]{:S(2)}) collective-permute-start(bf16[1,128,1024]{2,1,0:T(8,128)(2,1)S(1)} %slice.41), channel_id=1, source_target_pairs={{0,2},{1,3},{2,0},{3,1},{4,6},{5,7},{6,4},{7,5},{8,10},{9,11},{10,... | collective-permute-start | bytes 786440 | tf_op jit(solution)/shard_map/ppermute | solution.py:318
  55.4 27.3 %collective-permute-start.8 = (bf16[1,128,1024]{2,1,0:T(8,128)(2,1)S(1)}, bf16[1,128,1024]{2,1,0:T(8,128)(2,1)S(1)}, u32[]{:S(2)}, u32[]{:S(2)}) collective-permute-start(bf16[1,128,1024]{2,1,0:T(8,128)(2,1)S(1)} %slice.40), channel_id=1, source_target_pairs={{0,1},{1,0},{2,3},{3,2},{4,5},{5,4},{6,7},{7,6},{8,9},{9,8},{10,11... | collective-permute-start | bytes 786440 | tf_op jit(solution)/shard_map/ppermute | solution.py:318
  57.7 1.0 copy-start.7
  82.7 4.6 %copy-start.3 = (f32[2048,128]{1,0:T(8,128)S(1)}, f32[2048,128]{1,0:T(8,128)}, u32[]{:S(2)}) copy-start(f32[2048,128]{1,0:T(8,128)} %copy-done.2) | copy-start | bytes 3145732
  87.3 19.5 %copy-start.1 = (f32[2048,128]{1,0:T(8,128)S(1)}, f32[2048,128]{1,0:T(8,128)}, u32[]{:S(2)}) copy-start(f32[2048,128]{1,0:T(8,128)} %copy-done) | copy-start | bytes 3145732
  87.4 19.4 %collective-permute-start.10 = (f32[4,48,128]{2,1,0:T(8,128)S(1)}, f32[4,48,128]{2,1,0:T(8,128)S(1)}, u32[]{:S(2)}, u32[]{:S(2)}) collective-permute-start(f32[4,48,128]{2,1,0:T(8,128)S(1)} %pad_maximum_fusion.1), channel_id=1, source_target_pairs={{4,0},{8,4},{12,8},{16,12},{20,16},{24,20},{28,24},{5,1},{9,5},{13... | collective-permute-start | bytes 294920 | tf_op jit(solution)/shard_map/ppermute | solution.py:313
where the time goes:
time: 116 us; the launch traced here: 115 us
  starting transfers between devices  32.5 us (28%)
  Pallas kernels  32.1 us (28%)
  waiting for transfers between devices  18.6 us (16%)
  blocking collectives  15.5 us (13%)
  local copies, waits for them, and re-layouts  10.9 us (9%)
  other arithmetic  4.2 us (4%)
    pallas_call x7, Pallas kernels, call(): pl.pallas_call(kernel, out_shape=[jax.ShapeDtypeStruct(shape, kind) for s...  32.1 us
    ppermute x7, starting transfers between devices, shift(): return lax.ppermute(value, axis, pairs)  20 us
    ppermute x4, waiting for transfers between devices, exchange(): return lax.ppermute(value, axis, [(s, s ^ mask) for s in range(count)])  17.7 us
    all_gather x1, blocking collectives, gathered_state(): everyone = lax.all_gather(state, 'ctx', axis=0, tiled=False)  15.5 us
    ppermute x4, starting transfers between devices, exchange(): return lax.ppermute(value, axis, [(s, s ^ mask) for s in range(count)])  8.09 us
    unnamed x18, local copies, waits for them, and re-layouts  6.99 us
    all_to_all x1, starting transfers between devices, shards(): lax.all_to_all(partial_sums, 'ch', split_axis=0, concat_axis=0, tiled=True)  4.44 us
    reduce_sum x1, other arithmetic, shards(): projected = jnp.sum(arrived.astype(F32), axis=0).astype(BF16)  2.92 us
  transfers between devices with their start and end apart: 12, of which 2 were waited for; matrix products, arithmetic and copies ran while one was open for 5% of the time, Pallas kernels for 28%

commit v1 on v0

v1 whole, which is shorter than its diff:
```python
import functools

import jax
import jax.numpy as jnp
from jax import lax
from jax.experimental import pallas as pl
from jax.experimental.pallas import tpu as pltpu
from jax.sharding import PartitionSpec as P

SUB = 8
LANES = 128
STEP = 8
F32 = jnp.float32
BF16 = jnp.bfloat16
VMEM_LIMIT = 48 * 1024 * 1024


def as_tiles(rows):
    return rows.reshape(rows.shape[0] // SUB, SUB, LANES)


def as_rows(tiles):
    return tiles.reshape(tiles.shape[0] * SUB, LANES)


def tile(ref, token):
    return ref[pl.ds(pl.multiple_of(token * SUB, SUB), SUB), :]


def tree_sum(terms):
    while len(terms) > 1:
        terms = [
            terms[i] + terms[i + 1] if i + 1 < len(terms) else terms[i]
            for i in range(0, len(terms), 2)
        ]
    return terms[0]


def round16(value):
    return value.astype(BF16).astype(F32)


def scatter_tokens(ref, value, first_token):
    tokens, channels = value.shape
    for group in range(channels // LANES):
        ref[pl.ds(first_token * SUB + group, tokens, stride=SUB), :] = value[
            :, group * LANES : (group + 1) * LANES
        ]


def gather_tokens(ref, out_ref):
    tokens, channels = out_ref.shape
    for group in range(channels // LANES):
        out_ref[:, group * LANES : (group + 1) * LANES] = ref[
            pl.ds(group, tokens, stride=SUB), :
        ].astype(out_ref.dtype)


def advance_states(signal_ref, factors, states, first, count, reverse):
    last = signal_ref.shape[0] // SUB - 1

    def body(step, states):
        for inner in range(STEP):
            token = first + step * STEP + inner
            u = tile(signal_ref, last - token if reverse else token)
            states = [factor * state + u for factor, state in zip(factors, states)]
        return states

    return lax.fori_loop(0, count // STEP, body, states)


def zero_states(modes):
    return [jnp.zeros((SUB, LANES), F32) for _ in range(modes)]


def mode_rows(n):
    return slice(n * SUB, (n + 1) * SUB)


def fades(decay_ref, tokens):
    return [
        jnp.exp(-decay_ref[mode_rows(n), :] * tokens) for n in range(decay_ref.shape[0] // SUB)
    ]


def write_messages(out_ref, states, decay_ref, position_ref, tokens, direction):
    for other in range(out_ref.shape[0]):
        gap = direction * (other - position_ref[0]) - 1
        span = (jnp.maximum(gap, 0) * tokens).astype(F32)
        factor = jnp.where(gap >= 0, 1.0, 0.0).astype(F32)
        rows = [
            state * (fade * factor) for state, fade in zip(states, fades(decay_ref, span))
        ]
        out_ref[other] = jnp.concatenate(rows, axis=0).astype(out_ref.dtype)


def read_messages(in_ref):
    total = in_ref[0].astype(F32)
    for other in range(1, in_ref.shape[0]):
        total = total + in_ref[other].astype(F32)
    return [total[mode_rows(n)] for n in range(total.shape[0] // SUB)]


def rim_kernel(q_ref, k_ref, v_ref, out_ref):
    rows = q_ref.shape[0]
    for stream, source in enumerate((q_ref, k_ref, v_ref)):
        out_ref[stream * rows : (stream + 1) * rows, :] = source[...]


def filtered(window, taps_ref, stream, taps, steps, forward):
    total = None
    for tap in range(taps):
        first = taps - 1 - tap if forward else tap
        term = taps_ref[pl.ds((tap * 3 + stream) * SUB, SUB), :] * window[first : first + steps]
        total = term if total is None else total + term
    return total


def featurize_kernel(
    q_ref, k_ref, v_ref, taps_in_ref, residue_in_ref, decay_in_ref,
    qf_ref, kf_ref, vf_ref, mixed_ref, state_ref, taps_ref, scale_ref, decay_ref,
    narrow_ref, wide_ref, sems,
):
    tokens = q_ref.shape[0]
    taps = taps_in_ref.shape[0]
    modes = decay_in_ref.shape[1]
    sources = (q_ref, k_ref, v_ref)
    copies = [
        pltpu.make_async_copy(source, narrow_ref.at[stream], sems.at[stream])
        for stream, source in enumerate(sources)
    ]
    for copy in copies:
        copy.start()
    decays = decay_in_ref[...]
    scatter_tokens(decay_ref, decays.T, 0)
    scatter_tokens(scale_ref, (residue_in_ref[...] * jnp.sqrt(decays)).T, 0)
    for tap in range(taps):
        scatter_tokens(taps_ref, taps_in_ref[tap], tap * 3)
    for stream in range(3):
        copies[stream].wait()
        scatter_tokens(wide_ref.at[stream], narrow_ref[stream].astype(F32), 0)

    def body(step, carry):
        begin = pl.multiple_of((step + 1) * STEP * SUB, SUB)
        before = pl.multiple_of(begin - (taps - 1) * SUB, SUB)
        rows = pl.ds(begin, STEP * SUB)
        feats = []
        for stream, feat_ref in enumerate((qf_ref, kf_ref, vf_ref)):
            window = as_tiles(wide_ref[stream, pl.ds(before, (STEP + taps - 1) * SUB), :])
            feats.append(filtered(window, taps_ref, stream, taps, STEP, True))
            feat_ref[rows, :] = as_rows(feats[-1])
        mixed_ref[rows, :] = as_rows(round16(feats[1] * feats[2]))
        return carry

    lax.fori_loop(0, tokens // STEP - 1, body, 0)
    states = advance_states(
        mixed_ref, fades(decay_ref, 1.0), zero_states(modes), STEP, tokens - STEP, False
    )
    for n in range(modes):
        state_ref[mode_rows(n), :] = states[n]


def first_tokens_kernel(
    position_ref, q_ref, k_ref, v_ref, halo_ref, taps_ref, decay_ref, state_ref,
    qf_in, kf_in, vf_in, mixed_in, qf_ref, kf_ref, vf_ref, mixed_ref, message_ref,
    wide_ref, head_ref, sems, *, tokens, taps,
):
    rim = taps - 1
    modes = decay_ref.shape[0] // SUB
    block = q_ref.shape[0]
    copies = []
    feats = []
    for stream, source in enumerate((q_ref, k_ref, v_ref)):
        behind = halo_ref[stream * block : (stream + 1) * block, :].astype(F32)
        scatter_tokens(wide_ref, behind[block - rim :], 0)
        scatter_tokens(wide_ref, source[...].astype(F32)[:STEP], rim)
        window = as_tiles(wide_ref[...])
        feats.append(filtered(window, taps_ref, stream, taps, STEP, True))
        head_ref[stream] = as_rows(feats[-1])
    head_ref[3] = as_rows(round16(feats[1] * feats[2]))
    for stream, target in enumerate((qf_ref, kf_ref, vf_ref, mixed_ref)):
        copies.append(
            pltpu.make_async_copy(
                head_ref.at[stream], target.at[pl.ds(0, STEP * SUB), :], sems.at[stream]
            )
        )
        copies[-1].start()
    states = advance_states(
        head_ref.at[3], fades(decay_ref, 1.0), zero_states(modes), 0, STEP, False
    )
    later = fades(decay_ref, float(tokens - STEP))
    states = [
        state * fade + state_ref[mode_rows(n), :]
        for n, (state, fade) in enumerate(zip(states, later))
    ]
    write_messages(message_ref, states, decay_ref, position_ref, tokens, 1)
    for copy in copies:
        copy.wait()


def scales_of(scale_ref):
    return [scale_ref[mode_rows(n), :] for n in range(scale_ref.shape[0] // SUB)]


def local_conv_kernel(signal_ref, decay_ref, scale_ref, out_ref, *, reverse):
    tokens = signal_ref.shape[0] // SUB
    factors = fades(decay_ref, 1.0)
    scales = scales_of(scale_ref)

    def body(step, states):
        for inner in range(STEP):
            token = step * STEP + inner
            token = tokens - 1 - token if reverse else token
            u = tile(signal_ref, token)
            states = [factor * state + u for factor, state in zip(factors, states)]
            out_ref[pl.ds(pl.multiple_of(token * SUB, SUB), SUB), :] = tree_sum(
                [scale * state for scale, state in zip(scales, states)]
            )
        return states

    lax.fori_loop(0, tokens // STEP, body, zero_states(len(factors)))


def add_carried(local_ref, out_ref, states, decay_ref, scale_ref, reverse):
    tokens = local_ref.shape[0] // SUB
    factors = fades(decay_ref, 1.0)
    scaled = [scale * state for scale, state in zip(scales_of(scale_ref), states)]

    def body(step, scaled):
        for inner in range(STEP):
            token = step * STEP + inner
            token = tokens - 1 - token if reverse else token
            scaled = [factor * state for factor, state in zip(factors, scaled)]
            rows = pl.ds(pl.multiple_of(token * SUB, SUB), SUB)
            out_ref[rows, :] = local_ref[rows, :] + tree_sum(list(scaled))
        return scaled

    lax.fori_loop(0, tokens // STEP, body, scaled)


def project_kernel(
    message_ref, local_ref, decay_ref, scale_ref, qf_ref, weight_ref,
    conv_ref, out_ref, rows_ref, gated_ref, held_ref, sems,
):
    parts, _, width = out_ref.shape
    copies = [
        pltpu.make_async_copy(
            weight_ref.at[:, pl.ds(part * width, width)], held_ref.at[part], sems.at[part]
        )
        for part in range(parts)
    ]
    for copy in copies:
        copy.start()
    add_carried(local_ref, conv_ref, read_messages(message_ref), decay_ref, scale_ref, False)
    rows_ref[...] = qf_ref[...] * conv_ref[...]
    gather_tokens(rows_ref, gated_ref)
    block = min(width, 256)
    for part in range(parts):
        copies[part].wait()

        def body(step, carry):
            columns = pl.ds(pl.multiple_of(step * block, block), block)
            out_ref[part, :, columns] = jnp.dot(
                gated_ref[...], held_ref[part, :, columns], preferred_element_type=F32
            ).astype(out_ref.dtype)
            return carry

        lax.fori_loop(0, width // block, body, 0)


def add_parts_kernel(parts_ref, out_ref):
    out_ref[...] = tree_sum([parts_ref[n].astype(F32) for n in range(parts_ref.shape[0])]).astype(
        out_ref.dtype
    )


def back_products(index_ref, piece_refs, weight_ref, held_ref, sems, total_ref, base_ref):
    channels = total_ref.shape[0]
    parts = [(ref, inner) for ref in piece_refs for inner in range(ref.shape[0])]
    width = piece_refs[0].shape[2]
    copies = []
    for number in range(len(parts)):
        first = pl.multiple_of(index_ref[number] * width, width)
        copies.append(
            pltpu.make_async_copy(
                weight_ref.at[:, pl.ds(first, width)], held_ref.at[number], sems.at[number]
            )
        )
        copies[-1].start()
    block = min(channels, 256)
    for number, (ref, inner) in enumerate(parts):
        copies[number].wait()

        def body(step, carry):
            rows = pl.ds(pl.multiple_of(step * block, block), block)
            product = lax.dot_general(
                held_ref[number, rows, :], ref[inner],
                (((1,), (1,)), ((), ())), preferred_element_type=F32,
            )
            before = base_ref if number == 0 else total_ref
            total_ref[rows, :] = product if before is None else before[rows, :] + product
            return carry

        lax.fori_loop(0, channels // block, body, 0)


def back_part_kernel(*refs):
    index_ref, *pieces, weight_ref, total_ref, held_ref, sems = refs
    back_products(index_ref, pieces, weight_ref, held_ref, sems, total_ref, None)


def back_last_kernel(*refs, has_base):
    index_ref, *rest = refs
    (
        position_ref, weight_ref, qf_ref, decay_ref,
        grad_ref, mixed_ref, message_ref, total_ref, held_ref, sems,
    ) = rest[-10:]
    pieces = rest[:-10]
    base_ref = None
    if has_base:
        base_ref, *pieces = pieces
    back_products(index_ref, pieces, weight_ref, held_ref, sems, total_ref, base_ref)
    tokens = total_ref.shape[1]
    scatter_tokens(grad_ref, total_ref[...].T, 0)
    mixed_ref[...] = round16(grad_ref[...] * qf_ref[...])
    modes = decay_ref.shape[0] // SUB
    states = advance_states(
        mixed_ref, fades(decay_ref, 1.0), zero_states(modes), 0, tokens, True
    )
    write_messages(message_ref, states, decay_ref, position_ref, tokens, -1)


def finish_kernel(
    message_ref, local_ref, decay_ref, scale_ref, kf_ref, vf_ref, grad_ref, conv_ref, halo_ref,
    taps_ref, gq_ref, gk_ref, gv_ref, total_ref, wide_ref, rows_ref, *, taps,
):
    rim = taps - 1
    tokens = gq_ref.shape[0]
    states = read_messages(message_ref)
    add_carried(local_ref, total_ref, states, decay_ref, scale_ref, True)

    def body(step, carry):
        rows = pl.ds(pl.multiple_of(step * STEP * SUB, SUB), STEP * SUB)
        wide_ref[0, rows, :] = round16(grad_ref[rows, :] * conv_ref[rows, :])
        wide_ref[1, rows, :] = round16(total_ref[rows, :] * vf_ref[rows, :])
        wide_ref[2, rows, :] = round16(total_ref[rows, :] * kf_ref[rows, :])
        return carry

    lax.fori_loop(0, tokens // STEP, body, 0)
    growth = fades(decay_ref, -1.0)
    scales = scales_of(scale_ref)
    for ahead in range(rim):
        rows = pl.ds((tokens + ahead) * SUB, SUB)
        theirs = pl.ds(ahead * SUB, SUB)
        grad_conv = tree_sum([scale * state for scale, state in zip(scales, states)])
        wide_ref[0, rows, :] = halo_ref[0, theirs, :]
        wide_ref[1, rows, :] = round16(grad_conv * halo_ref[3, theirs, :])
        wide_ref[2, rows, :] = round16(grad_conv * halo_ref[2, theirs, :])
        arrived = halo_ref[1, theirs, :]
        states = [(state - arrived) * grow for state, grow in zip(states, growth)]

    def spread(step, carry):
        first = pl.multiple_of(step * STEP * SUB, SUB)
        for stream in range(3):
            window = as_tiles(wide_ref[stream, pl.ds(first, (STEP + rim) * SUB), :])
            rows_ref[stream, pl.ds(first, STEP * SUB), :] = as_rows(
                filtered(window, taps_ref, stream, taps, STEP, False)
            )
        return carry

    lax.fori_loop(0, tokens // STEP, spread, 0)
    for stream, out_ref in enumerate((gq_ref, gk_ref, gv_ref)):
        gather_tokens(rows_ref.at[stream], out_ref)


IN_VMEM = pl.BlockSpec(memory_space=pltpu.VMEM)
IN_SMEM = pl.BlockSpec(memory_space=pltpu.SMEM)
ANYWHERE = pl.BlockSpec(memory_space=pl.ANY)
HBM_RATE = 3.5e6


def call(kernel, outs, args, specs, scratch, name, micros, out_specs=None, **options):
    return pl.pallas_call(
        kernel,
        out_shape=[jax.ShapeDtypeStruct(shape, kind) for shape, kind in outs],
        in_specs=specs,
        out_specs=out_specs or [IN_VMEM] * len(outs),
        scratch_shapes=scratch,
        compiler_params=pltpu.CompilerParams(vmem_limit_bytes=VMEM_LIMIT),
        cost_estimate=pl.CostEstimate(
            flops=0, bytes_accessed=int(micros * HBM_RATE), transcendentals=0
        ),
        name=name,
        **options,
    )(*args)


def shift(value, axis, steps):
    count = lax.axis_size(axis)
    pairs = [(s, s + steps) for s in range(count) if 0 <= s + steps < count]
    return lax.ppermute(value, axis, pairs)


def exchange(value, axis, mask):
    count = lax.axis_size(axis)
    return lax.ppermute(value, axis, [(s, s ^ mask) for s in range(count)])


def shards(query_in, key_in, value_in, short_taps, residues, decays, out_weight, out_grad):
    tokens, channels = query_in.shape
    taps = short_taps.shape[0]
    rim = taps - 1
    modes = decays.shape[1]
    blocks = lax.axis_size("ctx")
    fans = lax.axis_size("ch")
    mine = lax.axis_index("ch")
    position = lax.axis_index("ctx")[None].astype(jnp.int32)
    tile_shape = (tokens * SUB, LANES)
    mode_shape = (modes * SUB, LANES)
    message_shape = (blocks,) + mode_shape
    streams = (query_in, key_in, value_in)
    rim_rows = 16

    def edge(index):
        return pl.BlockSpec((rim_rows, channels), lambda i: (index, 0))

    (halo,) = call(
        rim_kernel, [((3 * rim_rows, channels), BF16)], streams,
        [edge(tokens // rim_rows - 1)] * 3, [], "rim", 1.0,
        out_specs=[pl.BlockSpec((3 * rim_rows, channels), lambda i: (0, 0))], grid=(1,),
    )
    halo = shift(halo, "ctx", 1)

    query_feat, key_feat, value_feat, mixed, state, tap_tiles, scale_tiles, decay_tiles = call(
        featurize_kernel,
        [(tile_shape, F32)] * 4
        + [(mode_shape, F32), ((taps * 3 * SUB, LANES), F32), (mode_shape, F32), (mode_shape, F32)],
        streams + (short_taps, residues, decays),
        [ANYWHERE] * 3 + [IN_VMEM] * 3,
        [
            pltpu.VMEM((3, tokens, channels), BF16),
            pltpu.VMEM((3,) + tile_shape, F32),
            pltpu.SemaphoreType.DMA((3,)),
        ],
        "featurize", 4.0,
    )
    whole = lambda shape: pl.BlockSpec(shape, lambda i: (0,) * len(shape))
    query_feat, key_feat, value_feat, mixed, messages = call(
        functools.partial(first_tokens_kernel, tokens=tokens, taps=taps),
        [(tile_shape, F32)] * 4 + [(message_shape, BF16)],
        (position,) + streams
        + (halo, tap_tiles, decay_tiles, state, query_feat, key_feat, value_feat, mixed),
        [IN_SMEM] + [edge(0)] * 3
        + [whole(halo.shape), whole(tap_tiles.shape), whole(mode_shape), whole(mode_shape)]
        + [ANYWHERE] * 4,
        [
            pltpu.VMEM(((STEP + rim) * SUB, LANES), F32),
            pltpu.VMEM((4, STEP * SUB, LANES), F32),
            pltpu.SemaphoreType.DMA((4,)),
        ],
        "first_tokens", 1.0,
        out_specs=[ANYWHERE] * 4 + [whole(message_shape)], grid=(1,),
        input_output_aliases={8: 0, 9: 1, 10: 2, 11: 3},
    )
    arrived = lax.all_to_all(messages, "ctx", split_axis=0, concat_axis=0, tiled=True)
    (local,) = call(
        functools.partial(local_conv_kernel, reverse=False),
        [(tile_shape, F32)], (mixed, decay_tiles, scale_tiles), [IN_VMEM] * 3, [],
        "local_conv", 2.3,
    )
    conv_out, partial_sums = call(
        project_kernel,
        [(tile_shape, F32), ((fans, tokens, channels), BF16)],
        (arrived, local, decay_tiles, scale_tiles, query_feat, out_weight),
        [IN_VMEM] * 5 + [ANYWHERE],
        [
            pltpu.VMEM(tile_shape, F32),
            pltpu.VMEM((tokens, channels), BF16),
            pltpu.VMEM((fans, channels, channels), BF16),
            pltpu.SemaphoreType.DMA((fans,)),
        ],
        "project", 8.0,
    )
    parts = lax.all_to_all(partial_sums, "ch", split_axis=0, concat_axis=0, tiled=True)
    step_rows = tokens // 4
    (projected,) = call(
        add_parts_kernel, [((tokens, channels), BF16)], (parts,),
        [pl.BlockSpec((fans, step_rows, channels), lambda i: (0, i, 0))], [], "add_parts", 1.5,
        out_specs=[pl.BlockSpec((step_rows, channels), lambda i: (i, 0))],
        grid=(tokens // step_rows,),
    )

    def scratch_for(count):
        return [
            pltpu.VMEM((count, channels, channels), BF16),
            pltpu.SemaphoreType.DMA((count,)),
        ]

    own = out_grad[None]
    if fans == 4:
        near = exchange(own, "ch", 1)
        far = exchange(own, "ch", 2)
        half = tokens // 2
        top = exchange(far[:, :half], "ch", 1)
        bottom = exchange(near[:, half:], "ch", 2)
        across = jnp.concatenate([top, bottom], axis=1)
        first_index = jnp.stack([mine, mine ^ 1, mine ^ 2]).astype(jnp.int32)
        (base,) = call(
            back_part_kernel,
            [((channels, tokens), F32)],
            (first_index, own, near, far, out_weight),
            [IN_SMEM] + [IN_VMEM] * 3 + [ANYWHERE],
            scratch_for(3), "back_part", 5.0,
        )
        pieces, bases, count = [across], [base], 1
        last_index = (mine ^ 3)[None].astype(jnp.int32)
    else:
        pieces, bases, count = [lax.all_gather(out_grad, "ch", axis=0, tiled=False)], [], fans
        last_index = jnp.arange(fans, dtype=jnp.int32)
    grad_gated, grad_mixed, back_messages = call(
        functools.partial(back_last_kernel, has_base=bool(bases)),
        [(tile_shape, F32), (tile_shape, F32), (message_shape, BF16)],
        (last_index, *bases, *pieces, position, out_weight, query_feat, decay_tiles),
        [IN_SMEM] + [IN_VMEM] * (len(bases) + len(pieces)) + [IN_SMEM, ANYWHERE] + [IN_VMEM] * 2,
        [pltpu.VMEM((channels, tokens), F32)] + scratch_for(count),
        "back_last", 4.5,
    )
    back_arrived = lax.all_to_all(back_messages, "ctx", split_axis=0, concat_axis=0, tiled=True)
    (back_local,) = call(
        functools.partial(local_conv_kernel, reverse=True),
        [(tile_shape, F32)], (grad_mixed, decay_tiles, scale_tiles), [IN_VMEM] * 3, [],
        "back_local_conv", 2.3,
    )
    head = slice(0, rim * SUB)
    grad_query_head = (grad_gated[head] * conv_out[head]).astype(BF16).astype(F32)
    ahead = shift(
        jnp.stack([grad_query_head, grad_mixed[head], key_feat[head], value_feat[head]]), "ctx", -1
    )
    grad_query, grad_key, grad_value = call(
        functools.partial(finish_kernel, taps=taps),
        [((tokens, channels), BF16)] * 3,
        (
            back_arrived, back_local, decay_tiles, scale_tiles, key_feat, value_feat,
            grad_gated, conv_out, ahead, tap_tiles,
        ),
        [IN_VMEM] * 10,
        [
            pltpu.VMEM(tile_shape, F32),
            pltpu.VMEM((3, (tokens + rim) * SUB, LANES), F32),
            pltpu.VMEM((3,) + tile_shape, F32),
        ],
        "finish", 5.0,
    )
    return (projected, grad_query, grad_key, grad_value)


def solution(mesh):
    in_specs = (
        P("ctx", "ch"),
        P("ctx", "ch"),
        P("ctx", "ch"),
        P(None, None, "ch"),
        P("ch", None),
        P("ch", None),
        P("ch", None),
        P("ctx", "ch"),
    )
    out_specs = (P("ctx", "ch"), P("ctx", "ch"), P("ctx", "ch"), P("ctx", "ch"))
    return jax.shard_map(shards, mesh=mesh, in_specs=in_specs, out_specs=out_specs, check_vma=False)
```

time: 116 us -> 96 us (0.83)
  blocking collectives: 15.5 us -> 0 us
  starting transfers between devices: 32.5 us -> 22.7 us
  local copies, waits for them, and re-layouts: 10.9 us -> 19.5 us
  Pallas kernels: 32.1 us -> 37.9 us
  waiting for transfers between devices: 18.6 us -> 13.1 us
  other arithmetic: 4.2 us -> 0.88 us
    ppermute x4, waiting for transfers between devices: 17.7 us -> 0.9 us  [exchange(): return lax.ppermute(value, axis, [(s, s ^ mask) for s in range(count)])]
    ppermute x7 -> x2, starting transfers between devices: 20 us -> 3.37 us  [shift(): return lax.ppermute(value, axis, pairs)]
    all_gather x1 -> x0, blocking collectives: 15.5 us -> none  [gathered_state(): everyone = lax.all_gather(state, 'ctx', axis=0, tiled=False)]
    all_to_all x1, waiting for transfers between devices: 0.01 us -> 12.2 us  [shards(): lax.all_to_all(partial_sums, 'ch', split_axis=0, concat_axis=0, tiled=True)]
    all_to_all x0 -> x2, starting transfers between devices: none -> 9.88 us  [the longest x1 5.14 us: shards(): lax.all_to_all(messages, 'ctx', split_axis=0, concat_axis=0, tiled=True)]
    unnamed x18 -> x49, local copies, waits for them, and re-layouts: 6.99 us -> 15.9 us
    pallas_call x7 -> x10, Pallas kernels: 32.1 us -> 37.9 us  [call(): pl.pallas_call(kernel, out_shape=[jax.ShapeDtypeStruct(shape, kind) for s...]
    reduce_sum x2 -> x0, other arithmetic: 3.1 us -> none  [the longest x1 2.92 us: shards(): projected = jnp.sum(arrived.astype(F32), axis=0).astype(BF16)]
  transfers between devices with their start and end apart: 12 -> 9, of which waited for: 2 -> 2; matrix products, arithmetic and copies ran while one was open for 5% -> 8% of each run, Pallas kernels for 28% -> 38%
where the time goes in v1:
time: 96 us; the launch traced here: 95 us
  Pallas kernels  37.9 us (39%)
  starting transfers between devices  22.7 us (24%)
  local copies, waits for them, and re-layouts  19.5 us (20%)
  waiting for transfers between devices  13.1 us (14%)
    pallas_call x10, Pallas kernels, call(): pl.pallas_call(kernel, out_shape=[jax.ShapeDtypeStruct(shape, kind) for s...  37.9 us
    unnamed x49, local copies, waits for them, and re-layouts  15.9 us
    all_to_all x1, waiting for transfers between devices, shards(): lax.all_to_all(partial_sums, 'ch', split_axis=0, concat_axis=0, tiled=True)  12.2 us
    ppermute x4, starting transfers between devices, exchange(): return lax.ppermute(value, axis, [(s, s ^ mask) for s in range(count)])  5.69 us
    all_to_all x1, starting transfers between devices, shards(): lax.all_to_all(messages, 'ctx', split_axis=0, concat_axis=0, tiled=True)  5.14 us
    all_to_all x1, starting transfers between devices, shards(): lax.all_to_all(back_messages, 'ctx', split_axis=0, concat_axis=0, tiled=T...  4.74 us
    all_to_all x1, starting transfers between devices, shards(): lax.all_to_all(partial_sums, 'ch', split_axis=0, concat_axis=0, tiled=True)  3.74 us
    ppermute x2, starting transfers between devices, shift(): return lax.ppermute(value, axis, pairs)  3.37 us
  transfers between devices with their start and end apart: 9, of which 2 were waited for; matrix products, arithmetic and copies ran while one was open for 8% of the time, Pallas kernels for 38%

profile of v1, /device:TPU:0, one launch (start us, length us, event | category | flops | bytes accessed | tf_op | source)
XLA Modules:
  0.0 95.0 jit_solution(4339162502511662873)
XLA Ops:
  0.6 3.0 %collective-permute-start.1 = (bf16[1,256,1024]{2,1,0:T(8,128)(2,1)}, bf16[1,256,1024]{2,1,0:T(8,128)(2,1)}, u32[]{:S(2)}, u32[]{:S(2)}) collective-permute-start(bf16[1,256,1024]{2,1,0:T(8,128)(2,1)} %bitcast.17), channel_id=1, source_target_pairs={{0,1},{1,0},{2,3},{3,2},{4,5},{5,4},{6,7},{7,6},{8,9},{9,8},{10,11... | collective-permute-start | bytes 1572872 | tf_op jit(solution)/shard_map/ppermute | solution.py:406
  3.6 1.5 %collective-permute-start.2 = (bf16[1,256,1024]{2,1,0:T(8,128)(2,1)}, bf16[1,256,1024]{2,1,0:T(8,128)(2,1)}, u32[]{:S(2)}, u32[]{:S(2)}) collective-permute-start(bf16[1,256,1024]{2,1,0:T(8,128)(2,1)} %bitcast.18), channel_id=1, source_target_pairs={{0,2},{1,3},{2,0},{3,1},{4,6},{5,7},{6,4},{7,5},{8,10},{9,11},{10,... | collective-permute-start | bytes 1572872 | tf_op jit(solution)/shard_map/ppermute | solution.py:406
  5.2 1.0 %copy-done = bf16[256,1024]{1,0:T(8,128)(2,1)S(1)} copy-done((bf16[256,1024]{1,0:T(8,128)(2,1)S(1)}, bf16[256,1024]{1,0:T(8,128)(2,1)}, u32[]{:S(2)}) %copy-start) | copy-done | bytes 524312
  6.2 1.0 %copy-done.2 = bf16[256,1024]{1,0:T(8,128)(2,1)S(1)} copy-done((bf16[256,1024]{1,0:T(8,128)(2,1)S(1)}, bf16[256,1024]{1,0:T(8,128)(2,1)}, u32[]{:S(2)}) %copy-start.2) | copy-done | bytes 524312
  7.2 1.0 %copy-done.4 = bf16[256,1024]{1,0:T(8,128)(2,1)S(1)} copy-done((bf16[256,1024]{1,0:T(8,128)(2,1)S(1)}, bf16[256,1024]{1,0:T(8,128)(2,1)}, u32[]{:S(2)}) %copy-start.4) | copy-done | bytes 524312
  8.3 2.1 %collective-permute-start = (bf16[48,1024]{1,0:T(8,128)(2,1)S(1)}, bf16[48,1024]{1,0:T(8,128)(2,1)}, u32[]{:S(2)}, u32[]{:S(2)}) collective-permute-start(bf16[48,1024]{1,0:T(8,128)(2,1)S(1)} %rim.1), channel_id=1, source_target_pairs={{0,4},{4,8},{8,12},{12,16},{16,20},{20,24},{24,28},{1,5},{5,9},{9,... | collective-permute-start | bytes 294920 | tf_op jit(solution)/shard_map/ppermute | solution.py:401
  10.4 1.0 %copy.16.taps_in_ref = f32[7,3,1024]{2,1,0:T(4,128)S(1)} copy(f32[7,3,1024]{2,0,1:T(8,128)} %param.11) | data formatting | bytes 172032 | tf_op args[3]
  11.3 1.0 %copy.17.residue_in_ref = f32[1024,16]{1,0:T(8,128)S(1)} copy(f32[1024,16]{0,1:T(8,128)} %param.12) | data formatting | bytes 131072 | tf_op args[4]
  12.4 1.0 %copy.18.decay_in_ref = f32[1024,16]{1,0:T(8,128)} copy(f32[1024,16]{0,1:T(8,128)S(1)} %copy-done.22) | data formatting | bytes 131072 | tf_op args[5]
  13.4 1.0 %copy-done.12 = f32[1024,16]{1,0:T(8,128)S(1)} copy-done((f32[1024,16]{1,0:T(8,128)S(1)}, f32[1024,16]{1,0:T(8,128)}, u32[]{:S(2)}) %copy-start.12) | copy-done | bytes 65560
  14.4 4.9 %featurize.1 = (f32[2048,128]{1,0:T(8,128)S(1)}, f32[2048,128]{1,0:T(8,128)S(1)}, f32[2048,128]{1,0:T(8,128)S(1)}, f32[2048,128]{1,0:T(8,128)}, f32[128,128]{1,0...) custom-call(bf16[256,1024]{1,0:T(8,128)(2,1)S(1)} %copy-done.1, ...), custom_call_target="tpu_custom_call" | custom-call | bytes 14000000 | tf_op jit(solution)/shard_map/featurize/pallas_call | solution.py:383
  19.4 0.0 copy-start.20
  19.4 0.0 copy-start.19
  19.4 2.5 %first_tokens.1 = (f32[2048,128]{1,0:T(8,128)S(1)}, f32[2048,128]{1,0:T(8,128)S(1)}, f32[2048,128]{1,0:T(8,128)S(1)}, f32[2048,128]{1,0:T(8,128)}, bf16[8,128,128]{2,1,0:T(8,128)(2,1)}) custom-call(s32[1]{0:T(128)} %bitcast.position_ref.refs_3_, ...), custom_call_target="tpu_custom_call", output_to_operand_aliasing={{0}: (8, {}), {1}: (9, {}), {2}: (10, {}), {3}: (11, {})} | custom-call | bytes 3500000 | tf_op jit(solution)/shard_map/first_tokens/pallas_call | solution.py:383
  22.0 1.0 %copy-done.6 = f32[2048,128]{1,0:T(8,128)} copy-done((f32[2048,128]{1,0:T(8,128)}, f32[2048,128]{1,0:T(8,128)S(1)}, u32[]{:S(2)}) %copy-start.6) | copy-done | bytes 1048600
  23.0 1.0 %copy-done.8 = f32[2048,128]{1,0:T(8,128)} copy-done((f32[2048,128]{1,0:T(8,128)}, f32[2048,128]{1,0:T(8,128)S(1)}, u32[]{:S(2)}) %copy-start.8) | copy-done | bytes 1048600
  23.9 5.1 %all-to-all-start = ((bf16[8,128,128]{2,1,0:T(8,128)(2,1)}), bf16[8,128,128]{2,1,0:T(8,128)(2,1)S(1)}, u32[]{:S(2)}, u32[]{:S(2)}) async-start(bf16[8,128,128]{2,1,0:T(8,128)(2,1)} %get-tuple-element.32), calls=%async_computation | async-start | bytes 524288 | tf_op jit(solution)/shard_map/all_to_all | solution.py:465
  29.1 0.0 collective-permute-done.1.refs_2_
  29.1 1.0 %slice.29 = bf16[1,128,1024]{2,1,0:T(8,128)(2,1)S(1)} slice(bf16[1,256,1024]{2,1,0:T(8,128)(2,1)} %collective-permute-done.1.refs_2_), slice={[0:1], [128:256], [0:1024]} | slice | bytes 524288 | tf_op jit(solution)/shard_map/slice | solution.py:505
  30.1 0.6 collective-permute-start.4
  30.6 0.0 collective-permute-done.2.refs_3_
  30.6 1.0 %slice.28 = bf16[1,128,1024]{2,1,0:T(8,128)(2,1)S(1)} slice(bf16[1,256,1024]{2,1,0:T(8,128)(2,1)} %collective-permute-done.2.refs_3_), slice={[0:1], [0:128], [0:1024]} | slice | bytes 524288 | tf_op jit(solution)/shard_map/slice | solution.py:504
  31.6 0.6 collective-permute-start.3
  32.2 0.1 pad_add_fusion.refs_0_
  32.3 6.9 %back_part.1.refs_1_ = f32[1024,256]{1,0:T(8,128)S(1)} custom-call(s32[3]{0:T(128)S(1)} %pad_add_fusion.refs_0_, bf16[1,256,1024]{2,1,0:T(8,128)(2,1)S(1)} %bitcast.19, bf16[1,256,1024]{2,1,0:T(8,128)(2,1)} %collective-permute-done.1.refs_2_, bf16[1,256,1024]{2,1,0:T(8,128)(2,1)} %collective-permute-done.2.refs_3_, bf16[1024,4096]{1,0:T(8,128)(2,1)} %refs_4_.3), custom_call_target="tpu_custom_call" | custom-call | bytes 17500000 | tf_op jit(solution)/shard_map/back_part/pallas_call | solution.py:383
  39.2 0.0 collective-permute-done.4
  39.2 0.9 collective-permute-done.3
  40.1 5.6 %back_last.1 = (f32[2048,128]{1,0:T(8,128)S(1)}, f32[2048,128]{1,0:T(8,128)S(1)}, bf16[8,128,128]{2,1,0:T(8,128)(2,1)}) custom-call(s32[1]{0:T(128)} %bitcast.1.refs_0_, f32[1024,256]{1,0:T(8,128)S(1)} %back_part.1.refs_1_, bf16[1,256,1024]{2,1,0:T(8,128)(2,1)S(1)} %pad_maximum_fusion.refs_2_, s32[1]{0:T(128)} %bitcast.position_ref.refs_3_, ...), custom_call_target="tpu_custom_call" | custom-call | bytes 15750000 | tf_op jit(solution)/shard_map/back_last/pallas_call | solution.py:383
  45.7 1.0 %copy-done.13 = f32[2048,128]{1,0:T(8,128)} copy-done((f32[2048,128]{1,0:T(8,128)}, f32[2048,128]{1,0:T(8,128)S(1)}, u32[]{:S(2)}) %copy-start.13) | copy-done | bytes 1048600
  46.7 1.0 %copy-done.17 = f32[2048,128]{1,0:T(8,128)} copy-done((f32[2048,128]{1,0:T(8,128)}, f32[2048,128]{1,0:T(8,128)S(1)}, u32[]{:S(2)}) %copy-start.17) | copy-done | bytes 1048600
  47.7 0.0 all-to-all-done.message_ref
  47.7 4.7 %all-to-all-start.2 = ((bf16[8,128,128]{2,1,0:T(8,128)(2,1)}), bf16[8,128,128]{2,1,0:T(8,128)(2,1)S(1)}, u32[]{:S(2)}, u32[]{:S(2)}) async-start(bf16[8,128,128]{2,1,0:T(8,128)(2,1)} %get-tuple-element.37), calls=%async_computation.2 | async-start | bytes 524288 | tf_op jit(solution)/shard_map/all_to_all | solution.py:528
  52.5 2.3 %local_conv.1.local_ref = f32[2048,128]{1,0:T(8,128)S(1)} custom-call(f32[2048,128]{1,0:T(8,128)S(1)} %copy-done.10, f32[128,128]{1,0:T(8,128)S(1)} %get-tuple-element.26.decay_ref.refs_6_, f32[128,128]{1,0:T(8,128)S(1)} %get-tuple-element.34.scale_ref), custom_call_target="tpu_custom_call" | custom-call | bytes 8049999 | tf_op jit(solution)/shard_map/local_conv/pallas_call | solution.py:383
  54.8 6.8 %project.1 = (f32[2048,128]{1,0:T(8,128)S(1)}, bf16[4,256,1024]{2,1,0:T(8,128)(2,1)S(1)}) custom-call(bf16[8,128,128]{2,1,0:T(8,128)(2,1)S(1)} %all-to-all-done.message_ref, f32[2048,128]{1,0:T(8,128)S(1)} %local_conv.1.local_ref, f32[128,128]{1,0:T(8,128)S(1)} %get-tuple-element.26.decay_ref.refs_6_, f32[128,128]{1,0:T(8,128)S(1)} %get-tuple-element.34.scale_ref, ...), custom_call_target="tpu_custom_call" | custom-call | bytes 28000000 | tf_op jit(solution)/shard_map/project/pallas_call | solution.py:383
  61.5 1.3 %copy-done.11 = bf16[4,256,1024]{2,1,0:T(8,128)(2,1)} copy-done((bf16[4,256,1024]{2,1,0:T(8,128)(2,1)}, bf16[4,256,1024]{2,1,0:T(8,128)(2,1)S(1)}, u32[]{:S(2)}) %copy-start.11) | copy-done | bytes 2097176
  62.9 1.0 %copy-done.15 = f32[2048,128]{1,0:T(8,128)} copy-done((f32[2048,128]{1,0:T(8,128)}, f32[2048,128]{1,0:T(8,128)S(1)}, u32[]{:S(2)}) %copy-start.15) | copy-done | bytes 1048600
  63.8 0.0 all-to-all-done.2.message_ref
  63.9 3.7 %all-to-all-start.1 = ((bf16[4,256,1024]{2,1,0:T(8,128)(2,1)}), bf16[4,256,1024]{2,1,0:T(8,128)(2,1)S(1)}, u32[]{:S(2)}, u32[]{:S(2)}) async-start(bf16[4,256,1024]{2,1,0:T(8,128)(2,1)} %copy-done.11), calls=%async_computation.1 | async-start | bytes 4194304 | tf_op jit(solution)/shard_map/all_to_all | solution.py:484
  67.6 0.9 slice_bitcast_fusion
  68.5 0.7 slice_bitcast_fusion.2
  69.3 0.8 fusion.1
  70.0 1.3 %collective-permute-start.5 = (f32[4,48,128]{2,1,0:T(8,128)S(1)}, f32[4,48,128]{2,1,0:T(8,128)S(1)}, u32[]{:S(2)}, u32[]{:S(2)}) collective-permute-start(f32[4,48,128]{2,1,0:T(8,128)S(1)} %pad_maximum_fusion.1), channel_id=1, source_target_pairs={{4,0},{8,4},{12,8},{16,12},{20,16},{24,20},{28,24},{5,1},{9,5},{13... | collective-permute-start | bytes 294920 | tf_op jit(solution)/shard_map/ppermute | solution.py:401
  71.3 1.2 %copy-done.18 = f32[2048,128]{1,0:T(8,128)S(1)} copy-done((f32[2048,128]{1,0:T(8,128)S(1)}, f32[2048,128]{1,0:T(8,128)}, u32[]{:S(2)}) %copy-start.18) | copy-done | bytes 1048600
  72.6 2.3 %back_local_conv.1.local_ref = f32[2048,128]{1,0:T(8,128)S(1)} custom-call(f32[2048,128]{1,0:T(8,128)S(1)} %copy-done.18, f32[128,128]{1,0:T(8,128)S(1)} %get-tuple-element.26.decay_ref.refs_6_, f32[128,128]{1,0:T(8,128)S(1)} %get-tuple-element.34.scale_ref), custom_call_target="tpu_custom_call" | custom-call | bytes 8049999 | tf_op jit(solution)/shard_map/back_local_conv/pallas_call | solution.py:383
  74.9 1.2 %copy-done.16 = f32[2048,128]{1,0:T(8,128)S(1)} copy-done((f32[2048,128]{1,0:T(8,128)S(1)}, f32[2048,128]{1,0:T(8,128)}, u32[]{:S(2)}) %copy-start.16) | copy-done | bytes 1048600
  76.1 5.1 %finish.1 = (bf16[256,1024]{1,0:T(8,128)(2,1)}, bf16[256,1024]{1,0:T(8,128)(2,1)}, bf16[256,1024]{1,0:T(8,128)(2,1)}) custom-call(bf16[8,128,128]{2,1,0:T(8,128)(2,1)S(1)} %all-to-all-done.2.message_ref, f32[2048,128]{1,0:T(8,128)S(1)} %back_local_conv.1.local_ref, f32[128,128]{1,0:T(8,128)S(1)} %get-tuple-element.26.decay_ref.refs_6_, ...), custom_call_target="tpu_custom_call" | custom-call | bytes 17500000 | tf_op jit(solution)/shard_map/finish/pallas_call | solution.py:383
  81.2 12.2 %all-to-all-done.1.parts_ref = bf16[4,256,1024]{2,1,0:T(8,128)(2,1)S(1)} async-done(((bf16[4,256,1024]{2,1,0:T(8,128)(2,1)}), bf16[4,256,1024]{2,1,0:T(8,128)(2,1)S(1)}, u32[]{:S(2)}, u32[]{:S(2)}) %all-to-all-start.1) | async-done | bytes 2097184 | tf_op jit(solution)/shard_map/all_to_all | solution.py:484
  93.4 1.6 %add_parts.1 = bf16[256,1024]{1,0:T(8,128)(2,1)} custom-call(bf16[4,256,1024]{2,1,0:T(8,128)(2,1)S(1)} %all-to-all-done.1.parts_ref), custom_call_target="tpu_custom_call" | custom-call | bytes 5250000 | tf_op jit(solution)/shard_map/add_parts/pallas_call | solution.py:383
  (37 shorter events, 0.1 us)
Async XLA Ops:
  0.6 28.4 %collective-permute-start.1 = (bf16[1,256,1024]{2,1,0:T(8,128)(2,1)}, bf16[1,256,1024]{2,1,0:T(8,128)(2,1)}, u32[]{:S(2)}, u32[]{:S(2)}) collective-permute-start(bf16[1,256,1024]{2,1,0:T(8,128)(2,1)} %bitcast.17), channel_id=1, source_target_pairs={{0,1},{1,0},{2,3},{3,2},{4,5},{5,4},{6,7},{7,6},{8,9},{9,8},{10,11... | collective-permute-start | bytes 1572872 | tf_op jit(solution)/shard_map/ppermute | solution.py:406
  3.6 27.0 %collective-permute-start.2 = (bf16[1,256,1024]{2,1,0:T(8,128)(2,1)}, bf16[1,256,1024]{2,1,0:T(8,128)(2,1)}, u32[]{:S(2)}, u32[]{:S(2)}) collective-permute-start(bf16[1,256,1024]{2,1,0:T(8,128)(2,1)} %bitcast.18), channel_id=1, source_target_pairs={{0,2},{1,3},{2,0},{3,1},{4,6},{5,7},{6,4},{7,5},{8,10},{9,11},{10,... | collective-permute-start | bytes 1572872 | tf_op jit(solution)/shard_map/ppermute | solution.py:406
  5.2 1.0 %copy-start = (bf16[256,1024]{1,0:T(8,128)(2,1)S(1)}, bf16[256,1024]{1,0:T(8,128)(2,1)}, u32[]{:S(2)}) copy-start(bf16[256,1024]{1,0:T(8,128)(2,1)} %q_ref.5) | copy-start | bytes 1572868
  6.2 1.0 %copy-start.2 = (bf16[256,1024]{1,0:T(8,128)(2,1)S(1)}, bf16[256,1024]{1,0:T(8,128)(2,1)}, u32[]{:S(2)}) copy-start(bf16[256,1024]{1,0:T(8,128)(2,1)} %k_ref.5) | copy-start | bytes 1572868
  7.2 1.0 %copy-start.4 = (bf16[256,1024]{1,0:T(8,128)(2,1)S(1)}, bf16[256,1024]{1,0:T(8,128)(2,1)}, u32[]{:S(2)}) copy-start(bf16[256,1024]{1,0:T(8,128)(2,1)} %v_ref.5) | copy-start | bytes 1572868
  8.3 4.1 %copy-start.22 = (f32[1024,16]{0,1:T(8,128)S(1)}, f32[1024,16]{0,1:T(8,128)}, u32[]{:S(2)}) copy-start(f32[1024,16]{0,1:T(8,128)} %param.13) | copy-start | bytes 196612
  8.3 5.1 %copy-start.1 = (bf16[256,1024]{1,0:T(8,128)(2,1)S(1)}, bf16[256,1024]{1,0:T(8,128)(2,1)}, u32[]{:S(2)}) copy-start(bf16[256,1024]{1,0:T(8,128)(2,1)} %q_ref.5) | copy-start | bytes 1572868
  8.3 5.1 %copy-start.3 = (bf16[256,1024]{1,0:T(8,128)(2,1)S(1)}, bf16[256,1024]{1,0:T(8,128)(2,1)}, u32[]{:S(2)}) copy-start(bf16[256,1024]{1,0:T(8,128)(2,1)} %k_ref.5) | copy-start | bytes 1572868
  8.3 5.1 %copy-start.5 = (bf16[256,1024]{1,0:T(8,128)(2,1)S(1)}, bf16[256,1024]{1,0:T(8,128)(2,1)}, u32[]{:S(2)}) copy-start(bf16[256,1024]{1,0:T(8,128)(2,1)} %v_ref.5) | copy-start | bytes 1572868
  8.3 11.1 %collective-permute-start = (bf16[48,1024]{1,0:T(8,128)(2,1)S(1)}, bf16[48,1024]{1,0:T(8,128)(2,1)}, u32[]{:S(2)}, u32[]{:S(2)}) collective-permute-start(bf16[48,1024]{1,0:T(8,128)(2,1)S(1)} %rim.1), channel_id=1, source_target_pairs={{0,4},{4,8},{8,12},{12,16},{16,20},{20,24},{24,28},{1,5},{5,9},{9,... | collective-permute-start | bytes 294920 | tf_op jit(solution)/shard_map/ppermute | solution.py:401
  13.4 1.0 %copy-start.12 = (f32[1024,16]{1,0:T(8,128)S(1)}, f32[1024,16]{1,0:T(8,128)}, u32[]{:S(2)}) copy-start(f32[1024,16]{1,0:T(8,128)} %copy.18.decay_in_ref) | copy-start | bytes 196612
  19.4 2.6 %copy-start.20 = (f32[168,128]{1,0:T(8,128)}, f32[168,128]{1,0:T(8,128)S(1)}, u32[]{:S(2)}) copy-start(f32[168,128]{1,0:T(8,128)S(1)} %get-tuple-element.25.taps_ref) | copy-start | bytes 258052
  19.4 12.9 %copy-start.19 = (bf16[256,1024]{1,0:T(8,128)(2,1)S(1)}, bf16[256,1024]{1,0:T(8,128)(2,1)}, u32[]{:S(2)}) copy-start(bf16[256,1024]{1,0:T(8,128)(2,1)} %param.15) | copy-start | bytes 1572868
  21.9 1.0 %copy-start.6 = (f32[2048,128]{1,0:T(8,128)}, f32[2048,128]{1,0:T(8,128)S(1)}, u32[]{:S(2)}) copy-start(f32[2048,128]{1,0:T(8,128)S(1)} %get-tuple-element.39.kf_ref) | copy-start | bytes 3145732
  23.0 1.0 %copy-start.8 = (f32[2048,128]{1,0:T(8,128)}, f32[2048,128]{1,0:T(8,128)S(1)}, u32[]{:S(2)}) copy-start(f32[2048,128]{1,0:T(8,128)S(1)} %get-tuple-element.40.vf_ref) | copy-start | bytes 3145732
  23.9 23.8 %all-to-all-start = ((bf16[8,128,128]{2,1,0:T(8,128)(2,1)}), bf16[8,128,128]{2,1,0:T(8,128)(2,1)S(1)}, u32[]{:S(2)}, u32[]{:S(2)}) async-start(bf16[8,128,128]{2,1,0:T(8,128)(2,1)} %get-tuple-element.32), calls=%async_computation | async-start | bytes 524288 | tf_op jit(solution)/shard_map/all_to_all | solution.py:465
  30.1 9.1 %collective-permute-start.4 = (bf16[1,128,1024]{2,1,0:T(8,128)(2,1)S(1)}, bf16[1,128,1024]{2,1,0:T(8,128)(2,1)S(1)}, u32[]{:S(2)}, u32[]{:S(2)}) collective-permute-start(bf16[1,128,1024]{2,1,0:T(8,128)(2,1)S(1)} %slice.29), channel_id=1, source_target_pairs={{0,2},{1,3},{2,0},{3,1},{4,6},{5,7},{6,4},{7,5},{8,10},{9,11},{10,... | collective-permute-start | bytes 786440 | tf_op jit(solution)/shard_map/ppermute | solution.py:406
  31.6 8.5 %collective-permute-start.3 = (bf16[1,128,1024]{2,1,0:T(8,128)(2,1)S(1)}, bf16[1,128,1024]{2,1,0:T(8,128)(2,1)S(1)}, u32[]{:S(2)}, u32[]{:S(2)}) collective-permute-start(bf16[1,128,1024]{2,1,0:T(8,128)(2,1)S(1)} %slice.28), channel_id=1, source_target_pairs={{0,1},{1,0},{2,3},{3,2},{4,5},{5,4},{6,7},{7,6},{8,9},{9,8},{10,11... | collective-permute-start | bytes 786440 | tf_op jit(solution)/shard_map/ppermute | solution.py:406
  40.1 12.3 %copy-start.10 = (f32[2048,128]{1,0:T(8,128)S(1)}, f32[2048,128]{1,0:T(8,128)}, u32[]{:S(2)}) copy-start(f32[2048,128]{1,0:T(8,128)} %get-tuple-element.33.signal_ref) | copy-start | bytes 3145732
  45.7 1.0 %copy-start.13 = (f32[2048,128]{1,0:T(8,128)}, f32[2048,128]{1,0:T(8,128)S(1)}, u32[]{:S(2)}) copy-start(f32[2048,128]{1,0:T(8,128)S(1)} %get-tuple-element.41.grad_ref) | copy-start | bytes 3145732
  46.7 1.0 %copy-start.17 = (f32[2048,128]{1,0:T(8,128)}, f32[2048,128]{1,0:T(8,128)S(1)}, u32[]{:S(2)}) copy-start(f32[2048,128]{1,0:T(8,128)S(1)} %get-tuple-element.38.signal_ref) | copy-start | bytes 3145732
  47.7 16.1 %all-to-all-start.2 = ((bf16[8,128,128]{2,1,0:T(8,128)(2,1)}), bf16[8,128,128]{2,1,0:T(8,128)(2,1)S(1)}, u32[]{:S(2)}, u32[]{:S(2)}) async-start(bf16[8,128,128]{2,1,0:T(8,128)(2,1)} %get-tuple-element.37), calls=%async_computation.2 | async-start | bytes 524288 | tf_op jit(solution)/shard_map/all_to_all | solution.py:528
  61.5 1.4 %copy-start.11 = (bf16[4,256,1024]{2,1,0:T(8,128)(2,1)}, bf16[4,256,1024]{2,1,0:T(8,128)(2,1)S(1)}, u32[]{:S(2)}) copy-start(bf16[4,256,1024]{2,1,0:T(8,128)(2,1)S(1)} %get-tuple-element.36) | copy-start | bytes 6291460
  62.9 1.0 %copy-start.15 = (f32[2048,128]{1,0:T(8,128)}, f32[2048,128]{1,0:T(8,128)S(1)}, u32[]{:S(2)}) copy-start(f32[2048,128]{1,0:T(8,128)S(1)} %get-tuple-element.42.conv_ref) | copy-start | bytes 3145732
  63.9 3.8 %copy-start.7 = (f32[2048,128]{1,0:T(8,128)S(1)}, f32[2048,128]{1,0:T(8,128)}, u32[]{:S(2)}) copy-start(f32[2048,128]{1,0:T(8,128)} %copy-done.6) | copy-start | bytes 3145732
  63.9 29.5 %all-to-all-start.1 = ((bf16[4,256,1024]{2,1,0:T(8,128)(2,1)}), bf16[4,256,1024]{2,1,0:T(8,128)(2,1)S(1)}, u32[]{:S(2)}, u32[]{:S(2)}) async-start(bf16[4,256,1024]{2,1,0:T(8,128)(2,1)} %copy-done.11), calls=%async_computation.1 | async-start | bytes 4194304 | tf_op jit(solution)/shard_map/all_to_all | solution.py:484
  67.6 7.2 %copy-start.9 = (f32[2048,128]{1,0:T(8,128)S(1)}, f32[2048,128]{1,0:T(8,128)}, u32[]{:S(2)}) copy-start(f32[2048,128]{1,0:T(8,128)} %copy-done.8) | copy-start | bytes 3145732
  67.6 7.2 %copy-start.14 = (f32[2048,128]{1,0:T(8,128)S(1)}, f32[2048,128]{1,0:T(8,128)}, u32[]{:S(2)}) copy-start(f32[2048,128]{1,0:T(8,128)} %copy-done.13) | copy-start | bytes 3145732
  70.0 4.8 %collective-permute-start.5 = (f32[4,48,128]{2,1,0:T(8,128)S(1)}, f32[4,48,128]{2,1,0:T(8,128)S(1)}, u32[]{:S(2)}, u32[]{:S(2)}) collective-permute-start(f32[4,48,128]{2,1,0:T(8,128)S(1)} %pad_maximum_fusion.1), channel_id=1, source_target_pairs={{4,0},{8,4},{12,8},{16,12},{20,16},{24,20},{28,24},{5,1},{9,5},{13... | collective-permute-start | bytes 294920 | tf_op jit(solution)/shard_map/ppermute | solution.py:401
  71.3 1.2 %copy-start.18 = (f32[2048,128]{1,0:T(8,128)S(1)}, f32[2048,128]{1,0:T(8,128)}, u32[]{:S(2)}) copy-start(f32[2048,128]{1,0:T(8,128)} %copy-done.17) | copy-start | bytes 3145732
  72.6 2.3 %copy-start.21 = (f32[168,128]{1,0:T(8,128)S(1)}, f32[168,128]{1,0:T(8,128)}, u32[]{:S(2)}) copy-start(f32[168,128]{1,0:T(8,128)} %copy-done.20) | copy-start | bytes 258052
  74.9 1.2 %copy-start.16 = (f32[2048,128]{1,0:T(8,128)S(1)}, f32[2048,128]{1,0:T(8,128)}, u32[]{:S(2)}) copy-start(f32[2048,128]{1,0:T(8,128)} %copy-done.15) | copy-start | bytes 3145732

commit v2 on v1

v2 whole, which is shorter than its diff:
```python
import functools

import jax
import jax.numpy as jnp
from jax import lax
from jax.experimental import pallas as pl
from jax.experimental.pallas import tpu as pltpu
from jax.sharding import PartitionSpec as P

SUB = 8
LANES = 128
STEP = 8
F32 = jnp.float32
BF16 = jnp.bfloat16


def as_tiles(rows):
    return rows.reshape(rows.shape[0] // SUB, SUB, LANES)


def as_rows(tiles):
    return tiles.reshape(tiles.shape[0] * SUB, LANES)


def tile(ref, token):
    return ref[pl.ds(pl.multiple_of(token * SUB, SUB), SUB), :]


def tree_sum(terms):
    while len(terms) > 1:
        terms = [
            terms[i] + terms[i + 1] if i + 1 < len(terms) else terms[i]
            for i in range(0, len(terms), 2)
        ]
    return terms[0]


def round16(value):
    return value.astype(BF16).astype(F32)


def scatter_tokens(ref, value, first_token):
    tokens, channels = value.shape
    for group in range(channels // LANES):
        ref[pl.ds(first_token * SUB + group, tokens, stride=SUB), :] = value[
            :, group * LANES : (group + 1) * LANES
        ]


def gather_tokens(ref, out_ref):
    tokens, channels = out_ref.shape
    for group in range(channels // LANES):
        out_ref[:, group * LANES : (group + 1) * LANES] = ref[
            pl.ds(group, tokens, stride=SUB), :
        ].astype(out_ref.dtype)


def advance_states(signal_ref, factors, states, first, count, reverse):
    last = signal_ref.shape[0] // SUB - 1

    def body(step, states):
        for inner in range(STEP):
            token = first + step * STEP + inner
            u = tile(signal_ref, last - token if reverse else token)
            states = [factor * state + u for factor, state in zip(factors, states)]
        return states

    return lax.fori_loop(0, count // STEP, body, states)


def zero_states(modes):
    return [jnp.zeros((SUB, LANES), F32) for _ in range(modes)]


def mode_rows(n):
    return slice(n * SUB, (n + 1) * SUB)


def fades(decay_ref, tokens):
    return [
        jnp.exp(-decay_ref[mode_rows(n), :] * tokens) for n in range(decay_ref.shape[0] // SUB)
    ]


def write_messages(out_ref, states, decay_ref, position_ref, tokens, direction):
    for other in range(out_ref.shape[0]):
        gap = direction * (other - position_ref[0]) - 1
        span = (jnp.maximum(gap, 0) * tokens).astype(F32)
        factor = jnp.where(gap >= 0, 1.0, 0.0).astype(F32)
        rows = [
            state * (fade * factor) for state, fade in zip(states, fades(decay_ref, span))
        ]
        out_ref[other] = jnp.concatenate(rows, axis=0).astype(out_ref.dtype)


def read_messages(in_ref):
    total = in_ref[0].astype(F32)
    for other in range(1, in_ref.shape[0]):
        total = total + in_ref[other].astype(F32)
    return [total[mode_rows(n)] for n in range(total.shape[0] // SUB)]


def rim_kernel(q_ref, k_ref, v_ref, out_ref, sems):
    rows = out_ref.shape[0] // 3
    copies = [
        pltpu.make_async_copy(
            source.at[pl.ds(source.shape[0] - rows, rows), :],
            out_ref.at[pl.ds(stream * rows, rows), :],
            sems.at[stream],
        )
        for stream, source in enumerate((q_ref, k_ref, v_ref))
    ]
    for copy in copies:
        copy.start()
    for copy in copies:
        copy.wait()


def filtered(window, taps_ref, stream, taps, steps, forward):
    total = None
    for tap in range(taps):
        first = taps - 1 - tap if forward else tap
        term = taps_ref[pl.ds((stream * taps + tap) * SUB, SUB), :] * window[first : first + steps]
        total = term if total is None else total + term
    return total


def featurize_kernel(
    position_ref, q_ref, k_ref, v_ref, taps_in_ref, residue_in_ref, decay_in_ref, halo_ref,
    qf_ref, kf_ref, vf_ref, mixed_ref, message_ref, taps_ref, scale_ref, decay_ref,
    narrow_ref, wide_ref, taps_vmem, residue_vmem, decay_vmem, sems,
):
    tokens = q_ref.shape[0]
    _, taps, _ = taps_in_ref.shape
    rim = taps - 1
    modes = decay_in_ref.shape[0]
    copies = [
        pltpu.make_async_copy(source, target, sems.at[number])
        for number, (source, target) in enumerate(
            (
                (decay_in_ref, decay_vmem),
                (residue_in_ref, residue_vmem),
                (taps_in_ref, taps_vmem),
                (q_ref, narrow_ref.at[0]),
                (k_ref, narrow_ref.at[1]),
                (v_ref, narrow_ref.at[2]),
            )
        )
    ]
    for copy in copies:
        copy.start()
    held = halo_ref.shape[0] // 3
    for stream in range(3):
        behind = halo_ref[stream * held : (stream + 1) * held, :].astype(F32)
        scatter_tokens(wide_ref.at[stream], behind[held - rim :], 0)
    for copy in copies[:3]:
        copy.wait()
    decays = decay_vmem[...]
    scatter_tokens(decay_ref, decays, 0)
    scatter_tokens(scale_ref, residue_vmem[...] * jnp.sqrt(decays), 0)
    for stream in range(3):
        scatter_tokens(taps_ref, taps_vmem[stream], stream * taps)
    for stream in range(3):
        copies[3 + stream].wait()
        scatter_tokens(wide_ref.at[stream], narrow_ref[stream].astype(F32), rim)

    def body(step, carry):
        begin = pl.multiple_of(step * STEP * SUB, SUB)
        rows = pl.ds(begin, STEP * SUB)
        feats = []
        for stream, feat_ref in enumerate((qf_ref, kf_ref, vf_ref)):
            window = as_tiles(wide_ref[stream, pl.ds(begin, (STEP + rim) * SUB), :])
            feats.append(filtered(window, taps_ref, stream, taps, STEP, True))
            feat_ref[rows, :] = as_rows(feats[-1])
        mixed_ref[rows, :] = as_rows(round16(feats[1] * feats[2]))
        return carry

    lax.fori_loop(0, tokens // STEP, body, 0)
    states = advance_states(
        mixed_ref, fades(decay_ref, 1.0), zero_states(modes), 0, tokens, False
    )
    write_messages(message_ref, states, decay_ref, position_ref, tokens, 1)


def scales_of(scale_ref):
    return [scale_ref[mode_rows(n), :] for n in range(scale_ref.shape[0] // SUB)]


def local_conv_kernel(signal_ref, decay_ref, scale_ref, out_ref, *, reverse):
    tokens = signal_ref.shape[0] // SUB
    factors = fades(decay_ref, 1.0)
    scales = scales_of(scale_ref)

    def body(step, states):
        for inner in range(STEP):
            token = step * STEP + inner
            token = tokens - 1 - token if reverse else token
            u = tile(signal_ref, token)
            states = [factor * state + u for factor, state in zip(factors, states)]
            out_ref[pl.ds(pl.multiple_of(token * SUB, SUB), SUB), :] = tree_sum(
                [scale * state for scale, state in zip(scales, states)]
            )
        return states

    lax.fori_loop(0, tokens // STEP, body, zero_states(len(factors)))


def add_carried(local_ref, out_ref, states, decay_ref, scale_ref, reverse):
    tokens = local_ref.shape[0] // SUB
    factors = fades(decay_ref, 1.0)
    scaled = [scale * state for scale, state in zip(scales_of(scale_ref), states)]

    def body(step, scaled):
        for inner in range(STEP):
            token = step * STEP + inner
            token = tokens - 1 - token if reverse else token
            scaled = [factor * state for factor, state in zip(factors, scaled)]
            rows = pl.ds(pl.multiple_of(token * SUB, SUB), SUB)
            out_ref[rows, :] = local_ref[rows, :] + tree_sum(list(scaled))
        return scaled

    lax.fori_loop(0, tokens // STEP, body, scaled)


def project_kernel(
    index_ref, message_ref, local_ref, decay_ref, scale_ref, qf_ref, weight_ref, conv_ref, *refs
):
    *out_refs, rows_ref, gated_ref, held_ref, sems = refs
    width = out_refs[0].shape[1]
    copies = []
    for number in reversed(range(len(out_refs))):
        first = pl.multiple_of(index_ref[number] * width, width)
        copies.append(
            pltpu.make_async_copy(
                weight_ref.at[:, pl.ds(first, width)], held_ref.at[number], sems.at[number]
            )
        )
        copies[-1].start()
    add_carried(local_ref, conv_ref, read_messages(message_ref), decay_ref, scale_ref, False)
    rows_ref[...] = qf_ref[...] * conv_ref[...]
    gather_tokens(rows_ref, gated_ref)
    block = min(width, 256)
    for copy, number in zip(copies, reversed(range(len(out_refs)))):
        out_ref = out_refs[number]
        copy.wait()

        def body(step, carry):
            columns = pl.ds(pl.multiple_of(step * block, block), block)
            out_ref[:, columns] = jnp.dot(
                gated_ref[...], held_ref[number, :, columns], preferred_element_type=F32
            ).astype(out_ref.dtype)
            return carry

        lax.fori_loop(0, width // block, body, 0)


def add_parts_kernel(*refs):
    *part_refs, out_ref = refs
    out_ref[...] = tree_sum([ref[...].astype(F32) for ref in part_refs]).astype(out_ref.dtype)


def back_kernel(
    index_ref, position_ref, weight_ref, qf_ref, kf_ref, vf_ref, conv_ref, decay_ref, *refs, rim
):
    *piece_refs, grad_ref, mixed_ref, message_ref, ahead_ref, turned_ref, total_ref, held_ref, sems = refs
    channels, tokens = total_ref.shape
    width = piece_refs[0].shape[1]

    def fetch(number):
        first = pl.multiple_of(index_ref[number] * width, width)
        return pltpu.make_async_copy(
            weight_ref.at[:, pl.ds(first, width)], held_ref.at[number], sems.at[number]
        )

    for number in range(len(piece_refs)):
        fetch(number).start()
    for number, ref in enumerate(piece_refs):
        turned_ref[number] = ref[...].T
    total_ref[...] = jnp.zeros_like(total_ref)

    def body(number, carry):
        fetch(number).wait()
        total_ref[...] += jnp.dot(
            held_ref[number], turned_ref[number], preferred_element_type=F32
        )
        return carry

    lax.fori_loop(0, len(piece_refs), body, 0)
    scatter_tokens(grad_ref, total_ref[...].T, 0)
    mixed_ref[...] = round16(grad_ref[...] * qf_ref[...])
    head = slice(0, rim * SUB)
    ahead_ref[0] = round16(grad_ref[head, :] * conv_ref[head, :])
    ahead_ref[1] = mixed_ref[head, :]
    ahead_ref[2] = kf_ref[head, :]
    ahead_ref[3] = vf_ref[head, :]
    modes = decay_ref.shape[0] // SUB
    states = advance_states(
        mixed_ref, fades(decay_ref, 1.0), zero_states(modes), 0, tokens, True
    )
    write_messages(message_ref, states, decay_ref, position_ref, tokens, -1)


def finish_kernel(
    message_ref, local_ref, decay_ref, scale_ref, kf_ref, vf_ref, grad_ref, conv_ref, halo_ref,
    taps_ref, gq_ref, gk_ref, gv_ref, total_ref, wide_ref, rows_ref, *, taps,
):
    rim = taps - 1
    tokens = gq_ref.shape[0]
    states = read_messages(message_ref)
    add_carried(local_ref, total_ref, states, decay_ref, scale_ref, True)

    def body(step, carry):
        rows = pl.ds(pl.multiple_of(step * STEP * SUB, SUB), STEP * SUB)
        wide_ref[0, rows, :] = round16(grad_ref[rows, :] * conv_ref[rows, :])
        wide_ref[1, rows, :] = round16(total_ref[rows, :] * vf_ref[rows, :])
        wide_ref[2, rows, :] = round16(total_ref[rows, :] * kf_ref[rows, :])
        return carry

    lax.fori_loop(0, tokens // STEP, body, 0)
    growth = fades(decay_ref, -1.0)
    scales = scales_of(scale_ref)
    for ahead in range(rim):
        rows = pl.ds((tokens + ahead) * SUB, SUB)
        theirs = pl.ds(ahead * SUB, SUB)
        grad_conv = tree_sum([scale * state for scale, state in zip(scales, states)])
        wide_ref[0, rows, :] = halo_ref[0, theirs, :]
        wide_ref[1, rows, :] = round16(grad_conv * halo_ref[3, theirs, :])
        wide_ref[2, rows, :] = round16(grad_conv * halo_ref[2, theirs, :])
        arrived = halo_ref[1, theirs, :]
        states = [(state - arrived) * grow for state, grow in zip(states, growth)]

    def spread(step, carry):
        first = pl.multiple_of(step * STEP * SUB, SUB)
        for stream in range(3):
            window = as_tiles(wide_ref[stream, pl.ds(first, (STEP + rim) * SUB), :])
            rows_ref[stream, pl.ds(first, STEP * SUB), :] = as_rows(
                filtered(window, taps_ref, stream, taps, STEP, False)
            )
        return carry

    lax.fori_loop(0, tokens // STEP, spread, 0)
    for stream, out_ref in enumerate((gq_ref, gk_ref, gv_ref)):
        gather_tokens(rows_ref.at[stream], out_ref)


IN_VMEM = pl.BlockSpec(memory_space=pltpu.VMEM)
IN_SMEM = pl.BlockSpec(memory_space=pltpu.SMEM)
IN_HBM = pl.BlockSpec(memory_space=pltpu.HBM)
HBM_RATE = 3.5e6


def call(kernel, outs, args, specs, scratch, name, micros, mebibytes, out_specs=None, **options):
    args = [
        pltpu.with_memory_space_constraint(arg, pltpu.HBM) if spec is IN_HBM else arg
        for arg, spec in zip(args, specs)
    ]
    return pl.pallas_call(
        kernel,
        out_shape=[jax.ShapeDtypeStruct(shape, kind) for shape, kind in outs],
        in_specs=specs,
        out_specs=out_specs or [IN_VMEM] * len(outs),
        scratch_shapes=scratch,
        compiler_params=pltpu.CompilerParams(vmem_limit_bytes=mebibytes * 1024 * 1024),
        cost_estimate=pl.CostEstimate(
            flops=0, bytes_accessed=int(micros * HBM_RATE), transcendentals=0
        ),
        name=name,
        **options,
    )(*args)


def shift(value, axis, steps):
    count = lax.axis_size(axis)
    pairs = [(s, s + steps) for s in range(count) if 0 <= s + steps < count]
    return lax.ppermute(value, axis, pairs)


def exchange(value, axis, mask):
    count = lax.axis_size(axis)
    return lax.ppermute(value, axis, [(s, s ^ mask) for s in range(count)])


def shards(query_in, key_in, value_in, short_taps, residues, decays, out_weight, out_grad):
    tokens, channels = query_in.shape
    taps = short_taps.shape[0]
    rim = taps - 1
    modes = decays.shape[1]
    blocks = lax.axis_size("ctx")
    fans = lax.axis_size("ch")
    position = lax.axis_index("ctx")[None].astype(jnp.int32)
    tile_shape = (tokens * SUB, LANES)
    mode_shape = (modes * SUB, LANES)
    message_shape = (blocks,) + mode_shape
    streams = (query_in, key_in, value_in)
    rim_rows = 16

    (halo,) = call(
        rim_kernel, [((3 * rim_rows, channels), BF16)], streams, [IN_HBM] * 3,
        [pltpu.SemaphoreType.DMA((3,))], "rim", 1.0, 2,
    )
    halo, out_grad = lax.optimization_barrier((halo, out_grad))
    halo = shift(halo, "ctx", 1)
    if fans == 4:
        order = lax.axis_index("ch") ^ jnp.arange(fans, dtype=jnp.int32)
        pieces = [out_grad] + [exchange(out_grad, "ch", mask) for mask in range(1, fans)]
    else:
        order = jnp.arange(fans, dtype=jnp.int32)
        everyone = lax.all_gather(out_grad, "ch", axis=0, tiled=False)
        pieces = [everyone[number] for number in range(fans)]

    (
        query_feat, key_feat, value_feat, mixed, messages, tap_tiles, scale_tiles, decay_tiles,
    ) = call(
        featurize_kernel,
        [(tile_shape, F32)] * 4
        + [(message_shape, BF16), ((taps * 3 * SUB, LANES), F32), (mode_shape, F32), (mode_shape, F32)],
        (position,) + streams
        + (jnp.transpose(short_taps, (1, 0, 2)), residues.T, decays.T, halo),
        [IN_SMEM] + [IN_HBM] * 6 + [IN_VMEM],
        [
            pltpu.VMEM((3, tokens, channels), BF16),
            pltpu.VMEM((3, (tokens + rim) * SUB, LANES), F32),
            pltpu.VMEM((3, taps, channels), F32),
            pltpu.VMEM((modes, channels), F32),
            pltpu.VMEM((modes, channels), F32),
            pltpu.SemaphoreType.DMA((6,)),
        ],
        "featurize", 4.5, 8,
    )
    arrived = lax.all_to_all(messages, "ctx", split_axis=0, concat_axis=0, tiled=True)
    (local,) = call(
        functools.partial(local_conv_kernel, reverse=False),
        [(tile_shape, F32)], (mixed, decay_tiles, scale_tiles), [IN_VMEM] * 3, [],
        "local_conv", 2.3, 2,
    )
    conv_out, *partial_sums = call(
        project_kernel,
        [(tile_shape, F32)] + [((tokens, channels), BF16)] * fans,
        (order, arrived, local, decay_tiles, scale_tiles, query_feat, out_weight),
        [IN_SMEM] + [IN_VMEM] * 5 + [IN_HBM],
        [
            pltpu.VMEM(tile_shape, F32),
            pltpu.VMEM((tokens, channels), BF16),
            pltpu.VMEM((fans, channels, channels), BF16),
            pltpu.SemaphoreType.DMA((fans,)),
        ],
        "project", 7.0, 14,
    )
    if fans == 4:
        parts = [
            exchange(part, "ch", mask) if mask else part for mask, part in enumerate(partial_sums)
        ]
    else:
        parts = lax.all_to_all(
            jnp.stack(partial_sums), "ch", split_axis=0, concat_axis=0, tiled=True
        )
        parts = [parts[number] for number in range(fans)]
    (projected,) = call(
        add_parts_kernel, [((tokens, channels), BF16)], tuple(parts), [IN_VMEM] * fans, [],
        "add_parts", 1.5, 4,
    )

    grad_gated, grad_mixed, back_messages, ahead = call(
        functools.partial(back_kernel, rim=rim),
        [(tile_shape, F32)] * 2 + [(message_shape, BF16), ((4, rim * SUB, LANES), F32)],
        (
            order, position, out_weight, query_feat, key_feat, value_feat, conv_out, decay_tiles,
            *pieces,
        ),
        [IN_SMEM] * 2 + [IN_HBM] + [IN_VMEM] * (5 + fans),
        [
            pltpu.VMEM((fans, channels, tokens), BF16),
            pltpu.VMEM((channels, tokens), F32),
            pltpu.VMEM((fans, channels, channels), BF16),
            pltpu.SemaphoreType.DMA((fans,)),
        ],
        "back", 8.0, 18,
    )
    back_arrived = lax.all_to_all(back_messages, "ctx", split_axis=0, concat_axis=0, tiled=True)
    ahead = shift(ahead, "ctx", -1)
    (back_local,) = call(
        functools.partial(local_conv_kernel, reverse=True),
        [(tile_shape, F32)], (grad_mixed, decay_tiles, scale_tiles), [IN_VMEM] * 3, [],
        "back_local_conv", 2.3, 2,
    )
    grad_query, grad_key, grad_value = call(
        functools.partial(finish_kernel, taps=taps),
        [((tokens, channels), BF16)] * 3,
        (
            back_arrived, back_local, decay_tiles, scale_tiles, key_feat, value_feat,
            grad_gated, conv_out, ahead, tap_tiles,
        ),
        [IN_VMEM] * 10,
        [
            pltpu.VMEM(tile_shape, F32),
            pltpu.VMEM((3, (tokens + rim) * SUB, LANES), F32),
            pltpu.VMEM((3,) + tile_shape, F32),
        ],
        "finish", 5.0, 10,
    )
    return (projected, grad_query, grad_key, grad_value)


def solution(mesh):
    in_specs = (
        P("ctx", "ch"),
        P("ctx", "ch"),
        P("ctx", "ch"),
        P(None, None, "ch"),
        P("ch", None),
        P("ch", None),
        P("ch", None),
        P("ctx", "ch"),
    )
    out_specs = (P("ctx", "ch"), P("ctx", "ch"), P("ctx", "ch"), P("ctx", "ch"))
    return jax.shard_map(shards, mesh=mesh, in_specs=in_specs, out_specs=out_specs, check_vma=False)
```

time: 96 us -> 83.1 us (0.87)
  local copies, waits for them, and re-layouts: 19.5 us -> 15.2 us
  Pallas kernels: 37.9 us -> 35.3 us
  waiting for transfers between devices: 13.1 us -> 10.5 us
  starting transfers between devices: 22.7 us -> 20.5 us
    all_to_all x1 -> x0, waiting for transfers between devices: 12.2 us -> none  [shards(): lax.all_to_all(partial_sums, 'ch', split_axis=0, concat_axis=0, tiled=True)]
    all_to_all x1, waiting for transfers between devices: 0.01 us -> 6.25 us  [shards(): lax.all_to_all(messages, 'ctx', split_axis=0, concat_axis=0, tiled=True)]
    all_to_all x1, waiting for transfers between devices: 0.01 us -> 4.2 us  [shards(): lax.all_to_all(back_messages, 'ctx', split_axis=0, concat_axis=0, tiled=T...]
    all_to_all x1 -> x0, starting transfers between devices: 3.74 us -> none  [shards(): lax.all_to_all(partial_sums, 'ch', split_axis=0, concat_axis=0, tiled=True)]
    pallas_call x10 -> x8, Pallas kernels: 37.9 us -> 35.3 us  [call(): pl.pallas_call(kernel, out_shape=[jax.ShapeDtypeStruct(shape, kind) for s...]
    slice x2 -> x0, local copies, waits for them, and re-layouts: 1.94 us -> none  [the longest x1 0.97 us: shards(): bottom = exchange(near[:, half:], 'ch', 2)]
    ppermute x4 -> x6, starting transfers between devices: 5.69 us -> 7.48 us  [exchange(): return lax.ppermute(value, axis, [(s, s ^ mask) for s in range(count)])]
    another operation x2 -> x0, local copies, waits for them, and re-layouts: 1.63 us -> none  [shards(): jnp.stack([grad_query_head, grad_mixed[head], key_feat[head], value_feat[...]
  transfers between devices with their start and end apart: 9 -> 10, of which waited for: 2 -> 2; matrix products, arithmetic and copies ran while one was open for 8% -> 0% of each run, Pallas kernels for 38% -> 39%
where the time goes in v2:
time: 83.1 us; the launch traced here: 82.3 us
  Pallas kernels  35.3 us (42%)
  starting transfers between devices  20.5 us (25%)
  local copies, waits for them, and re-layouts  15.2 us (18%)
  waiting for transfers between devices  10.5 us (13%)
    pallas_call x8, Pallas kernels, call(): pl.pallas_call(kernel, out_shape=[jax.ShapeDtypeStruct(shape, kind) for s...  35.3 us
    unnamed x36, local copies, waits for them, and re-layouts  15.2 us
    ppermute x6, starting transfers between devices, exchange(): return lax.ppermute(value, axis, [(s, s ^ mask) for s in range(count)])  7.48 us
    all_to_all x1, waiting for transfers between devices, shards(): lax.all_to_all(messages, 'ctx', split_axis=0, concat_axis=0, tiled=True)  6.25 us
    all_to_all x1, starting transfers between devices, shards(): lax.all_to_all(messages, 'ctx', split_axis=0, concat_axis=0, tiled=True)  5.96 us
    all_to_all x1, waiting for transfers between devices, shards(): lax.all_to_all(back_messages, 'ctx', split_axis=0, concat_axis=0, tiled=T...  4.2 us
    ppermute x2, starting transfers between devices, shift(): return lax.ppermute(value, axis, pairs)  3.65 us
    all_to_all x1, starting transfers between devices, shards(): lax.all_to_all(back_messages, 'ctx', split_axis=0, concat_axis=0, tiled=T...  3.41 us
  transfers between devices with their start and end apart: 10, of which 2 were waited for; matrix products, arithmetic and copies ran while one was open for 0% of the time, Pallas kernels for 39%

profile of v2, /device:TPU:0, one launch (start us, length us, event | category | flops | bytes accessed | tf_op | source)
XLA Modules:
  0.0 82.3 jit_solution(18379678458844518633)
XLA Ops:
  0.6 0.8 rim.1
  1.5 2.4 %collective-permute-start = (bf16[48,1024]{1,0:T(8,128)(2,1)S(1)}, bf16[48,1024]{1,0:T(8,128)(2,1)S(1)}, u32[]{:S(2)}, u32[]{:S(2)}) collective-permute-start(bf16[48,1024]{1,0:T(8,128)(2,1)S(1)} %rim.1), channel_id=1, source_target_pairs={{0,4},{4,8},{8,12},{12,16},{16,20},{20,24},{24,28},{1,5},{5,9},{9,... | collective-permute-start | bytes 294920 | tf_op jit(solution)/shard_map/ppermute | solution.py:375
  3.8 2.4 %collective-permute-start.4 = (bf16[256,1024]{1,0:T(8,128)(2,1)}, bf16[256,1024]{1,0:T(8,128)(2,1)}, u32[]{:S(2)}, u32[]{:S(2)}) collective-permute-start(bf16[256,1024]{1,0:T(8,128)(2,1)} %refs_0_), channel_id=1, source_target_pairs={{0,1},{1,0},{2,3},{3,2},{4,5},{5,4},{6,7},{7,6},{8,9},{9,8},{10,11... | collective-permute-start | bytes 1572872 | tf_op jit(solution)/shard_map/ppermute | solution.py:380
  6.2 1.5 %collective-permute-start.5 = (bf16[256,1024]{1,0:T(8,128)(2,1)}, bf16[256,1024]{1,0:T(8,128)(2,1)}, u32[]{:S(2)}, u32[]{:S(2)}) collective-permute-start(bf16[256,1024]{1,0:T(8,128)(2,1)} %refs_0_), channel_id=1, source_target_pairs={{0,2},{1,3},{2,0},{3,1},{4,6},{5,7},{6,4},{7,5},{8,10},{9,11},{10,... | collective-permute-start | bytes 1572872 | tf_op jit(solution)/shard_map/ppermute | solution.py:380
  7.7 0.0 collective-permute-start.6
  7.8 0.0 collective-permute-done.halo_ref
  7.8 5.8 %featurize.1 = (f32[2048,128]{1,0:T(8,128)S(1)}, f32[2048,128]{1,0:T(8,128)S(1)}, f32[2048,128]{1,0:T(8,128)S(1)}, f32[2048,128]{1,0:T(8,128)S(1)}, bf16[8,128,1...) custom-call(s32[1]{0:T(128)} %bitcast.position_ref, ...), custom_call_target="tpu_custom_call" | custom-call | bytes 15750000 | tf_op jit(solution)/shard_map/featurize/pallas_call | solution.py:357
  13.5 0.0 copy-start.2
  13.6 1.0 %copy-done.2 = f32[2048,128]{1,0:T(8,128)} copy-done((f32[2048,128]{1,0:T(8,128)}, f32[2048,128]{1,0:T(8,128)S(1)}, u32[]{:S(2)}) %copy-start.2) | copy-done | bytes 1048600
  14.6 1.0 %copy-done.7 = f32[2048,128]{1,0:T(8,128)} copy-done((f32[2048,128]{1,0:T(8,128)}, f32[2048,128]{1,0:T(8,128)S(1)}, u32[]{:S(2)}) %copy-start.7) | copy-done | bytes 1048600
  15.5 0.6 copy-done.16
  16.2 6.0 %all-to-all-start = ((bf16[8,128,128]{2,1,0:T(8,128)(2,1)}), bf16[8,128,128]{2,1,0:T(8,128)(2,1)S(1)}, u32[]{:S(2)}, u32[]{:S(2)}) async-start(bf16[8,128,128]{2,1,0:T(8,128)(2,1)} %get-tuple-element.27), calls=%async_computation | async-start | bytes 524288 | tf_op jit(solution)/shard_map/all_to_all | solution.py:430
  22.1 0.0 copy-start.8
  22.1 1.2 %copy-done.8 = f32[2048,128]{1,0:T(8,128)S(1)} copy-done((f32[2048,128]{1,0:T(8,128)S(1)}, f32[2048,128]{1,0:T(8,128)}, u32[]{:S(2)}) %copy-start.8) | copy-done | bytes 1048600
  23.4 2.3 %local_conv.1.local_ref = f32[2048,128]{1,0:T(8,128)S(1)} custom-call(f32[2048,128]{1,0:T(8,128)S(1)} %copy-done.8, f32[128,128]{1,0:T(8,128)S(1)} %get-tuple-element.29.decay_ref, f32[128,128]{1,0:T(8,128)S(1)} %get-tuple-element.30.scale_ref), custom_call_target="tpu_custom_call" | custom-call | bytes 8049999 | tf_op jit(solution)/shard_map/local_conv/pallas_call | solution.py:357
  25.6 6.2 %all-to-all-done.message_ref = bf16[8,128,128]{2,1,0:T(8,128)(2,1)S(1)} async-done(((bf16[8,128,128]{2,1,0:T(8,128)(2,1)}), bf16[8,128,128]{2,1,0:T(8,128)(2,1)S(1)}, u32[]{:S(2)}, u32[]{:S(2)}) %all-to-all-start) | async-done | bytes 262176 | tf_op jit(solution)/shard_map/all_to_all | solution.py:430
  31.9 1.2 %copy-done.3 = f32[2048,128]{1,0:T(8,128)S(1)} copy-done((f32[2048,128]{1,0:T(8,128)S(1)}, f32[2048,128]{1,0:T(8,128)}, u32[]{:S(2)}) %copy-start.3) | copy-done | bytes 1048600
  33.1 8.2 %project.1 = (f32[2048,128]{1,0:T(8,128)S(1)}, bf16[256,1024]{1,0:T(8,128)(2,1)S(1)}, bf16[256,1024]{1,0:T(8,128)(2,1)}, bf16[256,1024]{1,0:T(8,128)(2,1)}, bf16[256,1024]{1,0:T(8,128)(2,1)}) custom-call(s32[4]{0:T(128)S(1)} %iota_xor_fusion.index_ref, bf16[8,128,128]{2,1,0:T(8,128)(2,1)S(1)} %all-to-all-done.message_ref, ...), custom_call_target="tpu_custom_call" | custom-call | bytes 24500000 | tf_op jit(solution)/shard_map/project/pallas_call | solution.py:357
  41.3 0.0 copy-start.11
  41.3 1.6 %collective-permute-start.1 = (bf16[256,1024]{1,0:T(8,128)(2,1)}, bf16[256,1024]{1,0:T(8,128)(2,1)}, u32[]{:S(2)}, u32[]{:S(2)}) collective-permute-start(bf16[256,1024]{1,0:T(8,128)(2,1)} %get-tuple-element.33), channel_id=1, source_target_pairs={{0,1},{1,0},{2,3},{3,2},{4,5},{5,4},{6,7},{7,6},{8,9},{9,8},{10,11... | collective-permute-start | bytes 1572872 | tf_op jit(solution)/shard_map/ppermute | solution.py:380
  42.8 1.5 %collective-permute-start.2 = (bf16[256,1024]{1,0:T(8,128)(2,1)}, bf16[256,1024]{1,0:T(8,128)(2,1)}, u32[]{:S(2)}, u32[]{:S(2)}) collective-permute-start(bf16[256,1024]{1,0:T(8,128)(2,1)} %get-tuple-element.34), channel_id=1, source_target_pairs={{0,2},{1,3},{2,0},{3,1},{4,6},{5,7},{6,4},{7,5},{8,10},{9,11},{10,... | collective-permute-start | bytes 1572872 | tf_op jit(solution)/shard_map/ppermute | solution.py:380
  44.3 0.0 collective-permute-done.4.refs_1_
  44.3 0.5 collective-permute-start.3
  44.8 0.0 collective-permute-done.5.refs_2_
  44.8 0.0 collective-permute-done.6.refs_3_
  44.9 8.5 %back.1 = (f32[2048,128]{1,0:T(8,128)S(1)}, f32[2048,128]{1,0:T(8,128)S(1)}, bf16[8,128,128]{2,1,0:T(8,128)(2,1)}, f32[4,48,128]{2,1,0:T(8,128)}) custom-call(s32[4]{0:T(128)S(1)} %iota_xor_fusion.index_ref, s32[1]{0:T(128)} %bitcast.position_ref, bf16[1024,4096]{1,0:T(8,128)(2,1)} %weight_ref.3, f32[2048,128]{1,0:T(8,128)S(1)} %copy-done.4, ...), custom_call_target="tpu_custom_call" | custom-call | bytes 28000000 | tf_op jit(solution)/shard_map/back/pallas_call | solution.py:357
  53.4 1.0 %copy-done = f32[2048,128]{1,0:T(8,128)} copy-done((f32[2048,128]{1,0:T(8,128)}, f32[2048,128]{1,0:T(8,128)S(1)}, u32[]{:S(2)}) %copy-start) | copy-done | bytes 1048600
  54.4 1.0 %copy-done.5 = f32[2048,128]{1,0:T(8,128)} copy-done((f32[2048,128]{1,0:T(8,128)}, f32[2048,128]{1,0:T(8,128)S(1)}, u32[]{:S(2)}) %copy-start.5) | copy-done | bytes 1048600
  55.4 1.0 %copy-done.9 = f32[2048,128]{1,0:T(8,128)} copy-done((f32[2048,128]{1,0:T(8,128)}, f32[2048,128]{1,0:T(8,128)S(1)}, u32[]{:S(2)}) %copy-start.9) | copy-done | bytes 1048600
  56.4 3.4 %all-to-all-start.1 = ((bf16[8,128,128]{2,1,0:T(8,128)(2,1)}), bf16[8,128,128]{2,1,0:T(8,128)(2,1)S(1)}, u32[]{:S(2)}, u32[]{:S(2)}) async-start(bf16[8,128,128]{2,1,0:T(8,128)(2,1)} %get-tuple-element.40), calls=%async_computation.1 | async-start | bytes 524288 | tf_op jit(solution)/shard_map/all_to_all | solution.py:479
  59.8 1.3 %collective-permute-start.7 = (f32[4,48,128]{2,1,0:T(8,128)}, f32[4,48,128]{2,1,0:T(8,128)S(1)}, u32[]{:S(2)}, u32[]{:S(2)}) collective-permute-start(f32[4,48,128]{2,1,0:T(8,128)} %get-tuple-element.43), channel_id=1, source_target_pairs={{4,0},{8,4},{12,8},{16,12},{20,16},{24,20},{28,24},{5,1},{9,5},{13... | collective-permute-start | bytes 294920 | tf_op jit(solution)/shard_map/ppermute | solution.py:375
  61.1 0.0 copy-start.10
  61.1 1.2 %copy-done.10 = f32[2048,128]{1,0:T(8,128)S(1)} copy-done((f32[2048,128]{1,0:T(8,128)S(1)}, f32[2048,128]{1,0:T(8,128)}, u32[]{:S(2)}) %copy-start.10) | copy-done | bytes 1048600
  62.3 2.3 %back_local_conv.1.local_ref = f32[2048,128]{1,0:T(8,128)S(1)} custom-call(f32[2048,128]{1,0:T(8,128)S(1)} %copy-done.10, f32[128,128]{1,0:T(8,128)S(1)} %get-tuple-element.29.decay_ref, f32[128,128]{1,0:T(8,128)S(1)} %get-tuple-element.30.scale_ref), custom_call_target="tpu_custom_call" | custom-call | bytes 8049999 | tf_op jit(solution)/shard_map/back_local_conv/pallas_call | solution.py:357
  64.6 0.0 collective-permute-done.7.halo_ref
  64.6 0.0 copy-start.14
  64.6 0.6 copy-done.14
  65.3 4.2 %all-to-all-done.1.message_ref = bf16[8,128,128]{2,1,0:T(8,128)(2,1)S(1)} async-done(((bf16[8,128,128]{2,1,0:T(8,128)(2,1)}), bf16[8,128,128]{2,1,0:T(8,128)(2,1)S(1)}, u32[]{:S(2)}, u32[]{:S(2)}) %all-to-all-start.1) | async-done | bytes 262176 | tf_op jit(solution)/shard_map/all_to_all | solution.py:479
  69.5 1.2 %copy-done.1 = f32[2048,128]{1,0:T(8,128)S(1)} copy-done((f32[2048,128]{1,0:T(8,128)S(1)}, f32[2048,128]{1,0:T(8,128)}, u32[]{:S(2)}) %copy-start.1) | copy-done | bytes 1048600
  70.7 1.2 %copy-done.6 = f32[2048,128]{1,0:T(8,128)S(1)} copy-done((f32[2048,128]{1,0:T(8,128)S(1)}, f32[2048,128]{1,0:T(8,128)}, u32[]{:S(2)}) %copy-start.6) | copy-done | bytes 1048600
  71.9 0.9 %copy-done.15 = f32[4,48,128]{2,1,0:T(8,128)S(1)} copy-done((f32[4,48,128]{2,1,0:T(8,128)S(1)}, f32[4,48,128]{2,1,0:T(8,128)}, u32[]{:S(2)}) %copy-start.15) | copy-done | bytes 98328
  72.8 0.9 %copy-done.17 = f32[168,128]{1,0:T(8,128)S(1)} copy-done((f32[168,128]{1,0:T(8,128)S(1)}, f32[168,128]{1,0:T(8,128)}, u32[]{:S(2)}) %copy-start.17) | copy-done | bytes 86040
  73.7 5.1 %finish.1 = (bf16[256,1024]{1,0:T(8,128)(2,1)}, bf16[256,1024]{1,0:T(8,128)(2,1)}, bf16[256,1024]{1,0:T(8,128)(2,1)}) custom-call(bf16[8,128,128]{2,1,0:T(8,128)(2,1)S(1)} %all-to-all-done.1.message_ref, f32[2048,128]{1,0:T(8,128)S(1)} %back_local_conv.1.local_ref, f32[128,128]{1,0:T(8,128)S(1)} %get-tuple-element.29.decay_ref, ...), custom_call_target="tpu_custom_call" | custom-call | bytes 17500000 | tf_op jit(solution)/shard_map/finish/pallas_call | solution.py:357
  78.8 0.0 collective-permute-done.1.refs_1_
  78.8 0.0 collective-permute-done.2.refs_2_
  78.8 0.0 collective-permute-done.3.refs_3_
  78.8 1.0 %copy-done.12 = bf16[256,1024]{1,0:T(8,128)(2,1)S(1)} copy-done((bf16[256,1024]{1,0:T(8,128)(2,1)S(1)}, bf16[256,1024]{1,0:T(8,128)(2,1)}, u32[]{:S(2)}) %copy-start.12) | copy-done | bytes 524312
  79.9 2.4 %add_parts.1 = bf16[256,1024]{1,0:T(8,128)(2,1)} custom-call(bf16[256,1024]{1,0:T(8,128)(2,1)S(1)} %copy-done.12, bf16[256,1024]{1,0:T(8,128)(2,1)} %collective-permute-done.1.refs_1_, bf16[256,1024]{1,0:T(8,128)(2,1)} %collective-permute-done.2.refs_2_, bf16[256,1024]{1,0:T(8,128)(2,1)} %collective-permute-done.3.refs_3_), custom_call_target="tpu_custom_call" | custom-call | bytes 5250000 | tf_op jit(solution)/shard_map/add_parts/pallas_call | solution.py:357
  (17 shorter events, 0.0 us)
Async XLA Ops:
  1.5 6.3 %collective-permute-start = (bf16[48,1024]{1,0:T(8,128)(2,1)S(1)}, bf16[48,1024]{1,0:T(8,128)(2,1)S(1)}, u32[]{:S(2)}, u32[]{:S(2)}) collective-permute-start(bf16[48,1024]{1,0:T(8,128)(2,1)S(1)} %rim.1), channel_id=1, source_target_pairs={{0,4},{4,8},{8,12},{12,16},{16,20},{20,24},{24,28},{1,5},{5,9},{9,... | collective-permute-start | bytes 294920 | tf_op jit(solution)/shard_map/ppermute | solution.py:375
  3.8 40.5 %collective-permute-start.4 = (bf16[256,1024]{1,0:T(8,128)(2,1)}, bf16[256,1024]{1,0:T(8,128)(2,1)}, u32[]{:S(2)}, u32[]{:S(2)}) collective-permute-start(bf16[256,1024]{1,0:T(8,128)(2,1)} %refs_0_), channel_id=1, source_target_pairs={{0,1},{1,0},{2,3},{3,2},{4,5},{5,4},{6,7},{7,6},{8,9},{9,8},{10,11... | collective-permute-start | bytes 1572872 | tf_op jit(solution)/shard_map/ppermute | solution.py:380
  6.2 38.6 %collective-permute-start.5 = (bf16[256,1024]{1,0:T(8,128)(2,1)}, bf16[256,1024]{1,0:T(8,128)(2,1)}, u32[]{:S(2)}, u32[]{:S(2)}) collective-permute-start(bf16[256,1024]{1,0:T(8,128)(2,1)} %refs_0_), channel_id=1, source_target_pairs={{0,2},{1,3},{2,0},{3,1},{4,6},{5,7},{6,4},{7,5},{8,10},{9,11},{10,... | collective-permute-start | bytes 1572872 | tf_op jit(solution)/shard_map/ppermute | solution.py:380
  7.7 37.1 %collective-permute-start.6 = (bf16[256,1024]{1,0:T(8,128)(2,1)}, bf16[256,1024]{1,0:T(8,128)(2,1)}, u32[]{:S(2)}, u32[]{:S(2)}) collective-permute-start(bf16[256,1024]{1,0:T(8,128)(2,1)} %refs_0_), channel_id=1, source_target_pairs={{0,3},{1,2},{2,1},{3,0},{4,7},{5,6},{6,5},{7,4},{8,11},{9,10},{10,... | collective-permute-start | bytes 1572872 | tf_op jit(solution)/shard_map/ppermute | solution.py:380
  13.5 1.0 %copy-start.2 = (f32[2048,128]{1,0:T(8,128)}, f32[2048,128]{1,0:T(8,128)S(1)}, u32[]{:S(2)}) copy-start(f32[2048,128]{1,0:T(8,128)S(1)} %get-tuple-element.31.qf_ref) | copy-start | bytes 3145732
  14.6 1.0 %copy-start.7 = (f32[2048,128]{1,0:T(8,128)}, f32[2048,128]{1,0:T(8,128)S(1)}, u32[]{:S(2)}) copy-start(f32[2048,128]{1,0:T(8,128)S(1)} %get-tuple-element.28.signal_ref) | copy-start | bytes 3145732
  15.5 0.6 copy-start.16
  16.2 15.7 %all-to-all-start = ((bf16[8,128,128]{2,1,0:T(8,128)(2,1)}), bf16[8,128,128]{2,1,0:T(8,128)(2,1)S(1)}, u32[]{:S(2)}, u32[]{:S(2)}) async-start(bf16[8,128,128]{2,1,0:T(8,128)(2,1)} %get-tuple-element.27), calls=%async_computation | async-start | bytes 524288 | tf_op jit(solution)/shard_map/all_to_all | solution.py:430
  22.1 1.2 %copy-start.8 = (f32[2048,128]{1,0:T(8,128)S(1)}, f32[2048,128]{1,0:T(8,128)}, u32[]{:S(2)}) copy-start(f32[2048,128]{1,0:T(8,128)} %copy-done.7) | copy-start | bytes 3145732
  31.9 1.2 %copy-start.3 = (f32[2048,128]{1,0:T(8,128)S(1)}, f32[2048,128]{1,0:T(8,128)}, u32[]{:S(2)}) copy-start(f32[2048,128]{1,0:T(8,128)} %copy-done.2) | copy-start | bytes 3145732
  33.1 11.7 %copy-start.4 = (f32[2048,128]{1,0:T(8,128)S(1)}, f32[2048,128]{1,0:T(8,128)}, u32[]{:S(2)}) copy-start(f32[2048,128]{1,0:T(8,128)} %copy-done.2) | copy-start | bytes 3145732
  33.1 11.8 %copy-start.13 = (bf16[256,1024]{1,0:T(8,128)(2,1)S(1)}, bf16[256,1024]{1,0:T(8,128)(2,1)}, u32[]{:S(2)}) copy-start(bf16[256,1024]{1,0:T(8,128)(2,1)} %refs_0_) | copy-start | bytes 1572868
  41.3 12.1 %copy-start.11 = (bf16[256,1024]{1,0:T(8,128)(2,1)}, bf16[256,1024]{1,0:T(8,128)(2,1)S(1)}, u32[]{:S(2)}) copy-start(bf16[256,1024]{1,0:T(8,128)(2,1)S(1)} %get-tuple-element.32.refs_0_) | copy-start | bytes 1572868
  41.3 37.5 %collective-permute-start.1 = (bf16[256,1024]{1,0:T(8,128)(2,1)}, bf16[256,1024]{1,0:T(8,128)(2,1)}, u32[]{:S(2)}, u32[]{:S(2)}) collective-permute-start(bf16[256,1024]{1,0:T(8,128)(2,1)} %get-tuple-element.33), channel_id=1, source_target_pairs={{0,1},{1,0},{2,3},{3,2},{4,5},{5,4},{6,7},{7,6},{8,9},{9,8},{10,11... | collective-permute-start | bytes 1572872 | tf_op jit(solution)/shard_map/ppermute | solution.py:380
  42.8 36.0 %collective-permute-start.2 = (bf16[256,1024]{1,0:T(8,128)(2,1)}, bf16[256,1024]{1,0:T(8,128)(2,1)}, u32[]{:S(2)}, u32[]{:S(2)}) collective-permute-start(bf16[256,1024]{1,0:T(8,128)(2,1)} %get-tuple-element.34), channel_id=1, source_target_pairs={{0,2},{1,3},{2,0},{3,1},{4,6},{5,7},{6,4},{7,5},{8,10},{9,11},{10,... | collective-permute-start | bytes 1572872 | tf_op jit(solution)/shard_map/ppermute | solution.py:380
  44.3 34.5 %collective-permute-start.3 = (bf16[256,1024]{1,0:T(8,128)(2,1)}, bf16[256,1024]{1,0:T(8,128)(2,1)}, u32[]{:S(2)}, u32[]{:S(2)}) collective-permute-start(bf16[256,1024]{1,0:T(8,128)(2,1)} %get-tuple-element.35), channel_id=1, source_target_pairs={{0,3},{1,2},{2,1},{3,0},{4,7},{5,6},{6,5},{7,4},{8,11},{9,10},{10,... | collective-permute-start | bytes 1572872 | tf_op jit(solution)/shard_map/ppermute | solution.py:380
  53.4 1.0 %copy-start = (f32[2048,128]{1,0:T(8,128)}, f32[2048,128]{1,0:T(8,128)S(1)}, u32[]{:S(2)}) copy-start(f32[2048,128]{1,0:T(8,128)S(1)} %get-tuple-element.38.conv_ref) | copy-start | bytes 3145732
  54.4 1.0 %copy-start.5 = (f32[2048,128]{1,0:T(8,128)}, f32[2048,128]{1,0:T(8,128)S(1)}, u32[]{:S(2)}) copy-start(f32[2048,128]{1,0:T(8,128)S(1)} %get-tuple-element.42.grad_ref) | copy-start | bytes 3145732
  55.4 1.0 %copy-start.9 = (f32[2048,128]{1,0:T(8,128)}, f32[2048,128]{1,0:T(8,128)S(1)}, u32[]{:S(2)}) copy-start(f32[2048,128]{1,0:T(8,128)S(1)} %get-tuple-element.41.signal_ref) | copy-start | bytes 3145732
  56.4 13.1 %all-to-all-start.1 = ((bf16[8,128,128]{2,1,0:T(8,128)(2,1)}), bf16[8,128,128]{2,1,0:T(8,128)(2,1)S(1)}, u32[]{:S(2)}, u32[]{:S(2)}) async-start(bf16[8,128,128]{2,1,0:T(8,128)(2,1)} %get-tuple-element.40), calls=%async_computation.1 | async-start | bytes 524288 | tf_op jit(solution)/shard_map/all_to_all | solution.py:479
  59.8 4.8 %collective-permute-start.7 = (f32[4,48,128]{2,1,0:T(8,128)}, f32[4,48,128]{2,1,0:T(8,128)S(1)}, u32[]{:S(2)}, u32[]{:S(2)}) collective-permute-start(f32[4,48,128]{2,1,0:T(8,128)} %get-tuple-element.43), channel_id=1, source_target_pairs={{4,0},{8,4},{12,8},{16,12},{20,16},{24,20},{28,24},{5,1},{9,5},{13... | collective-permute-start | bytes 294920 | tf_op jit(solution)/shard_map/ppermute | solution.py:375
  61.1 1.2 %copy-start.10 = (f32[2048,128]{1,0:T(8,128)S(1)}, f32[2048,128]{1,0:T(8,128)}, u32[]{:S(2)}) copy-start(f32[2048,128]{1,0:T(8,128)} %copy-done.9) | copy-start | bytes 3145732
  64.6 0.6 copy-start.14
  69.5 1.2 %copy-start.1 = (f32[2048,128]{1,0:T(8,128)S(1)}, f32[2048,128]{1,0:T(8,128)}, u32[]{:S(2)}) copy-start(f32[2048,128]{1,0:T(8,128)} %copy-done) | copy-start | bytes 3145732
  70.7 1.2 %copy-start.6 = (f32[2048,128]{1,0:T(8,128)S(1)}, f32[2048,128]{1,0:T(8,128)}, u32[]{:S(2)}) copy-start(f32[2048,128]{1,0:T(8,128)} %copy-done.5) | copy-start | bytes 3145732
  71.9 0.9 %copy-start.15 = (f32[4,48,128]{2,1,0:T(8,128)S(1)}, f32[4,48,128]{2,1,0:T(8,128)}, u32[]{:S(2)}) copy-start(f32[4,48,128]{2,1,0:T(8,128)} %copy-done.14) | copy-start | bytes 294916
  72.8 0.9 %copy-start.17 = (f32[168,128]{1,0:T(8,128)S(1)}, f32[168,128]{1,0:T(8,128)}, u32[]{:S(2)}) copy-start(f32[168,128]{1,0:T(8,128)} %copy-done.16) | copy-start | bytes 258052
  78.8 1.0 %copy-start.12 = (bf16[256,1024]{1,0:T(8,128)(2,1)S(1)}, bf16[256,1024]{1,0:T(8,128)(2,1)}, u32[]{:S(2)}) copy-start(bf16[256,1024]{1,0:T(8,128)(2,1)} %copy-done.11) | copy-start | bytes 1572868

commit v3 on v2

v3 whole, which is shorter than its diff:
```python
import functools

import jax
import jax.numpy as jnp
from jax import lax
from jax.experimental import pallas as pl
from jax.experimental.pallas import tpu as pltpu
from jax.sharding import PartitionSpec as P

SUB = 8
LANES = 128
STEP = 8
F32 = jnp.float32
BF16 = jnp.bfloat16


def as_tiles(rows):
    return rows.reshape(rows.shape[0] // SUB, SUB, LANES)


def as_rows(tiles):
    return tiles.reshape(tiles.shape[0] * SUB, LANES)


def tile(ref, token):
    return ref[pl.ds(pl.multiple_of(token * SUB, SUB), SUB), :]


def tree_sum(terms):
    while len(terms) > 1:
        terms = [
            terms[i] + terms[i + 1] if i + 1 < len(terms) else terms[i]
            for i in range(0, len(terms), 2)
        ]
    return terms[0]


def round16(value):
    return value.astype(BF16).astype(F32)


def scatter_tokens(ref, value, first_token):
    tokens, channels = value.shape
    for group in range(channels // LANES):
        ref[pl.ds(first_token * SUB + group, tokens, stride=SUB), :] = value[
            :, group * LANES : (group + 1) * LANES
        ]


def gather_tokens(rows, out_ref):
    for group in range(out_ref.shape[1] // LANES):
        out_ref[:, group * LANES : (group + 1) * LANES] = rows(group).astype(out_ref.dtype)


def group_rows(ref, group, tokens):
    return ref[pl.ds(group, tokens, stride=SUB), :]


def start_all(copies):
    for copy in copies:
        copy.start()
    return copies


def wait_all(copies):
    for copy in copies:
        copy.wait()


def advance_states(signal_ref, factors, states, first, count, reverse):
    last = signal_ref.shape[0] // SUB - 1

    def body(step, states):
        for inner in range(STEP):
            token = first + step * STEP + inner
            u = tile(signal_ref, last - token if reverse else token)
            states = [factor * state + u for factor, state in zip(factors, states)]
        return states

    return lax.fori_loop(0, count // STEP, body, states)


def zero_states(modes):
    return [jnp.zeros((SUB, LANES), F32) for _ in range(modes)]


def mode_rows(n):
    return slice(n * SUB, (n + 1) * SUB)


def fades(decay_ref, tokens):
    return [
        jnp.exp(-decay_ref[mode_rows(n), :] * tokens) for n in range(decay_ref.shape[0] // SUB)
    ]


def write_messages(out_ref, states, decay_ref, position_ref, tokens, direction):
    count = out_ref.shape[0]
    out_ref[...] = jnp.zeros_like(out_ref)
    fade = fades(decay_ref, float(tokens))
    for gap in range(count - 1):
        other = position_ref[0] + direction * (gap + 1)
        value = jnp.concatenate(states, axis=0).astype(out_ref.dtype)

        @pl.when((other >= 0) & (other < count))
        def _():
            out_ref[jnp.clip(other, 0, count - 1)] = value

        states = [state * factor for state, factor in zip(states, fade)]


def read_messages(in_ref):
    total = in_ref[0].astype(F32)
    for other in range(1, in_ref.shape[0]):
        total = total + in_ref[other].astype(F32)
    return [total[mode_rows(n)] for n in range(total.shape[0] // SUB)]


def rim_kernel(q_ref, k_ref, v_ref, out_ref, sems):
    rows = out_ref.shape[0] // 3
    copies = [
        pltpu.make_async_copy(
            source.at[pl.ds(source.shape[0] - rows, rows), :],
            out_ref.at[pl.ds(stream * rows, rows), :],
            sems.at[stream],
        )
        for stream, source in enumerate((q_ref, k_ref, v_ref))
    ]
    for copy in copies:
        copy.start()
    for copy in copies:
        copy.wait()


def filtered(window, taps_ref, stream, taps, steps, forward):
    total = None
    for tap in range(taps):
        first = taps - 1 - tap if forward else tap
        term = taps_ref[pl.ds((stream * taps + tap) * SUB, SUB), :] * window[first : first + steps]
        total = term if total is None else total + term
    return total


def featurize_kernel(
    position_ref, q_ref, k_ref, v_ref, taps_in_ref, residue_in_ref, decay_in_ref, halo_ref,
    qf_ref, kf_ref, vf_ref, mixed_ref, message_ref, scale_ref, decay_ref,
    narrow_ref, wide_ref, feat_ref, taps_ref, taps_vmem, residue_vmem, decay_vmem, sems,
):
    tokens = q_ref.shape[0]
    _, taps, _ = taps_in_ref.shape
    rim = taps - 1
    modes = decay_in_ref.shape[0]
    copies = start_all(
        [
            pltpu.make_async_copy(source, target, sems.at[number])
            for number, (source, target) in enumerate(
                (
                    (decay_in_ref, decay_vmem),
                    (residue_in_ref, residue_vmem),
                    (taps_in_ref, taps_vmem),
                    (q_ref, narrow_ref.at[0]),
                    (k_ref, narrow_ref.at[1]),
                    (v_ref, narrow_ref.at[2]),
                )
            )
        ]
    )
    held = halo_ref.shape[0] // 3
    for stream in range(3):
        behind = halo_ref[stream * held : (stream + 1) * held, :].astype(F32)
        scatter_tokens(wide_ref.at[stream], behind[held - rim :], 0)
    wait_all(copies[:3])
    decays = decay_vmem[...]
    scatter_tokens(decay_ref, decays, 0)
    scatter_tokens(scale_ref, residue_vmem[...] * jnp.sqrt(decays), 0)
    for stream in range(3):
        scatter_tokens(taps_ref, taps_vmem[stream], stream * taps)
    for stream in range(3):
        copies[3 + stream].wait()
        scatter_tokens(wide_ref.at[stream], narrow_ref[stream].astype(F32), rim)

    def body(step, carry):
        begin = pl.multiple_of(step * STEP * SUB, SUB)
        rows = pl.ds(begin, STEP * SUB)
        feats = []
        for stream in range(3):
            window = as_tiles(wide_ref[stream, pl.ds(begin, (STEP + rim) * SUB), :])
            feats.append(filtered(window, taps_ref, stream, taps, STEP, True))
            feat_ref[stream, rows, :] = as_rows(feats[-1])
        mixed_ref[rows, :] = as_rows(round16(feats[1] * feats[2]))
        return carry

    lax.fori_loop(0, tokens // STEP, body, 0)
    copies = start_all(
        [
            pltpu.make_async_copy(feat_ref.at[stream], target, sems.at[stream])
            for stream, target in enumerate((qf_ref, kf_ref, vf_ref))
        ]
    )
    states = advance_states(
        mixed_ref, fades(decay_ref, 1.0), zero_states(modes), 0, tokens, False
    )
    write_messages(message_ref, states, decay_ref, position_ref, tokens, 1)
    wait_all(copies)


def scales_of(scale_ref):
    return [scale_ref[mode_rows(n), :] for n in range(scale_ref.shape[0] // SUB)]


def local_conv_kernel(signal_ref, decay_ref, scale_ref, out_ref, *, reverse):
    tokens = signal_ref.shape[0] // SUB
    factors = fades(decay_ref, 1.0)
    scales = scales_of(scale_ref)

    def body(step, states):
        for inner in range(STEP):
            token = step * STEP + inner
            token = tokens - 1 - token if reverse else token
            u = tile(signal_ref, token)
            states = [factor * state + u for factor, state in zip(factors, states)]
            out_ref[pl.ds(pl.multiple_of(token * SUB, SUB), SUB), :] = tree_sum(
                [scale * state for scale, state in zip(scales, states)]
            )
        return states

    lax.fori_loop(0, tokens // STEP, body, zero_states(len(factors)))


def add_carried(local_ref, out_ref, states, decay_ref, scale_ref, reverse):
    tokens = local_ref.shape[0] // SUB
    factors = fades(decay_ref, 1.0)
    scaled = [scale * state for scale, state in zip(scales_of(scale_ref), states)]

    def body(step, scaled):
        for inner in range(STEP):
            token = step * STEP + inner
            token = tokens - 1 - token if reverse else token
            scaled = [factor * state for factor, state in zip(factors, scaled)]
            rows = pl.ds(pl.multiple_of(token * SUB, SUB), SUB)
            out_ref[rows, :] = local_ref[rows, :] + tree_sum(list(scaled))
        return scaled

    lax.fori_loop(0, tokens // STEP, body, scaled)


def project_kernel(
    index_ref, message_ref, local_ref, decay_ref, scale_ref, _, qf_ref, weight_ref, conv_ref, *refs
):
    *out_refs, rows_ref, feat_ref, gated_ref, held_ref, sems = refs
    parts = len(out_refs)
    tokens, width = out_refs[0].shape
    copies = []
    for number in reversed(range(parts)):
        first = pl.multiple_of(index_ref[number] * width, width)
        copies.append(
            pltpu.make_async_copy(
                weight_ref.at[:, pl.ds(first, width)], held_ref.at[number], sems.at[number]
            )
        )
    feat_copy = pltpu.make_async_copy(qf_ref, feat_ref, sems.at[parts])
    feat_copy.start()
    start_all(copies)
    add_carried(local_ref, rows_ref, read_messages(message_ref), decay_ref, scale_ref, False)
    conv_copy = pltpu.make_async_copy(rows_ref, conv_ref, sems.at[parts + 1])
    conv_copy.start()
    feat_copy.wait()
    gather_tokens(
        lambda group: group_rows(rows_ref, group, tokens) * group_rows(feat_ref, group, tokens),
        gated_ref,
    )
    block = min(width, 256)
    for copy, number in zip(copies, reversed(range(parts))):
        out_ref = out_refs[number]
        copy.wait()

        def body(step, carry):
            columns = pl.ds(pl.multiple_of(step * block, block), block)
            out_ref[:, columns] = jnp.dot(
                gated_ref[...], held_ref[number, :, columns], preferred_element_type=F32
            ).astype(out_ref.dtype)
            return carry

        lax.fori_loop(0, width // block, body, 0)
    conv_copy.wait()


def add_parts_kernel(*refs):
    *part_refs, _, out_ref, held_ref, total_ref, sems, out_sems = refs
    chunks = out_sems.shape[0]
    rows = out_ref.shape[0] // chunks

    def fetch(chunk, number):
        return pltpu.make_async_copy(
            part_refs[number].at[pl.ds(chunk * rows, rows), :],
            held_ref.at[number, pl.ds(chunk * rows, rows), :],
            sems.at[chunk, number],
        )

    numbers = range(len(part_refs))
    fetches = [start_all([fetch(chunk, number) for number in numbers]) for chunk in range(chunks)]
    outs = []
    for chunk in range(chunks):
        wait_all(fetches[chunk])
        here = pl.ds(chunk * rows, rows)
        total_ref[here, :] = tree_sum(
            [held_ref[number, here, :].astype(F32) for number in numbers]
        ).astype(total_ref.dtype)
        outs.append(
            pltpu.make_async_copy(total_ref.at[here, :], out_ref.at[here, :], out_sems.at[chunk])
        )
        outs[-1].start()
    wait_all(outs)


def back_products(index_ref, piece_refs, weight_ref, turned_ref, held_ref, sems, total_ref):
    width = piece_refs[0].shape[1]
    count = len(piece_refs)

    def fetch(number):
        first = pl.multiple_of(index_ref[number] * width, width)
        return pltpu.make_async_copy(
            weight_ref.at[:, pl.ds(first, width)], held_ref.at[number], sems.at[number]
        )

    start_all([fetch(number) for number in range(count)])
    for number, ref in enumerate(piece_refs):
        turned_ref[number] = ref[...].T

    def body(number, carry):
        fetch(number).wait()
        total_ref[...] += jnp.dot(
            held_ref[number], turned_ref[number], preferred_element_type=F32
        )
        return carry

    lax.fori_loop(0, count, body, 0)


def back_part_kernel(index_ref, weight_ref, *refs):
    *piece_refs, total_ref, turned_ref, held_ref, sems = refs
    total_ref[...] = jnp.zeros_like(total_ref)
    back_products(index_ref, piece_refs, weight_ref, turned_ref, held_ref, sems, total_ref)


def back_last_kernel(
    index_ref, position_ref, weight_ref, qf_ref, kf_ref, vf_ref, conv_ref, decay_ref, *refs, rim
):
    (
        *piece_refs, base_ref, grad_ref, mixed_ref, message_ref, ahead_ref,
        turned_ref, total_ref, rows_ref, feat_ref, conv_head_ref, held_ref, sems, own_sems,
    ) = refs
    channels, tokens = total_ref.shape
    head = slice(0, rim * SUB)
    heads = pl.ds(0, rim * SUB)
    copies = start_all(
        [
            pltpu.make_async_copy(qf_ref, feat_ref, own_sems.at[0]),
            pltpu.make_async_copy(conv_ref.at[heads, :], conv_head_ref, own_sems.at[1]),
            pltpu.make_async_copy(kf_ref.at[heads, :], ahead_ref.at[2], own_sems.at[2]),
            pltpu.make_async_copy(vf_ref.at[heads, :], ahead_ref.at[3], own_sems.at[3]),
        ]
    )
    total_ref[...] = base_ref[...]
    back_products(index_ref, piece_refs, weight_ref, turned_ref, held_ref, sems, total_ref)
    scatter_tokens(rows_ref, total_ref[...].T, 0)
    grad_copy = pltpu.make_async_copy(rows_ref, grad_ref, own_sems.at[4])
    grad_copy.start()
    wait_all(copies)
    mixed_ref[...] = round16(rows_ref[...] * feat_ref[...])
    ahead_ref[0] = round16(rows_ref[head, :] * conv_head_ref[...])
    ahead_ref[1] = mixed_ref[head, :]
    modes = decay_ref.shape[0] // SUB
    states = advance_states(
        mixed_ref, fades(decay_ref, 1.0), zero_states(modes), 0, tokens, True
    )
    write_messages(message_ref, states, decay_ref, position_ref, tokens, -1)
    grad_copy.wait()


def spread_back(wide_ref, taps_ref, stream, taps, rows_ref, out_ref):
    tokens = out_ref.shape[0]

    def body(step, carry):
        first = pl.multiple_of(step * STEP * SUB, SUB)
        window = as_tiles(wide_ref[pl.ds(first, (STEP + taps - 1) * SUB), :])
        rows_ref[pl.ds(first, STEP * SUB), :] = as_rows(
            filtered(window, taps_ref, stream, taps, STEP, False)
        )
        return carry

    lax.fori_loop(0, tokens // STEP, body, 0)
    gather_tokens(lambda group: group_rows(rows_ref, group, tokens), out_ref)


def finish_query_kernel(
    grad_ref, conv_ref, ahead_ref, taps_in_ref, gq_ref,
    grad_vmem, conv_vmem, wide_ref, rows_ref, out_vmem, taps_vmem, taps_ref, sems,
):
    taps = taps_in_ref.shape[1]
    tokens = gq_ref.shape[0]
    rim = taps - 1
    copies = start_all(
        [
            pltpu.make_async_copy(taps_in_ref.at[0], taps_vmem, sems.at[0]),
            pltpu.make_async_copy(
                ahead_ref.at[0], wide_ref.at[pl.ds(tokens * SUB, rim * SUB), :], sems.at[1]
            ),
            pltpu.make_async_copy(grad_ref, grad_vmem, sems.at[2]),
            pltpu.make_async_copy(conv_ref, conv_vmem, sems.at[3]),
        ]
    )
    copies[0].wait()
    scatter_tokens(taps_ref, taps_vmem[...], 0)
    wait_all(copies[1:])
    wide_ref[pl.ds(0, tokens * SUB), :] = round16(grad_vmem[...] * conv_vmem[...])
    spread_back(wide_ref, taps_ref, 0, taps, rows_ref, out_vmem)
    out = pltpu.make_async_copy(out_vmem, gq_ref, sems.at[0])
    out.start()
    out.wait()


def finish_kernel(
    message_ref, local_ref, decay_ref, scale_ref, kf_ref, vf_ref, ahead_ref, taps_in_ref,
    gk_ref, gv_ref, total_ref, feat_ref, halo_ref, wide_ref, rows_ref, out_vmem, taps_vmem,
    taps_ref, sems,
):
    taps = taps_in_ref.shape[1]
    tokens = gk_ref.shape[0]
    rim = taps - 1
    copies = start_all(
        [
            pltpu.make_async_copy(ahead_ref, halo_ref, sems.at[0]),
            pltpu.make_async_copy(taps_in_ref, taps_vmem, sems.at[1]),
            pltpu.make_async_copy(vf_ref, feat_ref.at[0], sems.at[2]),
            pltpu.make_async_copy(kf_ref, feat_ref.at[1], sems.at[3]),
        ]
    )
    states = read_messages(message_ref)
    add_carried(local_ref, total_ref, states, decay_ref, scale_ref, True)
    wait_all(copies[:2])
    for stream in (1, 2):
        scatter_tokens(taps_ref, taps_vmem[stream], stream * taps)
    growth = fades(decay_ref, -1.0)
    scales = scales_of(scale_ref)
    for ahead in range(rim):
        rows = pl.ds((tokens + ahead) * SUB, SUB)
        theirs = pl.ds(ahead * SUB, SUB)
        grad_conv = tree_sum([scale * state for scale, state in zip(scales, states)])
        wide_ref[0, rows, :] = round16(grad_conv * halo_ref[3, theirs, :])
        wide_ref[1, rows, :] = round16(grad_conv * halo_ref[2, theirs, :])
        arrived = halo_ref[1, theirs, :]
        states = [(state - arrived) * grow for state, grow in zip(states, growth)]
    outs = []
    for number, out_ref in enumerate((gk_ref, gv_ref)):
        copies[2 + number].wait()
        wide_ref[number, pl.ds(0, tokens * SUB), :] = round16(total_ref[...] * feat_ref[number])
        spread_back(
            wide_ref.at[number], taps_ref, 1 + number, taps, rows_ref, out_vmem.at[number]
        )
        outs.append(pltpu.make_async_copy(out_vmem.at[number], out_ref, sems.at[number]))
        outs[-1].start()
    wait_all(outs)


IN_VMEM = pl.BlockSpec(memory_space=pltpu.VMEM)
IN_SMEM = pl.BlockSpec(memory_space=pltpu.SMEM)
IN_HBM = pl.BlockSpec(memory_space=pltpu.HBM)
HBM_RATE = 3.5e6


def in_hbm(shape, kind):
    return pltpu.HBM(shape, kind)


def call(kernel, outs, args, specs, scratch, name, micros, mebibytes):
    args = [
        pltpu.with_memory_space_constraint(arg, pltpu.HBM) if spec is IN_HBM else arg
        for arg, spec in zip(args, specs)
    ]
    held = [isinstance(out, tuple) for out in outs]
    return pl.pallas_call(
        kernel,
        out_shape=[jax.ShapeDtypeStruct(*out) if own else out for own, out in zip(held, outs)],
        in_specs=specs,
        out_specs=[IN_VMEM if own else IN_HBM for own in held],
        scratch_shapes=scratch,
        compiler_params=pltpu.CompilerParams(vmem_limit_bytes=mebibytes * 1024 * 1024),
        cost_estimate=pl.CostEstimate(
            flops=0, bytes_accessed=int(micros * HBM_RATE), transcendentals=0
        ),
        name=name,
    )(*args)


def shift(value, axis, steps):
    count = lax.axis_size(axis)
    pairs = [(s, s + steps) for s in range(count) if 0 <= s + steps < count]
    return lax.ppermute(value, axis, pairs)


def exchange(value, axis, mask):
    count = lax.axis_size(axis)
    return lax.ppermute(value, axis, [(s, s ^ mask) for s in range(count)])


def shards(query_in, key_in, value_in, short_taps, residues, decays, out_weight, out_grad):
    tokens, channels = query_in.shape
    taps = short_taps.shape[0]
    rim = taps - 1
    modes = decays.shape[1]
    blocks = lax.axis_size("ctx")
    fans = lax.axis_size("ch")
    position = lax.axis_index("ctx")[None].astype(jnp.int32)
    tile_shape = (tokens * SUB, LANES)
    mode_shape = (modes * SUB, LANES)
    message_shape = (blocks,) + mode_shape
    streams = (query_in, key_in, value_in)
    rim_rows = 16

    (halo,) = call(
        rim_kernel, [((3 * rim_rows, channels), BF16)], streams, [IN_HBM] * 3,
        [pltpu.SemaphoreType.DMA((3,))], "rim", 1.0, 2,
    )
    halo, out_grad = lax.optimization_barrier((halo, out_grad))
    halo = shift(halo, "ctx", 1)
    if fans == 4:
        order = lax.axis_index("ch") ^ jnp.arange(fans, dtype=jnp.int32)
        pieces = [out_grad] + [exchange(out_grad, "ch", mask) for mask in range(1, fans)]
    else:
        order = jnp.arange(fans, dtype=jnp.int32)
        everyone = lax.all_gather(out_grad, "ch", axis=0, tiled=False)
        pieces = [everyone[number] for number in range(fans)]
    tap_rows = jnp.transpose(short_taps, (1, 0, 2))
    tap_tiles = pltpu.VMEM((3 * taps * SUB, LANES), F32)
    tile = pltpu.VMEM(tile_shape, F32)
    wide_rows = (tokens + rim) * SUB

    query_feat, key_feat, value_feat, mixed, messages, scale_tiles, decay_tiles = call(
        featurize_kernel,
        [in_hbm(tile_shape, F32)] * 3
        + [(tile_shape, F32), (message_shape, BF16), (mode_shape, F32), (mode_shape, F32)],
        (position,) + streams + (tap_rows, residues.T, decays.T, halo),
        [IN_SMEM] + [IN_HBM] * 6 + [IN_VMEM],
        [
            pltpu.VMEM((3, tokens, channels), BF16),
            pltpu.VMEM((3, wide_rows, LANES), F32),
            pltpu.VMEM((3,) + tile_shape, F32),
            tap_tiles,
            pltpu.VMEM((3, taps, channels), F32),
            pltpu.VMEM((modes, channels), F32),
            pltpu.VMEM((modes, channels), F32),
            pltpu.SemaphoreType.DMA((6,)),
        ],
        "featurize", 5.0, 10,
    )
    arrived = lax.all_to_all(messages, "ctx", split_axis=0, concat_axis=0, tiled=True)
    (local,) = call(
        functools.partial(local_conv_kernel, reverse=False),
        [(tile_shape, F32)], (mixed, decay_tiles, scale_tiles), [IN_VMEM] * 3, [],
        "local_conv", 2.3, 2,
    )

    def back_scratch(count):
        return [
            pltpu.VMEM((count, channels, tokens), BF16),
            pltpu.VMEM((channels, tokens), F32),
            tile,
            tile,
            pltpu.VMEM((rim * SUB, LANES), F32),
            pltpu.VMEM((count, channels, channels), BF16),
            pltpu.SemaphoreType.DMA((count,)),
            pltpu.SemaphoreType.DMA((5,)),
        ]

    early = fans - 1
    (base,) = call(
        back_part_kernel,
        [((channels, tokens), F32)],
        (order[:early], out_weight, *pieces[:early]),
        [IN_SMEM, IN_HBM] + [IN_VMEM] * early,
        [
            pltpu.VMEM((early, channels, tokens), BF16),
            pltpu.VMEM((early, channels, channels), BF16),
            pltpu.SemaphoreType.DMA((early,)),
        ],
        "back_part", 6.0, 10,
    )
    conv_out, *partial_sums = call(
        project_kernel,
        [in_hbm(tile_shape, F32)] + [((tokens, channels), BF16)] * fans,
        (order, arrived, local, decay_tiles, scale_tiles, base, query_feat, out_weight),
        [IN_SMEM] + [IN_VMEM] * 5 + [IN_HBM] * 2,
        [
            tile,
            tile,
            pltpu.VMEM((tokens, channels), BF16),
            pltpu.VMEM((fans, channels, channels), BF16),
            pltpu.SemaphoreType.DMA((fans + 2,)),
        ],
        "project", 7.0, 16,
    )
    if fans == 4:
        parts = [
            exchange(part, "ch", mask) if mask else part for mask, part in enumerate(partial_sums)
        ]
    else:
        parts = lax.all_to_all(
            jnp.stack(partial_sums), "ch", split_axis=0, concat_axis=0, tiled=True
        )
        parts = [parts[number] for number in range(fans)]
    grad_gated, grad_mixed, back_messages, ahead = call(
        functools.partial(back_last_kernel, rim=rim),
        [in_hbm(tile_shape, F32), (tile_shape, F32), (message_shape, BF16)]
        + [((4, rim * SUB, LANES), F32)],
        (
            order[early:], position, out_weight, query_feat, key_feat, value_feat, conv_out,
            decay_tiles, *pieces[early:], base,
        ),
        [IN_SMEM] * 2 + [IN_HBM] * 5 + [IN_VMEM] * 3,
        back_scratch(fans - early),
        "back_last", 5.0, 8,
    )
    back_arrived = lax.all_to_all(back_messages, "ctx", split_axis=0, concat_axis=0, tiled=True)
    ahead = shift(ahead, "ctx", -1)
    (back_local,) = call(
        functools.partial(local_conv_kernel, reverse=True),
        [(tile_shape, F32)], (grad_mixed, decay_tiles, scale_tiles), [IN_VMEM] * 3, [],
        "back_local_conv", 2.3, 2,
    )
    (grad_query,) = call(
        finish_query_kernel,
        [in_hbm((tokens, channels), BF16)],
        (grad_gated, conv_out, ahead, tap_rows),
        [IN_HBM] * 4,
        [
            tile,
            tile,
            pltpu.VMEM((wide_rows, LANES), F32),
            tile,
            pltpu.VMEM((tokens, channels), BF16),
            pltpu.VMEM((taps, channels), F32),
            tap_tiles,
            pltpu.SemaphoreType.DMA((4,)),
        ],
        "finish_query", 2.5, 7,
    )
    grad_key, grad_value = call(
        finish_kernel,
        [in_hbm((tokens, channels), BF16)] * 2,
        (
            back_arrived, back_local, decay_tiles, scale_tiles, key_feat, value_feat, ahead,
            tap_rows,
        ),
        [IN_VMEM] * 4 + [IN_HBM] * 4,
        [
            tile,
            pltpu.VMEM((2,) + tile_shape, F32),
            pltpu.VMEM((4, rim * SUB, LANES), F32),
            pltpu.VMEM((2, wide_rows, LANES), F32),
            tile,
            pltpu.VMEM((2, tokens, channels), BF16),
            pltpu.VMEM((3, taps, channels), F32),
            tap_tiles,
            pltpu.SemaphoreType.DMA((4,)),
        ],
        "finish", 4.0, 10,
    )
    (projected,) = call(
        add_parts_kernel, [in_hbm((tokens, channels), BF16)], (*parts, grad_key),
        [IN_HBM] * (fans + 1),
        [
            pltpu.VMEM((fans, tokens, channels), BF16),
            pltpu.VMEM((tokens, channels), BF16),
            pltpu.SemaphoreType.DMA((4, fans)),
            pltpu.SemaphoreType.DMA((4,)),
        ],
        "add_parts", 1.5, 4,
    )
    return (projected, grad_query, grad_key, grad_value)


def solution(mesh):
    in_specs = (
        P("ctx", "ch"),
        P("ctx", "ch"),
        P("ctx", "ch"),
        P(None, None, "ch"),
        P("ch", None),
        P("ch", None),
        P("ch", None),
        P("ctx", "ch"),
    )
    out_specs = (P("ctx", "ch"), P("ctx", "ch"), P("ctx", "ch"), P("ctx", "ch"))
    return jax.shard_map(shards, mesh=mesh, in_specs=in_specs, out_specs=out_specs, check_vma=False)
```

time: 83.1 us -> 84.2 us (1.013)
  the two profiles are of different devices: /device:TPU:0 before, /device:TPU:9 now
where the time goes in v3:
time: 84.2 us; the launch traced here: 83.5 us
  Pallas kernels  41.5 us (49%)
  starting transfers between devices  21.6 us (26%)
  waiting for transfers between devices  14.7 us (17%)
  local copies, waits for them, and re-layouts  4.94 us (6%)
    pallas_call x10, Pallas kernels, call(): pl.pallas_call(kernel, out_shape=[jax.ShapeDtypeStruct(*out) if own else...  41.5 us
    ppermute x6, waiting for transfers between devices, exchange(): return lax.ppermute(value, axis, [(s, s ^ mask) for s in range(count)])  9.87 us
    ppermute x2, starting transfers between devices, shift(): return lax.ppermute(value, axis, pairs)  6.02 us
    ppermute x6, starting transfers between devices, exchange(): return lax.ppermute(value, axis, [(s, s ^ mask) for s in range(count)])  5.36 us
    all_to_all x1, starting transfers between devices, shards(): lax.all_to_all(back_messages, 'ctx', split_axis=0, concat_axis=0, tiled=T...  5.14 us
    all_to_all x1, starting transfers between devices, shards(): lax.all_to_all(messages, 'ctx', split_axis=0, concat_axis=0, tiled=True)  5.09 us
    ppermute x2, waiting for transfers between devices, shift(): return lax.ppermute(value, axis, pairs)  4.86 us
    unnamed x10, local copies, waits for them, and re-layouts  4.3 us
  transfers between devices with their start and end apart: 10, of which 2 were waited for; matrix products, arithmetic and copies ran while one was open for 1% of the time, Pallas kernels for 46%

profile of v3, /device:TPU:9, one launch (start us, length us, event | category | flops | bytes accessed | tf_op | source)
XLA Modules:
  0.0 83.5 jit_solution(14321327227376436496)
XLA Ops:
  0.6 0.8 rim.1
  1.5 3.8 %collective-permute-start = (bf16[48,1024]{1,0:T(8,128)(2,1)S(1)}, bf16[48,1024]{1,0:T(8,128)(2,1)S(1)}, u32[]{:S(2)}, u32[]{:S(2)}) collective-permute-start(bf16[48,1024]{1,0:T(8,128)(2,1)S(1)} %rim.1), channel_id=1, source_target_pairs={{0,4},{4,8},{8,12},{12,16},{16,20},{20,24},{24,28},{1,5},{5,9},{9,... | collective-permute-start | bytes 294920 | tf_op jit(solution)/shard_map/ppermute | solution.py:499
  5.2 1.3 %collective-permute-start.1 = (bf16[256,1024]{1,0:T(8,128)(2,1)}, bf16[256,1024]{1,0:T(8,128)(2,1)S(1)}, u32[]{:S(2)}, u32[]{:S(2)}) collective-permute-start(bf16[256,1024]{1,0:T(8,128)(2,1)} %refs_0_), channel_id=1, source_target_pairs={{0,1},{1,0},{2,3},{3,2},{4,5},{5,4},{6,7},{7,6},{8,9},{9,8},{10,11... | collective-permute-start | bytes 1572872 | tf_op jit(solution)/shard_map/ppermute | solution.py:504
  6.5 1.2 %collective-permute-start.2 = (bf16[256,1024]{1,0:T(8,128)(2,1)}, bf16[256,1024]{1,0:T(8,128)(2,1)}, u32[]{:S(2)}, u32[]{:S(2)}) collective-permute-start(bf16[256,1024]{1,0:T(8,128)(2,1)} %refs_0_), channel_id=1, source_target_pairs={{0,2},{1,3},{2,0},{3,1},{4,6},{5,7},{6,4},{7,5},{8,10},{9,11},{10,... | collective-permute-start | bytes 1572872 | tf_op jit(solution)/shard_map/ppermute | solution.py:504
  7.7 0.2 collective-permute-start.6
  7.9 0.0 collective-permute-done.halo_ref
  7.9 6.1 %featurize.1 = (f32[2048,128]{1,0:T(8,128)}, f32[2048,128]{1,0:T(8,128)}, f32[2048,128]{1,0:T(8,128)}, f32[2048,128]{1,0:T(8,128)S(1)}, bf16[8,128,128]{2,1,0:T(...) custom-call(s32[1]{0:T(128)} %bitcast.position_ref, bf16[256,1024]{1,0:T(8,128)(2,1)} %q_ref.3, ...), custom_call_target="tpu_custom_call" | custom-call | bytes 17500000 | tf_op jit(solution)/shard_map/featurize/pallas_call | solution.py:482
  14.1 5.1 %all-to-all-start = ((bf16[8,128,128]{2,1,0:T(8,128)(2,1)}), bf16[8,128,128]{2,1,0:T(8,128)(2,1)S(1)}, u32[]{:S(2)}, u32[]{:S(2)}) async-start(bf16[8,128,128]{2,1,0:T(8,128)(2,1)} %get-tuple-element.25), calls=%async_computation | async-start | bytes 524288 | tf_op jit(solution)/shard_map/all_to_all | solution.py:557
  19.1 2.3 %local_conv.1.local_ref = f32[2048,128]{1,0:T(8,128)S(1)} custom-call(f32[2048,128]{1,0:T(8,128)S(1)} %get-tuple-element.26.signal_ref, f32[128,128]{1,0:T(8,128)S(1)} %get-tuple-element.27.decay_ref, f32[128,128]{1,0:T(8,128)S(1)} %get-tuple-element.28.scale_ref), custom_call_target="tpu_custom_call" | custom-call | bytes 8049999 | tf_op jit(solution)/shard_map/local_conv/pallas_call | solution.py:482
  21.4 0.0 collective-permute-done.1.refs_1_
  21.4 9.9 %collective-permute-done.2.refs_2_ = bf16[256,1024]{1,0:T(8,128)(2,1)} collective-permute-done((bf16[256,1024]{1,0:T(8,128)(2,1)}, bf16[256,1024]{1,0:T(8,128)(2,1)}, u32[]{:S(2)}, u32[]{:S(2)}) %collective-permute-start.2) | collective-permute-done | bytes 524320 | tf_op jit(solution)/shard_map/ppermute | solution.py:504
  31.3 0.0 copy-start.2
  31.3 1.0 %copy-done.2 = bf16[256,1024]{1,0:T(8,128)(2,1)S(1)} copy-done((bf16[256,1024]{1,0:T(8,128)(2,1)S(1)}, bf16[256,1024]{1,0:T(8,128)(2,1)}, u32[]{:S(2)}) %copy-start.2) | copy-done | bytes 524312
  32.3 5.1 %back_part.1._.refs_1_ = f32[1024,256]{1,0:T(8,128)S(1)} custom-call(s32[3]{0:T(128)S(1)} %bitcast.5, bf16[1024,4096]{1,0:T(8,128)(2,1)} %weight_ref.5, bf16[256,1024]{1,0:T(8,128)(2,1)S(1)} %copy-done.2, bf16[256,1024]{1,0:T(8,128)(2,1)S(1)} %collective-permute-done.1.refs_1_, bf16[256,1024]{1,0:T(8,128)(2,1)} %collective-permute-done.2.refs_2_), custom_call_target="tpu_custom_call" | custom-call | bytes 21000000 | tf_op jit(solution)/shard_map/back_part/pallas_call | solution.py:482
  37.4 0.0 all-to-all-done.message_ref
  37.4 8.8 %project.1 = (f32[2048,128]{1,0:T(8,128)}, bf16[256,1024]{1,0:T(8,128)(2,1)S(1)}, bf16[256,1024]{1,0:T(8,128)(2,1)}, bf16[256,1024]{1,0:T(8,128)(2,1)}, bf16[256,1024]{1,0:T(8,128)(2,1)}) custom-call(s32[4]{0:T(128)S(1)} %iota_xor_fusion.index_ref, bf16[8,128,128]{2,1,0:T(8,128)(2,1)S(1)} %all-to-all-done.message_ref, f32[2048,128]{1,0:T(8,128)S(1)} %local_conv.1.local_ref, ...), custom_call_target="tpu_custom_call" | custom-call | bytes 24500000 | tf_op jit(solution)/shard_map/project/pallas_call | solution.py:482
  46.2 0.0 copy-start.3
  46.2 0.8 copy-done.3
  47.0 0.0 collective-permute-start.3
  47.0 1.5 %collective-permute-start.4 = (bf16[256,1024]{1,0:T(8,128)(2,1)}, bf16[256,1024]{1,0:T(8,128)(2,1)}, u32[]{:S(2)}, u32[]{:S(2)}) collective-permute-start(bf16[256,1024]{1,0:T(8,128)(2,1)} %get-tuple-element.33), channel_id=1, source_target_pairs={{0,2},{1,3},{2,0},{3,1},{4,6},{5,7},{6,4},{7,5},{8,10},{9,11},{10,... | collective-permute-start | bytes 1572872 | tf_op jit(solution)/shard_map/ppermute | solution.py:504
  48.5 1.2 %collective-permute-start.5 = (bf16[256,1024]{1,0:T(8,128)(2,1)}, bf16[256,1024]{1,0:T(8,128)(2,1)}, u32[]{:S(2)}, u32[]{:S(2)}) collective-permute-start(bf16[256,1024]{1,0:T(8,128)(2,1)} %get-tuple-element.34), channel_id=1, source_target_pairs={{0,3},{1,2},{2,1},{3,0},{4,7},{5,6},{6,5},{7,4},{8,11},{9,10},{10,... | collective-permute-start | bytes 1572872 | tf_op jit(solution)/shard_map/ppermute | solution.py:504
  49.6 0.6 slice.7.index_ref
  50.3 0.0 collective-permute-done.6.refs_0_
  50.3 0.0 copy-start
  50.3 0.8 copy-done
  51.1 0.0 copy-start.1
  51.1 1.0 %copy-done.1 = bf16[256,1024]{1,0:T(8,128)(2,1)S(1)} copy-done((bf16[256,1024]{1,0:T(8,128)(2,1)S(1)}, bf16[256,1024]{1,0:T(8,128)(2,1)}, u32[]{:S(2)}) %copy-start.1) | copy-done | bytes 524312
  52.1 5.8 %back_last.1 = (f32[2048,128]{1,0:T(8,128)}, f32[2048,128]{1,0:T(8,128)S(1)}, bf16[8,128,128]{2,1,0:T(8,128)(2,1)}, f32[4,48,128]{2,1,0:T(8,128)S(1)}) custom-call(s32[1]{0:T(128)} %slice.7.index_ref, s32[1]{0:T(128)} %bitcast.position_ref, bf16[1024,4096]{1,0:T(8,128)(2,1)} %weight_ref.5, f32[2048,128]{1,0:T(8,128)} %get-tuple-element.30.qf_ref, ...), custom_call_target="tpu_custom_call" | custom-call | bytes 17500000 | tf_op jit(solution)/shard_map/back_last/pallas_call | solution.py:482
  57.9 5.1 %all-to-all-start.1 = ((bf16[8,128,128]{2,1,0:T(8,128)(2,1)}), bf16[8,128,128]{2,1,0:T(8,128)(2,1)S(1)}, u32[]{:S(2)}, u32[]{:S(2)}) async-start(bf16[8,128,128]{2,1,0:T(8,128)(2,1)} %get-tuple-element.38), calls=%async_computation.1 | async-start | bytes 524288 | tf_op jit(solution)/shard_map/all_to_all | solution.py:624
  63.0 2.3 %collective-permute-start.7 = (f32[4,48,128]{2,1,0:T(8,128)S(1)}, f32[4,48,128]{2,1,0:T(8,128)S(1)}, u32[]{:S(2)}, u32[]{:S(2)}) collective-permute-start(f32[4,48,128]{2,1,0:T(8,128)S(1)} %get-tuple-element.40), channel_id=1, source_target_pairs={{4,0},{8,4},{12,8},{16,12},{20,16},{24,20},{28,24},{5,1},{9,5},{13... | collective-permute-start | bytes 294920 | tf_op jit(solution)/shard_map/ppermute | solution.py:499
  65.3 2.3 %back_local_conv.1.local_ref = f32[2048,128]{1,0:T(8,128)S(1)} custom-call(f32[2048,128]{1,0:T(8,128)S(1)} %get-tuple-element.39.signal_ref, f32[128,128]{1,0:T(8,128)S(1)} %get-tuple-element.27.decay_ref, f32[128,128]{1,0:T(8,128)S(1)} %get-tuple-element.28.scale_ref), custom_call_target="tpu_custom_call" | custom-call | bytes 8049999 | tf_op jit(solution)/shard_map/back_local_conv/pallas_call | solution.py:482
  67.6 4.9 %collective-permute-done.7.ahead_ref = f32[4,48,128]{2,1,0:T(8,128)S(1)} collective-permute-done((f32[4,48,128]{2,1,0:T(8,128)S(1)}, f32[4,48,128]{2,1,0:T(8,128)S(1)}, u32[]{:S(2)}, u32[]{:S(2)}) %collective-permute-start.7) | collective-permute-done | bytes 98336 | tf_op jit(solution)/shard_map/ppermute | solution.py:499
  72.5 0.0 copy-start.4
  72.5 0.6 copy-done.4
  73.1 3.4 %finish_query.1 = bf16[256,1024]{1,0:T(8,128)(2,1)} custom-call(f32[2048,128]{1,0:T(8,128)} %get-tuple-element.42.grad_ref, f32[2048,128]{1,0:T(8,128)} %get-tuple-element.37.conv_ref, f32[4,48,128]{2,1,0:T(8,128)} %copy-done.4, f32[3,7,1024]{2,1,0:T(8,128)} %bitcast.7), custom_call_target="tpu_custom_call" | custom-call | bytes 8750000 | tf_op jit(solution)/shard_map/finish_query/pallas_call | solution.py:482
  76.5 0.0 all-to-all-done.1.message_ref
  76.5 4.5 %finish.1 = (bf16[256,1024]{1,0:T(8,128)(2,1)}, bf16[256,1024]{1,0:T(8,128)(2,1)}) custom-call(bf16[8,128,128]{2,1,0:T(8,128)(2,1)S(1)} %all-to-all-done.1.message_ref, f32[2048,128]{1,0:T(8,128)S(1)} %back_local_conv.1.local_ref, f32[128,128]{1,0:T(8,128)S(1)} %get-tuple-element.27.decay_ref, f32[128,128]{1,0:T(8,128)S(1)} %get-tuple-element.28.scale_ref, ...), custom_call_target="tpu_custom_call" | custom-call | bytes 14000000 | tf_op jit(solution)/shard_map/finish/pallas_call | solution.py:482
  81.0 0.0 collective-permute-done.3.refs_1_
  81.0 0.0 collective-permute-done.4.refs_2_
  81.0 0.0 collective-permute-done.5.refs_3_
  81.0 2.5 %add_parts.1 = bf16[256,1024]{1,0:T(8,128)(2,1)} custom-call(bf16[256,1024]{1,0:T(8,128)(2,1)} %copy-done.3, bf16[256,1024]{1,0:T(8,128)(2,1)} %collective-permute-done.3.refs_1_, bf16[256,1024]{1,0:T(8,128)(2,1)} %collective-permute-done.4.refs_2_, bf16[256,1024]{1,0:T(8,128)(2,1)} %collective-permute-done.5.refs_3_, ...), custom_call_target="tpu_custom_call" | custom-call | bytes 5250000 | tf_op jit(solution)/shard_map/add_parts/pallas_call | solution.py:482
  (1 shorter events, 0.0 us)
Async XLA Ops:
  1.5 6.5 %collective-permute-start = (bf16[48,1024]{1,0:T(8,128)(2,1)S(1)}, bf16[48,1024]{1,0:T(8,128)(2,1)S(1)}, u32[]{:S(2)}, u32[]{:S(2)}) collective-permute-start(bf16[48,1024]{1,0:T(8,128)(2,1)S(1)} %rim.1), channel_id=1, source_target_pairs={{0,4},{4,8},{8,12},{12,16},{16,20},{20,24},{24,28},{1,5},{5,9},{9,... | collective-permute-start | bytes 294920 | tf_op jit(solution)/shard_map/ppermute | solution.py:499
  5.2 16.2 %collective-permute-start.1 = (bf16[256,1024]{1,0:T(8,128)(2,1)}, bf16[256,1024]{1,0:T(8,128)(2,1)S(1)}, u32[]{:S(2)}, u32[]{:S(2)}) collective-permute-start(bf16[256,1024]{1,0:T(8,128)(2,1)} %refs_0_), channel_id=1, source_target_pairs={{0,1},{1,0},{2,3},{3,2},{4,5},{5,4},{6,7},{7,6},{8,9},{9,8},{10,11... | collective-permute-start | bytes 1572872 | tf_op jit(solution)/shard_map/ppermute | solution.py:504
  6.5 24.8 %collective-permute-start.2 = (bf16[256,1024]{1,0:T(8,128)(2,1)}, bf16[256,1024]{1,0:T(8,128)(2,1)}, u32[]{:S(2)}, u32[]{:S(2)}) collective-permute-start(bf16[256,1024]{1,0:T(8,128)(2,1)} %refs_0_), channel_id=1, source_target_pairs={{0,2},{1,3},{2,0},{3,1},{4,6},{5,7},{6,4},{7,5},{8,10},{9,11},{10,... | collective-permute-start | bytes 1572872 | tf_op jit(solution)/shard_map/ppermute | solution.py:504
  7.7 42.5 %collective-permute-start.6 = (bf16[256,1024]{1,0:T(8,128)(2,1)}, bf16[256,1024]{1,0:T(8,128)(2,1)S(1)}, u32[]{:S(2)}, u32[]{:S(2)}) collective-permute-start(bf16[256,1024]{1,0:T(8,128)(2,1)} %refs_0_), channel_id=1, source_target_pairs={{0,3},{1,2},{2,1},{3,0},{4,7},{5,6},{6,5},{7,4},{8,11},{9,10},{10,... | collective-permute-start | bytes 1572872 | tf_op jit(solution)/shard_map/ppermute | solution.py:504
  14.1 23.4 %all-to-all-start = ((bf16[8,128,128]{2,1,0:T(8,128)(2,1)}), bf16[8,128,128]{2,1,0:T(8,128)(2,1)S(1)}, u32[]{:S(2)}, u32[]{:S(2)}) async-start(bf16[8,128,128]{2,1,0:T(8,128)(2,1)} %get-tuple-element.25), calls=%async_computation | async-start | bytes 524288 | tf_op jit(solution)/shard_map/all_to_all | solution.py:557
  31.3 1.0 %copy-start.2 = (bf16[256,1024]{1,0:T(8,128)(2,1)S(1)}, bf16[256,1024]{1,0:T(8,128)(2,1)}, u32[]{:S(2)}) copy-start(bf16[256,1024]{1,0:T(8,128)(2,1)} %refs_0_) | copy-start | bytes 1572868
  46.2 0.8 copy-start.3
  47.0 34.0 %collective-permute-start.3 = (bf16[256,1024]{1,0:T(8,128)(2,1)}, bf16[256,1024]{1,0:T(8,128)(2,1)}, u32[]{:S(2)}, u32[]{:S(2)}) collective-permute-start(bf16[256,1024]{1,0:T(8,128)(2,1)} %get-tuple-element.32), channel_id=1, source_target_pairs={{0,1},{1,0},{2,3},{3,2},{4,5},{5,4},{6,7},{7,6},{8,9},{9,8},{10,11... | collective-permute-start | bytes 1572872 | tf_op jit(solution)/shard_map/ppermute | solution.py:504
  47.0 34.0 %collective-permute-start.4 = (bf16[256,1024]{1,0:T(8,128)(2,1)}, bf16[256,1024]{1,0:T(8,128)(2,1)}, u32[]{:S(2)}, u32[]{:S(2)}) collective-permute-start(bf16[256,1024]{1,0:T(8,128)(2,1)} %get-tuple-element.33), channel_id=1, source_target_pairs={{0,2},{1,3},{2,0},{3,1},{4,6},{5,7},{6,4},{7,5},{8,10},{9,11},{10,... | collective-permute-start | bytes 1572872 | tf_op jit(solution)/shard_map/ppermute | solution.py:504
  48.5 32.5 %collective-permute-start.5 = (bf16[256,1024]{1,0:T(8,128)(2,1)}, bf16[256,1024]{1,0:T(8,128)(2,1)}, u32[]{:S(2)}, u32[]{:S(2)}) collective-permute-start(bf16[256,1024]{1,0:T(8,128)(2,1)} %get-tuple-element.34), channel_id=1, source_target_pairs={{0,3},{1,2},{2,1},{3,0},{4,7},{5,6},{6,5},{7,4},{8,11},{9,10},{10,... | collective-permute-start | bytes 1572872 | tf_op jit(solution)/shard_map/ppermute | solution.py:504
  50.3 0.8 copy-start
  51.1 1.0 %copy-start.1 = (bf16[256,1024]{1,0:T(8,128)(2,1)S(1)}, bf16[256,1024]{1,0:T(8,128)(2,1)}, u32[]{:S(2)}) copy-start(bf16[256,1024]{1,0:T(8,128)(2,1)} %copy-done) | copy-start | bytes 1572868
  57.9 18.6 %all-to-all-start.1 = ((bf16[8,128,128]{2,1,0:T(8,128)(2,1)}), bf16[8,128,128]{2,1,0:T(8,128)(2,1)S(1)}, u32[]{:S(2)}, u32[]{:S(2)}) async-start(bf16[8,128,128]{2,1,0:T(8,128)(2,1)} %get-tuple-element.38), calls=%async_computation.1 | async-start | bytes 524288 | tf_op jit(solution)/shard_map/all_to_all | solution.py:624
  63.0 9.4 %collective-permute-start.7 = (f32[4,48,128]{2,1,0:T(8,128)S(1)}, f32[4,48,128]{2,1,0:T(8,128)S(1)}, u32[]{:S(2)}, u32[]{:S(2)}) collective-permute-start(f32[4,48,128]{2,1,0:T(8,128)S(1)} %get-tuple-element.40), channel_id=1, source_target_pairs={{4,0},{8,4},{12,8},{16,12},{20,16},{24,20},{28,24},{5,1},{9,5},{13... | collective-permute-start | bytes 294920 | tf_op jit(solution)/shard_map/ppermute | solution.py:499
  72.5 0.6 copy-start.4

commit v4 on v3

--- a/solution.py
+++ b/solution.py
@@ -208,7 +208,7 @@
     return [scale_ref[mode_rows(n), :] for n in range(scale_ref.shape[0] // SUB)]
 
 
-def local_conv_kernel(signal_ref, decay_ref, scale_ref, out_ref, *, reverse):
+def local_conv(signal_ref, decay_ref, scale_ref, out_ref, reverse):
     tokens = signal_ref.shape[0] // SUB
     factors = fades(decay_ref, 1.0)
     scales = scales_of(scale_ref)
@@ -227,6 +227,10 @@
     lax.fori_loop(0, tokens // STEP, body, zero_states(len(factors)))
 
 
+def back_local_kernel(signal_ref, decay_ref, scale_ref, out_ref):
+    local_conv(signal_ref, decay_ref, scale_ref, out_ref, True)
+
+
 def add_carried(local_ref, out_ref, states, decay_ref, scale_ref, reverse):
     tokens = local_ref.shape[0] // SUB
     factors = fades(decay_ref, 1.0)
@@ -245,19 +249,22 @@
 
 
 def project_kernel(
-    index_ref, message_ref, local_ref, decay_ref, scale_ref, _, qf_ref, weight_ref, conv_ref, *refs
+    message_ref, local_ref, decay_ref, scale_ref, qf_ref, weight_ref, *refs
 ):
-    *out_refs, rows_ref, feat_ref, gated_ref, held_ref, sems = refs
-    parts = len(out_refs)
-    tokens, width = out_refs[0].shape
-    copies = []
-    for number in reversed(range(parts)):
-        first = pl.multiple_of(index_ref[number] * width, width)
-        copies.append(
-            pltpu.make_async_copy(
-                weight_ref.at[:, pl.ds(first, width)], held_ref.at[number], sems.at[number]
-            )
+    conv_ref, out_ref, rows_ref, feat_ref, gated_ref, held_ref, sent_ref, sems, out_sems = refs[-9:]
+    parts, tokens, width = sent_ref.shape
+    copies = [
+        pltpu.make_async_copy(
+            weight_ref.at[:, pl.ds(part * width, width)], held_ref.at[part], sems.at[part]
         )
+        for part in range(parts)
+    ]
+    outs = [
+        pltpu.make_async_copy(
+            sent_ref.at[part], out_ref.at[:, pl.ds(part * width, width)], out_sems.at[part]
+        )
+        for part in range(parts)
+    ]
     feat_copy = pltpu.make_async_copy(qf_ref, feat_ref, sems.at[parts])
     feat_copy.start()
     start_all(copies)
@@ -270,112 +277,95 @@
         gated_ref,
     )
     block = min(width, 256)
-    for copy, number in zip(copies, reversed(range(parts))):
-        out_ref = out_refs[number]
-        copy.wait()
+    for part in range(parts):
+        copies[part].wait()
 
         def body(step, carry):
             columns = pl.ds(pl.multiple_of(step * block, block), block)
-            out_ref[:, columns] = jnp.dot(
-                gated_ref[...], held_ref[number, :, columns], preferred_element_type=F32
-            ).astype(out_ref.dtype)
+            sent_ref[part, :, columns] = jnp.dot(
+                gated_ref[...], held_ref[part, :, columns], preferred_element_type=F32
+            ).astype(sent_ref.dtype)
             return carry
 
         lax.fori_loop(0, width // block, body, 0)
+        outs[part].start()
     conv_copy.wait()
-
-
-def add_parts_kernel(*refs):
-    *part_refs, _, out_ref, held_ref, total_ref, sems, out_sems = refs
-    chunks = out_sems.shape[0]
-    rows = out_ref.shape[0] // chunks
-
-    def fetch(chunk, number):
-        return pltpu.make_async_copy(
-            part_refs[number].at[pl.ds(chunk * rows, rows), :],
-            held_ref.at[number, pl.ds(chunk * rows, rows), :],
-            sems.at[chunk, number],
+    wait_all(outs)
+
+
+def start_back(index_ref, piece_refs, weight_ref, piece_vmem, held_ref, sems):
+    count = len(piece_refs)
+    width = held_ref.shape[2]
+    pieces = start_all(
+        [
+            pltpu.make_async_copy(ref, piece_vmem.at[number], sems.at[count + number])
+            for number, ref in enumerate(piece_refs)
+        ]
+    )
+    weights = [
+        pltpu.make_async_copy(
+            weight_ref.at[:, pl.ds(pl.multiple_of(index_ref[number] * width, width), width)],
+            held_ref.at[number],
+            sems.at[number],
         )
-
-    numbers = range(len(part_refs))
-    fetches = [start_all([fetch(chunk, number) for number in numbers]) for chunk in range(chunks)]
-    outs = []
-    for chunk in range(chunks):
-        wait_all(fetches[chunk])
-        here = pl.ds(chunk * rows, rows)
-        total_ref[here, :] = tree_sum(
-            [held_ref[number, here, :].astype(F32) for number in numbers]
-        ).astype(total_ref.dtype)
-        outs.append(
-            pltpu.make_async_copy(total_ref.at[here, :], out_ref.at[here, :], out_sems.at[chunk])
-        )
-        outs[-1].start()
-    wait_all(outs)
-
-
-def back_products(index_ref, piece_refs, weight_ref, turned_ref, held_ref, sems, total_ref):
-    width = piece_refs[0].shape[1]
-    count = len(piece_refs)
-
-    def fetch(number):
-        first = pl.multiple_of(index_ref[number] * width, width)
-        return pltpu.make_async_copy(
-            weight_ref.at[:, pl.ds(first, width)], held_ref.at[number], sems.at[number]
-        )
-
-    start_all([fetch(number) for number in range(count)])
-    for number, ref in enumerate(piece_refs):
-        turned_ref[number] = ref[...].T
-
-    def body(number, carry):
-        fetch(number).wait()
-        total_ref[...] += jnp.dot(
-            held_ref[number], turned_ref[number], preferred_element_type=F32
-        )
-        return carry
-
-    lax.fori_loop(0, count, body, 0)
-
-
-def back_part_kernel(index_ref, weight_ref, *refs):
-    *piece_refs, total_ref, turned_ref, held_ref, sems = refs
-    total_ref[...] = jnp.zeros_like(total_ref)
-    back_products(index_ref, piece_refs, weight_ref, turned_ref, held_ref, sems, total_ref)
+        for number in range(count)
+    ]
+    return pieces, start_all(weights)
+
+
+def back_products(copies, piece_vmem, turned_ref, held_ref, total_ref, before_ref):
+    pieces, weights = copies
+    for number in range(len(pieces)):
+        pieces[number].wait()
+        turned_ref[number] = piece_vmem[number].T
+    for number in range(len(pieces)):
+        weights[number].wait()
+        product = jnp.dot(held_ref[number], turned_ref[number], preferred_element_type=F32)
+        earlier = before_ref if number == 0 else total_ref
+        total_ref[...] = product if earlier is None else earlier[...] + product
+
+
+def middle_kernel(index_ref, signal_ref, decay_ref, scale_ref, weight_ref, *refs):
+    *piece_refs, local_ref, total_ref, piece_vmem, turned_ref, held_ref, sems = refs
+    copies = start_back(index_ref, piece_refs, weight_ref, piece_vmem, held_ref, sems)
+    local_conv(signal_ref, decay_ref, scale_ref, local_ref, False)
+    back_products(copies, piece_vmem, turned_ref, held_ref, total_ref, None)
 
 
 def back_last_kernel(
-    index_ref, position_ref, weight_ref, qf_ref, kf_ref, vf_ref, conv_ref, decay_ref, *refs, rim
+    index_ref, position_ref, base_ref, decay_ref, weight_ref, qf_ref, kf_ref, vf_ref, conv_ref,
+    *refs, rim,
 ):
     (
-        *piece_refs, base_ref, grad_ref, mixed_ref, message_ref, ahead_ref,
-        turned_ref, total_ref, rows_ref, feat_ref, conv_head_ref, held_ref, sems, own_sems,
+        *piece_refs, back_query_ref, mixed_ref, message_ref, ahead_ref,
+        piece_vmem, turned_ref, total_ref, rows_ref, feat_ref, conv_vmem, held_ref, sems, own_sems,
     ) = refs
-    channels, tokens = total_ref.shape
-    head = slice(0, rim * SUB)
+    tokens = total_ref.shape[1]
     heads = pl.ds(0, rim * SUB)
+    products = start_back(index_ref, piece_refs, weight_ref, piece_vmem, held_ref, sems)
     copies = start_all(
         [
             pltpu.make_async_copy(qf_ref, feat_ref, own_sems.at[0]),
-            pltpu.make_async_copy(conv_ref.at[heads, :], conv_head_ref, own_sems.at[1]),
+            pltpu.make_async_copy(conv_ref, conv_vmem, own_sems.at[1]),
             pltpu.make_async_copy(kf_ref.at[heads, :], ahead_ref.at[2], own_sems.at[2]),
             pltpu.make_async_copy(vf_ref.at[heads, :], ahead_ref.at[3], own_sems.at[3]),
         ]
     )
-    total_ref[...] = base_ref[...]
-    back_products(index_ref, piece_refs, weight_ref, turned_ref, held_ref, sems, total_ref)
+    back_products(products, piece_vmem, turned_ref, held_ref, total_ref, base_ref)
     scatter_tokens(rows_ref, total_ref[...].T, 0)
-    grad_copy = pltpu.make_async_copy(rows_ref, grad_ref, own_sems.at[4])
-    grad_copy.start()
     wait_all(copies)
     mixed_ref[...] = round16(rows_ref[...] * feat_ref[...])
-    ahead_ref[0] = round16(rows_ref[head, :] * conv_head_ref[...])
-    ahead_ref[1] = mixed_ref[head, :]
+    rows_ref[...] = round16(rows_ref[...] * conv_vmem[...])
+    out = pltpu.make_async_copy(rows_ref, back_query_ref, own_sems.at[4])
+    out.start()
+    ahead_ref[0] = rows_ref[: rim * SUB, :]
+    ahead_ref[1] = mixed_ref[: rim * SUB, :]
     modes = decay_ref.shape[0] // SUB
     states = advance_states(
         mixed_ref, fades(decay_ref, 1.0), zero_states(modes), 0, tokens, True
     )
     write_messages(message_ref, states, decay_ref, position_ref, tokens, -1)
-    grad_copy.wait()
+    out.wait()
 
 
 def spread_back(wide_ref, taps_ref, stream, taps, rows_ref, out_ref):
@@ -394,8 +384,8 @@
 
 
 def finish_query_kernel(
-    grad_ref, conv_ref, ahead_ref, taps_in_ref, gq_ref,
-    grad_vmem, conv_vmem, wide_ref, rows_ref, out_vmem, taps_vmem, taps_ref, sems,
+    back_query_ref, ahead_ref, taps_in_ref, gq_ref,
+    wide_ref, rows_ref, out_vmem, taps_vmem, taps_ref, sems,
 ):
     taps = taps_in_ref.shape[1]
     tokens = gq_ref.shape[0]
@@ -406,14 +396,14 @@
             pltpu.make_async_copy(
                 ahead_ref.at[0], wide_ref.at[pl.ds(tokens * SUB, rim * SUB), :], sems.at[1]
             ),
-            pltpu.make_async_copy(grad_ref, grad_vmem, sems.at[2]),
-            pltpu.make_async_copy(conv_ref, conv_vmem, sems.at[3]),
+            pltpu.make_async_copy(
+                back_query_ref, wide_ref.at[pl.ds(0, tokens * SUB), :], sems.at[2]
+            ),
         ]
     )
     copies[0].wait()
     scatter_tokens(taps_ref, taps_vmem[...], 0)
     wait_all(copies[1:])
-    wide_ref[pl.ds(0, tokens * SUB), :] = round16(grad_vmem[...] * conv_vmem[...])
     spread_back(wide_ref, taps_ref, 0, taps, rows_ref, out_vmem)
     out = pltpu.make_async_copy(out_vmem, gq_ref, sems.at[0])
     out.start()
@@ -555,95 +545,81 @@
         "featurize", 5.0, 10,
     )
     arrived = lax.all_to_all(messages, "ctx", split_axis=0, concat_axis=0, tiled=True)
-    (local,) = call(
-        functools.partial(local_conv_kernel, reverse=False),
-        [(tile_shape, F32)], (mixed, decay_tiles, scale_tiles), [IN_VMEM] * 3, [],
-        "local_conv", 2.3, 2,
-    )
+    early = fans // 2
 
     def back_scratch(count):
         return [
+            pltpu.VMEM((count, tokens, channels), BF16),
             pltpu.VMEM((count, channels, tokens), BF16),
-            pltpu.VMEM((channels, tokens), F32),
-            tile,
-            tile,
-            pltpu.VMEM((rim * SUB, LANES), F32),
+        ]
+
+    def weight_scratch(count):
+        return [
             pltpu.VMEM((count, channels, channels), BF16),
-            pltpu.SemaphoreType.DMA((count,)),
-            pltpu.SemaphoreType.DMA((5,)),
-        ]
-
-    early = fans - 1
-    (base,) = call(
-        back_part_kernel,
-        [((channels, tokens), F32)],
-        (order[:early], out_weight, *pieces[:early]),
-        [IN_SMEM, IN_HBM] + [IN_VMEM] * early,
-        [
-            pltpu.VMEM((early, channels, tokens), BF16),
-            pltpu.VMEM((early, channels, channels), BF16),
-            pltpu.SemaphoreType.DMA((early,)),
-        ],
-        "back_part", 6.0, 10,
-    )
-    conv_out, *partial_sums = call(
+            pltpu.SemaphoreType.DMA((2 * count,)),
+        ]
+
+    local, base = call(
+        middle_kernel,
+        [(tile_shape, F32), ((channels, tokens), F32)],
+        (order[:early], mixed, decay_tiles, scale_tiles, out_weight, *pieces[:early]),
+        [IN_SMEM] + [IN_VMEM] * 3 + [IN_HBM] * (1 + early),
+        back_scratch(early) + weight_scratch(early),
+        "middle", 6.0, 8,
+    )
+    conv_out, partial_sums = call(
         project_kernel,
-        [in_hbm(tile_shape, F32)] + [((tokens, channels), BF16)] * fans,
-        (order, arrived, local, decay_tiles, scale_tiles, base, query_feat, out_weight),
-        [IN_SMEM] + [IN_VMEM] * 5 + [IN_HBM] * 2,
+        [in_hbm(tile_shape, F32), in_hbm((tokens, fans * channels), BF16)],
+        (arrived, local, decay_tiles, scale_tiles, query_feat, out_weight, *pieces[early:]),
+        [IN_VMEM] * 4 + [IN_HBM] * (2 + fans - early),
         [
             tile,
             tile,
             pltpu.VMEM((tokens, channels), BF16),
             pltpu.VMEM((fans, channels, channels), BF16),
+            pltpu.VMEM((fans, tokens, channels), BF16),
             pltpu.SemaphoreType.DMA((fans + 2,)),
+            pltpu.SemaphoreType.DMA((fans,)),
         ],
         "project", 7.0, 16,
     )
-    if fans == 4:
-        parts = [
-            exchange(part, "ch", mask) if mask else part for mask, part in enumerate(partial_sums)
-        ]
-    else:
-        parts = lax.all_to_all(
-            jnp.stack(partial_sums), "ch", split_axis=0, concat_axis=0, tiled=True
-        )
-        parts = [parts[number] for number in range(fans)]
-    grad_gated, grad_mixed, back_messages, ahead = call(
+    projected = lax.psum_scatter(partial_sums, "ch", scatter_dimension=1, tiled=True)
+    back_query, grad_mixed, back_messages, ahead = call(
         functools.partial(back_last_kernel, rim=rim),
         [in_hbm(tile_shape, F32), (tile_shape, F32), (message_shape, BF16)]
         + [((4, rim * SUB, LANES), F32)],
         (
-            order[early:], position, out_weight, query_feat, key_feat, value_feat, conv_out,
-            decay_tiles, *pieces[early:], base,
+            order[early:], position, base, decay_tiles, out_weight, query_feat, key_feat,
+            value_feat, conv_out, *pieces[early:],
         ),
-        [IN_SMEM] * 2 + [IN_HBM] * 5 + [IN_VMEM] * 3,
-        back_scratch(fans - early),
-        "back_last", 5.0, 8,
+        [IN_SMEM] * 2 + [IN_VMEM] * 2 + [IN_HBM] * (5 + fans - early),
+        back_scratch(fans - early)
+        + [pltpu.VMEM((channels, tokens), F32), tile, tile, tile]
+        + weight_scratch(fans - early)
+        + [pltpu.SemaphoreType.DMA((5,))],
+        "back_last", 6.0, 12,
     )
     back_arrived = lax.all_to_all(back_messages, "ctx", split_axis=0, concat_axis=0, tiled=True)
     ahead = shift(ahead, "ctx", -1)
     (back_local,) = call(
-        functools.partial(local_conv_kernel, reverse=True),
+        back_local_kernel,
         [(tile_shape, F32)], (grad_mixed, decay_tiles, scale_tiles), [IN_VMEM] * 3, [],
-        "back_local_conv", 2.3, 2,
+        "back_local", 2.3, 2,
     )
     (grad_query,) = call(
         finish_query_kernel,
         [in_hbm((tokens, channels), BF16)],
-        (grad_gated, conv_out, ahead, tap_rows),
-        [IN_HBM] * 4,
-        [
-            tile,
-            tile,
+        (back_query, ahead, tap_rows),
+        [IN_HBM] * 3,
+        [
             pltpu.VMEM((wide_rows, LANES), F32),
             tile,
             pltpu.VMEM((tokens, channels), BF16),
             pltpu.VMEM((taps, channels), F32),
             tap_tiles,
-            pltpu.SemaphoreType.DMA((4,)),
+            pltpu.SemaphoreType.DMA((3,)),
         ],
-        "finish_query", 2.5, 7,
+        "finish_query", 2.5, 5,
     )
     grad_key, grad_value = call(
         finish_kernel,
@@ -666,17 +642,6 @@
         ],
         "finish", 4.0, 10,
     )
-    (projected,) = call(
-        add_parts_kernel, [in_hbm((tokens, channels), BF16)], (*parts, grad_key),
-        [IN_HBM] * (fans + 1),
-        [
-            pltpu.VMEM((fans, tokens, channels), BF16),
-            pltpu.VMEM((tokens, channels), BF16),
-            pltpu.SemaphoreType.DMA((4, fans)),
-            pltpu.SemaphoreType.DMA((4,)),
-        ],
-        "add_parts", 1.5, 4,
-    )
     return (projected, grad_query, grad_key, grad_value)
 
 

time: 84.2 us -> 88.9 us (1.056)
  the two profiles are of different devices: /device:TPU:9 before, /device:TPU:0 now
where the time goes in v4:
time: 88.9 us; the launch traced here: 88.4 us
  Pallas kernels  38.4 us (43%)
  starting transfers between devices  18.6 us (21%)
  waiting for transfers between devices  15.7 us (18%)
  between operations  14.1 us (16%)
  local copies, waits for them, and re-layouts  1.5 us (2%)
    pallas_call x8, Pallas kernels, call(): pl.pallas_call(kernel, out_shape=[jax.ShapeDtypeStruct(*out) if own else...  38.4 us
    reduce_scatter x1, waiting for transfers between devices, shards(): lax.psum_scatter(partial_sums, 'ch', scatter_dimension=1, tiled=True)  8.33 us
    all_to_all x1, starting transfers between devices, shards(): lax.all_to_all(messages, 'ctx', split_axis=0, concat_axis=0, tiled=True)  5.97 us
    all_to_all x1, starting transfers between devices, shards(): lax.all_to_all(back_messages, 'ctx', split_axis=0, concat_axis=0, tiled=T...  5.03 us
    ppermute x3, waiting for transfers between devices, exchange(): return lax.ppermute(value, axis, [(s, s ^ mask) for s in range(count)])  4.81 us
    ppermute x3, starting transfers between devices, exchange(): return lax.ppermute(value, axis, [(s, s ^ mask) for s in range(count)])  3.93 us
    ppermute x2, starting transfers between devices, shift(): return lax.ppermute(value, axis, pairs)  3.64 us
    all_to_all x1, waiting for transfers between devices, shards(): lax.all_to_all(back_messages, 'ctx', split_axis=0, concat_axis=0, tiled=T...  2.56 us
  transfers between devices with their start and end apart: 8, of which 4 were waited for; matrix products, arithmetic and copies ran while one was open for 0% of the time, Pallas kernels for 34%

profile of v4, /device:TPU:0, one launch (start us, length us, event | category | flops | bytes accessed | tf_op | source)
XLA Modules:
  0.0 88.4 jit_solution(14651812507836531860)
XLA Ops:
  7.2 0.8 rim.1
  8.0 2.4 %collective-permute-start = (bf16[48,1024]{1,0:T(8,128)(2,1)S(1)}, bf16[48,1024]{1,0:T(8,128)(2,1)S(1)}, u32[]{:S(2)}, u32[]{:S(2)}) collective-permute-start(bf16[48,1024]{1,0:T(8,128)(2,1)S(1)} %rim.1), channel_id=1, source_target_pairs={{0,4},{4,8},{8,12},{12,16},{16,20},{20,24},{24,28},{1,5},{5,9},{9,... | collective-permute-start | bytes 294920 | tf_op jit(solution)/shard_map/ppermute | solution.py:489
  10.4 2.4 %collective-permute-start.1 = (bf16[256,1024]{1,0:T(8,128)(2,1)}, bf16[256,1024]{1,0:T(8,128)(2,1)S(1)}, u32[]{:S(2)}, u32[]{:S(2)}) collective-permute-start(bf16[256,1024]{1,0:T(8,128)(2,1)} %refs_0_), channel_id=1, source_target_pairs={{0,1},{1,0},{2,3},{3,2},{4,5},{5,4},{6,7},{7,6},{8,9},{9,8},{10,11... | collective-permute-start | bytes 1572872 | tf_op jit(solution)/shard_map/ppermute | solution.py:494
  12.7 1.5 %collective-permute-start.2 = (bf16[256,1024]{1,0:T(8,128)(2,1)}, bf16[256,1024]{1,0:T(8,128)(2,1)}, u32[]{:S(2)}, u32[]{:S(2)}) collective-permute-start(bf16[256,1024]{1,0:T(8,128)(2,1)} %refs_0_), channel_id=1, source_target_pairs={{0,2},{1,3},{2,0},{3,1},{4,6},{5,7},{6,4},{7,5},{8,10},{9,11},{10,... | collective-permute-start | bytes 1572872 | tf_op jit(solution)/shard_map/ppermute | solution.py:494
  14.3 0.0 collective-permute-start.3
  14.3 0.0 collective-permute-done.halo_ref
  14.3 6.1 %featurize.1 = (f32[2048,128]{1,0:T(8,128)}, f32[2048,128]{1,0:T(8,128)}, f32[2048,128]{1,0:T(8,128)}, f32[2048,128]{1,0:T(8,128)S(1)}, bf16[8,128,128]{2,1,0:T(...) custom-call(s32[1]{0:T(128)} %bitcast.position_ref, bf16[256,1024]{1,0:T(8,128)(2,1)} %q_ref.3, ...), custom_call_target="tpu_custom_call" | custom-call | bytes 17500000 | tf_op jit(solution)/shard_map/featurize/pallas_call | solution.py:472
  20.4 6.0 %all-to-all-start = ((bf16[8,128,128]{2,1,0:T(8,128)(2,1)}), bf16[8,128,128]{2,1,0:T(8,128)(2,1)S(1)}, u32[]{:S(2)}, u32[]{:S(2)}) async-start(bf16[8,128,128]{2,1,0:T(8,128)(2,1)} %get-tuple-element.24), calls=%async_computation | async-start | bytes 524288 | tf_op jit(solution)/shard_map/all_to_all | solution.py:547
  26.4 0.0 reduce-scatter.2.cloned.1.call-start
  26.4 0.1 fusion
  26.5 0.0 collective-permute-done.1.refs_1_
  26.5 0.0 copy-start
  26.5 0.8 copy-done
  27.3 5.7 %middle.1 = (f32[2048,128]{1,0:T(8,128)S(1)}, f32[1024,256]{1,0:T(8,128)S(1)}) custom-call(s32[2]{0:T(128)S(1)} %get-tuple-element.43.index_ref, f32[2048,128]{1,0:T(8,128)S(1)} %get-tuple-element.25.signal_ref, f32[128,128]{1,0:T(8,128)S(1)} %get-tuple-element.26.decay_ref, f32[128,128]{1,0:T(8,128)S(1)} %get-tuple-element.27.scale_ref, ...), custom_call_target="tpu_custom_call" | custom-call | bytes 21000000 | tf_op jit(solution)/shard_map/middle/pallas_call | solution.py:472
  33.0 4.6 %collective-permute-done.2.refs_0_ = bf16[256,1024]{1,0:T(8,128)(2,1)} collective-permute-done((bf16[256,1024]{1,0:T(8,128)(2,1)}, bf16[256,1024]{1,0:T(8,128)(2,1)}, u32[]{:S(2)}, u32[]{:S(2)}) %collective-permute-start.2) | collective-permute-done | bytes 524320 | tf_op jit(solution)/shard_map/ppermute | solution.py:494
  37.6 0.2 collective-permute-done.3.refs_1_
  37.8 0.0 all-to-all-done.message_ref
  37.8 7.9 %project.1 = (f32[2048,128]{1,0:T(8,128)}, bf16[256,4096]{1,0:T(8,128)(2,1)}) custom-call(bf16[8,128,128]{2,1,0:T(8,128)(2,1)S(1)} %all-to-all-done.message_ref, f32[2048,128]{1,0:T(8,128)S(1)} %get-tuple-element.29.local_ref, f32[128,128]{1,0:T(8,128)S(1)} %get-tuple-element.26.decay_ref, f32[128,128]{1,0:T(8,128)S(1)} %get-tuple-element.27.scale_ref, ...), custom_call_target="tpu_custom_call" | custom-call | bytes 24500000 | tf_op jit(solution)/shard_map/project/pallas_call | solution.py:472
  45.7 0.0 reduce-scatter.2.cloned.1.call-update
  45.7 8.2 %back_last.1 = (f32[2048,128]{1,0:T(8,128)}, f32[2048,128]{1,0:T(8,128)S(1)}, bf16[8,128,128]{2,1,0:T(8,128)(2,1)}, f32[4,48,128]{2,1,0:T(8,128)}) custom-call(s32[2]{0:T(128)S(1)} %get-tuple-element.42.index_ref, s32[1]{0:T(128)} %bitcast.position_ref, f32[1024,256]{1,0:T(8,128)S(1)} %get-tuple-element.32.base_ref, ...), custom_call_target="tpu_custom_call" | custom-call | bytes 21000000 | tf_op jit(solution)/shard_map/back_last/pallas_call | solution.py:472
  54.0 5.0 %all-to-all-start.1 = ((bf16[8,128,128]{2,1,0:T(8,128)(2,1)}), bf16[8,128,128]{2,1,0:T(8,128)(2,1)S(1)}, u32[]{:S(2)}, u32[]{:S(2)}) async-start(bf16[8,128,128]{2,1,0:T(8,128)(2,1)} %get-tuple-element.38), calls=%async_computation.2 | async-start | bytes 524288 | tf_op jit(solution)/shard_map/all_to_all | solution.py:602
  59.0 1.3 %collective-permute-start.4 = (f32[4,48,128]{2,1,0:T(8,128)}, f32[4,48,128]{2,1,0:T(8,128)S(1)}, u32[]{:S(2)}, u32[]{:S(2)}) collective-permute-start(f32[4,48,128]{2,1,0:T(8,128)} %get-tuple-element.37), channel_id=1, source_target_pairs={{4,0},{8,4},{12,8},{16,12},{20,16},{24,20},{28,24},{5,1},{9,5},{13... | collective-permute-start | bytes 294920 | tf_op jit(solution)/shard_map/ppermute | solution.py:489
  60.3 2.3 %back_local.1.local_ref = f32[2048,128]{1,0:T(8,128)S(1)} custom-call(f32[2048,128]{1,0:T(8,128)S(1)} %get-tuple-element.39.signal_ref, f32[128,128]{1,0:T(8,128)S(1)} %get-tuple-element.26.decay_ref, f32[128,128]{1,0:T(8,128)S(1)} %get-tuple-element.27.scale_ref), custom_call_target="tpu_custom_call" | custom-call | bytes 8049999 | tf_op jit(solution)/shard_map/back_local/pallas_call | solution.py:472
  62.6 0.0 collective-permute-done.4.ahead_ref
  62.6 0.0 copy-start.1
  62.6 0.6 copy-done.1
  63.2 3.0 %finish_query.1 = bf16[256,1024]{1,0:T(8,128)(2,1)} custom-call(f32[2048,128]{1,0:T(8,128)} %get-tuple-element.36.back_query_ref, f32[4,48,128]{2,1,0:T(8,128)} %copy-done.1, f32[3,7,1024]{2,1,0:T(8,128)} %bitcast.5), custom_call_target="tpu_custom_call" | custom-call | bytes 8750000 | tf_op jit(solution)/shard_map/finish_query/pallas_call | solution.py:472
  66.2 2.6 %all-to-all-done.1.message_ref = bf16[8,128,128]{2,1,0:T(8,128)(2,1)S(1)} async-done(((bf16[8,128,128]{2,1,0:T(8,128)(2,1)}), bf16[8,128,128]{2,1,0:T(8,128)(2,1)S(1)}, u32[]{:S(2)}, u32[]{:S(2)}) %all-to-all-start.1) | async-done | bytes 262176 | tf_op jit(solution)/shard_map/all_to_all | solution.py:602
  68.7 4.5 %finish.1 = (bf16[256,1024]{1,0:T(8,128)(2,1)}, bf16[256,1024]{1,0:T(8,128)(2,1)}) custom-call(bf16[8,128,128]{2,1,0:T(8,128)(2,1)S(1)} %all-to-all-done.1.message_ref, f32[2048,128]{1,0:T(8,128)S(1)} %back_local.1.local_ref, f32[128,128]{1,0:T(8,128)S(1)} %get-tuple-element.26.decay_ref, f32[128,128]{1,0:T(8,128)S(1)} %get-tuple-element.27.scale_ref, ...), custom_call_target="tpu_custom_call" | custom-call | bytes 14000000 | tf_op jit(solution)/shard_map/finish/pallas_call | solution.py:472
  73.2 8.3 %reduce-scatter.2.cloned.1.call-done = bf16[256,1024]{1,0:T(8,128)(2,1)} async-done(((bf16[256,4096]{1,0:T(8,128)(2,1)}), bf16[256,1024]{1,0:T(8,128)(2,1)}) %reduce-scatter.2.cloned.1.call-update) | async-done | bytes 524304 | tf_op jit(solution)/shard_map/reduce_scatter | solution.py:586
  (1 shorter events, 0.0 us)
Async XLA Ops:
  8.0 6.3 %collective-permute-start = (bf16[48,1024]{1,0:T(8,128)(2,1)S(1)}, bf16[48,1024]{1,0:T(8,128)(2,1)S(1)}, u32[]{:S(2)}, u32[]{:S(2)}) collective-permute-start(bf16[48,1024]{1,0:T(8,128)(2,1)S(1)} %rim.1), channel_id=1, source_target_pairs={{0,4},{4,8},{8,12},{12,16},{16,20},{20,24},{24,28},{1,5},{5,9},{9,... | collective-permute-start | bytes 294920 | tf_op jit(solution)/shard_map/ppermute | solution.py:489
  10.4 16.1 %collective-permute-start.1 = (bf16[256,1024]{1,0:T(8,128)(2,1)}, bf16[256,1024]{1,0:T(8,128)(2,1)S(1)}, u32[]{:S(2)}, u32[]{:S(2)}) collective-permute-start(bf16[256,1024]{1,0:T(8,128)(2,1)} %refs_0_), channel_id=1, source_target_pairs={{0,1},{1,0},{2,3},{3,2},{4,5},{5,4},{6,7},{7,6},{8,9},{9,8},{10,11... | collective-permute-start | bytes 1572872 | tf_op jit(solution)/shard_map/ppermute | solution.py:494
  12.7 24.8 %collective-permute-start.2 = (bf16[256,1024]{1,0:T(8,128)(2,1)}, bf16[256,1024]{1,0:T(8,128)(2,1)}, u32[]{:S(2)}, u32[]{:S(2)}) collective-permute-start(bf16[256,1024]{1,0:T(8,128)(2,1)} %refs_0_), channel_id=1, source_target_pairs={{0,2},{1,3},{2,0},{3,1},{4,6},{5,7},{6,4},{7,5},{8,10},{9,11},{10,... | collective-permute-start | bytes 1572872 | tf_op jit(solution)/shard_map/ppermute | solution.py:494
  14.3 23.5 %collective-permute-start.3 = (bf16[256,1024]{1,0:T(8,128)(2,1)}, bf16[256,1024]{1,0:T(8,128)(2,1)}, u32[]{:S(2)}, u32[]{:S(2)}) collective-permute-start(bf16[256,1024]{1,0:T(8,128)(2,1)} %refs_0_), channel_id=1, source_target_pairs={{0,3},{1,2},{2,1},{3,0},{4,7},{5,6},{6,5},{7,4},{8,11},{9,10},{10,... | collective-permute-start | bytes 1572872 | tf_op jit(solution)/shard_map/ppermute | solution.py:494
  20.4 17.4 %all-to-all-start = ((bf16[8,128,128]{2,1,0:T(8,128)(2,1)}), bf16[8,128,128]{2,1,0:T(8,128)(2,1)S(1)}, u32[]{:S(2)}, u32[]{:S(2)}) async-start(bf16[8,128,128]{2,1,0:T(8,128)(2,1)} %get-tuple-element.24), calls=%async_computation | async-start | bytes 524288 | tf_op jit(solution)/shard_map/all_to_all | solution.py:547
  26.4 55.2 %reduce-scatter.2.cloned.1.call-start = ((), (), s32[]{:S(2)}) async-start(), calls=%async_computation.3 | async-start | bytes 2621440 | tf_op jit(solution)/shard_map/reduce_scatter | solution.py:586
  26.5 0.8 copy-start
  54.0 14.8 %all-to-all-start.1 = ((bf16[8,128,128]{2,1,0:T(8,128)(2,1)}), bf16[8,128,128]{2,1,0:T(8,128)(2,1)S(1)}, u32[]{:S(2)}, u32[]{:S(2)}) async-start(bf16[8,128,128]{2,1,0:T(8,128)(2,1)} %get-tuple-element.38), calls=%async_computation.2 | async-start | bytes 524288 | tf_op jit(solution)/shard_map/all_to_all | solution.py:602
  59.0 3.6 %collective-permute-start.4 = (f32[4,48,128]{2,1,0:T(8,128)}, f32[4,48,128]{2,1,0:T(8,128)S(1)}, u32[]{:S(2)}, u32[]{:S(2)}) collective-permute-start(f32[4,48,128]{2,1,0:T(8,128)} %get-tuple-element.37), channel_id=1, source_target_pairs={{4,0},{8,4},{12,8},{16,12},{20,16},{24,20},{28,24},{5,1},{9,5},{13... | collective-permute-start | bytes 294920 | tf_op jit(solution)/shard_map/ppermute | solution.py:489
  62.6 0.6 copy-start.1
Sparse Core Ops, SparseCore 0:
  45.9 35.6 reduce-scatter.1

commit v5 on v4

v5 whole, which is shorter than its diff:
```python
import functools

import jax
import jax.numpy as jnp
from jax import lax
from jax.experimental import pallas as pl
from jax.experimental.pallas import tpu as pltpu
from jax.sharding import PartitionSpec as P

SUB = 8
LANES = 128
STEP = 8
F32 = jnp.float32
BF16 = jnp.bfloat16


def as_tiles(rows):
    return rows.reshape(rows.shape[0] // SUB, SUB, LANES)


def as_rows(tiles):
    return tiles.reshape(tiles.shape[0] * SUB, LANES)


def tile(ref, token):
    return ref[pl.ds(pl.multiple_of(token * SUB, SUB), SUB), :]


def tree_sum(terms):
    while len(terms) > 1:
        terms = [
            terms[i] + terms[i + 1] if i + 1 < len(terms) else terms[i]
            for i in range(0, len(terms), 2)
        ]
    return terms[0]


def round16(value):
    return value.astype(BF16).astype(F32)


def scatter_tokens(ref, value, first_token):
    tokens, channels = value.shape
    for group in range(channels // LANES):
        ref[pl.ds(first_token * SUB + group, tokens, stride=SUB), :] = value[
            :, group * LANES : (group + 1) * LANES
        ]


def gather_tokens(rows, out_ref):
    for group in range(out_ref.shape[1] // LANES):
        out_ref[:, group * LANES : (group + 1) * LANES] = rows(group).astype(out_ref.dtype)


def group_rows(ref, group, tokens):
    return ref[pl.ds(group, tokens, stride=SUB), :]


def start_all(copies):
    for copy in copies:
        copy.start()
    return copies


def wait_all(copies):
    for copy in copies:
        copy.wait()


def advance_states(signal_ref, factors, states, first, count, reverse):
    last = signal_ref.shape[0] // SUB - 1

    def body(step, states):
        for inner in range(STEP):
            token = first + step * STEP + inner
            u = tile(signal_ref, last - token if reverse else token)
            states = [factor * state + u for factor, state in zip(factors, states)]
        return states

    return lax.fori_loop(0, count // STEP, body, states)


def zero_states(modes):
    return [jnp.zeros((SUB, LANES), F32) for _ in range(modes)]


def mode_rows(n):
    return slice(n * SUB, (n + 1) * SUB)


def fades(decay_ref, tokens):
    return [
        jnp.exp(-decay_ref[mode_rows(n), :] * tokens) for n in range(decay_ref.shape[0] // SUB)
    ]


def write_messages(out_ref, states, decay_ref, position_ref, tokens, direction):
    count = out_ref.shape[0]
    out_ref[...] = jnp.zeros_like(out_ref)
    fade = fades(decay_ref, float(tokens))
    for gap in range(count - 1):
        other = position_ref[0] + direction * (gap + 1)
        value = jnp.concatenate(states, axis=0).astype(out_ref.dtype)

        @pl.when((other >= 0) & (other < count))
        def _():
            out_ref[jnp.clip(other, 0, count - 1)] = value

        states = [state * factor for state, factor in zip(states, fade)]


def read_messages(in_ref):
    total = in_ref[0].astype(F32)
    for other in range(1, in_ref.shape[0]):
        total = total + in_ref[other].astype(F32)
    return [total[mode_rows(n)] for n in range(total.shape[0] // SUB)]


def rim_kernel(
    q_ref, k_ref, v_ref, taps_ref, residue_ref, decay_ref,
    rim_ref, streams_ref, taps_vmem, residue_vmem, decay_vmem, sems,
):
    rows = rim_ref.shape[0] // 3
    streams = (q_ref, k_ref, v_ref)
    rims = [
        pltpu.make_async_copy(
            source.at[pl.ds(source.shape[0] - rows, rows), :],
            rim_ref.at[pl.ds(stream * rows, rows), :],
            sems.at[stream],
        )
        for stream, source in enumerate(streams)
    ]
    pairs = [(source, streams_ref.at[stream]) for stream, source in enumerate(streams)]
    pairs += [(taps_ref, taps_vmem), (residue_ref, residue_vmem), (decay_ref, decay_vmem)]
    others = [
        pltpu.make_async_copy(source, target, sems.at[3 + number])
        for number, (source, target) in enumerate(pairs)
    ]
    wait_all(start_all(rims + others))


def filtered(window, taps_ref, stream, taps, steps, forward):
    total = None
    for tap in range(taps):
        first = taps - 1 - tap if forward else tap
        term = taps_ref[pl.ds((stream * taps + tap) * SUB, SUB), :] * window[first : first + steps]
        total = term if total is None else total + term
    return total


def featurize_kernel(
    position_ref, streams_ref, taps_in_ref, residue_ref, decay_in_ref, halo_ref,
    qf_ref, kf_ref, vf_ref, mixed_ref, message_ref, taps_ref, scale_ref, decay_ref,
    wide_ref, feat_ref, sems,
):
    tokens = streams_ref.shape[1]
    _, taps, _ = taps_in_ref.shape
    rim = taps - 1
    modes = decay_in_ref.shape[0]
    held = halo_ref.shape[0] // 3
    decays = decay_in_ref[...]
    scatter_tokens(decay_ref, decays, 0)
    scatter_tokens(scale_ref, residue_ref[...] * jnp.sqrt(decays), 0)
    for stream in range(3):
        scatter_tokens(taps_ref, taps_in_ref[stream], stream * taps)
        behind = halo_ref[stream * held : (stream + 1) * held, :].astype(F32)
        scatter_tokens(wide_ref.at[stream], behind[held - rim :], 0)
        scatter_tokens(wide_ref.at[stream], streams_ref[stream].astype(F32), rim)

    def body(step, carry):
        begin = pl.multiple_of(step * STEP * SUB, SUB)
        rows = pl.ds(begin, STEP * SUB)
        feats = []
        for stream in range(3):
            window = as_tiles(wide_ref[stream, pl.ds(begin, (STEP + rim) * SUB), :])
            feats.append(filtered(window, taps_ref, stream, taps, STEP, True))
            feat_ref[stream, rows, :] = as_rows(feats[-1])
        mixed_ref[rows, :] = as_rows(round16(feats[1] * feats[2]))
        return carry

    lax.fori_loop(0, tokens // STEP, body, 0)
    copies = start_all(
        [
            pltpu.make_async_copy(feat_ref.at[stream], target, sems.at[stream])
            for stream, target in enumerate((qf_ref, kf_ref, vf_ref))
        ]
    )
    states = advance_states(
        mixed_ref, fades(decay_ref, 1.0), zero_states(modes), 0, tokens, False
    )
    write_messages(message_ref, states, decay_ref, position_ref, tokens, 1)
    wait_all(copies)


def scales_of(scale_ref):
    return [scale_ref[mode_rows(n), :] for n in range(scale_ref.shape[0] // SUB)]


def local_conv(signal_ref, decay_ref, scale_ref, out_ref, reverse):
    tokens = signal_ref.shape[0] // SUB
    factors = fades(decay_ref, 1.0)
    scales = scales_of(scale_ref)

    def body(step, states):
        for inner in range(STEP):
            token = step * STEP + inner
            token = tokens - 1 - token if reverse else token
            u = tile(signal_ref, token)
            states = [factor * state + u for factor, state in zip(factors, states)]
            out_ref[pl.ds(pl.multiple_of(token * SUB, SUB), SUB), :] = tree_sum(
                [scale * state for scale, state in zip(scales, states)]
            )
        return states

    lax.fori_loop(0, tokens // STEP, body, zero_states(len(factors)))


def back_local_kernel(signal_ref, decay_ref, scale_ref, out_ref):
    local_conv(signal_ref, decay_ref, scale_ref, out_ref, True)


def add_carried(local_ref, out_ref, states, decay_ref, scale_ref, reverse):
    tokens = local_ref.shape[0] // SUB
    factors = fades(decay_ref, 1.0)
    scaled = [scale * state for scale, state in zip(scales_of(scale_ref), states)]

    def body(step, scaled):
        for inner in range(STEP):
            token = step * STEP + inner
            token = tokens - 1 - token if reverse else token
            scaled = [factor * state for factor, state in zip(factors, scaled)]
            rows = pl.ds(pl.multiple_of(token * SUB, SUB), SUB)
            out_ref[rows, :] = local_ref[rows, :] + tree_sum(list(scaled))
        return scaled

    lax.fori_loop(0, tokens // STEP, body, scaled)


def project_kernel(
    index_ref, message_ref, local_ref, decay_ref, scale_ref, _, qf_ref, weight_ref, conv_ref, *refs
):
    *out_refs, rows_ref, feat_ref, gated_ref, held_ref, sent_ref, sems, out_sems = refs
    parts, tokens, width = sent_ref.shape
    order = list(reversed(range(parts)))
    copies = [
        pltpu.make_async_copy(
            weight_ref.at[:, pl.ds(pl.multiple_of(index_ref[part] * width, width), width)],
            held_ref.at[part],
            sems.at[part],
        )
        for part in range(parts)
    ]
    outs = [
        pltpu.make_async_copy(sent_ref.at[part], out_refs[part], out_sems.at[part])
        for part in range(parts)
    ]
    feat_copy = pltpu.make_async_copy(qf_ref, feat_ref, sems.at[parts])
    feat_copy.start()
    start_all([copies[part] for part in order])
    add_carried(local_ref, rows_ref, read_messages(message_ref), decay_ref, scale_ref, False)
    conv_copy = pltpu.make_async_copy(rows_ref, conv_ref, sems.at[parts + 1])
    conv_copy.start()
    feat_copy.wait()
    gather_tokens(
        lambda group: group_rows(rows_ref, group, tokens) * group_rows(feat_ref, group, tokens),
        gated_ref,
    )
    for part in order:
        copies[part].wait()
        sent_ref[part] = jnp.dot(
            gated_ref[...], held_ref[part], preferred_element_type=F32
        ).astype(sent_ref.dtype)
        outs[part].start()
    conv_copy.wait()
    wait_all(outs)


def add_parts_kernel(*refs):
    *part_refs, _, out_ref, held_ref, total_ref, sems, out_sems = refs
    chunks = out_sems.shape[0]
    rows = out_ref.shape[0] // chunks
    numbers = range(len(part_refs))
    fetches = [
        start_all(
            [
                pltpu.make_async_copy(
                    part_refs[number].at[pl.ds(chunk * rows, rows), :],
                    held_ref.at[number, pl.ds(chunk * rows, rows), :],
                    sems.at[chunk, number],
                )
                for number in numbers
            ]
        )
        for chunk in range(chunks)
    ]
    outs = []
    for chunk in range(chunks):
        wait_all(fetches[chunk])
        here = pl.ds(chunk * rows, rows)
        total_ref[here, :] = tree_sum(
            [held_ref[number, here, :].astype(F32) for number in numbers]
        ).astype(total_ref.dtype)
        outs.append(
            pltpu.make_async_copy(total_ref.at[here, :], out_ref.at[here, :], out_sems.at[chunk])
        )
        outs[-1].start()
    wait_all(outs)


def start_weights(index_ref, weight_ref, held_ref, sems):
    count, _, width = held_ref.shape
    return start_all(
        [
            pltpu.make_async_copy(
                weight_ref.at[:, pl.ds(pl.multiple_of(index_ref[number] * width, width), width)],
                held_ref.at[number],
                sems.at[number],
            )
            for number in range(count)
        ]
    )


def back_products(weights, piece_refs, turned_ref, held_ref, total_ref, before_ref):
    for number, ref in enumerate(piece_refs):
        turned_ref[number] = ref[...].T
    for number in range(len(piece_refs)):
        weights[number].wait()
        product = jnp.dot(held_ref[number], turned_ref[number], preferred_element_type=F32)
        earlier = before_ref if number == 0 else total_ref
        total_ref[...] = product if earlier is None else earlier[...] + product


def middle_kernel(index_ref, signal_ref, decay_ref, scale_ref, weight_ref, own_ref, *refs):
    *piece_refs, local_ref, total_ref, own_vmem, turned_ref, held_ref, own_sem, sems = refs
    own = pltpu.make_async_copy(own_ref, own_vmem, own_sem)
    own.start()
    weights = start_weights(index_ref, weight_ref, held_ref, sems)
    local_conv(signal_ref, decay_ref, scale_ref, local_ref, False)
    own.wait()
    back_products(weights, [own_vmem, *piece_refs], turned_ref, held_ref, total_ref, None)


def back_last_kernel(
    index_ref, position_ref, base_ref, decay_ref, weight_ref, qf_ref, kf_ref, vf_ref, conv_ref,
    *refs, rim,
):
    (
        *piece_refs, back_query_ref, mixed_ref, message_ref, ahead_ref,
        turned_ref, total_ref, rows_ref, feat_ref, conv_vmem, held_ref, sems, own_sems,
    ) = refs
    tokens = total_ref.shape[1]
    heads = pl.ds(0, rim * SUB)
    weights = start_weights(index_ref, weight_ref, held_ref, sems)
    copies = start_all(
        [
            pltpu.make_async_copy(qf_ref, feat_ref, own_sems.at[0]),
            pltpu.make_async_copy(conv_ref, conv_vmem, own_sems.at[1]),
            pltpu.make_async_copy(kf_ref.at[heads, :], ahead_ref.at[2], own_sems.at[2]),
            pltpu.make_async_copy(vf_ref.at[heads, :], ahead_ref.at[3], own_sems.at[3]),
        ]
    )
    back_products(weights, piece_refs, turned_ref, held_ref, total_ref, base_ref)
    scatter_tokens(rows_ref, total_ref[...].T, 0)
    wait_all(copies)
    mixed_ref[...] = round16(rows_ref[...] * feat_ref[...])
    rows_ref[...] = round16(rows_ref[...] * conv_vmem[...])
    out = pltpu.make_async_copy(rows_ref, back_query_ref, own_sems.at[4])
    out.start()
    ahead_ref[0] = rows_ref[: rim * SUB, :]
    ahead_ref[1] = mixed_ref[: rim * SUB, :]
    modes = decay_ref.shape[0] // SUB
    states = advance_states(
        mixed_ref, fades(decay_ref, 1.0), zero_states(modes), 0, tokens, True
    )
    write_messages(message_ref, states, decay_ref, position_ref, tokens, -1)
    out.wait()


def spread_back(wide_ref, taps_ref, stream, taps, rows_ref, out_ref):
    tokens = out_ref.shape[0]

    def body(step, carry):
        first = pl.multiple_of(step * STEP * SUB, SUB)
        window = as_tiles(wide_ref[pl.ds(first, (STEP + taps - 1) * SUB), :])
        rows_ref[pl.ds(first, STEP * SUB), :] = as_rows(
            filtered(window, taps_ref, stream, taps, STEP, False)
        )
        return carry

    lax.fori_loop(0, tokens // STEP, body, 0)
    gather_tokens(lambda group: group_rows(rows_ref, group, tokens), out_ref)


def finish_kernel(
    message_ref, local_ref, decay_ref, scale_ref, taps_ref, ahead_ref, query_ref, kf_ref, vf_ref,
    gq_ref, gk_ref, gv_ref, total_ref, feat_ref, wide_ref, rows_ref, out_vmem, sems, *, taps,
):
    tokens = gk_ref.shape[0]
    rim = taps - 1
    inside = pl.ds(0, tokens * SUB)
    copies = start_all(
        [
            pltpu.make_async_copy(query_ref, wide_ref.at[0, inside, :], sems.at[0]),
            pltpu.make_async_copy(vf_ref, feat_ref.at[0], sems.at[1]),
            pltpu.make_async_copy(kf_ref, feat_ref.at[1], sems.at[2]),
        ]
    )
    states = read_messages(message_ref)
    add_carried(local_ref, total_ref, states, decay_ref, scale_ref, True)
    growth = fades(decay_ref, -1.0)
    scales = scales_of(scale_ref)
    for ahead in range(rim):
        rows = pl.ds((tokens + ahead) * SUB, SUB)
        theirs = pl.ds(ahead * SUB, SUB)
        grad_conv = tree_sum([scale * state for scale, state in zip(scales, states)])
        wide_ref[0, rows, :] = ahead_ref[0, theirs, :]
        wide_ref[1, rows, :] = round16(grad_conv * ahead_ref[3, theirs, :])
        wide_ref[2, rows, :] = round16(grad_conv * ahead_ref[2, theirs, :])
        arrived = ahead_ref[1, theirs, :]
        states = [(state - arrived) * grow for state, grow in zip(states, growth)]
    outs = []
    for stream, out_ref in enumerate((gq_ref, gk_ref, gv_ref)):
        copies[stream].wait()
        if stream:
            wide_ref[stream, inside, :] = round16(total_ref[...] * feat_ref[stream - 1])
        spread_back(
            wide_ref.at[stream], taps_ref, stream, taps, rows_ref, out_vmem.at[stream]
        )
        outs.append(pltpu.make_async_copy(out_vmem.at[stream], out_ref, sems.at[stream]))
        outs[-1].start()
    wait_all(outs)


IN_VMEM = pl.BlockSpec(memory_space=pltpu.VMEM)
IN_SMEM = pl.BlockSpec(memory_space=pltpu.SMEM)
IN_HBM = pl.BlockSpec(memory_space=pltpu.HBM)
HBM_RATE = 3.5e6


def in_hbm(shape, kind):
    return pltpu.HBM(shape, kind)


def call(kernel, outs, args, specs, scratch, name, micros, mebibytes):
    args = [
        pltpu.with_memory_space_constraint(arg, pltpu.HBM) if spec is IN_HBM else arg
        for arg, spec in zip(args, specs)
    ]
    held = [isinstance(out, tuple) for out in outs]
    return pl.pallas_call(
        kernel,
        out_shape=[jax.ShapeDtypeStruct(*out) if own else out for own, out in zip(held, outs)],
        in_specs=specs,
        out_specs=[IN_VMEM if own else IN_HBM for own in held],
        scratch_shapes=scratch,
        compiler_params=pltpu.CompilerParams(vmem_limit_bytes=mebibytes * 1024 * 1024),
        cost_estimate=pl.CostEstimate(
            flops=0, bytes_accessed=int(micros * HBM_RATE), transcendentals=0
        ),
        name=name,
    )(*args)


def shift(value, axis, steps):
    count = lax.axis_size(axis)
    pairs = [(s, s + steps) for s in range(count) if 0 <= s + steps < count]
    return lax.ppermute(value, axis, pairs)


def exchange(value, axis, mask):
    count = lax.axis_size(axis)
    return lax.ppermute(value, axis, [(s, s ^ mask) for s in range(count)])


def shards(query_in, key_in, value_in, short_taps, residues, decays, out_weight, out_grad):
    tokens, channels = query_in.shape
    taps = short_taps.shape[0]
    rim = taps - 1
    modes = decays.shape[1]
    blocks = lax.axis_size("ctx")
    fans = lax.axis_size("ch")
    position = lax.axis_index("ctx")[None].astype(jnp.int32)
    tile_shape = (tokens * SUB, LANES)
    mode_shape = (modes * SUB, LANES)
    message_shape = (blocks,) + mode_shape
    streams = (query_in, key_in, value_in)
    rim_rows = 16

    tap_rows = jnp.transpose(short_taps, (1, 0, 2))
    halo, narrow, taps_vmem, residues_vmem, decays_vmem = call(
        rim_kernel,
        [
            ((3 * rim_rows, channels), BF16),
            ((3, tokens, channels), BF16),
            ((3, taps, channels), F32),
            ((modes, channels), F32),
            ((modes, channels), F32),
        ],
        streams + (tap_rows, residues.T, decays.T), [IN_HBM] * 6,
        [pltpu.SemaphoreType.DMA((9,))], "rim", 1.2, 2,
    )
    halo, out_grad = lax.optimization_barrier((halo, out_grad))
    halo = shift(halo, "ctx", 1)
    if fans == 4:
        order = lax.axis_index("ch") ^ jnp.arange(fans, dtype=jnp.int32)
        near, far = exchange(out_grad, "ch", 1), exchange(out_grad, "ch", 2)
        pieces = [out_grad, near, far, exchange(near, "ch", 2)]
    else:
        order = jnp.arange(fans, dtype=jnp.int32)
        everyone = lax.all_gather(out_grad, "ch", axis=0, tiled=False)
        pieces = [everyone[number] for number in range(fans)]
    tile = pltpu.VMEM(tile_shape, F32)
    wide_rows = (tokens + rim) * SUB

    query_feat, key_feat, value_feat, mixed, messages, tap_tiles, scale_tiles, decay_tiles = call(
        featurize_kernel,
        [in_hbm(tile_shape, F32)] * 3
        + [(tile_shape, F32), (message_shape, BF16), ((3 * taps * SUB, LANES), F32)]
        + [(mode_shape, F32)] * 2,
        (position, narrow, taps_vmem, residues_vmem, decays_vmem, halo),
        [IN_SMEM] + [IN_VMEM] * 5,
        [
            pltpu.VMEM((3, wide_rows, LANES), F32),
            pltpu.VMEM((3,) + tile_shape, F32),
            pltpu.SemaphoreType.DMA((3,)),
        ],
        "featurize", 5.0, 8,
    )
    arrived = lax.all_to_all(messages, "ctx", split_axis=0, concat_axis=0, tiled=True)

    def weight_scratch(count):
        return [
            pltpu.VMEM((count, channels, channels), BF16),
            pltpu.SemaphoreType.DMA((count,)),
        ]

    early = fans - 1
    weights = weight_scratch(early)
    local, base = call(
        middle_kernel,
        [(tile_shape, F32), ((channels, tokens), F32)],
        (order[:early], mixed, decay_tiles, scale_tiles, out_weight, *pieces[:early]),
        [IN_SMEM] + [IN_VMEM] * 3 + [IN_HBM] * 2 + [IN_VMEM] * (early - 1),
        [
            pltpu.VMEM((tokens, channels), BF16),
            pltpu.VMEM((early, channels, tokens), BF16),
            weights[0],
            pltpu.SemaphoreType.DMA,
            weights[1],
        ],
        "middle", 6.0, 10,
    )
    conv_out, *partial_sums = call(
        project_kernel,
        [in_hbm(tile_shape, F32)] + [in_hbm((tokens, channels), BF16)] * fans,
        (order, arrived, local, decay_tiles, scale_tiles, base, query_feat, out_weight),
        [IN_SMEM] + [IN_VMEM] * 5 + [IN_HBM] * 2,
        [
            tile,
            tile,
            pltpu.VMEM((tokens, channels), BF16),
            pltpu.VMEM((fans, channels, channels), BF16),
            pltpu.VMEM((fans, tokens, channels), BF16),
            pltpu.SemaphoreType.DMA((fans + 2,)),
            pltpu.SemaphoreType.DMA((fans,)),
        ],
        "project", 7.0, 16,
    )
    if fans == 4:
        parts = [
            exchange(part, "ch", mask) if mask else part for mask, part in enumerate(partial_sums)
        ]
    else:
        parts = lax.all_to_all(
            jnp.stack(partial_sums), "ch", split_axis=0, concat_axis=0, tiled=True
        )
        parts = [parts[number] for number in range(fans)]
    back_query, grad_mixed, back_messages, ahead = call(
        functools.partial(back_last_kernel, rim=rim),
        [in_hbm(tile_shape, F32), (tile_shape, F32), (message_shape, BF16)]
        + [((4, rim * SUB, LANES), F32)],
        (
            order[early:], position, base, decay_tiles, out_weight, query_feat, key_feat,
            value_feat, conv_out, *pieces[early:],
        ),
        [IN_SMEM] * 2 + [IN_VMEM] * 2 + [IN_HBM] * 5 + [IN_VMEM] * (fans - early),
        [
            pltpu.VMEM((fans - early, channels, tokens), BF16),
            pltpu.VMEM((channels, tokens), F32),
            tile,
            tile,
            tile,
        ]
        + weight_scratch(fans - early)
        + [pltpu.SemaphoreType.DMA((5,))],
        "back_last", 6.0, 9,
    )
    back_arrived = lax.all_to_all(back_messages, "ctx", split_axis=0, concat_axis=0, tiled=True)
    ahead = shift(ahead, "ctx", -1)
    (back_local,) = call(
        back_local_kernel,
        [(tile_shape, F32)], (grad_mixed, decay_tiles, scale_tiles), [IN_VMEM] * 3, [],
        "back_local", 2.3, 2,
    )
    grad_query, grad_key, grad_value = call(
        functools.partial(finish_kernel, taps=taps),
        [in_hbm((tokens, channels), BF16)] * 3,
        (
            back_arrived, back_local, decay_tiles, scale_tiles, tap_tiles, ahead, back_query,
            key_feat, value_feat,
        ),
        [IN_VMEM] * 6 + [IN_HBM] * 3,
        [
            tile,
            pltpu.VMEM((2,) + tile_shape, F32),
            pltpu.VMEM((3, wide_rows, LANES), F32),
            tile,
            pltpu.VMEM((3, tokens, channels), BF16),
            pltpu.SemaphoreType.DMA((3,)),
        ],
        "finish", 5.5, 10,
    )
    (projected,) = call(
        add_parts_kernel, [in_hbm((tokens, channels), BF16)], (*parts, grad_key),
        [IN_HBM] * (fans + 1),
        [
            pltpu.VMEM((fans, tokens, channels), BF16),
            pltpu.VMEM((tokens, channels), BF16),
            pltpu.SemaphoreType.DMA((4, fans)),
            pltpu.SemaphoreType.DMA((4,)),
        ],
        "add_parts", 1.5, 4,
    )
    return (projected, grad_query, grad_key, grad_value)


def solution(mesh):
    in_specs = (
        P("ctx", "ch"),
        P("ctx", "ch"),
        P("ctx", "ch"),
        P(None, None, "ch"),
        P("ch", None),
        P("ch", None),
        P("ch", None),
        P("ctx", "ch"),
    )
    out_specs = (P("ctx", "ch"), P("ctx", "ch"), P("ctx", "ch"), P("ctx", "ch"))
    return jax.shard_map(shards, mesh=mesh, in_specs=in_specs, out_specs=out_specs, check_vma=False)
```

time: 88.9 us -> 74.2 us (0.83)
  between operations: 14.1 us -> 0.78 us
  waiting for transfers between devices: 15.7 us -> 9.43 us
  starting transfers between devices: 18.6 us -> 22.6 us
  local copies, waits for them, and re-layouts: 1.5 us -> 4.6 us
  Pallas kernels: 38.4 us -> 36.2 us
    reduce_scatter x1 -> x0, waiting for transfers between devices: 8.33 us -> none  [shards(): lax.psum_scatter(partial_sums, 'ch', scatter_dimension=1, tiled=True)]
    ppermute x3 -> x6, starting transfers between devices: 3.93 us -> 9.91 us  [exchange(): return lax.ppermute(value, axis, [(s, s ^ mask) for s in range(count)])]
    all_to_all x1, waiting for transfers between devices: 2.56 us -> 6.16 us  [shards(): lax.all_to_all(back_messages, 'ctx', split_axis=0, concat_axis=0, tiled=T...]
    unnamed x4 -> x8, local copies, waits for them, and re-layouts: 1.42 us -> 4.02 us
    pallas_call x8, Pallas kernels: 38.4 us -> 36.2 us  [call(): pl.pallas_call(kernel, out_shape=[jax.ShapeDtypeStruct(*out) if own else...]
    ppermute x3 -> x6, waiting for transfers between devices: 4.81 us -> 3.26 us  [exchange(): return lax.ppermute(value, axis, [(s, s ^ mask) for s in range(count)])]
    all_to_all x1, starting transfers between devices: 5.97 us -> 4.88 us  [shards(): lax.all_to_all(messages, 'ctx', split_axis=0, concat_axis=0, tiled=True)]
    ppermute x2, starting transfers between devices: 3.64 us -> 2.73 us  [shift(): return lax.ppermute(value, axis, pairs)]
  transfers between devices with their start and end apart: 8 -> 10, of which waited for: 4 -> 2; matrix products, arithmetic and copies ran while one was open for 0% -> 1% of each run, Pallas kernels for 34% -> 44%
where the time goes in v5:
time: 74.2 us; the launch traced here: 73.7 us
  Pallas kernels  36.2 us (49%)
  starting transfers between devices  22.6 us (30%)
  waiting for transfers between devices  9.43 us (13%)
  local copies, waits for them, and re-layouts  4.6 us (6%)
  between operations  0.78 us (1%)
    pallas_call x8, Pallas kernels, call(): pl.pallas_call(kernel, out_shape=[jax.ShapeDtypeStruct(*out) if own else...  36.2 us
    ppermute x6, starting transfers between devices, exchange(): return lax.ppermute(value, axis, [(s, s ^ mask) for s in range(count)])  9.91 us
    all_to_all x1, waiting for transfers between devices, shards(): lax.all_to_all(back_messages, 'ctx', split_axis=0, concat_axis=0, tiled=T...  6.16 us
    all_to_all x1, starting transfers between devices, shards(): lax.all_to_all(back_messages, 'ctx', split_axis=0, concat_axis=0, tiled=T...  5.11 us
    all_to_all x1, starting transfers between devices, shards(): lax.all_to_all(messages, 'ctx', split_axis=0, concat_axis=0, tiled=True)  4.88 us
    unnamed x8, local copies, waits for them, and re-layouts  4.02 us
    ppermute x6, waiting for transfers between devices, exchange(): return lax.ppermute(value, axis, [(s, s ^ mask) for s in range(count)])  3.26 us
    ppermute x2, starting transfers between devices, shift(): return lax.ppermute(value, axis, pairs)  2.73 us
  transfers between devices with their start and end apart: 10, of which 2 were waited for; matrix products, arithmetic and copies ran while one was open for 1% of the time, Pallas kernels for 44%

profile of v5, /device:TPU:0, one launch (start us, length us, event | category | flops | bytes accessed | tf_op | source)
XLA Modules:
  0.0 73.7 jit_solution(14825579176723979705)
XLA Ops:
  0.6 1.5 %rim.1 = (bf16[48,1024]{1,0:T(8,128)(2,1)S(1)}, bf16[3,256,1024]{2,1,0:T(8,128)(2,1)S(1)}, f32[3,7,1024]{2,1,0:T(8,128)S(1)}, f32[16,1024]{1,0:T(8,128)S(1)}, f32[16,1024]{1,0:T(8,128)S(1)}) custom-call(bf16[256,1024]{1,0:T(8,128)(2,1)} %q_ref.1, bf16[256,1024]{1,0:T(8,128)(2,1)} %k_ref.1, bf16[256,1024]{1,0:T(8,128)(2,1)} %v_ref.1, f32[3,7,1024]{2,1,0:T(8,128)} %bitcast.6, ...), custom_call_target="tpu_custom_call" | custom-call | bytes 4200000 | tf_op jit(solution)/shard_map/rim/pallas_call | solution.py:451
  2.1 3.0 %collective-permute-start.1 = (bf16[256,1024]{1,0:T(8,128)(2,1)}, bf16[256,1024]{1,0:T(8,128)(2,1)}, u32[]{:S(2)}, u32[]{:S(2)}) collective-permute-start(bf16[256,1024]{1,0:T(8,128)(2,1)} %own_ref), channel_id=1, source_target_pairs={{0,1},{1,0},{2,3},{3,2},{4,5},{5,4},{6,7},{7,6},{8,9},{9,8},{10,11... | collective-permute-start | bytes 1572872 | tf_op jit(solution)/shard_map/ppermute | solution.py:473
  5.2 1.5 %collective-permute-start = (bf16[48,1024]{1,0:T(8,128)(2,1)S(1)}, bf16[48,1024]{1,0:T(8,128)(2,1)S(1)}, u32[]{:S(2)}, u32[]{:S(2)}) collective-permute-start(bf16[48,1024]{1,0:T(8,128)(2,1)S(1)} %get-tuple-element.38), channel_id=1, source_target_pairs={{0,4},{4,8},{8,12},{12,16},{16,20},{20,24},{24,28},{1,5},{5,9},{9,... | collective-permute-start | bytes 294920 | tf_op jit(solution)/shard_map/ppermute | solution.py:468
  6.6 1.6 %collective-permute-start.2 = (bf16[256,1024]{1,0:T(8,128)(2,1)}, bf16[256,1024]{1,0:T(8,128)(2,1)S(1)}, u32[]{:S(2)}, u32[]{:S(2)}) collective-permute-start(bf16[256,1024]{1,0:T(8,128)(2,1)} %own_ref), channel_id=1, source_target_pairs={{0,2},{1,3},{2,0},{3,1},{4,6},{5,7},{6,4},{7,5},{8,10},{9,11},{10,... | collective-permute-start | bytes 1572872 | tf_op jit(solution)/shard_map/ppermute | solution.py:473
  8.2 0.0 collective-permute-done.halo_ref
  8.2 5.0 %featurize.1 = (f32[2048,128]{1,0:T(8,128)}, f32[2048,128]{1,0:T(8,128)}, f32[2048,128]{1,0:T(8,128)}, f32[2048,128]{1,0:T(8,128)S(1)}, bf16[8,128,128]{2,1,0:T(...) custom-call(s32[1]{0:T(128)} %bitcast.position_ref, ...), custom_call_target="tpu_custom_call" | custom-call | bytes 17500000 | tf_op jit(solution)/shard_map/featurize/pallas_call | solution.py:451
  13.2 0.0 copy-start
  13.2 1.0 %copy-done = f32[2048,128]{1,0:T(8,128)} copy-done((f32[2048,128]{1,0:T(8,128)}, f32[2048,128]{1,0:T(8,128)S(1)}, u32[]{:S(2)}) %copy-start) | copy-done | bytes 1048600
  14.1 3.2 %collective-permute-done.1.refs_0_ = bf16[256,1024]{1,0:T(8,128)(2,1)} collective-permute-done((bf16[256,1024]{1,0:T(8,128)(2,1)}, bf16[256,1024]{1,0:T(8,128)(2,1)}, u32[]{:S(2)}, u32[]{:S(2)}) %collective-permute-start.1) | collective-permute-done | bytes 524320 | tf_op jit(solution)/shard_map/ppermute | solution.py:473
  17.4 1.8 %collective-permute-start.6 = (bf16[256,1024]{1,0:T(8,128)(2,1)}, bf16[256,1024]{1,0:T(8,128)(2,1)S(1)}, u32[]{:S(2)}, u32[]{:S(2)}) collective-permute-start(bf16[256,1024]{1,0:T(8,128)(2,1)} %collective-permute-done.1.refs_0_), channel_id=1, source_target_pairs={{0,2},{1,3},{2,0},{3,1},{4,6},{5,7},{6,4},{7,5},{8,10},{9,11},{10,... | collective-permute-start | bytes 1572872 | tf_op jit(solution)/shard_map/ppermute | solution.py:473
  19.2 4.9 %all-to-all-start = ((bf16[8,128,128]{2,1,0:T(8,128)(2,1)}), bf16[8,128,128]{2,1,0:T(8,128)(2,1)S(1)}, u32[]{:S(2)}, u32[]{:S(2)}) async-start(bf16[8,128,128]{2,1,0:T(8,128)(2,1)} %get-tuple-element.39), calls=%async_computation | async-start | bytes 524288 | tf_op jit(solution)/shard_map/all_to_all | solution.py:530
  24.0 0.0 collective-permute-done.2.refs_1_
  24.1 0.0 copy-start.2
  24.1 0.8 %copy-done.2 = bf16[256,1024]{1,0:T(8,128)(2,1)} copy-done((bf16[256,1024]{1,0:T(8,128)(2,1)}, bf16[256,1024]{1,0:T(8,128)(2,1)S(1)}, u32[]{:S(2)}) %copy-start.2) | copy-done | bytes 524312
  24.9 0.0 copy-start.1
  24.9 1.2 %copy-done.1 = f32[2048,128]{1,0:T(8,128)S(1)} copy-done((f32[2048,128]{1,0:T(8,128)S(1)}, f32[2048,128]{1,0:T(8,128)}, u32[]{:S(2)}) %copy-start.1) | copy-done | bytes 1048600
  26.1 0.0 copy-start.3
  26.1 1.0 %copy-done.3 = bf16[256,1024]{1,0:T(8,128)(2,1)S(1)} copy-done((bf16[256,1024]{1,0:T(8,128)(2,1)S(1)}, bf16[256,1024]{1,0:T(8,128)(2,1)}, u32[]{:S(2)}) %copy-start.3) | copy-done | bytes 524312
  27.1 6.9 %middle.1 = (f32[2048,128]{1,0:T(8,128)S(1)}, f32[1024,256]{1,0:T(8,128)S(1)}) custom-call(s32[3]{0:T(128)S(1)} %bitcast.5, f32[2048,128]{1,0:T(8,128)S(1)} %copy-done.1, f32[128,128]{1,0:T(8,128)S(1)} %get-tuple-element.41.decay_ref, f32[128,128]{1,0:T(8,128)S(1)} %get-tuple-element.42.scale_ref, bf16[1024,4096]{1,0:T(8,128)(2,1)} %weight_ref.5, ...), custom_call_target="tpu_custom_call" | custom-call | bytes 21000000 | tf_op jit(solution)/shard_map/middle/pallas_call | solution.py:451
  34.0 0.0 all-to-all-done.message_ref
  34.0 6.5 %project.1 = (f32[2048,128]{1,0:T(8,128)}, bf16[256,1024]{1,0:T(8,128)(2,1)}, bf16[256,1024]{1,0:T(8,128)(2,1)}, bf16[256,1024]{1,0:T(8,128)(2,1)}, bf16[256,1024]{1,0:T(8,128)(2,1)}) custom-call(s32[4]{0:T(128)S(1)} %iota_xor_fusion.index_ref, bf16[8,128,128]{2,1,0:T(8,128)(2,1)S(1)} %all-to-all-done.message_ref, ...), custom_call_target="tpu_custom_call" | custom-call | bytes 24500000 | tf_op jit(solution)/shard_map/project/pallas_call | solution.py:451
  40.6 1.6 %collective-permute-start.3 = (bf16[256,1024]{1,0:T(8,128)(2,1)}, bf16[256,1024]{1,0:T(8,128)(2,1)}, u32[]{:S(2)}, u32[]{:S(2)}) collective-permute-start(bf16[256,1024]{1,0:T(8,128)(2,1)} %get-tuple-element.48), channel_id=1, source_target_pairs={{0,1},{1,0},{2,3},{3,2},{4,5},{5,4},{6,7},{7,6},{8,9},{9,8},{10,11... | collective-permute-start | bytes 1572872 | tf_op jit(solution)/shard_map/ppermute | solution.py:473
  42.1 0.5 collective-permute-start.4
  42.6 1.5 %collective-permute-start.5 = (bf16[256,1024]{1,0:T(8,128)(2,1)}, bf16[256,1024]{1,0:T(8,128)(2,1)}, u32[]{:S(2)}, u32[]{:S(2)}) collective-permute-start(bf16[256,1024]{1,0:T(8,128)(2,1)} %get-tuple-element.50), channel_id=1, source_target_pairs={{0,3},{1,2},{2,1},{3,0},{4,7},{5,6},{6,5},{7,4},{8,11},{9,10},{10,... | collective-permute-start | bytes 1572872 | tf_op jit(solution)/shard_map/ppermute | solution.py:473
  44.1 0.6 slice.7.index_ref
  44.7 0.0 collective-permute-done.6.refs_0_
  44.7 6.2 %back_last.1 = (f32[2048,128]{1,0:T(8,128)}, f32[2048,128]{1,0:T(8,128)S(1)}, bf16[8,128,128]{2,1,0:T(8,128)(2,1)}, f32[4,48,128]{2,1,0:T(8,128)S(1)}) custom-call(s32[1]{0:T(128)} %slice.7.index_ref, s32[1]{0:T(128)} %bitcast.position_ref, f32[1024,256]{1,0:T(8,128)S(1)} %get-tuple-element.45._.base_ref, f32[128,128]{1,0:T(8,128)S(1)} %get-tuple-element.41.decay_ref, ...), custom_call_target="tpu_custom_call" | custom-call | bytes 21000000 | tf_op jit(solution)/shard_map/back_last/pallas_call | solution.py:451
  50.9 5.1 %all-to-all-start.1 = ((bf16[8,128,128]{2,1,0:T(8,128)(2,1)}), bf16[8,128,128]{2,1,0:T(8,128)(2,1)S(1)}, u32[]{:S(2)}, u32[]{:S(2)}) async-start(bf16[8,128,128]{2,1,0:T(8,128)(2,1)} %get-tuple-element.54), calls=%async_computation.1 | async-start | bytes 524288 | tf_op jit(solution)/shard_map/all_to_all | solution.py:599
  56.0 1.3 %collective-permute-start.7 = (f32[4,48,128]{2,1,0:T(8,128)S(1)}, f32[4,48,128]{2,1,0:T(8,128)S(1)}, u32[]{:S(2)}, u32[]{:S(2)}) collective-permute-start(f32[4,48,128]{2,1,0:T(8,128)S(1)} %get-tuple-element.57), channel_id=1, source_target_pairs={{4,0},{8,4},{12,8},{16,12},{20,16},{24,20},{28,24},{5,1},{9,5},{13... | collective-permute-start | bytes 294920 | tf_op jit(solution)/shard_map/ppermute | solution.py:468
  57.3 2.3 %back_local.1.local_ref = f32[2048,128]{1,0:T(8,128)S(1)} custom-call(f32[2048,128]{1,0:T(8,128)S(1)} %get-tuple-element.55.signal_ref, f32[128,128]{1,0:T(8,128)S(1)} %get-tuple-element.41.decay_ref, f32[128,128]{1,0:T(8,128)S(1)} %get-tuple-element.42.scale_ref), custom_call_target="tpu_custom_call" | custom-call | bytes 8049999 | tf_op jit(solution)/shard_map/back_local/pallas_call | solution.py:451
  59.6 0.0 collective-permute-done.7.ahead_ref
  59.6 6.2 %all-to-all-done.1.message_ref = bf16[8,128,128]{2,1,0:T(8,128)(2,1)S(1)} async-done(((bf16[8,128,128]{2,1,0:T(8,128)(2,1)}), bf16[8,128,128]{2,1,0:T(8,128)(2,1)S(1)}, u32[]{:S(2)}, u32[]{:S(2)}) %all-to-all-start.1) | async-done | bytes 262176 | tf_op jit(solution)/shard_map/all_to_all | solution.py:599
  65.8 5.3 %finish.1 = (bf16[256,1024]{1,0:T(8,128)(2,1)}, bf16[256,1024]{1,0:T(8,128)(2,1)}, bf16[256,1024]{1,0:T(8,128)(2,1)}) custom-call(bf16[8,128,128]{2,1,0:T(8,128)(2,1)S(1)} %all-to-all-done.1.message_ref, f32[2048,128]{1,0:T(8,128)S(1)} %back_local.1.local_ref, f32[128,128]{1,0:T(8,128)S(1)} %get-tuple-element.41.decay_ref, ...), custom_call_target="tpu_custom_call" | custom-call | bytes 19250000 | tf_op jit(solution)/shard_map/finish/pallas_call | solution.py:451
  71.1 0.0 collective-permute-done.3.refs_1_
  71.2 0.0 collective-permute-done.4.refs_2_
  71.2 0.0 collective-permute-done.5.refs_3_
  71.2 2.5 %add_parts.1 = bf16[256,1024]{1,0:T(8,128)(2,1)} custom-call(bf16[256,1024]{1,0:T(8,128)(2,1)} %get-tuple-element.47.refs_0_, bf16[256,1024]{1,0:T(8,128)(2,1)} %collective-permute-done.3.refs_1_, bf16[256,1024]{1,0:T(8,128)(2,1)} %collective-permute-done.4.refs_2_, bf16[256,1024]{1,0:T(8,128)(2,1)} %collective-permute-done.5.refs_3_, ...), custom_call_target="tpu_custom_call" | custom-call | bytes 5250000 | tf_op jit(solution)/shard_map/add_parts/pallas_call | solution.py:451
  (1 shorter events, 0.0 us)
Async XLA Ops:
  2.1 15.2 %collective-permute-start.1 = (bf16[256,1024]{1,0:T(8,128)(2,1)}, bf16[256,1024]{1,0:T(8,128)(2,1)}, u32[]{:S(2)}, u32[]{:S(2)}) collective-permute-start(bf16[256,1024]{1,0:T(8,128)(2,1)} %own_ref), channel_id=1, source_target_pairs={{0,1},{1,0},{2,3},{3,2},{4,5},{5,4},{6,7},{7,6},{8,9},{9,8},{10,11... | collective-permute-start | bytes 1572872 | tf_op jit(solution)/shard_map/ppermute | solution.py:473
  5.2 3.0 %collective-permute-start = (bf16[48,1024]{1,0:T(8,128)(2,1)S(1)}, bf16[48,1024]{1,0:T(8,128)(2,1)S(1)}, u32[]{:S(2)}, u32[]{:S(2)}) collective-permute-start(bf16[48,1024]{1,0:T(8,128)(2,1)S(1)} %get-tuple-element.38), channel_id=1, source_target_pairs={{0,4},{4,8},{8,12},{12,16},{16,20},{20,24},{24,28},{1,5},{5,9},{9,... | collective-permute-start | bytes 294920 | tf_op jit(solution)/shard_map/ppermute | solution.py:468
  6.6 17.4 %collective-permute-start.2 = (bf16[256,1024]{1,0:T(8,128)(2,1)}, bf16[256,1024]{1,0:T(8,128)(2,1)S(1)}, u32[]{:S(2)}, u32[]{:S(2)}) collective-permute-start(bf16[256,1024]{1,0:T(8,128)(2,1)} %own_ref), channel_id=1, source_target_pairs={{0,2},{1,3},{2,0},{3,1},{4,6},{5,7},{6,4},{7,5},{8,10},{9,11},{10,... | collective-permute-start | bytes 1572872 | tf_op jit(solution)/shard_map/ppermute | solution.py:473
  13.2 1.0 %copy-start = (f32[2048,128]{1,0:T(8,128)}, f32[2048,128]{1,0:T(8,128)S(1)}, u32[]{:S(2)}) copy-start(f32[2048,128]{1,0:T(8,128)S(1)} %get-tuple-element.40.signal_ref) | copy-start | bytes 3145732
  17.4 27.3 %collective-permute-start.6 = (bf16[256,1024]{1,0:T(8,128)(2,1)}, bf16[256,1024]{1,0:T(8,128)(2,1)S(1)}, u32[]{:S(2)}, u32[]{:S(2)}) collective-permute-start(bf16[256,1024]{1,0:T(8,128)(2,1)} %collective-permute-done.1.refs_0_), channel_id=1, source_target_pairs={{0,2},{1,3},{2,0},{3,1},{4,6},{5,7},{6,4},{7,5},{8,10},{9,11},{10,... | collective-permute-start | bytes 1572872 | tf_op jit(solution)/shard_map/ppermute | solution.py:473
  19.2 14.9 %all-to-all-start = ((bf16[8,128,128]{2,1,0:T(8,128)(2,1)}), bf16[8,128,128]{2,1,0:T(8,128)(2,1)S(1)}, u32[]{:S(2)}, u32[]{:S(2)}) async-start(bf16[8,128,128]{2,1,0:T(8,128)(2,1)} %get-tuple-element.39), calls=%async_computation | async-start | bytes 524288 | tf_op jit(solution)/shard_map/all_to_all | solution.py:530
  24.1 0.8 %copy-start.2 = (bf16[256,1024]{1,0:T(8,128)(2,1)}, bf16[256,1024]{1,0:T(8,128)(2,1)S(1)}, u32[]{:S(2)}) copy-start(bf16[256,1024]{1,0:T(8,128)(2,1)S(1)} %collective-permute-done.2.refs_1_) | copy-start | bytes 1572868
  24.9 1.2 %copy-start.1 = (f32[2048,128]{1,0:T(8,128)S(1)}, f32[2048,128]{1,0:T(8,128)}, u32[]{:S(2)}) copy-start(f32[2048,128]{1,0:T(8,128)} %copy-done) | copy-start | bytes 3145732
  26.1 1.0 %copy-start.3 = (bf16[256,1024]{1,0:T(8,128)(2,1)S(1)}, bf16[256,1024]{1,0:T(8,128)(2,1)}, u32[]{:S(2)}) copy-start(bf16[256,1024]{1,0:T(8,128)(2,1)} %copy-done.2) | copy-start | bytes 1572868
  40.6 30.6 %collective-permute-start.3 = (bf16[256,1024]{1,0:T(8,128)(2,1)}, bf16[256,1024]{1,0:T(8,128)(2,1)}, u32[]{:S(2)}, u32[]{:S(2)}) collective-permute-start(bf16[256,1024]{1,0:T(8,128)(2,1)} %get-tuple-element.48), channel_id=1, source_target_pairs={{0,1},{1,0},{2,3},{3,2},{4,5},{5,4},{6,7},{7,6},{8,9},{9,8},{10,11... | collective-permute-start | bytes 1572872 | tf_op jit(solution)/shard_map/ppermute | solution.py:473
  42.1 29.0 %collective-permute-start.4 = (bf16[256,1024]{1,0:T(8,128)(2,1)}, bf16[256,1024]{1,0:T(8,128)(2,1)}, u32[]{:S(2)}, u32[]{:S(2)}) collective-permute-start(bf16[256,1024]{1,0:T(8,128)(2,1)} %get-tuple-element.49), channel_id=1, source_target_pairs={{0,2},{1,3},{2,0},{3,1},{4,6},{5,7},{6,4},{7,5},{8,10},{9,11},{10,... | collective-permute-start | bytes 1572872 | tf_op jit(solution)/shard_map/ppermute | solution.py:473
  42.6 28.5 %collective-permute-start.5 = (bf16[256,1024]{1,0:T(8,128)(2,1)}, bf16[256,1024]{1,0:T(8,128)(2,1)}, u32[]{:S(2)}, u32[]{:S(2)}) collective-permute-start(bf16[256,1024]{1,0:T(8,128)(2,1)} %get-tuple-element.50), channel_id=1, source_target_pairs={{0,3},{1,2},{2,1},{3,0},{4,7},{5,6},{6,5},{7,4},{8,11},{9,10},{10,... | collective-permute-start | bytes 1572872 | tf_op jit(solution)/shard_map/ppermute | solution.py:473
  50.9 14.9 %all-to-all-start.1 = ((bf16[8,128,128]{2,1,0:T(8,128)(2,1)}), bf16[8,128,128]{2,1,0:T(8,128)(2,1)S(1)}, u32[]{:S(2)}, u32[]{:S(2)}) async-start(bf16[8,128,128]{2,1,0:T(8,128)(2,1)} %get-tuple-element.54), calls=%async_computation.1 | async-start | bytes 524288 | tf_op jit(solution)/shard_map/all_to_all | solution.py:599
  56.0 3.6 %collective-permute-start.7 = (f32[4,48,128]{2,1,0:T(8,128)S(1)}, f32[4,48,128]{2,1,0:T(8,128)S(1)}, u32[]{:S(2)}, u32[]{:S(2)}) collective-permute-start(f32[4,48,128]{2,1,0:T(8,128)S(1)} %get-tuple-element.57), channel_id=1, source_target_pairs={{4,0},{8,4},{12,8},{16,12},{20,16},{24,20},{28,24},{5,1},{9,5},{13... | collective-permute-start | bytes 294920 | tf_op jit(solution)/shard_map/ppermute | solution.py:468

commit v6 on v5

--- a/solution.py
+++ b/solution.py
@@ -149,10 +149,12 @@
 
 
 def featurize_kernel(
-    position_ref, streams_ref, taps_in_ref, residue_ref, decay_in_ref, halo_ref,
-    qf_ref, kf_ref, vf_ref, mixed_ref, message_ref, taps_ref, scale_ref, decay_ref,
+    position_ref, streams_ref, taps_in_ref, residue_ref, decay_in_ref, halo_ref, grad_in_ref,
+    qf_ref, kf_ref, vf_ref, mixed_ref, grad_copy_ref, message_ref, taps_ref, scale_ref, decay_ref,
     wide_ref, feat_ref, sems,
 ):
+    grad_copy = pltpu.make_async_copy(grad_in_ref, grad_copy_ref, sems.at[4])
+    grad_copy.start()
     tokens = streams_ref.shape[1]
     _, taps, _ = taps_in_ref.shape
     rim = taps - 1
@@ -175,18 +177,18 @@
             window = as_tiles(wide_ref[stream, pl.ds(begin, (STEP + rim) * SUB), :])
             feats.append(filtered(window, taps_ref, stream, taps, STEP, True))
             feat_ref[stream, rows, :] = as_rows(feats[-1])
-        mixed_ref[rows, :] = as_rows(round16(feats[1] * feats[2]))
+        feat_ref[3, rows, :] = as_rows(round16(feats[1] * feats[2]))
         return carry
 
     lax.fori_loop(0, tokens // STEP, body, 0)
-    copies = start_all(
-        [
-            pltpu.make_async_copy(feat_ref.at[stream], target, sems.at[stream])
-            for stream, target in enumerate((qf_ref, kf_ref, vf_ref))
+    copies = [grad_copy] + start_all(
+        [
+            pltpu.make_async_copy(feat_ref.at[number], target, sems.at[number])
+            for number, target in enumerate((qf_ref, kf_ref, vf_ref, mixed_ref))
         ]
     )
     states = advance_states(
-        mixed_ref, fades(decay_ref, 1.0), zero_states(modes), 0, tokens, False
+        feat_ref.at[3], fades(decay_ref, 1.0), zero_states(modes), 0, tokens, False
     )
     write_messages(message_ref, states, decay_ref, position_ref, tokens, 1)
     wait_all(copies)
@@ -275,44 +277,14 @@
     wait_all(outs)
 
 
-def add_parts_kernel(*refs):
-    *part_refs, _, out_ref, held_ref, total_ref, sems, out_sems = refs
-    chunks = out_sems.shape[0]
-    rows = out_ref.shape[0] // chunks
-    numbers = range(len(part_refs))
-    fetches = [
-        start_all(
-            [
-                pltpu.make_async_copy(
-                    part_refs[number].at[pl.ds(chunk * rows, rows), :],
-                    held_ref.at[number, pl.ds(chunk * rows, rows), :],
-                    sems.at[chunk, number],
-                )
-                for number in numbers
-            ]
-        )
-        for chunk in range(chunks)
-    ]
-    outs = []
-    for chunk in range(chunks):
-        wait_all(fetches[chunk])
-        here = pl.ds(chunk * rows, rows)
-        total_ref[here, :] = tree_sum(
-            [held_ref[number, here, :].astype(F32) for number in numbers]
-        ).astype(total_ref.dtype)
-        outs.append(
-            pltpu.make_async_copy(total_ref.at[here, :], out_ref.at[here, :], out_sems.at[chunk])
-        )
-        outs[-1].start()
-    wait_all(outs)
-
-
-def start_weights(index_ref, weight_ref, held_ref, sems):
+def start_weights(index_ref, first, weight_ref, held_ref, sems):
     count, _, width = held_ref.shape
     return start_all(
         [
             pltpu.make_async_copy(
-                weight_ref.at[:, pl.ds(pl.multiple_of(index_ref[number] * width, width), width)],
+                weight_ref.at[
+                    :, pl.ds(pl.multiple_of(index_ref[first + number] * width, width), width)
+                ],
                 held_ref.at[number],
                 sems.at[number],
             )
@@ -331,12 +303,14 @@
         total_ref[...] = product if earlier is None else earlier[...] + product
 
 
-def middle_kernel(index_ref, signal_ref, decay_ref, scale_ref, weight_ref, own_ref, *refs):
-    *piece_refs, local_ref, total_ref, own_vmem, turned_ref, held_ref, own_sem, sems = refs
-    own = pltpu.make_async_copy(own_ref, own_vmem, own_sem)
-    own.start()
-    weights = start_weights(index_ref, weight_ref, held_ref, sems)
-    local_conv(signal_ref, decay_ref, scale_ref, local_ref, False)
+def middle_kernel(index_ref, decay_ref, scale_ref, signal_ref, weight_ref, own_ref, *refs):
+    *piece_refs, local_ref, total_ref, mixed_vmem, own_vmem, turned_ref, held_ref, own_sems, sems = refs
+    mixed = pltpu.make_async_copy(signal_ref, mixed_vmem, own_sems.at[0])
+    own = pltpu.make_async_copy(own_ref, own_vmem, own_sems.at[1])
+    start_all([mixed, own])
+    weights = start_weights(index_ref, 0, weight_ref, held_ref, sems)
+    mixed.wait()
+    local_conv(mixed_vmem, decay_ref, scale_ref, local_ref, False)
     own.wait()
     back_products(weights, [own_vmem, *piece_refs], turned_ref, held_ref, total_ref, None)
 
@@ -351,7 +325,9 @@
     ) = refs
     tokens = total_ref.shape[1]
     heads = pl.ds(0, rim * SUB)
-    weights = start_weights(index_ref, weight_ref, held_ref, sems)
+    weights = start_weights(
+        index_ref, index_ref.shape[0] - len(piece_refs), weight_ref, held_ref, sems
+    )
     copies = start_all(
         [
             pltpu.make_async_copy(qf_ref, feat_ref, own_sems.at[0]),
@@ -394,8 +370,12 @@
 
 def finish_kernel(
     message_ref, local_ref, decay_ref, scale_ref, taps_ref, ahead_ref, query_ref, kf_ref, vf_ref,
-    gq_ref, gk_ref, gv_ref, total_ref, feat_ref, wide_ref, rows_ref, out_vmem, sems, *, taps,
+    *refs, taps,
 ):
+    (
+        *part_refs, gq_ref, gk_ref, gv_ref, projected_ref,
+        total_ref, feat_ref, wide_ref, rows_ref, out_vmem, parts_vmem, sems, part_sems,
+    ) = refs
     tokens = gk_ref.shape[0]
     rim = taps - 1
     inside = pl.ds(0, tokens * SUB)
@@ -404,6 +384,12 @@
             pltpu.make_async_copy(query_ref, wide_ref.at[0, inside, :], sems.at[0]),
             pltpu.make_async_copy(vf_ref, feat_ref.at[0], sems.at[1]),
             pltpu.make_async_copy(kf_ref, feat_ref.at[1], sems.at[2]),
+        ]
+    )
+    parts = start_all(
+        [
+            pltpu.make_async_copy(ref, parts_vmem.at[number], part_sems.at[number])
+            for number, ref in enumerate(part_refs)
         ]
     )
     states = read_messages(message_ref)
@@ -429,6 +415,13 @@
         )
         outs.append(pltpu.make_async_copy(out_vmem.at[stream], out_ref, sems.at[stream]))
         outs[-1].start()
+        if stream == 0:
+            wait_all(parts)
+            out_vmem[3] = tree_sum(
+                [parts_vmem[number].astype(F32) for number in range(len(part_refs))]
+            ).astype(out_vmem.dtype)
+            outs.append(pltpu.make_async_copy(out_vmem.at[3], projected_ref, sems.at[3]))
+            outs[-1].start()
     wait_all(outs)
 
 
@@ -504,8 +497,7 @@
     halo = shift(halo, "ctx", 1)
     if fans == 4:
         order = lax.axis_index("ch") ^ jnp.arange(fans, dtype=jnp.int32)
-        near, far = exchange(out_grad, "ch", 1), exchange(out_grad, "ch", 2)
-        pieces = [out_grad, near, far, exchange(near, "ch", 2)]
+        pieces = [out_grad] + [exchange(out_grad, "ch", mask) for mask in range(1, fans - 1)]
     else:
         order = jnp.arange(fans, dtype=jnp.int32)
         everyone = lax.all_gather(out_grad, "ch", axis=0, tiled=False)
@@ -513,20 +505,25 @@
     tile = pltpu.VMEM(tile_shape, F32)
     wide_rows = (tokens + rim) * SUB
 
-    query_feat, key_feat, value_feat, mixed, messages, tap_tiles, scale_tiles, decay_tiles = call(
+    (
+        query_feat, key_feat, value_feat, mixed, grad_copy, messages,
+        tap_tiles, scale_tiles, decay_tiles,
+    ) = call(
         featurize_kernel,
-        [in_hbm(tile_shape, F32)] * 3
-        + [(tile_shape, F32), (message_shape, BF16), ((3 * taps * SUB, LANES), F32)]
-        + [(mode_shape, F32)] * 2,
-        (position, narrow, taps_vmem, residues_vmem, decays_vmem, halo),
-        [IN_SMEM] + [IN_VMEM] * 5,
+        [in_hbm(tile_shape, F32)] * 4
+        + [in_hbm((tokens, channels), BF16), (message_shape, BF16)]
+        + [((3 * taps * SUB, LANES), F32), (mode_shape, F32), (mode_shape, F32)],
+        (position, narrow, taps_vmem, residues_vmem, decays_vmem, halo, out_grad),
+        [IN_SMEM] + [IN_VMEM] * 5 + [IN_HBM],
         [
             pltpu.VMEM((3, wide_rows, LANES), F32),
-            pltpu.VMEM((3,) + tile_shape, F32),
-            pltpu.SemaphoreType.DMA((3,)),
+            pltpu.VMEM((4,) + tile_shape, F32),
+            pltpu.SemaphoreType.DMA((5,)),
         ],
-        "featurize", 5.0, 8,
-    )
+        "featurize", 5.0, 9,
+    )
+    if fans == 4:
+        pieces.append(exchange(grad_copy, "ch", fans - 1))
     arrived = lax.all_to_all(messages, "ctx", split_axis=0, concat_axis=0, tiled=True)
 
     def weight_scratch(count):
@@ -540,16 +537,17 @@
     local, base = call(
         middle_kernel,
         [(tile_shape, F32), ((channels, tokens), F32)],
-        (order[:early], mixed, decay_tiles, scale_tiles, out_weight, *pieces[:early]),
-        [IN_SMEM] + [IN_VMEM] * 3 + [IN_HBM] * 2 + [IN_VMEM] * (early - 1),
-        [
+        (order, decay_tiles, scale_tiles, mixed, out_weight, *pieces[:early]),
+        [IN_SMEM] + [IN_VMEM] * 2 + [IN_HBM] * 3 + [IN_VMEM] * (early - 1),
+        [
+            tile,
             pltpu.VMEM((tokens, channels), BF16),
             pltpu.VMEM((early, channels, tokens), BF16),
             weights[0],
-            pltpu.SemaphoreType.DMA,
+            pltpu.SemaphoreType.DMA((2,)),
             weights[1],
         ],
-        "middle", 6.0, 10,
+        "middle", 7.0, 11,
     )
     conv_out, *partial_sums = call(
         project_kernel,
@@ -581,7 +579,7 @@
         [in_hbm(tile_shape, F32), (tile_shape, F32), (message_shape, BF16)]
         + [((4, rim * SUB, LANES), F32)],
         (
-            order[early:], position, base, decay_tiles, out_weight, query_feat, key_feat,
+            order, position, base, decay_tiles, out_weight, query_feat, key_feat,
             value_feat, conv_out, *pieces[early:],
         ),
         [IN_SMEM] * 2 + [IN_VMEM] * 2 + [IN_HBM] * 5 + [IN_VMEM] * (fans - early),
@@ -603,34 +601,25 @@
         [(tile_shape, F32)], (grad_mixed, decay_tiles, scale_tiles), [IN_VMEM] * 3, [],
         "back_local", 2.3, 2,
     )
-    grad_query, grad_key, grad_value = call(
+    grad_query, grad_key, grad_value, projected = call(
         functools.partial(finish_kernel, taps=taps),
-        [in_hbm((tokens, channels), BF16)] * 3,
+        [in_hbm((tokens, channels), BF16)] * 4,
         (
             back_arrived, back_local, decay_tiles, scale_tiles, tap_tiles, ahead, back_query,
-            key_feat, value_feat,
+            key_feat, value_feat, *parts,
         ),
-        [IN_VMEM] * 6 + [IN_HBM] * 3,
+        [IN_VMEM] * 6 + [IN_HBM] * (3 + fans),
         [
             tile,
             pltpu.VMEM((2,) + tile_shape, F32),
             pltpu.VMEM((3, wide_rows, LANES), F32),
             tile,
-            pltpu.VMEM((3, tokens, channels), BF16),
-            pltpu.SemaphoreType.DMA((3,)),
+            pltpu.VMEM((4, tokens, channels), BF16),
+            pltpu.VMEM((fans, tokens, channels), BF16),
+            pltpu.SemaphoreType.DMA((4,)),
+            pltpu.SemaphoreType.DMA((fans,)),
         ],
-        "finish", 5.5, 10,
-    )
-    (projected,) = call(
-        add_parts_kernel, [in_hbm((tokens, channels), BF16)], (*parts, grad_key),
-        [IN_HBM] * (fans + 1),
-        [
-            pltpu.VMEM((fans, tokens, channels), BF16),
-            pltpu.VMEM((tokens, channels), BF16),
-            pltpu.SemaphoreType.DMA((4, fans)),
-            pltpu.SemaphoreType.DMA((4,)),
-        ],
-        "add_parts", 1.5, 4,
+        "finish", 6.0, 13,
     )
     return (projected, grad_query, grad_key, grad_value)
 

time: 74.2 us -> 85.2 us (1.15)
  Pallas kernels: 36.2 us -> 48 us
  starting transfers between devices: 22.6 us -> 24.7 us
  waiting for transfers between devices: 9.43 us -> 7.57 us
  local copies, waits for them, and re-layouts: 4.6 us -> 3.67 us
    pallas_call x8 -> x7, Pallas kernels: 36.2 us -> 48 us  [call(): pl.pallas_call(kernel, out_shape=[jax.ShapeDtypeStruct(*out) if own else...]
    ppermute x6, waiting for transfers between devices: 3.26 us -> 1.41 us  [exchange(): return lax.ppermute(value, axis, [(s, s ^ mask) for s in range(count)])]
    all_to_all x1, starting transfers between devices: 4.88 us -> 5.99 us  [shards(): lax.all_to_all(messages, 'ctx', split_axis=0, concat_axis=0, tiled=True)]
    ppermute x2, starting transfers between devices: 2.73 us -> 3.64 us  [shift(): return lax.ppermute(value, axis, pairs)]
  transfers between devices with their start and end apart: 10 -> 10, of which waited for: 2 -> 2; matrix products, arithmetic and copies ran while one was open for 1% -> 0% of each run, Pallas kernels for 44% -> 48%
where the time goes in v6:
time: 85.2 us; the launch traced here: 84.7 us
  Pallas kernels  48 us (56%)
  starting transfers between devices  24.7 us (29%)
  waiting for transfers between devices  7.57 us (9%)
  local copies, waits for them, and re-layouts  3.67 us (4%)
    pallas_call x7, Pallas kernels, call(): pl.pallas_call(kernel, out_shape=[jax.ShapeDtypeStruct(*out) if own else...  48 us
    ppermute x6, starting transfers between devices, exchange(): return lax.ppermute(value, axis, [(s, s ^ mask) for s in range(count)])  9.91 us
    all_to_all x1, waiting for transfers between devices, shards(): lax.all_to_all(back_messages, 'ctx', split_axis=0, concat_axis=0, tiled=T...  6.15 us
    all_to_all x1, starting transfers between devices, shards(): lax.all_to_all(messages, 'ctx', split_axis=0, concat_axis=0, tiled=True)  5.99 us
    all_to_all x1, starting transfers between devices, shards(): lax.all_to_all(back_messages, 'ctx', split_axis=0, concat_axis=0, tiled=T...  5.12 us
    unnamed x8, local copies, waits for them, and re-layouts  3.67 us
    ppermute x2, starting transfers between devices, shift(): return lax.ppermute(value, axis, pairs)  3.64 us
  transfers between devices with their start and end apart: 10, of which 2 were waited for; matrix products, arithmetic and copies ran while one was open for 0% of the time, Pallas kernels for 48%

profile of v6, /device:TPU:0, one launch (start us, length us, event | category | flops | bytes accessed | tf_op | source)
XLA Modules:
  0.0 84.7 jit_solution(8803790664056085769)
XLA Ops:
  0.6 1.5 %rim.1 = (bf16[48,1024]{1,0:T(8,128)(2,1)S(1)}, bf16[3,256,1024]{2,1,0:T(8,128)(2,1)S(1)}, f32[3,7,1024]{2,1,0:T(8,128)S(1)}, f32[16,1024]{1,0:T(8,128)S(1)}, f32[16,1024]{1,0:T(8,128)S(1)}) custom-call(bf16[256,1024]{1,0:T(8,128)(2,1)} %q_ref.1, bf16[256,1024]{1,0:T(8,128)(2,1)} %k_ref.1, bf16[256,1024]{1,0:T(8,128)(2,1)} %v_ref.1, f32[3,7,1024]{2,1,0:T(8,128)} %bitcast.4, ...), custom_call_target="tpu_custom_call" | custom-call | bytes 4200000 | tf_op jit(solution)/shard_map/rim/pallas_call | solution.py:444
  2.1 2.4 %collective-permute-start = (bf16[48,1024]{1,0:T(8,128)(2,1)S(1)}, bf16[48,1024]{1,0:T(8,128)(2,1)S(1)}, u32[]{:S(2)}, u32[]{:S(2)}) collective-permute-start(bf16[48,1024]{1,0:T(8,128)(2,1)S(1)} %get-tuple-element.40), channel_id=1, source_target_pairs={{0,4},{4,8},{8,12},{12,16},{16,20},{20,24},{24,28},{1,5},{5,9},{9,... | collective-permute-start | bytes 294920 | tf_op jit(solution)/shard_map/ppermute | solution.py:461
  4.5 2.4 %collective-permute-start.2 = (bf16[256,1024]{1,0:T(8,128)(2,1)}, bf16[256,1024]{1,0:T(8,128)(2,1)S(1)}, u32[]{:S(2)}, u32[]{:S(2)}) collective-permute-start(bf16[256,1024]{1,0:T(8,128)(2,1)} %own_ref), channel_id=1, source_target_pairs={{0,2},{1,3},{2,0},{3,1},{4,6},{5,7},{6,4},{7,5},{8,10},{9,11},{10,... | collective-permute-start | bytes 1572872 | tf_op jit(solution)/shard_map/ppermute | solution.py:466
  6.9 1.5 %collective-permute-start.1 = (bf16[256,1024]{1,0:T(8,128)(2,1)}, bf16[256,1024]{1,0:T(8,128)(2,1)S(1)}, u32[]{:S(2)}, u32[]{:S(2)}) collective-permute-start(bf16[256,1024]{1,0:T(8,128)(2,1)} %own_ref), channel_id=1, source_target_pairs={{0,1},{1,0},{2,3},{3,2},{4,5},{5,4},{6,7},{7,6},{8,9},{9,8},{10,11... | collective-permute-start | bytes 1572872 | tf_op jit(solution)/shard_map/ppermute | solution.py:466
  8.4 0.0 collective-permute-done.halo_ref
  8.4 17.7 %featurize.1 = (f32[2048,128]{1,0:T(8,128)}, f32[2048,128]{1,0:T(8,128)}, f32[2048,128]{1,0:T(8,128)}, f32[2048,128]{1,0:T(8,128)}, bf16[256,1024]{1,0:T(8,128)(...) custom-call(s32[1]{0:T(128)} %bitcast.position_ref, ...), custom_call_target="tpu_custom_call" | custom-call | bytes 17500000 | tf_op jit(solution)/shard_map/featurize/pallas_call | solution.py:444
  26.2 6.0 %all-to-all-start = ((bf16[8,128,128]{2,1,0:T(8,128)(2,1)}), bf16[8,128,128]{2,1,0:T(8,128)(2,1)S(1)}, u32[]{:S(2)}, u32[]{:S(2)}) async-start(bf16[8,128,128]{2,1,0:T(8,128)(2,1)} %get-tuple-element.49), calls=%async_computation | async-start | bytes 524288 | tf_op jit(solution)/shard_map/all_to_all | solution.py:527
  32.2 2.4 %collective-permute-start.3 = (bf16[256,1024]{1,0:T(8,128)(2,1)}, bf16[256,1024]{1,0:T(8,128)(2,1)S(1)}, u32[]{:S(2)}, u32[]{:S(2)}) collective-permute-start(bf16[256,1024]{1,0:T(8,128)(2,1)} %get-tuple-element.52), channel_id=1, source_target_pairs={{0,3},{1,2},{2,1},{3,0},{4,7},{5,6},{6,5},{7,4},{8,11},{9,10},{10,... | collective-permute-start | bytes 1572872 | tf_op jit(solution)/shard_map/ppermute | solution.py:466
  34.6 0.0 collective-permute-done.2.refs_1_
  34.6 0.0 copy-start
  34.6 0.8 copy-done
  35.4 0.0 collective-permute-done.1.refs_0_
  35.4 0.0 copy-start.2
  35.4 0.8 copy-done.2
  36.2 0.0 copy-start.1
  36.2 1.0 %copy-done.1 = bf16[256,1024]{1,0:T(8,128)(2,1)S(1)} copy-done((bf16[256,1024]{1,0:T(8,128)(2,1)S(1)}, bf16[256,1024]{1,0:T(8,128)(2,1)}, u32[]{:S(2)}) %copy-start.1) | copy-done | bytes 524312
  37.3 0.0 copy-start.3
  37.3 1.0 %copy-done.3 = bf16[256,1024]{1,0:T(8,128)(2,1)S(1)} copy-done((bf16[256,1024]{1,0:T(8,128)(2,1)S(1)}, bf16[256,1024]{1,0:T(8,128)(2,1)}, u32[]{:S(2)}) %copy-start.3) | copy-done | bytes 524312
  38.3 8.2 %middle.1 = (f32[2048,128]{1,0:T(8,128)S(1)}, f32[1024,256]{1,0:T(8,128)S(1)}) custom-call(s32[4]{0:T(128)S(1)} %iota_xor_fusion.index_ref, f32[128,128]{1,0:T(8,128)S(1)} %get-tuple-element.42.decay_ref, f32[128,128]{1,0:T(8,128)S(1)} %get-tuple-element.43.scale_ref, f32[2048,128]{1,0:T(8,128)} %get-tuple-element.44.signal_ref, ...), custom_call_target="tpu_custom_call" | custom-call | bytes 24500000 | tf_op jit(solution)/shard_map/middle/pallas_call | solution.py:444
  46.5 0.0 all-to-all-done.message_ref
  46.5 6.5 %project.1 = (f32[2048,128]{1,0:T(8,128)}, bf16[256,1024]{1,0:T(8,128)(2,1)}, bf16[256,1024]{1,0:T(8,128)(2,1)}, bf16[256,1024]{1,0:T(8,128)(2,1)}, bf16[256,1024]{1,0:T(8,128)(2,1)}) custom-call(s32[4]{0:T(128)S(1)} %iota_xor_fusion.index_ref, bf16[8,128,128]{2,1,0:T(8,128)(2,1)S(1)} %all-to-all-done.message_ref, ...), custom_call_target="tpu_custom_call" | custom-call | bytes 24500000 | tf_op jit(solution)/shard_map/project/pallas_call | solution.py:444
  53.1 0.6 collective-permute-start.5
  53.7 0.5 collective-permute-start.6
  54.2 2.4 %collective-permute-start.7 = (bf16[256,1024]{1,0:T(8,128)(2,1)}, bf16[256,1024]{1,0:T(8,128)(2,1)}, u32[]{:S(2)}, u32[]{:S(2)}) collective-permute-start(bf16[256,1024]{1,0:T(8,128)(2,1)} %get-tuple-element.61), channel_id=1, source_target_pairs={{0,3},{1,2},{2,1},{3,0},{4,7},{5,6},{6,5},{7,4},{8,11},{9,10},{10,... | collective-permute-start | bytes 1572872 | tf_op jit(solution)/shard_map/ppermute | solution.py:466
  56.6 0.0 collective-permute-done.3.refs_0_
  56.6 6.1 %back_last.1 = (f32[2048,128]{1,0:T(8,128)}, f32[2048,128]{1,0:T(8,128)S(1)}, bf16[8,128,128]{2,1,0:T(8,128)(2,1)}, f32[4,48,128]{2,1,0:T(8,128)S(1)}) custom-call(s32[4]{0:T(128)S(1)} %iota_xor_fusion.index_ref, s32[1]{0:T(128)} %bitcast.position_ref, f32[1024,256]{1,0:T(8,128)S(1)} %get-tuple-element.45._.base_ref, ...), custom_call_target="tpu_custom_call" | custom-call | bytes 21000000 | tf_op jit(solution)/shard_map/back_last/pallas_call | solution.py:444
  62.7 5.1 %all-to-all-start.1 = ((bf16[8,128,128]{2,1,0:T(8,128)(2,1)}), bf16[8,128,128]{2,1,0:T(8,128)(2,1)S(1)}, u32[]{:S(2)}, u32[]{:S(2)}) async-start(bf16[8,128,128]{2,1,0:T(8,128)(2,1)} %get-tuple-element.53), calls=%async_computation.1 | async-start | bytes 524288 | tf_op jit(solution)/shard_map/all_to_all | solution.py:597
  67.8 1.3 %collective-permute-start.4 = (f32[4,48,128]{2,1,0:T(8,128)S(1)}, f32[4,48,128]{2,1,0:T(8,128)S(1)}, u32[]{:S(2)}, u32[]{:S(2)}) collective-permute-start(f32[4,48,128]{2,1,0:T(8,128)S(1)} %get-tuple-element.56), channel_id=1, source_target_pairs={{4,0},{8,4},{12,8},{16,12},{20,16},{24,20},{28,24},{5,1},{9,5},{13... | collective-permute-start | bytes 294920 | tf_op jit(solution)/shard_map/ppermute | solution.py:461
  69.1 2.3 %back_local.1.local_ref = f32[2048,128]{1,0:T(8,128)S(1)} custom-call(f32[2048,128]{1,0:T(8,128)S(1)} %get-tuple-element.54.signal_ref, f32[128,128]{1,0:T(8,128)S(1)} %get-tuple-element.42.decay_ref, f32[128,128]{1,0:T(8,128)S(1)} %get-tuple-element.43.scale_ref), custom_call_target="tpu_custom_call" | custom-call | bytes 8049999 | tf_op jit(solution)/shard_map/back_local/pallas_call | solution.py:444
  71.4 0.0 collective-permute-done.4.ahead_ref
  71.4 6.1 %all-to-all-done.1.message_ref = bf16[8,128,128]{2,1,0:T(8,128)(2,1)S(1)} async-done(((bf16[8,128,128]{2,1,0:T(8,128)(2,1)}), bf16[8,128,128]{2,1,0:T(8,128)(2,1)S(1)}, u32[]{:S(2)}, u32[]{:S(2)}) %all-to-all-start.1) | async-done | bytes 262176 | tf_op jit(solution)/shard_map/all_to_all | solution.py:597
  77.6 0.0 collective-permute-done.5.refs_1_
  77.6 1.4 %collective-permute-done.6.refs_2_ = bf16[256,1024]{1,0:T(8,128)(2,1)} collective-permute-done((bf16[256,1024]{1,0:T(8,128)(2,1)}, bf16[256,1024]{1,0:T(8,128)(2,1)}, u32[]{:S(2)}, u32[]{:S(2)}) %collective-permute-start.6) | collective-permute-done | bytes 524320 | tf_op jit(solution)/shard_map/ppermute | solution.py:466
  79.0 0.0 collective-permute-done.7.refs_3_
  79.0 5.7 %finish.1 = (bf16[256,1024]{1,0:T(8,128)(2,1)}, bf16[256,1024]{1,0:T(8,128)(2,1)}, bf16[256,1024]{1,0:T(8,128)(2,1)}, bf16[256,1024]{1,0:T(8,128)(2,1)}) custom-call(bf16[8,128,128]{2,1,0:T(8,128)(2,1)S(1)} %all-to-all-done.1.message_ref, f32[2048,128]{1,0:T(8,128)S(1)} %back_local.1.local_ref, f32[128,128]{1,0:T(8,128)S(1)} %get-tuple-element.42.decay_ref, ...), custom_call_target="tpu_custom_call" | custom-call | bytes 21000000 | tf_op jit(solution)/shard_map/finish/pallas_call | solution.py:444
  (1 shorter events, 0.0 us)
Async XLA Ops:
  2.1 6.3 %collective-permute-start = (bf16[48,1024]{1,0:T(8,128)(2,1)S(1)}, bf16[48,1024]{1,0:T(8,128)(2,1)S(1)}, u32[]{:S(2)}, u32[]{:S(2)}) collective-permute-start(bf16[48,1024]{1,0:T(8,128)(2,1)S(1)} %get-tuple-element.40), channel_id=1, source_target_pairs={{0,4},{4,8},{8,12},{12,16},{16,20},{20,24},{24,28},{1,5},{5,9},{9,... | collective-permute-start | bytes 294920 | tf_op jit(solution)/shard_map/ppermute | solution.py:461
  4.5 30.1 %collective-permute-start.2 = (bf16[256,1024]{1,0:T(8,128)(2,1)}, bf16[256,1024]{1,0:T(8,128)(2,1)S(1)}, u32[]{:S(2)}, u32[]{:S(2)}) collective-permute-start(bf16[256,1024]{1,0:T(8,128)(2,1)} %own_ref), channel_id=1, source_target_pairs={{0,2},{1,3},{2,0},{3,1},{4,6},{5,7},{6,4},{7,5},{8,10},{9,11},{10,... | collective-permute-start | bytes 1572872 | tf_op jit(solution)/shard_map/ppermute | solution.py:466
  6.9 28.5 %collective-permute-start.1 = (bf16[256,1024]{1,0:T(8,128)(2,1)}, bf16[256,1024]{1,0:T(8,128)(2,1)S(1)}, u32[]{:S(2)}, u32[]{:S(2)}) collective-permute-start(bf16[256,1024]{1,0:T(8,128)(2,1)} %own_ref), channel_id=1, source_target_pairs={{0,1},{1,0},{2,3},{3,2},{4,5},{5,4},{6,7},{7,6},{8,9},{9,8},{10,11... | collective-permute-start | bytes 1572872 | tf_op jit(solution)/shard_map/ppermute | solution.py:466
  26.2 20.3 %all-to-all-start = ((bf16[8,128,128]{2,1,0:T(8,128)(2,1)}), bf16[8,128,128]{2,1,0:T(8,128)(2,1)S(1)}, u32[]{:S(2)}, u32[]{:S(2)}) async-start(bf16[8,128,128]{2,1,0:T(8,128)(2,1)} %get-tuple-element.49), calls=%async_computation | async-start | bytes 524288 | tf_op jit(solution)/shard_map/all_to_all | solution.py:527
  32.2 24.5 %collective-permute-start.3 = (bf16[256,1024]{1,0:T(8,128)(2,1)}, bf16[256,1024]{1,0:T(8,128)(2,1)S(1)}, u32[]{:S(2)}, u32[]{:S(2)}) collective-permute-start(bf16[256,1024]{1,0:T(8,128)(2,1)} %get-tuple-element.52), channel_id=1, source_target_pairs={{0,3},{1,2},{2,1},{3,0},{4,7},{5,6},{6,5},{7,4},{8,11},{9,10},{10,... | collective-permute-start | bytes 1572872 | tf_op jit(solution)/shard_map/ppermute | solution.py:466
  34.6 0.8 copy-start
  35.4 0.8 copy-start.2
  36.2 1.0 %copy-start.1 = (bf16[256,1024]{1,0:T(8,128)(2,1)S(1)}, bf16[256,1024]{1,0:T(8,128)(2,1)}, u32[]{:S(2)}) copy-start(bf16[256,1024]{1,0:T(8,128)(2,1)} %copy-done) | copy-start | bytes 1572868
  37.3 1.0 %copy-start.3 = (bf16[256,1024]{1,0:T(8,128)(2,1)S(1)}, bf16[256,1024]{1,0:T(8,128)(2,1)}, u32[]{:S(2)}) copy-start(bf16[256,1024]{1,0:T(8,128)(2,1)} %copy-done.2) | copy-start | bytes 1572868
  53.1 24.5 %collective-permute-start.5 = (bf16[256,1024]{1,0:T(8,128)(2,1)}, bf16[256,1024]{1,0:T(8,128)(2,1)}, u32[]{:S(2)}, u32[]{:S(2)}) collective-permute-start(bf16[256,1024]{1,0:T(8,128)(2,1)} %get-tuple-element.59), channel_id=1, source_target_pairs={{0,1},{1,0},{2,3},{3,2},{4,5},{5,4},{6,7},{7,6},{8,9},{9,8},{10,11... | collective-permute-start | bytes 1572872 | tf_op jit(solution)/shard_map/ppermute | solution.py:466
  53.7 25.3 %collective-permute-start.6 = (bf16[256,1024]{1,0:T(8,128)(2,1)}, bf16[256,1024]{1,0:T(8,128)(2,1)}, u32[]{:S(2)}, u32[]{:S(2)}) collective-permute-start(bf16[256,1024]{1,0:T(8,128)(2,1)} %get-tuple-element.60), channel_id=1, source_target_pairs={{0,2},{1,3},{2,0},{3,1},{4,6},{5,7},{6,4},{7,5},{8,10},{9,11},{10,... | collective-permute-start | bytes 1572872 | tf_op jit(solution)/shard_map/ppermute | solution.py:466
  54.2 24.8 %collective-permute-start.7 = (bf16[256,1024]{1,0:T(8,128)(2,1)}, bf16[256,1024]{1,0:T(8,128)(2,1)}, u32[]{:S(2)}, u32[]{:S(2)}) collective-permute-start(bf16[256,1024]{1,0:T(8,128)(2,1)} %get-tuple-element.61), channel_id=1, source_target_pairs={{0,3},{1,2},{2,1},{3,0},{4,7},{5,6},{6,5},{7,4},{8,11},{9,10},{10,... | collective-permute-start | bytes 1572872 | tf_op jit(solution)/shard_map/ppermute | solution.py:466
  62.7 14.9 %all-to-all-start.1 = ((bf16[8,128,128]{2,1,0:T(8,128)(2,1)}), bf16[8,128,128]{2,1,0:T(8,128)(2,1)S(1)}, u32[]{:S(2)}, u32[]{:S(2)}) async-start(bf16[8,128,128]{2,1,0:T(8,128)(2,1)} %get-tuple-element.53), calls=%async_computation.1 | async-start | bytes 524288 | tf_op jit(solution)/shard_map/all_to_all | solution.py:597
  67.8 3.6 %collective-permute-start.4 = (f32[4,48,128]{2,1,0:T(8,128)S(1)}, f32[4,48,128]{2,1,0:T(8,128)S(1)}, u32[]{:S(2)}, u32[]{:S(2)}) collective-permute-start(f32[4,48,128]{2,1,0:T(8,128)S(1)} %get-tuple-element.56), channel_id=1, source_target_pairs={{4,0},{8,4},{12,8},{16,12},{20,16},{24,20},{28,24},{5,1},{9,5},{13... | collective-permute-start | bytes 294920 | tf_op jit(solution)/shard_map/ppermute | solution.py:461

commit v7 on v6

--- a/solution.py
+++ b/solution.py
@@ -150,11 +150,11 @@
 
 def featurize_kernel(
     position_ref, streams_ref, taps_in_ref, residue_ref, decay_in_ref, halo_ref, grad_in_ref,
-    qf_ref, kf_ref, vf_ref, mixed_ref, grad_copy_ref, message_ref, taps_ref, scale_ref, decay_ref,
-    wide_ref, feat_ref, sems,
+    qf_ref, kf_ref, vf_ref, local_ref, grad_copy_ref, message_ref, taps_ref, scale_ref, decay_ref,
+    wide_ref, feat_ref, grad_vmem, sems,
 ):
-    grad_copy = pltpu.make_async_copy(grad_in_ref, grad_copy_ref, sems.at[4])
-    grad_copy.start()
+    grad_in = pltpu.make_async_copy(grad_in_ref, grad_vmem, sems.at[4])
+    grad_in.start()
     tokens = streams_ref.shape[1]
     _, taps, _ = taps_in_ref.shape
     rim = taps - 1
@@ -181,15 +181,23 @@
         return carry
 
     lax.fori_loop(0, tokens // STEP, body, 0)
-    copies = [grad_copy] + start_all(
-        [
-            pltpu.make_async_copy(feat_ref.at[number], target, sems.at[number])
-            for number, target in enumerate((qf_ref, kf_ref, vf_ref, mixed_ref))
-        ]
-    )
-    states = advance_states(
-        feat_ref.at[3], fades(decay_ref, 1.0), zero_states(modes), 0, tokens, False
-    )
+    grad_in.wait()
+    copies = start_all(
+        [
+            pltpu.make_async_copy(source, target, sems.at[number])
+            for number, (source, target) in enumerate(
+                (
+                    (feat_ref.at[0], qf_ref),
+                    (feat_ref.at[1], kf_ref),
+                    (feat_ref.at[2], vf_ref),
+                    (grad_vmem, grad_copy_ref),
+                )
+            )
+        ]
+    )
+    local_vmem = wide_ref.at[0, pl.ds(0, tokens * SUB), :]
+    states = local_conv(feat_ref.at[3], decay_ref, scale_ref, local_vmem, False)
+    copies += start_all([pltpu.make_async_copy(local_vmem, local_ref, sems.at[4])])
     write_messages(message_ref, states, decay_ref, position_ref, tokens, 1)
     wait_all(copies)
 
@@ -214,15 +222,11 @@
             )
         return states
 
-    lax.fori_loop(0, tokens // STEP, body, zero_states(len(factors)))
-
-
-def back_local_kernel(signal_ref, decay_ref, scale_ref, out_ref):
-    local_conv(signal_ref, decay_ref, scale_ref, out_ref, True)
-
-
-def add_carried(local_ref, out_ref, states, decay_ref, scale_ref, reverse):
-    tokens = local_ref.shape[0] // SUB
+    return lax.fori_loop(0, tokens // STEP, body, zero_states(len(factors)))
+
+
+def carried(out_ref, states, decay_ref, scale_ref, reverse, local_ref=None):
+    tokens = out_ref.shape[0] // SUB
     factors = fades(decay_ref, 1.0)
     scaled = [scale * state for scale, state in zip(scales_of(scale_ref), states)]
 
@@ -232,16 +236,18 @@
             token = tokens - 1 - token if reverse else token
             scaled = [factor * state for factor, state in zip(factors, scaled)]
             rows = pl.ds(pl.multiple_of(token * SUB, SUB), SUB)
-            out_ref[rows, :] = local_ref[rows, :] + tree_sum(list(scaled))
+            total = tree_sum(list(scaled))
+            out_ref[rows, :] = total if local_ref is None else local_ref[rows, :] + total
         return scaled
 
     lax.fori_loop(0, tokens // STEP, body, scaled)
 
 
 def project_kernel(
-    index_ref, message_ref, local_ref, decay_ref, scale_ref, _, qf_ref, weight_ref, conv_ref, *refs
+    index_ref, message_ref, decay_ref, scale_ref, _, qf_ref, local_ref, weight_ref, *refs
 ):
-    *out_refs, rows_ref, feat_ref, gated_ref, held_ref, sent_ref, sems, out_sems = refs
+    rows_ref, feat_ref, local_vmem, gated_ref, held_ref, sent_ref, sems, out_sems = refs[-8:]
+    conv_ref, *out_refs = refs[-9 - sent_ref.shape[0] : -8]
     parts, tokens, width = sent_ref.shape
     order = list(reversed(range(parts)))
     copies = [
@@ -256,10 +262,13 @@
         pltpu.make_async_copy(sent_ref.at[part], out_refs[part], out_sems.at[part])
         for part in range(parts)
     ]
+    local_copy = pltpu.make_async_copy(local_ref, local_vmem, sems.at[parts + 1])
     feat_copy = pltpu.make_async_copy(qf_ref, feat_ref, sems.at[parts])
-    feat_copy.start()
+    start_all([local_copy, feat_copy])
     start_all([copies[part] for part in order])
-    add_carried(local_ref, rows_ref, read_messages(message_ref), decay_ref, scale_ref, False)
+    carried(rows_ref, read_messages(message_ref), decay_ref, scale_ref, False)
+    local_copy.wait()
+    rows_ref[...] += local_vmem[...]
     conv_copy = pltpu.make_async_copy(rows_ref, conv_ref, sems.at[parts + 1])
     conv_copy.start()
     feat_copy.wait()
@@ -303,16 +312,18 @@
         total_ref[...] = product if earlier is None else earlier[...] + product
 
 
-def middle_kernel(index_ref, decay_ref, scale_ref, signal_ref, weight_ref, own_ref, *refs):
-    *piece_refs, local_ref, total_ref, mixed_vmem, own_vmem, turned_ref, held_ref, own_sems, sems = refs
-    mixed = pltpu.make_async_copy(signal_ref, mixed_vmem, own_sems.at[0])
-    own = pltpu.make_async_copy(own_ref, own_vmem, own_sems.at[1])
-    start_all([mixed, own])
+def middle_kernel(index_ref, weight_ref, *refs):
+    *piece_refs, total_ref, piece_vmem, turned_ref, held_ref, sems, piece_sems = refs
+    pieces = start_all(
+        [
+            pltpu.make_async_copy(ref, piece_vmem.at[number], piece_sems.at[number])
+            for number, ref in enumerate(piece_refs)
+        ]
+    )
     weights = start_weights(index_ref, 0, weight_ref, held_ref, sems)
-    mixed.wait()
-    local_conv(mixed_vmem, decay_ref, scale_ref, local_ref, False)
-    own.wait()
-    back_products(weights, [own_vmem, *piece_refs], turned_ref, held_ref, total_ref, None)
+    wait_all(pieces)
+    held = [piece_vmem.at[number] for number in range(len(piece_refs))]
+    back_products(weights, held, turned_ref, held_ref, total_ref, None)
 
 
 def back_last_kernel(
@@ -368,20 +379,43 @@
     gather_tokens(lambda group: group_rows(rows_ref, group, tokens), out_ref)
 
 
+def back_local_kernel(
+    signal_ref, decay_ref, scale_ref, taps_ref, query_ref, local_ref, gq_ref,
+    wide_ref, rows_ref, out_vmem, sem, *, taps,
+):
+    inside = query_ref.shape[0]
+    copy = pltpu.make_async_copy(query_ref, wide_ref.at[pl.ds(0, inside), :], sem)
+    copy.start()
+    local_conv(signal_ref, decay_ref, scale_ref, local_ref, True)
+    copy.wait()
+    rest = (taps - 1) * SUB
+    wide_ref[pl.ds(inside, rest), :] = jnp.zeros((rest, LANES), F32)
+    spread_back(wide_ref, taps_ref, 0, taps, rows_ref, out_vmem)
+    out = pltpu.make_async_copy(out_vmem, gq_ref, sem)
+    out.start()
+    out.wait()
+
+
 def finish_kernel(
     message_ref, local_ref, decay_ref, scale_ref, taps_ref, ahead_ref, query_ref, kf_ref, vf_ref,
     *refs, taps,
 ):
     (
-        *part_refs, gq_ref, gk_ref, gv_ref, projected_ref,
-        total_ref, feat_ref, wide_ref, rows_ref, out_vmem, parts_vmem, sems, part_sems,
+        *part_refs, _, gq_ref, gk_ref, gv_ref, projected_ref,
+        total_ref, feat_ref, query_vmem, wide_ref, rows_ref, tail_ref, out_vmem, parts_vmem,
+        sems, part_sems,
     ) = refs
     tokens = gk_ref.shape[0]
+    tail = tail_ref.shape[0]
     rim = taps - 1
     inside = pl.ds(0, tokens * SUB)
     copies = start_all(
         [
-            pltpu.make_async_copy(query_ref, wide_ref.at[0, inside, :], sems.at[0]),
+            pltpu.make_async_copy(
+                query_ref.at[pl.ds((tokens - tail) * SUB, tail * SUB), :],
+                query_vmem.at[pl.ds(0, tail * SUB), :],
+                sems.at[0],
+            ),
             pltpu.make_async_copy(vf_ref, feat_ref.at[0], sems.at[1]),
             pltpu.make_async_copy(kf_ref, feat_ref.at[1], sems.at[2]),
         ]
@@ -393,35 +427,37 @@
         ]
     )
     states = read_messages(message_ref)
-    add_carried(local_ref, total_ref, states, decay_ref, scale_ref, True)
+    carried(total_ref, states, decay_ref, scale_ref, True, local_ref)
     growth = fades(decay_ref, -1.0)
     scales = scales_of(scale_ref)
     for ahead in range(rim):
         rows = pl.ds((tokens + ahead) * SUB, SUB)
         theirs = pl.ds(ahead * SUB, SUB)
         grad_conv = tree_sum([scale * state for scale, state in zip(scales, states)])
-        wide_ref[0, rows, :] = ahead_ref[0, theirs, :]
-        wide_ref[1, rows, :] = round16(grad_conv * ahead_ref[3, theirs, :])
-        wide_ref[2, rows, :] = round16(grad_conv * ahead_ref[2, theirs, :])
+        query_vmem[pl.ds((tail + ahead) * SUB, SUB), :] = ahead_ref[0, theirs, :]
+        wide_ref[0, rows, :] = round16(grad_conv * ahead_ref[3, theirs, :])
+        wide_ref[1, rows, :] = round16(grad_conv * ahead_ref[2, theirs, :])
         arrived = ahead_ref[1, theirs, :]
         states = [(state - arrived) * grow for state, grow in zip(states, growth)]
-    outs = []
-    for stream, out_ref in enumerate((gq_ref, gk_ref, gv_ref)):
-        copies[stream].wait()
-        if stream:
-            wide_ref[stream, inside, :] = round16(total_ref[...] * feat_ref[stream - 1])
+    copies[0].wait()
+    spread_back(query_vmem, taps_ref, 0, taps, rows_ref, tail_ref)
+    outs = [
+        pltpu.make_async_copy(tail_ref, gq_ref.at[pl.ds(tokens - tail, tail), :], sems.at[0])
+    ]
+    wait_all(parts)
+    out_vmem[2] = tree_sum(
+        [parts_vmem[number].astype(F32) for number in range(len(part_refs))]
+    ).astype(out_vmem.dtype)
+    outs.append(pltpu.make_async_copy(out_vmem.at[2], projected_ref, sems.at[3]))
+    start_all(outs)
+    for stream, out_ref in enumerate((gk_ref, gv_ref)):
+        copies[1 + stream].wait()
+        wide_ref[stream, inside, :] = round16(total_ref[...] * feat_ref[stream])
         spread_back(
-            wide_ref.at[stream], taps_ref, stream, taps, rows_ref, out_vmem.at[stream]
+            wide_ref.at[stream], taps_ref, 1 + stream, taps, rows_ref, out_vmem.at[stream]
         )
-        outs.append(pltpu.make_async_copy(out_vmem.at[stream], out_ref, sems.at[stream]))
+        outs.append(pltpu.make_async_copy(out_vmem.at[stream], out_ref, sems.at[1 + stream]))
         outs[-1].start()
-        if stream == 0:
-            wait_all(parts)
-            out_vmem[3] = tree_sum(
-                [parts_vmem[number].astype(F32) for number in range(len(part_refs))]
-            ).astype(out_vmem.dtype)
-            outs.append(pltpu.make_async_copy(out_vmem.at[3], projected_ref, sems.at[3]))
-            outs[-1].start()
     wait_all(outs)
 
 
@@ -435,7 +471,7 @@
     return pltpu.HBM(shape, kind)
 
 
-def call(kernel, outs, args, specs, scratch, name, micros, mebibytes):
+def call(kernel, outs, args, specs, scratch, name, micros, mebibytes, aliases=None):
     args = [
         pltpu.with_memory_space_constraint(arg, pltpu.HBM) if spec is IN_HBM else arg
         for arg, spec in zip(args, specs)
@@ -452,6 +488,7 @@
             flops=0, bytes_accessed=int(micros * HBM_RATE), transcendentals=0
         ),
         name=name,
+        input_output_aliases=aliases or {},
     )(*args)
 
 
@@ -506,7 +543,7 @@
     wide_rows = (tokens + rim) * SUB
 
     (
-        query_feat, key_feat, value_feat, mixed, grad_copy, messages,
+        query_feat, key_feat, value_feat, local, grad_copy, messages,
         tap_tiles, scale_tiles, decay_tiles,
     ) = call(
         featurize_kernel,
@@ -518,9 +555,10 @@
         [
             pltpu.VMEM((3, wide_rows, LANES), F32),
             pltpu.VMEM((4,) + tile_shape, F32),
+            pltpu.VMEM((tokens, channels), BF16),
             pltpu.SemaphoreType.DMA((5,)),
         ],
-        "featurize", 5.0, 9,
+        "featurize", 6.0, 10,
     )
     if fans == 4:
         pieces.append(exchange(grad_copy, "ch", fans - 1))
@@ -533,28 +571,29 @@
         ]
 
     early = fans - 1
-    weights = weight_scratch(early)
-    local, base = call(
+    (base,) = call(
         middle_kernel,
-        [(tile_shape, F32), ((channels, tokens), F32)],
-        (order, decay_tiles, scale_tiles, mixed, out_weight, *pieces[:early]),
-        [IN_SMEM] + [IN_VMEM] * 2 + [IN_HBM] * 3 + [IN_VMEM] * (early - 1),
-        [
-            tile,
-            pltpu.VMEM((tokens, channels), BF16),
+        [((channels, tokens), F32)],
+        (order, out_weight, *pieces[:early]),
+        [IN_SMEM] + [IN_HBM] * (1 + early),
+        [
+            pltpu.VMEM((early, tokens, channels), BF16),
             pltpu.VMEM((early, channels, tokens), BF16),
-            weights[0],
-            pltpu.SemaphoreType.DMA((2,)),
-            weights[1],
-        ],
-        "middle", 7.0, 11,
+        ]
+        + weight_scratch(early)
+        + [pltpu.SemaphoreType.DMA((early,))],
+        "middle", 6.0, 11,
     )
     conv_out, *partial_sums = call(
         project_kernel,
         [in_hbm(tile_shape, F32)] + [in_hbm((tokens, channels), BF16)] * fans,
-        (order, arrived, local, decay_tiles, scale_tiles, base, query_feat, out_weight),
-        [IN_SMEM] + [IN_VMEM] * 5 + [IN_HBM] * 2,
-        [
+        (
+            order, arrived, decay_tiles, scale_tiles, base, query_feat, local, out_weight,
+            *pieces[1:early],
+        ),
+        [IN_SMEM] + [IN_VMEM] * 4 + [IN_HBM] * (2 + early),
+        [
+            tile,
             tile,
             tile,
             pltpu.VMEM((tokens, channels), BF16),
@@ -596,30 +635,42 @@
     )
     back_arrived = lax.all_to_all(back_messages, "ctx", split_axis=0, concat_axis=0, tiled=True)
     ahead = shift(ahead, "ctx", -1)
-    (back_local,) = call(
-        back_local_kernel,
-        [(tile_shape, F32)], (grad_mixed, decay_tiles, scale_tiles), [IN_VMEM] * 3, [],
-        "back_local", 2.3, 2,
-    )
+    back_local, grad_query = call(
+        functools.partial(back_local_kernel, taps=taps),
+        [(tile_shape, F32), in_hbm((tokens, channels), BF16)],
+        (grad_mixed, decay_tiles, scale_tiles, tap_tiles, back_query),
+        [IN_VMEM] * 4 + [IN_HBM],
+        [
+            pltpu.VMEM((wide_rows, LANES), F32),
+            tile,
+            pltpu.VMEM((tokens, channels), BF16),
+            pltpu.SemaphoreType.DMA,
+        ],
+        "back_local", 4.5, 5,
+    )
+    tail = 16
     grad_query, grad_key, grad_value, projected = call(
         functools.partial(finish_kernel, taps=taps),
         [in_hbm((tokens, channels), BF16)] * 4,
         (
             back_arrived, back_local, decay_tiles, scale_tiles, tap_tiles, ahead, back_query,
-            key_feat, value_feat, *parts,
+            key_feat, value_feat, *parts, grad_query,
         ),
-        [IN_VMEM] * 6 + [IN_HBM] * (3 + fans),
+        [IN_VMEM] * 6 + [IN_HBM] * (4 + fans),
         [
             tile,
             pltpu.VMEM((2,) + tile_shape, F32),
-            pltpu.VMEM((3, wide_rows, LANES), F32),
-            tile,
-            pltpu.VMEM((4, tokens, channels), BF16),
+            pltpu.VMEM(((tail + rim) * SUB, LANES), F32),
+            pltpu.VMEM((2, wide_rows, LANES), F32),
+            tile,
+            pltpu.VMEM((tail, channels), BF16),
+            pltpu.VMEM((3, tokens, channels), BF16),
             pltpu.VMEM((fans, tokens, channels), BF16),
             pltpu.SemaphoreType.DMA((4,)),
             pltpu.SemaphoreType.DMA((fans,)),
         ],
-        "finish", 6.0, 13,
+        "finish", 5.0, 12,
+        {9 + fans: 0},
     )
     return (projected, grad_query, grad_key, grad_value)
 

time: 85.2 us -> 69.8 us (0.82)
  Pallas kernels: 48 us -> 37.1 us
  local copies, waits for them, and re-layouts: 3.67 us -> 0.78 us
  waiting for transfers between devices: 7.57 us -> 6.09 us
    pallas_call x7, Pallas kernels: 48 us -> 37.1 us  [call(): pl.pallas_call(kernel, out_shape=[jax.ShapeDtypeStruct(*out) if own else...]
    unnamed x8 -> x2, local copies, waits for them, and re-layouts: 3.67 us -> 0.78 us
    all_to_all x1, waiting for transfers between devices: 6.15 us -> 4.43 us  [shards(): lax.all_to_all(back_messages, 'ctx', split_axis=0, concat_axis=0, tiled=T...]
  transfers between devices with their start and end apart: 10 -> 10, of which waited for: 2 -> 2; matrix products, arithmetic and copies ran while one was open for 0% -> 0% of each run, Pallas kernels for 48% -> 44%
where the time goes in v7:
time: 69.8 us; the launch traced here: 69.4 us
  Pallas kernels  37.1 us (53%)
  starting transfers between devices  24.7 us (35%)
  waiting for transfers between devices  6.09 us (9%)
  local copies, waits for them, and re-layouts  0.78 us (1%)
  between operations  0.73 us (1%)
    pallas_call x7, Pallas kernels, call(): pl.pallas_call(kernel, out_shape=[jax.ShapeDtypeStruct(*out) if own else...  37.1 us
    ppermute x6, starting transfers between devices, exchange(): return lax.ppermute(value, axis, [(s, s ^ mask) for s in range(count)])  9.91 us
    all_to_all x1, starting transfers between devices, shards(): lax.all_to_all(messages, 'ctx', split_axis=0, concat_axis=0, tiled=True)  5.99 us
    all_to_all x1, starting transfers between devices, shards(): lax.all_to_all(back_messages, 'ctx', split_axis=0, concat_axis=0, tiled=T...  5.12 us
    all_to_all x1, waiting for transfers between devices, shards(): lax.all_to_all(back_messages, 'ctx', split_axis=0, concat_axis=0, tiled=T...  4.43 us
    ppermute x2, starting transfers between devices, shift(): return lax.ppermute(value, axis, pairs)  3.64 us
    ppermute x6, waiting for transfers between devices, exchange(): return lax.ppermute(value, axis, [(s, s ^ mask) for s in range(count)])  1.65 us
  transfers between devices with their start and end apart: 10, of which 2 were waited for; matrix products, arithmetic and copies ran while one was open for 0% of the time, Pallas kernels for 44%

profile of v7, /device:TPU:0, one launch (start us, length us, event | category | flops | bytes accessed | tf_op | source)
XLA Modules:
  0.0 69.4 jit_solution(2176520647750371627)
XLA Ops:
  0.6 1.5 %rim.1 = (bf16[48,1024]{1,0:T(8,128)(2,1)S(1)}, bf16[3,256,1024]{2,1,0:T(8,128)(2,1)S(1)}, f32[3,7,1024]{2,1,0:T(8,128)S(1)}, f32[16,1024]{1,0:T(8,128)S(1)}, f32[16,1024]{1,0:T(8,128)S(1)}) custom-call(bf16[256,1024]{1,0:T(8,128)(2,1)} %q_ref.1, bf16[256,1024]{1,0:T(8,128)(2,1)} %k_ref.1, bf16[256,1024]{1,0:T(8,128)(2,1)} %v_ref.1, f32[3,7,1024]{2,1,0:T(8,128)} %bitcast.4, ...), custom_call_target="tpu_custom_call" | custom-call | bytes 4200000 | tf_op jit(solution)/shard_map/rim/pallas_call | solution.py:480
  2.1 2.4 %collective-permute-start.2 = (bf16[48,1024]{1,0:T(8,128)(2,1)S(1)}, bf16[48,1024]{1,0:T(8,128)(2,1)S(1)}, u32[]{:S(2)}, u32[]{:S(2)}) collective-permute-start(bf16[48,1024]{1,0:T(8,128)(2,1)S(1)} %get-tuple-element.41), channel_id=1, source_target_pairs={{0,4},{4,8},{8,12},{12,16},{16,20},{20,24},{24,28},{1,5},{5,9},{9,... | collective-permute-start | bytes 294920 | tf_op jit(solution)/shard_map/ppermute | solution.py:498
  4.5 2.4 %collective-permute-start.1 = (bf16[256,1024]{1,0:T(8,128)(2,1)}, bf16[256,1024]{1,0:T(8,128)(2,1)S(1)}, u32[]{:S(2)}, u32[]{:S(2)}) collective-permute-start(bf16[256,1024]{1,0:T(8,128)(2,1)} %grad_in_ref), channel_id=1, source_target_pairs={{0,2},{1,3},{2,0},{3,1},{4,6},{5,7},{6,4},{7,5},{8,10},{9,11},{10,... | collective-permute-start | bytes 1572872 | tf_op jit(solution)/shard_map/ppermute | solution.py:503
  6.9 1.5 %collective-permute-start = (bf16[256,1024]{1,0:T(8,128)(2,1)}, bf16[256,1024]{1,0:T(8,128)(2,1)}, u32[]{:S(2)}, u32[]{:S(2)}) collective-permute-start(bf16[256,1024]{1,0:T(8,128)(2,1)} %grad_in_ref), channel_id=1, source_target_pairs={{0,1},{1,0},{2,3},{3,2},{4,5},{5,4},{6,7},{7,6},{8,9},{9,8},{10,11... | collective-permute-start | bytes 1572872 | tf_op jit(solution)/shard_map/ppermute | solution.py:503
  8.4 0.0 collective-permute-done.2.halo_ref
  8.4 6.6 %featurize.1 = (f32[2048,128]{1,0:T(8,128)}, f32[2048,128]{1,0:T(8,128)}, f32[2048,128]{1,0:T(8,128)}, f32[2048,128]{1,0:T(8,128)}, bf16[256,1024]{1,0:T(8,128)(...) custom-call(s32[1]{0:T(128)} %bitcast.position_ref, ...), custom_call_target="tpu_custom_call" | custom-call | bytes 21000000 | tf_op jit(solution)/shard_map/featurize/pallas_call | solution.py:480
  15.1 6.0 %all-to-all-start = ((bf16[8,128,128]{2,1,0:T(8,128)(2,1)}), bf16[8,128,128]{2,1,0:T(8,128)(2,1)S(1)}, u32[]{:S(2)}, u32[]{:S(2)}) async-start(bf16[8,128,128]{2,1,0:T(8,128)(2,1)} %get-tuple-element.46), calls=%async_computation | async-start | bytes 524288 | tf_op jit(solution)/shard_map/all_to_all | solution.py:565
  21.1 2.4 %collective-permute-start.3 = (bf16[256,1024]{1,0:T(8,128)(2,1)}, bf16[256,1024]{1,0:T(8,128)(2,1)S(1)}, u32[]{:S(2)}, u32[]{:S(2)}) collective-permute-start(bf16[256,1024]{1,0:T(8,128)(2,1)} %get-tuple-element.50), channel_id=1, source_target_pairs={{0,3},{1,2},{2,1},{3,0},{4,7},{5,6},{6,5},{7,4},{8,11},{9,10},{10,... | collective-permute-start | bytes 1572872 | tf_op jit(solution)/shard_map/ppermute | solution.py:503
  23.5 0.0 collective-permute-done.1.refs_2_.refs_1_
  23.5 0.0 copy-start
  23.5 0.0 collective-permute-done.refs_1_.refs_0_
  23.5 0.8 %copy-done = bf16[256,1024]{1,0:T(8,128)(2,1)} copy-done((bf16[256,1024]{1,0:T(8,128)(2,1)}, bf16[256,1024]{1,0:T(8,128)(2,1)S(1)}, u32[]{:S(2)}) %copy-start) | copy-done | bytes 524312
  24.3 6.7 %middle.1._.base_ref = f32[1024,256]{1,0:T(8,128)S(1)} custom-call(s32[4]{0:T(128)S(1)} %iota_xor_fusion.index_ref, bf16[1024,4096]{1,0:T(8,128)(2,1)} %weight_ref.5, bf16[256,1024]{1,0:T(8,128)(2,1)} %grad_in_ref, bf16[256,1024]{1,0:T(8,128)(2,1)} %collective-permute-done.refs_1_.refs_0_, bf16[256,1024]{1,0:T(8,128)(2,1)} %copy-done), custom_call_target="tpu_custom_call" | custom-call | bytes 21000000 | tf_op jit(solution)/shard_map/middle/pallas_call | solution.py:480
  31.0 0.0 all-to-all-done.message_ref
  31.0 6.9 %project.1 = (f32[2048,128]{1,0:T(8,128)}, bf16[256,1024]{1,0:T(8,128)(2,1)}, bf16[256,1024]{1,0:T(8,128)(2,1)}, bf16[256,1024]{1,0:T(8,128)(2,1)}, bf16[256,1024]{1,0:T(8,128)(2,1)}) custom-call(s32[4]{0:T(128)S(1)} %iota_xor_fusion.index_ref, bf16[8,128,128]{2,1,0:T(8,128)(2,1)S(1)} %all-to-all-done.message_ref, ...), custom_call_target="tpu_custom_call" | custom-call | bytes 24500000 | tf_op jit(solution)/shard_map/project/pallas_call | solution.py:480
  37.9 1.3 %collective-permute-start.5 = (bf16[256,1024]{1,0:T(8,128)(2,1)}, bf16[256,1024]{1,0:T(8,128)(2,1)}, u32[]{:S(2)}, u32[]{:S(2)}) collective-permute-start(bf16[256,1024]{1,0:T(8,128)(2,1)} %get-tuple-element.58), channel_id=1, source_target_pairs={{0,1},{1,0},{2,3},{3,2},{4,5},{5,4},{6,7},{7,6},{8,9},{9,8},{10,11... | collective-permute-start | bytes 1572872 | tf_op jit(solution)/shard_map/ppermute | solution.py:503
  39.2 1.5 %collective-permute-start.6 = (bf16[256,1024]{1,0:T(8,128)(2,1)}, bf16[256,1024]{1,0:T(8,128)(2,1)}, u32[]{:S(2)}, u32[]{:S(2)}) collective-permute-start(bf16[256,1024]{1,0:T(8,128)(2,1)} %get-tuple-element.59), channel_id=1, source_target_pairs={{0,2},{1,3},{2,0},{3,1},{4,6},{5,7},{6,4},{7,5},{8,10},{9,11},{10,... | collective-permute-start | bytes 1572872 | tf_op jit(solution)/shard_map/ppermute | solution.py:503
  40.7 0.7 %collective-permute-start.7 = (bf16[256,1024]{1,0:T(8,128)(2,1)}, bf16[256,1024]{1,0:T(8,128)(2,1)}, u32[]{:S(2)}, u32[]{:S(2)}) collective-permute-start(bf16[256,1024]{1,0:T(8,128)(2,1)} %get-tuple-element.60), channel_id=1, source_target_pairs={{0,3},{1,2},{2,1},{3,0},{4,7},{5,6},{6,5},{7,4},{8,11},{9,10},{10,... | collective-permute-start | bytes 1572872 | tf_op jit(solution)/shard_map/ppermute | solution.py:503
  41.5 0.0 collective-permute-done.3.refs_0_
  41.5 6.1 %back_last.1 = (f32[2048,128]{1,0:T(8,128)}, f32[2048,128]{1,0:T(8,128)S(1)}, bf16[8,128,128]{2,1,0:T(8,128)(2,1)}, f32[4,48,128]{2,1,0:T(8,128)S(1)}) custom-call(s32[4]{0:T(128)S(1)} %iota_xor_fusion.index_ref, s32[1]{0:T(128)} %bitcast.position_ref, f32[1024,256]{1,0:T(8,128)S(1)} %middle.1._.base_ref, f32[128,128]{1,0:T(8,128)S(1)} %get-tuple-element.42.decay_ref, ...), custom_call_target="tpu_custom_call" | custom-call | bytes 21000000 | tf_op jit(solution)/shard_map/back_last/pallas_call | solution.py:480
  47.6 5.1 %all-to-all-start.1 = ((bf16[8,128,128]{2,1,0:T(8,128)(2,1)}), bf16[8,128,128]{2,1,0:T(8,128)(2,1)S(1)}, u32[]{:S(2)}, u32[]{:S(2)}) async-start(bf16[8,128,128]{2,1,0:T(8,128)(2,1)} %get-tuple-element.51), calls=%async_computation.1 | async-start | bytes 524288 | tf_op jit(solution)/shard_map/all_to_all | solution.py:636
  52.7 1.3 %collective-permute-start.4 = (f32[4,48,128]{2,1,0:T(8,128)S(1)}, f32[4,48,128]{2,1,0:T(8,128)S(1)}, u32[]{:S(2)}, u32[]{:S(2)}) collective-permute-start(f32[4,48,128]{2,1,0:T(8,128)S(1)} %get-tuple-element.56), channel_id=1, source_target_pairs={{4,0},{8,4},{12,8},{16,12},{20,16},{24,20},{28,24},{5,1},{9,5},{13... | collective-permute-start | bytes 294920 | tf_op jit(solution)/shard_map/ppermute | solution.py:498
  54.0 4.0 %back_local.1 = (f32[2048,128]{1,0:T(8,128)S(1)}, bf16[256,1024]{1,0:T(8,128)(2,1)}) custom-call(f32[2048,128]{1,0:T(8,128)S(1)} %get-tuple-element.52.signal_ref, f32[128,128]{1,0:T(8,128)S(1)} %get-tuple-element.42.decay_ref, f32[128,128]{1,0:T(8,128)S(1)} %get-tuple-element.47.scale_ref, f32[168,128]{1,0:T(8,128)S(1)} %get-tuple-element.53.taps_ref, ...), custom_call_target="tpu_custom_call" | custom-call | bytes 15750000 | tf_op jit(solution)/shard_map/back_local/pallas_call | solution.py:480
  58.0 0.0 collective-permute-done.4.ahead_ref
  58.0 4.4 %all-to-all-done.1.message_ref = bf16[8,128,128]{2,1,0:T(8,128)(2,1)S(1)} async-done(((bf16[8,128,128]{2,1,0:T(8,128)(2,1)}), bf16[8,128,128]{2,1,0:T(8,128)(2,1)S(1)}, u32[]{:S(2)}, u32[]{:S(2)}) %all-to-all-start.1) | async-done | bytes 262176 | tf_op jit(solution)/shard_map/all_to_all | solution.py:636
  62.4 0.0 collective-permute-done.5.refs_1_
  62.4 1.6 %collective-permute-done.6.refs_2_ = bf16[256,1024]{1,0:T(8,128)(2,1)} collective-permute-done((bf16[256,1024]{1,0:T(8,128)(2,1)}, bf16[256,1024]{1,0:T(8,128)(2,1)}, u32[]{:S(2)}, u32[]{:S(2)}) %collective-permute-start.6) | collective-permute-done | bytes 524320 | tf_op jit(solution)/shard_map/ppermute | solution.py:503
  64.1 0.0 collective-permute-done.7.refs_3_
  64.1 5.3 %finish.1 = (bf16[256,1024]{1,0:T(8,128)(2,1)}, bf16[256,1024]{1,0:T(8,128)(2,1)}, bf16[256,1024]{1,0:T(8,128)(2,1)}, bf16[256,1024]{1,0:T(8,128)(2,1)}) custom-call(bf16[8,128,128]{2,1,0:T(8,128)(2,1)S(1)} %all-to-all-done.1.message_ref, f32[2048,128]{1,0:T(8,128)S(1)} %get-tuple-element.55.local_ref, ...), custom_call_target="tpu_custom_call", output_to_operand_aliasing={{0}: (13, {})} | custom-call | bytes 17500000 | tf_op jit(solution)/shard_map/finish/pallas_call | solution.py:480
  (1 shorter events, 0.0 us)
Async XLA Ops:
  2.1 6.3 %collective-permute-start.2 = (bf16[48,1024]{1,0:T(8,128)(2,1)S(1)}, bf16[48,1024]{1,0:T(8,128)(2,1)S(1)}, u32[]{:S(2)}, u32[]{:S(2)}) collective-permute-start(bf16[48,1024]{1,0:T(8,128)(2,1)S(1)} %get-tuple-element.41), channel_id=1, source_target_pairs={{0,4},{4,8},{8,12},{12,16},{16,20},{20,24},{24,28},{1,5},{5,9},{9,... | collective-permute-start | bytes 294920 | tf_op jit(solution)/shard_map/ppermute | solution.py:498
  4.5 19.0 %collective-permute-start.1 = (bf16[256,1024]{1,0:T(8,128)(2,1)}, bf16[256,1024]{1,0:T(8,128)(2,1)S(1)}, u32[]{:S(2)}, u32[]{:S(2)}) collective-permute-start(bf16[256,1024]{1,0:T(8,128)(2,1)} %grad_in_ref), channel_id=1, source_target_pairs={{0,2},{1,3},{2,0},{3,1},{4,6},{5,7},{6,4},{7,5},{8,10},{9,11},{10,... | collective-permute-start | bytes 1572872 | tf_op jit(solution)/shard_map/ppermute | solution.py:503
  6.9 16.6 %collective-permute-start = (bf16[256,1024]{1,0:T(8,128)(2,1)}, bf16[256,1024]{1,0:T(8,128)(2,1)}, u32[]{:S(2)}, u32[]{:S(2)}) collective-permute-start(bf16[256,1024]{1,0:T(8,128)(2,1)} %grad_in_ref), channel_id=1, source_target_pairs={{0,1},{1,0},{2,3},{3,2},{4,5},{5,4},{6,7},{7,6},{8,9},{9,8},{10,11... | collective-permute-start | bytes 1572872 | tf_op jit(solution)/shard_map/ppermute | solution.py:503
  15.1 16.0 %all-to-all-start = ((bf16[8,128,128]{2,1,0:T(8,128)(2,1)}), bf16[8,128,128]{2,1,0:T(8,128)(2,1)S(1)}, u32[]{:S(2)}, u32[]{:S(2)}) async-start(bf16[8,128,128]{2,1,0:T(8,128)(2,1)} %get-tuple-element.46), calls=%async_computation | async-start | bytes 524288 | tf_op jit(solution)/shard_map/all_to_all | solution.py:565
  21.1 20.4 %collective-permute-start.3 = (bf16[256,1024]{1,0:T(8,128)(2,1)}, bf16[256,1024]{1,0:T(8,128)(2,1)S(1)}, u32[]{:S(2)}, u32[]{:S(2)}) collective-permute-start(bf16[256,1024]{1,0:T(8,128)(2,1)} %get-tuple-element.50), channel_id=1, source_target_pairs={{0,3},{1,2},{2,1},{3,0},{4,7},{5,6},{6,5},{7,4},{8,11},{9,10},{10,... | collective-permute-start | bytes 1572872 | tf_op jit(solution)/shard_map/ppermute | solution.py:503
  23.5 0.8 %copy-start = (bf16[256,1024]{1,0:T(8,128)(2,1)}, bf16[256,1024]{1,0:T(8,128)(2,1)S(1)}, u32[]{:S(2)}) copy-start(bf16[256,1024]{1,0:T(8,128)(2,1)S(1)} %collective-permute-done.1.refs_2_.refs_1_) | copy-start | bytes 1572868
  37.9 24.5 %collective-permute-start.5 = (bf16[256,1024]{1,0:T(8,128)(2,1)}, bf16[256,1024]{1,0:T(8,128)(2,1)}, u32[]{:S(2)}, u32[]{:S(2)}) collective-permute-start(bf16[256,1024]{1,0:T(8,128)(2,1)} %get-tuple-element.58), channel_id=1, source_target_pairs={{0,1},{1,0},{2,3},{3,2},{4,5},{5,4},{6,7},{7,6},{8,9},{9,8},{10,11... | collective-permute-start | bytes 1572872 | tf_op jit(solution)/shard_map/ppermute | solution.py:503
  39.2 24.9 %collective-permute-start.6 = (bf16[256,1024]{1,0:T(8,128)(2,1)}, bf16[256,1024]{1,0:T(8,128)(2,1)}, u32[]{:S(2)}, u32[]{:S(2)}) collective-permute-start(bf16[256,1024]{1,0:T(8,128)(2,1)} %get-tuple-element.59), channel_id=1, source_target_pairs={{0,2},{1,3},{2,0},{3,1},{4,6},{5,7},{6,4},{7,5},{8,10},{9,11},{10,... | collective-permute-start | bytes 1572872 | tf_op jit(solution)/shard_map/ppermute | solution.py:503
  40.7 23.3 %collective-permute-start.7 = (bf16[256,1024]{1,0:T(8,128)(2,1)}, bf16[256,1024]{1,0:T(8,128)(2,1)}, u32[]{:S(2)}, u32[]{:S(2)}) collective-permute-start(bf16[256,1024]{1,0:T(8,128)(2,1)} %get-tuple-element.60), channel_id=1, source_target_pairs={{0,3},{1,2},{2,1},{3,0},{4,7},{5,6},{6,5},{7,4},{8,11},{9,10},{10,... | collective-permute-start | bytes 1572872 | tf_op jit(solution)/shard_map/ppermute | solution.py:503
  47.6 14.9 %all-to-all-start.1 = ((bf16[8,128,128]{2,1,0:T(8,128)(2,1)}), bf16[8,128,128]{2,1,0:T(8,128)(2,1)S(1)}, u32[]{:S(2)}, u32[]{:S(2)}) async-start(bf16[8,128,128]{2,1,0:T(8,128)(2,1)} %get-tuple-element.51), calls=%async_computation.1 | async-start | bytes 524288 | tf_op jit(solution)/shard_map/all_to_all | solution.py:636
  52.7 5.3 %collective-permute-start.4 = (f32[4,48,128]{2,1,0:T(8,128)S(1)}, f32[4,48,128]{2,1,0:T(8,128)S(1)}, u32[]{:S(2)}, u32[]{:S(2)}) collective-permute-start(f32[4,48,128]{2,1,0:T(8,128)S(1)} %get-tuple-element.56), channel_id=1, source_target_pairs={{4,0},{8,4},{12,8},{16,12},{20,16},{24,20},{28,24},{5,1},{9,5},{13... | collective-permute-start | bytes 294920 | tf_op jit(solution)/shard_map/ppermute | solution.py:498

commit v8 on v7

--- a/solution.py
+++ b/solution.py
@@ -334,6 +334,7 @@
         *piece_refs, back_query_ref, mixed_ref, message_ref, ahead_ref,
         turned_ref, total_ref, rows_ref, feat_ref, conv_vmem, held_ref, sems, own_sems,
     ) = refs
+    piece_refs = piece_refs[-turned_ref.shape[0] :]
     tokens = total_ref.shape[1]
     heads = pl.ds(0, rim * SUB)
     weights = start_weights(
@@ -605,9 +606,8 @@
         "project", 7.0, 16,
     )
     if fans == 4:
-        parts = [
-            exchange(part, "ch", mask) if mask else part for mask, part in enumerate(partial_sums)
-        ]
+        parts = [exchange(partial_sums[mask], "ch", mask) for mask in reversed(range(1, fans))]
+        parts.append(partial_sums[0])
     else:
         parts = lax.all_to_all(
             jnp.stack(partial_sums), "ch", split_axis=0, concat_axis=0, tiled=True
@@ -619,9 +619,9 @@
         + [((4, rim * SUB, LANES), F32)],
         (
             order, position, base, decay_tiles, out_weight, query_feat, key_feat,
-            value_feat, conv_out, *pieces[early:],
+            value_feat, conv_out, *pieces[1:early], *pieces[early:],
         ),
-        [IN_SMEM] * 2 + [IN_VMEM] * 2 + [IN_HBM] * 5 + [IN_VMEM] * (fans - early),
+        [IN_SMEM] * 2 + [IN_VMEM] * 2 + [IN_HBM] * (4 + early) + [IN_VMEM] * (fans - early),
         [
             pltpu.VMEM((fans - early, channels, tokens), BF16),
             pltpu.VMEM((channels, tokens), F32),

time: 69.8 us -> 70.2 us (level)
  transfers between devices with their start and end apart: 10 -> 10, of which waited for: 2 -> 2; matrix products, arithmetic and copies ran while one was open for 0% -> 0% of each run, Pallas kernels for 44% -> 43%
where the time goes in v8:
time: 70.2 us; the launch traced here: 69.8 us
  Pallas kernels  37.2 us (53%)
  starting transfers between devices  24.7 us (35%)
  waiting for transfers between devices  6.49 us (9%)
  local copies, waits for them, and re-layouts  0.78 us (1%)
  between operations  0.73 us (1%)
    pallas_call x7, Pallas kernels, call(): pl.pallas_call(kernel, out_shape=[jax.ShapeDtypeStruct(*out) if own else...  37.2 us
    ppermute x6, starting transfers between devices, exchange(): return lax.ppermute(value, axis, [(s, s ^ mask) for s in range(count)])  9.91 us
    all_to_all x1, starting transfers between devices, shards(): lax.all_to_all(messages, 'ctx', split_axis=0, concat_axis=0, tiled=True)  5.99 us
    all_to_all x1, starting transfers between devices, shards(): lax.all_to_all(back_messages, 'ctx', split_axis=0, concat_axis=0, tiled=T...  5.12 us
    all_to_all x1, waiting for transfers between devices, shards(): lax.all_to_all(back_messages, 'ctx', split_axis=0, concat_axis=0, tiled=T...  4.43 us
    ppermute x2, starting transfers between devices, shift(): return lax.ppermute(value, axis, pairs)  3.64 us
    ppermute x6, waiting for transfers between devices, exchange(): return lax.ppermute(value, axis, [(s, s ^ mask) for s in range(count)])  2.05 us
  transfers between devices with their start and end apart: 10, of which 2 were waited for; matrix products, arithmetic and copies ran while one was open for 0% of the time, Pallas kernels for 43%

profile of v8, /device:TPU:0, one launch (start us, length us, event | category | flops | bytes accessed | tf_op | source)
XLA Modules:
  0.0 69.8 jit_solution(17281569711169229567)
XLA Ops:
  0.6 1.5 %rim.1 = (bf16[48,1024]{1,0:T(8,128)(2,1)S(1)}, bf16[3,256,1024]{2,1,0:T(8,128)(2,1)S(1)}, f32[3,7,1024]{2,1,0:T(8,128)S(1)}, f32[16,1024]{1,0:T(8,128)S(1)}, f32[16,1024]{1,0:T(8,128)S(1)}) custom-call(bf16[256,1024]{1,0:T(8,128)(2,1)} %q_ref.1, bf16[256,1024]{1,0:T(8,128)(2,1)} %k_ref.1, bf16[256,1024]{1,0:T(8,128)(2,1)} %v_ref.1, f32[3,7,1024]{2,1,0:T(8,128)} %bitcast.4, ...), custom_call_target="tpu_custom_call" | custom-call | bytes 4200000 | tf_op jit(solution)/shard_map/rim/pallas_call | solution.py:481
  2.1 2.4 %collective-permute-start.2 = (bf16[48,1024]{1,0:T(8,128)(2,1)S(1)}, bf16[48,1024]{1,0:T(8,128)(2,1)S(1)}, u32[]{:S(2)}, u32[]{:S(2)}) collective-permute-start(bf16[48,1024]{1,0:T(8,128)(2,1)S(1)} %get-tuple-element.41), channel_id=1, source_target_pairs={{0,4},{4,8},{8,12},{12,16},{16,20},{20,24},{24,28},{1,5},{5,9},{9,... | collective-permute-start | bytes 294920 | tf_op jit(solution)/shard_map/ppermute | solution.py:499
  4.5 2.4 %collective-permute-start.1 = (bf16[256,1024]{1,0:T(8,128)(2,1)}, bf16[256,1024]{1,0:T(8,128)(2,1)S(1)}, u32[]{:S(2)}, u32[]{:S(2)}) collective-permute-start(bf16[256,1024]{1,0:T(8,128)(2,1)} %grad_in_ref), channel_id=1, source_target_pairs={{0,2},{1,3},{2,0},{3,1},{4,6},{5,7},{6,4},{7,5},{8,10},{9,11},{10,... | collective-permute-start | bytes 1572872 | tf_op jit(solution)/shard_map/ppermute | solution.py:504
  6.9 1.5 %collective-permute-start = (bf16[256,1024]{1,0:T(8,128)(2,1)}, bf16[256,1024]{1,0:T(8,128)(2,1)}, u32[]{:S(2)}, u32[]{:S(2)}) collective-permute-start(bf16[256,1024]{1,0:T(8,128)(2,1)} %grad_in_ref), channel_id=1, source_target_pairs={{0,1},{1,0},{2,3},{3,2},{4,5},{5,4},{6,7},{7,6},{8,9},{9,8},{10,11... | collective-permute-start | bytes 1572872 | tf_op jit(solution)/shard_map/ppermute | solution.py:504
  8.4 0.0 collective-permute-done.2.halo_ref
  8.4 6.6 %featurize.1 = (f32[2048,128]{1,0:T(8,128)}, f32[2048,128]{1,0:T(8,128)}, f32[2048,128]{1,0:T(8,128)}, f32[2048,128]{1,0:T(8,128)}, bf16[256,1024]{1,0:T(8,128)(...) custom-call(s32[1]{0:T(128)} %bitcast.position_ref, ...), custom_call_target="tpu_custom_call" | custom-call | bytes 21000000 | tf_op jit(solution)/shard_map/featurize/pallas_call | solution.py:481
  15.1 6.0 %all-to-all-start = ((bf16[8,128,128]{2,1,0:T(8,128)(2,1)}), bf16[8,128,128]{2,1,0:T(8,128)(2,1)S(1)}, u32[]{:S(2)}, u32[]{:S(2)}) async-start(bf16[8,128,128]{2,1,0:T(8,128)(2,1)} %get-tuple-element.46), calls=%async_computation | async-start | bytes 524288 | tf_op jit(solution)/shard_map/all_to_all | solution.py:566
  21.1 2.4 %collective-permute-start.3 = (bf16[256,1024]{1,0:T(8,128)(2,1)}, bf16[256,1024]{1,0:T(8,128)(2,1)S(1)}, u32[]{:S(2)}, u32[]{:S(2)}) collective-permute-start(bf16[256,1024]{1,0:T(8,128)(2,1)} %get-tuple-element.50), channel_id=1, source_target_pairs={{0,3},{1,2},{2,1},{3,0},{4,7},{5,6},{6,5},{7,4},{8,11},{9,10},{10,... | collective-permute-start | bytes 1572872 | tf_op jit(solution)/shard_map/ppermute | solution.py:504
  23.5 0.0 collective-permute-done.1.refs_2_.refs_1_
  23.5 0.0 copy-start
  23.5 0.0 collective-permute-done.refs_1_.refs_0_
  23.5 0.8 %copy-done = bf16[256,1024]{1,0:T(8,128)(2,1)} copy-done((bf16[256,1024]{1,0:T(8,128)(2,1)}, bf16[256,1024]{1,0:T(8,128)(2,1)S(1)}, u32[]{:S(2)}) %copy-start) | copy-done | bytes 524312
  24.3 6.7 %middle.1._.base_ref = f32[1024,256]{1,0:T(8,128)S(1)} custom-call(s32[4]{0:T(128)S(1)} %iota_xor_fusion.index_ref, bf16[1024,4096]{1,0:T(8,128)(2,1)} %weight_ref.5, bf16[256,1024]{1,0:T(8,128)(2,1)} %grad_in_ref, bf16[256,1024]{1,0:T(8,128)(2,1)} %collective-permute-done.refs_1_.refs_0_, bf16[256,1024]{1,0:T(8,128)(2,1)} %copy-done), custom_call_target="tpu_custom_call" | custom-call | bytes 21000000 | tf_op jit(solution)/shard_map/middle/pallas_call | solution.py:481
  31.1 0.0 all-to-all-done.message_ref
  31.1 6.8 %project.1 = (f32[2048,128]{1,0:T(8,128)}, bf16[256,1024]{1,0:T(8,128)(2,1)}, bf16[256,1024]{1,0:T(8,128)(2,1)}, bf16[256,1024]{1,0:T(8,128)(2,1)}, bf16[256,1024]{1,0:T(8,128)(2,1)}) custom-call(s32[4]{0:T(128)S(1)} %iota_xor_fusion.index_ref, bf16[8,128,128]{2,1,0:T(8,128)(2,1)S(1)} %all-to-all-done.message_ref, ...), custom_call_target="tpu_custom_call" | custom-call | bytes 24500000 | tf_op jit(solution)/shard_map/project/pallas_call | solution.py:481
  37.9 2.3 %collective-permute-start.5 = (bf16[256,1024]{1,0:T(8,128)(2,1)}, bf16[256,1024]{1,0:T(8,128)(2,1)}, u32[]{:S(2)}, u32[]{:S(2)}) collective-permute-start(bf16[256,1024]{1,0:T(8,128)(2,1)} %get-tuple-element.57), channel_id=1, source_target_pairs={{0,3},{1,2},{2,1},{3,0},{4,7},{5,6},{6,5},{7,4},{8,11},{9,10},{10,... | collective-permute-start | bytes 1572872 | tf_op jit(solution)/shard_map/ppermute | solution.py:504
  40.2 0.5 collective-permute-start.6
  40.7 0.8 %collective-permute-start.7 = (bf16[256,1024]{1,0:T(8,128)(2,1)}, bf16[256,1024]{1,0:T(8,128)(2,1)}, u32[]{:S(2)}, u32[]{:S(2)}) collective-permute-start(bf16[256,1024]{1,0:T(8,128)(2,1)} %get-tuple-element.59), channel_id=1, source_target_pairs={{0,1},{1,0},{2,3},{3,2},{4,5},{5,4},{6,7},{7,6},{8,9},{9,8},{10,11... | collective-permute-start | bytes 1572872 | tf_op jit(solution)/shard_map/ppermute | solution.py:504
  41.5 0.0 collective-permute-done.3.refs_2_
  41.5 6.1 %back_last.1 = (f32[2048,128]{1,0:T(8,128)}, f32[2048,128]{1,0:T(8,128)S(1)}, bf16[8,128,128]{2,1,0:T(8,128)(2,1)}, f32[4,48,128]{2,1,0:T(8,128)S(1)}) custom-call(s32[4]{0:T(128)S(1)} %iota_xor_fusion.index_ref, s32[1]{0:T(128)} %bitcast.position_ref, f32[1024,256]{1,0:T(8,128)S(1)} %middle.1._.base_ref, f32[128,128]{1,0:T(8,128)S(1)} %get-tuple-element.42.decay_ref, ...), custom_call_target="tpu_custom_call" | custom-call | bytes 21000000 | tf_op jit(solution)/shard_map/back_last/pallas_call | solution.py:481
  47.6 5.1 %all-to-all-start.1 = ((bf16[8,128,128]{2,1,0:T(8,128)(2,1)}), bf16[8,128,128]{2,1,0:T(8,128)(2,1)S(1)}, u32[]{:S(2)}, u32[]{:S(2)}) async-start(bf16[8,128,128]{2,1,0:T(8,128)(2,1)} %get-tuple-element.51), calls=%async_computation.1 | async-start | bytes 524288 | tf_op jit(solution)/shard_map/all_to_all | solution.py:636
  52.7 1.3 %collective-permute-start.4 = (f32[4,48,128]{2,1,0:T(8,128)S(1)}, f32[4,48,128]{2,1,0:T(8,128)S(1)}, u32[]{:S(2)}, u32[]{:S(2)}) collective-permute-start(f32[4,48,128]{2,1,0:T(8,128)S(1)} %get-tuple-element.56), channel_id=1, source_target_pairs={{4,0},{8,4},{12,8},{16,12},{20,16},{24,20},{28,24},{5,1},{9,5},{13... | collective-permute-start | bytes 294920 | tf_op jit(solution)/shard_map/ppermute | solution.py:499
  54.0 4.0 %back_local.1 = (f32[2048,128]{1,0:T(8,128)S(1)}, bf16[256,1024]{1,0:T(8,128)(2,1)}) custom-call(f32[2048,128]{1,0:T(8,128)S(1)} %get-tuple-element.52.signal_ref, f32[128,128]{1,0:T(8,128)S(1)} %get-tuple-element.42.decay_ref, f32[128,128]{1,0:T(8,128)S(1)} %get-tuple-element.47.scale_ref, f32[168,128]{1,0:T(8,128)S(1)} %get-tuple-element.53.taps_ref, ...), custom_call_target="tpu_custom_call" | custom-call | bytes 15750000 | tf_op jit(solution)/shard_map/back_local/pallas_call | solution.py:481
  58.0 0.0 collective-permute-done.4.ahead_ref
  58.0 4.4 %all-to-all-done.1.message_ref = bf16[8,128,128]{2,1,0:T(8,128)(2,1)S(1)} async-done(((bf16[8,128,128]{2,1,0:T(8,128)(2,1)}), bf16[8,128,128]{2,1,0:T(8,128)(2,1)S(1)}, u32[]{:S(2)}, u32[]{:S(2)}) %all-to-all-start.1) | async-done | bytes 262176 | tf_op jit(solution)/shard_map/all_to_all | solution.py:636
  62.4 0.0 collective-permute-done.5.refs_0_
  62.4 2.0 %collective-permute-done.6.refs_1_ = bf16[256,1024]{1,0:T(8,128)(2,1)} collective-permute-done((bf16[256,1024]{1,0:T(8,128)(2,1)}, bf16[256,1024]{1,0:T(8,128)(2,1)}, u32[]{:S(2)}, u32[]{:S(2)}) %collective-permute-start.6) | collective-permute-done | bytes 524320 | tf_op jit(solution)/shard_map/ppermute | solution.py:504
  64.5 0.0 collective-permute-done.7.refs_2_
  64.5 5.3 %finish.1 = (bf16[256,1024]{1,0:T(8,128)(2,1)}, bf16[256,1024]{1,0:T(8,128)(2,1)}, bf16[256,1024]{1,0:T(8,128)(2,1)}, bf16[256,1024]{1,0:T(8,128)(2,1)}) custom-call(bf16[8,128,128]{2,1,0:T(8,128)(2,1)S(1)} %all-to-all-done.1.message_ref, f32[2048,128]{1,0:T(8,128)S(1)} %get-tuple-element.55.local_ref, ...), custom_call_target="tpu_custom_call", output_to_operand_aliasing={{0}: (13, {})} | custom-call | bytes 17500000 | tf_op jit(solution)/shard_map/finish/pallas_call | solution.py:481
  (1 shorter events, 0.0 us)
Async XLA Ops:
  2.1 6.3 %collective-permute-start.2 = (bf16[48,1024]{1,0:T(8,128)(2,1)S(1)}, bf16[48,1024]{1,0:T(8,128)(2,1)S(1)}, u32[]{:S(2)}, u32[]{:S(2)}) collective-permute-start(bf16[48,1024]{1,0:T(8,128)(2,1)S(1)} %get-tuple-element.41), channel_id=1, source_target_pairs={{0,4},{4,8},{8,12},{12,16},{16,20},{20,24},{24,28},{1,5},{5,9},{9,... | collective-permute-start | bytes 294920 | tf_op jit(solution)/shard_map/ppermute | solution.py:499
  4.5 19.0 %collective-permute-start.1 = (bf16[256,1024]{1,0:T(8,128)(2,1)}, bf16[256,1024]{1,0:T(8,128)(2,1)S(1)}, u32[]{:S(2)}, u32[]{:S(2)}) collective-permute-start(bf16[256,1024]{1,0:T(8,128)(2,1)} %grad_in_ref), channel_id=1, source_target_pairs={{0,2},{1,3},{2,0},{3,1},{4,6},{5,7},{6,4},{7,5},{8,10},{9,11},{10,... | collective-permute-start | bytes 1572872 | tf_op jit(solution)/shard_map/ppermute | solution.py:504
  6.9 16.6 %collective-permute-start = (bf16[256,1024]{1,0:T(8,128)(2,1)}, bf16[256,1024]{1,0:T(8,128)(2,1)}, u32[]{:S(2)}, u32[]{:S(2)}) collective-permute-start(bf16[256,1024]{1,0:T(8,128)(2,1)} %grad_in_ref), channel_id=1, source_target_pairs={{0,1},{1,0},{2,3},{3,2},{4,5},{5,4},{6,7},{7,6},{8,9},{9,8},{10,11... | collective-permute-start | bytes 1572872 | tf_op jit(solution)/shard_map/ppermute | solution.py:504
  15.1 16.0 %all-to-all-start = ((bf16[8,128,128]{2,1,0:T(8,128)(2,1)}), bf16[8,128,128]{2,1,0:T(8,128)(2,1)S(1)}, u32[]{:S(2)}, u32[]{:S(2)}) async-start(bf16[8,128,128]{2,1,0:T(8,128)(2,1)} %get-tuple-element.46), calls=%async_computation | async-start | bytes 524288 | tf_op jit(solution)/shard_map/all_to_all | solution.py:566
  21.1 20.4 %collective-permute-start.3 = (bf16[256,1024]{1,0:T(8,128)(2,1)}, bf16[256,1024]{1,0:T(8,128)(2,1)S(1)}, u32[]{:S(2)}, u32[]{:S(2)}) collective-permute-start(bf16[256,1024]{1,0:T(8,128)(2,1)} %get-tuple-element.50), channel_id=1, source_target_pairs={{0,3},{1,2},{2,1},{3,0},{4,7},{5,6},{6,5},{7,4},{8,11},{9,10},{10,... | collective-permute-start | bytes 1572872 | tf_op jit(solution)/shard_map/ppermute | solution.py:504
  23.5 0.8 %copy-start = (bf16[256,1024]{1,0:T(8,128)(2,1)}, bf16[256,1024]{1,0:T(8,128)(2,1)S(1)}, u32[]{:S(2)}) copy-start(bf16[256,1024]{1,0:T(8,128)(2,1)S(1)} %collective-permute-done.1.refs_2_.refs_1_) | copy-start | bytes 1572868
  37.9 24.5 %collective-permute-start.5 = (bf16[256,1024]{1,0:T(8,128)(2,1)}, bf16[256,1024]{1,0:T(8,128)(2,1)}, u32[]{:S(2)}, u32[]{:S(2)}) collective-permute-start(bf16[256,1024]{1,0:T(8,128)(2,1)} %get-tuple-element.57), channel_id=1, source_target_pairs={{0,3},{1,2},{2,1},{3,0},{4,7},{5,6},{6,5},{7,4},{8,11},{9,10},{10,... | collective-permute-start | bytes 1572872 | tf_op jit(solution)/shard_map/ppermute | solution.py:504
  40.2 24.3 %collective-permute-start.6 = (bf16[256,1024]{1,0:T(8,128)(2,1)}, bf16[256,1024]{1,0:T(8,128)(2,1)}, u32[]{:S(2)}, u32[]{:S(2)}) collective-permute-start(bf16[256,1024]{1,0:T(8,128)(2,1)} %get-tuple-element.58), channel_id=1, source_target_pairs={{0,2},{1,3},{2,0},{3,1},{4,6},{5,7},{6,4},{7,5},{8,10},{9,11},{10,... | collective-permute-start | bytes 1572872 | tf_op jit(solution)/shard_map/ppermute | solution.py:504
  40.7 23.8 %collective-permute-start.7 = (bf16[256,1024]{1,0:T(8,128)(2,1)}, bf16[256,1024]{1,0:T(8,128)(2,1)}, u32[]{:S(2)}, u32[]{:S(2)}) collective-permute-start(bf16[256,1024]{1,0:T(8,128)(2,1)} %get-tuple-element.59), channel_id=1, source_target_pairs={{0,1},{1,0},{2,3},{3,2},{4,5},{5,4},{6,7},{7,6},{8,9},{9,8},{10,11... | collective-permute-start | bytes 1572872 | tf_op jit(solution)/shard_map/ppermute | solution.py:504
  47.6 14.9 %all-to-all-start.1 = ((bf16[8,128,128]{2,1,0:T(8,128)(2,1)}), bf16[8,128,128]{2,1,0:T(8,128)(2,1)S(1)}, u32[]{:S(2)}, u32[]{:S(2)}) async-start(bf16[8,128,128]{2,1,0:T(8,128)(2,1)} %get-tuple-element.51), calls=%async_computation.1 | async-start | bytes 524288 | tf_op jit(solution)/shard_map/all_to_all | solution.py:636
  52.7 5.3 %collective-permute-start.4 = (f32[4,48,128]{2,1,0:T(8,128)S(1)}, f32[4,48,128]{2,1,0:T(8,128)S(1)}, u32[]{:S(2)}, u32[]{:S(2)}) collective-permute-start(f32[4,48,128]{2,1,0:T(8,128)S(1)} %get-tuple-element.56), channel_id=1, source_target_pairs={{4,0},{8,4},{12,8},{16,12},{20,16},{24,20},{28,24},{5,1},{9,5},{13... | collective-permute-start | bytes 294920 | tf_op jit(solution)/shard_map/ppermute | solution.py:499

commit v9 on v7

--- a/solution.py
+++ b/solution.py
@@ -331,9 +331,16 @@
     *refs, rim,
 ):
     (
-        *piece_refs, back_query_ref, mixed_ref, message_ref, ahead_ref,
-        turned_ref, total_ref, rows_ref, feat_ref, conv_vmem, held_ref, sems, own_sems,
+        *piece_refs, back_query_ref, mixed_ref, message_ref, ahead_ref, piece_vmem,
+        turned_ref, total_ref, rows_ref, feat_ref, conv_vmem, held_ref, sems, piece_sems, own_sems,
     ) = refs
+    piece_refs = piece_refs[-turned_ref.shape[0] :]
+    pieces = start_all(
+        [
+            pltpu.make_async_copy(ref, piece_vmem.at[number], piece_sems.at[number])
+            for number, ref in enumerate(piece_refs)
+        ]
+    )
     tokens = total_ref.shape[1]
     heads = pl.ds(0, rim * SUB)
     weights = start_weights(
@@ -347,7 +354,9 @@
             pltpu.make_async_copy(vf_ref.at[heads, :], ahead_ref.at[3], own_sems.at[3]),
         ]
     )
-    back_products(weights, piece_refs, turned_ref, held_ref, total_ref, base_ref)
+    wait_all(pieces)
+    held = [piece_vmem.at[number] for number in range(len(piece_refs))]
+    back_products(weights, held, turned_ref, held_ref, total_ref, base_ref)
     scatter_tokens(rows_ref, total_ref[...].T, 0)
     wait_all(copies)
     mixed_ref[...] = round16(rows_ref[...] * feat_ref[...])
@@ -380,9 +389,9 @@
 
 
 def back_local_kernel(
-    signal_ref, decay_ref, scale_ref, taps_ref, query_ref, local_ref, gq_ref,
-    wide_ref, rows_ref, out_vmem, sem, *, taps,
+    signal_ref, decay_ref, scale_ref, taps_ref, query_ref, *refs, taps
 ):
+    local_ref, gq_ref, wide_ref, rows_ref, out_vmem, sem = refs[-6:]
     inside = query_ref.shape[0]
     copy = pltpu.make_async_copy(query_ref, wide_ref.at[pl.ds(0, inside), :], sem)
     copy.start()
@@ -570,7 +579,7 @@
             pltpu.SemaphoreType.DMA((count,)),
         ]
 
-    early = fans - 1
+    early = fans // 2
     (base,) = call(
         middle_kernel,
         [((channels, tokens), F32)],
@@ -619,10 +628,11 @@
         + [((4, rim * SUB, LANES), F32)],
         (
             order, position, base, decay_tiles, out_weight, query_feat, key_feat,
-            value_feat, conv_out, *pieces[early:],
+            value_feat, conv_out, *pieces[1:early], *pieces[early:],
         ),
-        [IN_SMEM] * 2 + [IN_VMEM] * 2 + [IN_HBM] * 5 + [IN_VMEM] * (fans - early),
-        [
+        [IN_SMEM] * 2 + [IN_VMEM] * 2 + [IN_HBM] * (4 + fans),
+        [
+            pltpu.VMEM((fans - early, tokens, channels), BF16),
             pltpu.VMEM((fans - early, channels, tokens), BF16),
             pltpu.VMEM((channels, tokens), F32),
             tile,
@@ -630,16 +640,16 @@
             tile,
         ]
         + weight_scratch(fans - early)
-        + [pltpu.SemaphoreType.DMA((5,))],
-        "back_last", 6.0, 9,
+        + [pltpu.SemaphoreType.DMA((fans - early,)), pltpu.SemaphoreType.DMA((5,))],
+        "back_last", 7.0, 13,
     )
     back_arrived = lax.all_to_all(back_messages, "ctx", split_axis=0, concat_axis=0, tiled=True)
     ahead = shift(ahead, "ctx", -1)
     back_local, grad_query = call(
         functools.partial(back_local_kernel, taps=taps),
         [(tile_shape, F32), in_hbm((tokens, channels), BF16)],
-        (grad_mixed, decay_tiles, scale_tiles, tap_tiles, back_query),
-        [IN_VMEM] * 4 + [IN_HBM],
+        (grad_mixed, decay_tiles, scale_tiles, tap_tiles, back_query, *pieces[early:]),
+        [IN_VMEM] * 4 + [IN_HBM] * (1 + fans - early),
         [
             pltpu.VMEM((wide_rows, LANES), F32),
             tile,

time: 69.8 us -> 70.6 us (1.011)
  local copies, waits for them, and re-layouts: 0.78 us -> 2.37 us
  starting transfers between devices: 24.7 us -> 23.4 us
  Pallas kernels: 37.1 us -> 38 us
    unnamed x2 -> x6, local copies, waits for them, and re-layouts: 0.78 us -> 2.37 us
    ppermute x6, waiting for transfers between devices: 1.65 us -> 0.08 us  [exchange(): return lax.ppermute(value, axis, [(s, s ^ mask) for s in range(count)])]
    all_to_all x1, waiting for transfers between devices: 0.01 us -> 1.29 us  [shards(): lax.all_to_all(messages, 'ctx', split_axis=0, concat_axis=0, tiled=True)]
    all_to_all x1, starting transfers between devices: 5.12 us -> 3.85 us  [shards(): lax.all_to_all(back_messages, 'ctx', split_axis=0, concat_axis=0, tiled=T...]
    pallas_call x7, Pallas kernels: 37.1 us -> 38 us  [call(): pl.pallas_call(kernel, out_shape=[jax.ShapeDtypeStruct(*out) if own else...]
  transfers between devices with their start and end apart: 10 -> 10, of which waited for: 2 -> 3; matrix products, arithmetic and copies ran while one was open for 0% -> 0% of each run, Pallas kernels for 44% -> 44%
where the time goes in v9:
time: 70.6 us; the launch traced here: 70.3 us
  Pallas kernels  38 us (54%)
  starting transfers between devices  23.4 us (33%)
  waiting for transfers between devices  5.8 us (8%)
  local copies, waits for them, and re-layouts  2.37 us (3%)
  between operations  0.72 us (1%)
    pallas_call x7, Pallas kernels, call(): pl.pallas_call(kernel, out_shape=[jax.ShapeDtypeStruct(*out) if own else...  38 us
    ppermute x6, starting transfers between devices, exchange(): return lax.ppermute(value, axis, [(s, s ^ mask) for s in range(count)])  9.91 us
    all_to_all x1, starting transfers between devices, shards(): lax.all_to_all(messages, 'ctx', split_axis=0, concat_axis=0, tiled=True)  5.99 us
    all_to_all x1, waiting for transfers between devices, shards(): lax.all_to_all(back_messages, 'ctx', split_axis=0, concat_axis=0, tiled=T...  4.43 us
    all_to_all x1, starting transfers between devices, shards(): lax.all_to_all(back_messages, 'ctx', split_axis=0, concat_axis=0, tiled=T...  3.85 us
    ppermute x2, starting transfers between devices, shift(): return lax.ppermute(value, axis, pairs)  3.64 us
    unnamed x6, local copies, waits for them, and re-layouts  2.37 us
  transfers between devices with their start and end apart: 10, of which 3 were waited for; matrix products, arithmetic and copies ran while one was open for 0% of the time, Pallas kernels for 44%

profile of v9, /device:TPU:0, one launch (start us, length us, event | category | flops | bytes accessed | tf_op | source)
XLA Modules:
  0.0 70.3 jit_solution(4819286816915829902)
XLA Ops:
  0.6 1.5 %rim.1 = (bf16[48,1024]{1,0:T(8,128)(2,1)S(1)}, bf16[3,256,1024]{2,1,0:T(8,128)(2,1)S(1)}, f32[3,7,1024]{2,1,0:T(8,128)S(1)}, f32[16,1024]{1,0:T(8,128)S(1)}, f32[16,1024]{1,0:T(8,128)S(1)}) custom-call(bf16[256,1024]{1,0:T(8,128)(2,1)} %q_ref.1, bf16[256,1024]{1,0:T(8,128)(2,1)} %k_ref.1, bf16[256,1024]{1,0:T(8,128)(2,1)} %v_ref.1, f32[3,7,1024]{2,1,0:T(8,128)} %bitcast.4, ...), custom_call_target="tpu_custom_call" | custom-call | bytes 4200000 | tf_op jit(solution)/shard_map/rim/pallas_call | solution.py:489
  2.1 2.4 %collective-permute-start.1 = (bf16[48,1024]{1,0:T(8,128)(2,1)S(1)}, bf16[48,1024]{1,0:T(8,128)(2,1)S(1)}, u32[]{:S(2)}, u32[]{:S(2)}) collective-permute-start(bf16[48,1024]{1,0:T(8,128)(2,1)S(1)} %get-tuple-element.41), channel_id=1, source_target_pairs={{0,4},{4,8},{8,12},{12,16},{16,20},{20,24},{24,28},{1,5},{5,9},{9,... | collective-permute-start | bytes 294920 | tf_op jit(solution)/shard_map/ppermute | solution.py:507
  4.5 2.4 %collective-permute-start = (bf16[256,1024]{1,0:T(8,128)(2,1)}, bf16[256,1024]{1,0:T(8,128)(2,1)S(1)}, u32[]{:S(2)}, u32[]{:S(2)}) collective-permute-start(bf16[256,1024]{1,0:T(8,128)(2,1)} %grad_in_ref), channel_id=1, source_target_pairs={{0,1},{1,0},{2,3},{3,2},{4,5},{5,4},{6,7},{7,6},{8,9},{9,8},{10,11... | collective-permute-start | bytes 1572872 | tf_op jit(solution)/shard_map/ppermute | solution.py:512
  6.9 1.5 %collective-permute-start.2 = (bf16[256,1024]{1,0:T(8,128)(2,1)}, bf16[256,1024]{1,0:T(8,128)(2,1)S(1)}, u32[]{:S(2)}, u32[]{:S(2)}) collective-permute-start(bf16[256,1024]{1,0:T(8,128)(2,1)} %grad_in_ref), channel_id=1, source_target_pairs={{0,2},{1,3},{2,0},{3,1},{4,6},{5,7},{6,4},{7,5},{8,10},{9,11},{10,... | collective-permute-start | bytes 1572872 | tf_op jit(solution)/shard_map/ppermute | solution.py:512
  8.4 0.0 collective-permute-done.1.halo_ref
  8.4 6.6 %featurize.1 = (f32[2048,128]{1,0:T(8,128)}, f32[2048,128]{1,0:T(8,128)}, f32[2048,128]{1,0:T(8,128)}, f32[2048,128]{1,0:T(8,128)}, bf16[256,1024]{1,0:T(8,128)(...) custom-call(s32[1]{0:T(128)} %bitcast.position_ref, ...), custom_call_target="tpu_custom_call" | custom-call | bytes 21000000 | tf_op jit(solution)/shard_map/featurize/pallas_call | solution.py:489
  15.1 6.0 %all-to-all-start = ((bf16[8,128,128]{2,1,0:T(8,128)(2,1)}), bf16[8,128,128]{2,1,0:T(8,128)(2,1)S(1)}, u32[]{:S(2)}, u32[]{:S(2)}) async-start(bf16[8,128,128]{2,1,0:T(8,128)(2,1)} %get-tuple-element.46), calls=%async_computation | async-start | bytes 524288 | tf_op jit(solution)/shard_map/all_to_all | solution.py:574
  21.1 2.4 %collective-permute-start.3 = (bf16[256,1024]{1,0:T(8,128)(2,1)}, bf16[256,1024]{1,0:T(8,128)(2,1)}, u32[]{:S(2)}, u32[]{:S(2)}) collective-permute-start(bf16[256,1024]{1,0:T(8,128)(2,1)} %get-tuple-element.50), channel_id=1, source_target_pairs={{0,3},{1,2},{2,1},{3,0},{4,7},{5,6},{6,5},{7,4},{8,11},{9,10},{10,... | collective-permute-start | bytes 1572872 | tf_op jit(solution)/shard_map/ppermute | solution.py:512
  23.5 0.0 collective-permute-done.refs_1_.refs_0_
  23.5 0.0 copy-start
  23.5 0.8 %copy-done = bf16[256,1024]{1,0:T(8,128)(2,1)} copy-done((bf16[256,1024]{1,0:T(8,128)(2,1)}, bf16[256,1024]{1,0:T(8,128)(2,1)S(1)}, u32[]{:S(2)}) %copy-start) | copy-done | bytes 524312
  24.3 5.2 %middle.1._.base_ref = f32[1024,256]{1,0:T(8,128)S(1)} custom-call(s32[4]{0:T(128)S(1)} %iota_xor_fusion.index_ref, bf16[1024,4096]{1,0:T(8,128)(2,1)} %weight_ref.5, bf16[256,1024]{1,0:T(8,128)(2,1)} %grad_in_ref, bf16[256,1024]{1,0:T(8,128)(2,1)} %copy-done), custom_call_target="tpu_custom_call" | custom-call | bytes 21000000 | tf_op jit(solution)/shard_map/middle/pallas_call | solution.py:489
  29.5 1.3 %all-to-all-done.message_ref = bf16[8,128,128]{2,1,0:T(8,128)(2,1)S(1)} async-done(((bf16[8,128,128]{2,1,0:T(8,128)(2,1)}), bf16[8,128,128]{2,1,0:T(8,128)(2,1)S(1)}, u32[]{:S(2)}, u32[]{:S(2)}) %all-to-all-start) | async-done | bytes 262176 | tf_op jit(solution)/shard_map/all_to_all | solution.py:574
  30.8 6.8 %project.1 = (f32[2048,128]{1,0:T(8,128)}, bf16[256,1024]{1,0:T(8,128)(2,1)}, bf16[256,1024]{1,0:T(8,128)(2,1)}, bf16[256,1024]{1,0:T(8,128)(2,1)}, bf16[256,1024]{1,0:T(8,128)(2,1)}) custom-call(s32[4]{0:T(128)S(1)} %iota_xor_fusion.index_ref, bf16[8,128,128]{2,1,0:T(8,128)(2,1)S(1)} %all-to-all-done.message_ref, ...), custom_call_target="tpu_custom_call" | custom-call | bytes 24500000 | tf_op jit(solution)/shard_map/project/pallas_call | solution.py:489
  37.7 1.6 %collective-permute-start.5 = (bf16[256,1024]{1,0:T(8,128)(2,1)}, bf16[256,1024]{1,0:T(8,128)(2,1)S(1)}, u32[]{:S(2)}, u32[]{:S(2)}) collective-permute-start(bf16[256,1024]{1,0:T(8,128)(2,1)} %get-tuple-element.58), channel_id=1, source_target_pairs={{0,1},{1,0},{2,3},{3,2},{4,5},{5,4},{6,7},{7,6},{8,9},{9,8},{10,11... | collective-permute-start | bytes 1572872 | tf_op jit(solution)/shard_map/ppermute | solution.py:512
  39.2 1.5 %collective-permute-start.6 = (bf16[256,1024]{1,0:T(8,128)(2,1)}, bf16[256,1024]{1,0:T(8,128)(2,1)}, u32[]{:S(2)}, u32[]{:S(2)}) collective-permute-start(bf16[256,1024]{1,0:T(8,128)(2,1)} %get-tuple-element.59), channel_id=1, source_target_pairs={{0,2},{1,3},{2,0},{3,1},{4,6},{5,7},{6,4},{7,5},{8,10},{9,11},{10,... | collective-permute-start | bytes 1572872 | tf_op jit(solution)/shard_map/ppermute | solution.py:512
  40.7 0.5 collective-permute-start.7
  41.2 0.0 collective-permute-done.2.refs_1_.refs_0_
  41.2 0.0 copy-start.1
  41.2 0.0 collective-permute-done.3.refs_2_.refs_1_
  41.2 0.9 %copy-done.1 = bf16[256,1024]{1,0:T(8,128)(2,1)} copy-done((bf16[256,1024]{1,0:T(8,128)(2,1)}, bf16[256,1024]{1,0:T(8,128)(2,1)S(1)}, u32[]{:S(2)}) %copy-start.1) | copy-done | bytes 524312
  42.1 8.4 %back_last.1 = (f32[2048,128]{1,0:T(8,128)}, f32[2048,128]{1,0:T(8,128)S(1)}, bf16[8,128,128]{2,1,0:T(8,128)(2,1)}, f32[4,48,128]{2,1,0:T(8,128)S(1)}) custom-call(s32[4]{0:T(128)S(1)} %iota_xor_fusion.index_ref, s32[1]{0:T(128)} %bitcast.position_ref, f32[1024,256]{1,0:T(8,128)S(1)} %middle.1._.base_ref, f32[128,128]{1,0:T(8,128)S(1)} %get-tuple-element.42.decay_ref, ...), custom_call_target="tpu_custom_call" | custom-call | bytes 24500000 | tf_op jit(solution)/shard_map/back_last/pallas_call | solution.py:489
  50.5 3.9 %all-to-all-start.1 = ((bf16[8,128,128]{2,1,0:T(8,128)(2,1)}), bf16[8,128,128]{2,1,0:T(8,128)(2,1)S(1)}, u32[]{:S(2)}, u32[]{:S(2)}) async-start(bf16[8,128,128]{2,1,0:T(8,128)(2,1)} %get-tuple-element.51), calls=%async_computation.1 | async-start | bytes 524288 | tf_op jit(solution)/shard_map/all_to_all | solution.py:646
  54.4 1.3 %collective-permute-start.4 = (f32[4,48,128]{2,1,0:T(8,128)S(1)}, f32[4,48,128]{2,1,0:T(8,128)S(1)}, u32[]{:S(2)}, u32[]{:S(2)}) collective-permute-start(f32[4,48,128]{2,1,0:T(8,128)S(1)} %get-tuple-element.56), channel_id=1, source_target_pairs={{4,0},{8,4},{12,8},{16,12},{20,16},{24,20},{28,24},{5,1},{9,5},{13... | collective-permute-start | bytes 294920 | tf_op jit(solution)/shard_map/ppermute | solution.py:507
  55.7 4.0 %back_local.1 = (f32[2048,128]{1,0:T(8,128)S(1)}, bf16[256,1024]{1,0:T(8,128)(2,1)}) custom-call(f32[2048,128]{1,0:T(8,128)S(1)} %get-tuple-element.52.signal_ref, f32[128,128]{1,0:T(8,128)S(1)} %get-tuple-element.42.decay_ref, f32[128,128]{1,0:T(8,128)S(1)} %get-tuple-element.47.scale_ref, f32[168,128]{1,0:T(8,128)S(1)} %get-tuple-element.53.taps_ref, ...), custom_call_target="tpu_custom_call" | custom-call | bytes 15750000 | tf_op jit(solution)/shard_map/back_local/pallas_call | solution.py:489
  59.7 0.0 collective-permute-done.4.ahead_ref
  59.7 4.4 %all-to-all-done.1.message_ref = bf16[8,128,128]{2,1,0:T(8,128)(2,1)S(1)} async-done(((bf16[8,128,128]{2,1,0:T(8,128)(2,1)}), bf16[8,128,128]{2,1,0:T(8,128)(2,1)S(1)}, u32[]{:S(2)}, u32[]{:S(2)}) %all-to-all-start.1) | async-done | bytes 262176 | tf_op jit(solution)/shard_map/all_to_all | solution.py:646
  64.1 0.0 collective-permute-done.5.refs_1_
  64.1 0.0 copy-start.2
  64.1 0.1 collective-permute-done.6.refs_2_
  64.2 0.0 collective-permute-done.7.refs_3_
  64.2 0.7 %copy-done.2 = bf16[256,1024]{1,0:T(8,128)(2,1)} copy-done((bf16[256,1024]{1,0:T(8,128)(2,1)}, bf16[256,1024]{1,0:T(8,128)(2,1)S(1)}, u32[]{:S(2)}) %copy-start.2) | copy-done | bytes 524312
  64.9 5.3 %finish.1 = (bf16[256,1024]{1,0:T(8,128)(2,1)}, bf16[256,1024]{1,0:T(8,128)(2,1)}, bf16[256,1024]{1,0:T(8,128)(2,1)}, bf16[256,1024]{1,0:T(8,128)(2,1)}) custom-call(bf16[8,128,128]{2,1,0:T(8,128)(2,1)S(1)} %all-to-all-done.1.message_ref, f32[2048,128]{1,0:T(8,128)S(1)} %get-tuple-element.55.local_ref, ...), custom_call_target="tpu_custom_call", output_to_operand_aliasing={{0}: (13, {})} | custom-call | bytes 17500000 | tf_op jit(solution)/shard_map/finish/pallas_call | solution.py:489
  (1 shorter events, 0.0 us)
Async XLA Ops:
  2.1 6.3 %collective-permute-start.1 = (bf16[48,1024]{1,0:T(8,128)(2,1)S(1)}, bf16[48,1024]{1,0:T(8,128)(2,1)S(1)}, u32[]{:S(2)}, u32[]{:S(2)}) collective-permute-start(bf16[48,1024]{1,0:T(8,128)(2,1)S(1)} %get-tuple-element.41), channel_id=1, source_target_pairs={{0,4},{4,8},{8,12},{12,16},{16,20},{20,24},{24,28},{1,5},{5,9},{9,... | collective-permute-start | bytes 294920 | tf_op jit(solution)/shard_map/ppermute | solution.py:507
  4.5 19.0 %collective-permute-start = (bf16[256,1024]{1,0:T(8,128)(2,1)}, bf16[256,1024]{1,0:T(8,128)(2,1)S(1)}, u32[]{:S(2)}, u32[]{:S(2)}) collective-permute-start(bf16[256,1024]{1,0:T(8,128)(2,1)} %grad_in_ref), channel_id=1, source_target_pairs={{0,1},{1,0},{2,3},{3,2},{4,5},{5,4},{6,7},{7,6},{8,9},{9,8},{10,11... | collective-permute-start | bytes 1572872 | tf_op jit(solution)/shard_map/ppermute | solution.py:512
  6.9 34.3 %collective-permute-start.2 = (bf16[256,1024]{1,0:T(8,128)(2,1)}, bf16[256,1024]{1,0:T(8,128)(2,1)S(1)}, u32[]{:S(2)}, u32[]{:S(2)}) collective-permute-start(bf16[256,1024]{1,0:T(8,128)(2,1)} %grad_in_ref), channel_id=1, source_target_pairs={{0,2},{1,3},{2,0},{3,1},{4,6},{5,7},{6,4},{7,5},{8,10},{9,11},{10,... | collective-permute-start | bytes 1572872 | tf_op jit(solution)/shard_map/ppermute | solution.py:512
  15.1 15.7 %all-to-all-start = ((bf16[8,128,128]{2,1,0:T(8,128)(2,1)}), bf16[8,128,128]{2,1,0:T(8,128)(2,1)S(1)}, u32[]{:S(2)}, u32[]{:S(2)}) async-start(bf16[8,128,128]{2,1,0:T(8,128)(2,1)} %get-tuple-element.46), calls=%async_computation | async-start | bytes 524288 | tf_op jit(solution)/shard_map/all_to_all | solution.py:574
  21.1 20.2 %collective-permute-start.3 = (bf16[256,1024]{1,0:T(8,128)(2,1)}, bf16[256,1024]{1,0:T(8,128)(2,1)}, u32[]{:S(2)}, u32[]{:S(2)}) collective-permute-start(bf16[256,1024]{1,0:T(8,128)(2,1)} %get-tuple-element.50), channel_id=1, source_target_pairs={{0,3},{1,2},{2,1},{3,0},{4,7},{5,6},{6,5},{7,4},{8,11},{9,10},{10,... | collective-permute-start | bytes 1572872 | tf_op jit(solution)/shard_map/ppermute | solution.py:512
  23.5 0.8 %copy-start = (bf16[256,1024]{1,0:T(8,128)(2,1)}, bf16[256,1024]{1,0:T(8,128)(2,1)S(1)}, u32[]{:S(2)}) copy-start(bf16[256,1024]{1,0:T(8,128)(2,1)S(1)} %collective-permute-done.refs_1_.refs_0_) | copy-start | bytes 1572868
  37.7 26.5 %collective-permute-start.5 = (bf16[256,1024]{1,0:T(8,128)(2,1)}, bf16[256,1024]{1,0:T(8,128)(2,1)S(1)}, u32[]{:S(2)}, u32[]{:S(2)}) collective-permute-start(bf16[256,1024]{1,0:T(8,128)(2,1)} %get-tuple-element.58), channel_id=1, source_target_pairs={{0,1},{1,0},{2,3},{3,2},{4,5},{5,4},{6,7},{7,6},{8,9},{9,8},{10,11... | collective-permute-start | bytes 1572872 | tf_op jit(solution)/shard_map/ppermute | solution.py:512
  39.2 25.0 %collective-permute-start.6 = (bf16[256,1024]{1,0:T(8,128)(2,1)}, bf16[256,1024]{1,0:T(8,128)(2,1)}, u32[]{:S(2)}, u32[]{:S(2)}) collective-permute-start(bf16[256,1024]{1,0:T(8,128)(2,1)} %get-tuple-element.59), channel_id=1, source_target_pairs={{0,2},{1,3},{2,0},{3,1},{4,6},{5,7},{6,4},{7,5},{8,10},{9,11},{10,... | collective-permute-start | bytes 1572872 | tf_op jit(solution)/shard_map/ppermute | solution.py:512
  40.7 23.5 %collective-permute-start.7 = (bf16[256,1024]{1,0:T(8,128)(2,1)}, bf16[256,1024]{1,0:T(8,128)(2,1)}, u32[]{:S(2)}, u32[]{:S(2)}) collective-permute-start(bf16[256,1024]{1,0:T(8,128)(2,1)} %get-tuple-element.60), channel_id=1, source_target_pairs={{0,3},{1,2},{2,1},{3,0},{4,7},{5,6},{6,5},{7,4},{8,11},{9,10},{10,... | collective-permute-start | bytes 1572872 | tf_op jit(solution)/shard_map/ppermute | solution.py:512
  41.2 0.9 %copy-start.1 = (bf16[256,1024]{1,0:T(8,128)(2,1)}, bf16[256,1024]{1,0:T(8,128)(2,1)S(1)}, u32[]{:S(2)}) copy-start(bf16[256,1024]{1,0:T(8,128)(2,1)S(1)} %collective-permute-done.2.refs_1_.refs_0_) | copy-start | bytes 1572868
  50.5 13.6 %all-to-all-start.1 = ((bf16[8,128,128]{2,1,0:T(8,128)(2,1)}), bf16[8,128,128]{2,1,0:T(8,128)(2,1)S(1)}, u32[]{:S(2)}, u32[]{:S(2)}) async-start(bf16[8,128,128]{2,1,0:T(8,128)(2,1)} %get-tuple-element.51), calls=%async_computation.1 | async-start | bytes 524288 | tf_op jit(solution)/shard_map/all_to_all | solution.py:646
  54.4 5.3 %collective-permute-start.4 = (f32[4,48,128]{2,1,0:T(8,128)S(1)}, f32[4,48,128]{2,1,0:T(8,128)S(1)}, u32[]{:S(2)}, u32[]{:S(2)}) collective-permute-start(f32[4,48,128]{2,1,0:T(8,128)S(1)} %get-tuple-element.56), channel_id=1, source_target_pairs={{4,0},{8,4},{12,8},{16,12},{20,16},{24,20},{28,24},{5,1},{9,5},{13... | collective-permute-start | bytes 294920 | tf_op jit(solution)/shard_map/ppermute | solution.py:507
  64.1 0.8 %copy-start.2 = (bf16[256,1024]{1,0:T(8,128)(2,1)}, bf16[256,1024]{1,0:T(8,128)(2,1)S(1)}, u32[]{:S(2)}) copy-start(bf16[256,1024]{1,0:T(8,128)(2,1)S(1)} %collective-permute-done.5.refs_1_) | copy-start | bytes 1572868

commit v10 on v9

--- a/solution.py
+++ b/solution.py
@@ -94,25 +94,18 @@
     ]
 
 
-def write_messages(out_ref, states, decay_ref, position_ref, tokens, direction):
-    count = out_ref.shape[0]
-    out_ref[...] = jnp.zeros_like(out_ref)
-    fade = fades(decay_ref, float(tokens))
-    for gap in range(count - 1):
-        other = position_ref[0] + direction * (gap + 1)
-        value = jnp.concatenate(states, axis=0).astype(out_ref.dtype)
-
-        @pl.when((other >= 0) & (other < count))
-        def _():
-            out_ref[jnp.clip(other, 0, count - 1)] = value
-
-        states = [state * factor for state, factor in zip(states, fade)]
-
-
-def read_messages(in_ref):
-    total = in_ref[0].astype(F32)
-    for other in range(1, in_ref.shape[0]):
-        total = total + in_ref[other].astype(F32)
+def write_state(out_ref, states):
+    out_ref[...] = jnp.concatenate(states, axis=0)
+
+
+def comes_first(position, direction):
+    return (position % 2 == 0) == (direction > 0)
+
+
+def incoming(position_ref, partner_ref, message_refs, decay_ref, tokens, direction):
+    total = tree_sum([ref[...].astype(F32) for ref in message_refs])
+    faded = total * jnp.exp(-decay_ref[...] * float(tokens)) + partner_ref[...]
+    total = jnp.where(comes_first(position_ref[0], direction), total, faded)
     return [total[mode_rows(n)] for n in range(total.shape[0] // SUB)]
 
 
@@ -149,8 +142,8 @@
 
 
 def featurize_kernel(
-    position_ref, streams_ref, taps_in_ref, residue_ref, decay_in_ref, halo_ref, grad_in_ref,
-    qf_ref, kf_ref, vf_ref, local_ref, grad_copy_ref, message_ref, taps_ref, scale_ref, decay_ref,
+    streams_ref, taps_in_ref, residue_ref, decay_in_ref, halo_ref, grad_in_ref,
+    qf_ref, kf_ref, vf_ref, local_ref, grad_copy_ref, state_ref, taps_ref, scale_ref, decay_ref,
     wide_ref, feat_ref, grad_vmem, sems,
 ):
     grad_in = pltpu.make_async_copy(grad_in_ref, grad_vmem, sems.at[4])
@@ -198,7 +191,7 @@
     local_vmem = wide_ref.at[0, pl.ds(0, tokens * SUB), :]
     states = local_conv(feat_ref.at[3], decay_ref, scale_ref, local_vmem, False)
     copies += start_all([pltpu.make_async_copy(local_vmem, local_ref, sems.at[4])])
-    write_messages(message_ref, states, decay_ref, position_ref, tokens, 1)
+    write_state(state_ref, states)
     wait_all(copies)
 
 
@@ -244,10 +237,12 @@
 
 
 def project_kernel(
-    index_ref, message_ref, decay_ref, scale_ref, _, qf_ref, local_ref, weight_ref, *refs
+    index_ref, position_ref, decay_ref, scale_ref, qf_ref, local_ref, weight_ref, partner_ref, *refs
 ):
     rows_ref, feat_ref, local_vmem, gated_ref, held_ref, sent_ref, sems, out_sems = refs[-8:]
-    conv_ref, *out_refs = refs[-9 - sent_ref.shape[0] : -8]
+    outputs = 1 + sent_ref.shape[0]
+    message_refs = refs[: -8 - outputs]
+    conv_ref, *out_refs = refs[-8 - outputs : -8]
     parts, tokens, width = sent_ref.shape
     order = list(reversed(range(parts)))
     copies = [
@@ -266,7 +261,8 @@
     feat_copy = pltpu.make_async_copy(qf_ref, feat_ref, sems.at[parts])
     start_all([local_copy, feat_copy])
     start_all([copies[part] for part in order])
-    carried(rows_ref, read_messages(message_ref), decay_ref, scale_ref, False)
+    states = incoming(position_ref, partner_ref, message_refs, decay_ref, tokens, 1)
+    carried(rows_ref, states, decay_ref, scale_ref, False)
     local_copy.wait()
     rows_ref[...] += local_vmem[...]
     conv_copy = pltpu.make_async_copy(rows_ref, conv_ref, sems.at[parts + 1])
@@ -286,13 +282,13 @@
     wait_all(outs)
 
 
-def start_weights(index_ref, first, weight_ref, held_ref, sems):
+def start_weights(index_ref, weight_ref, held_ref, sems):
     count, _, width = held_ref.shape
     return start_all(
         [
             pltpu.make_async_copy(
                 weight_ref.at[
-                    :, pl.ds(pl.multiple_of(index_ref[first + number] * width, width), width)
+                    :, pl.ds(pl.multiple_of(index_ref[number] * width, width), width)
                 ],
                 held_ref.at[number],
                 sems.at[number],
@@ -302,50 +298,31 @@
     )
 
 
-def back_products(weights, piece_refs, turned_ref, held_ref, total_ref, before_ref):
+def back_products(weights, piece_refs, turned_ref, held_ref, total_ref):
     for number, ref in enumerate(piece_refs):
         turned_ref[number] = ref[...].T
     for number in range(len(piece_refs)):
         weights[number].wait()
         product = jnp.dot(held_ref[number], turned_ref[number], preferred_element_type=F32)
-        earlier = before_ref if number == 0 else total_ref
-        total_ref[...] = product if earlier is None else earlier[...] + product
-
-
-def middle_kernel(index_ref, weight_ref, *refs):
-    *piece_refs, total_ref, piece_vmem, turned_ref, held_ref, sems, piece_sems = refs
+        total_ref[...] = product if number == 0 else total_ref[...] + product
+
+
+def back_last_kernel(
+    index_ref, decay_ref, weight_ref, qf_ref, kf_ref, vf_ref, conv_ref, *refs, rim
+):
+    (
+        *piece_refs, back_query_ref, mixed_ref, state_ref, ahead_ref, piece_vmem,
+        turned_ref, total_ref, rows_ref, feat_ref, conv_vmem, held_ref, sems, piece_sems, own_sems,
+    ) = refs
     pieces = start_all(
         [
             pltpu.make_async_copy(ref, piece_vmem.at[number], piece_sems.at[number])
             for number, ref in enumerate(piece_refs)
         ]
     )
-    weights = start_weights(index_ref, 0, weight_ref, held_ref, sems)
-    wait_all(pieces)
-    held = [piece_vmem.at[number] for number in range(len(piece_refs))]
-    back_products(weights, held, turned_ref, held_ref, total_ref, None)
-
-
-def back_last_kernel(
-    index_ref, position_ref, base_ref, decay_ref, weight_ref, qf_ref, kf_ref, vf_ref, conv_ref,
-    *refs, rim,
-):
-    (
-        *piece_refs, back_query_ref, mixed_ref, message_ref, ahead_ref, piece_vmem,
-        turned_ref, total_ref, rows_ref, feat_ref, conv_vmem, held_ref, sems, piece_sems, own_sems,
-    ) = refs
-    piece_refs = piece_refs[-turned_ref.shape[0] :]
-    pieces = start_all(
-        [
-            pltpu.make_async_copy(ref, piece_vmem.at[number], piece_sems.at[number])
-            for number, ref in enumerate(piece_refs)
-        ]
-    )
     tokens = total_ref.shape[1]
     heads = pl.ds(0, rim * SUB)
-    weights = start_weights(
-        index_ref, index_ref.shape[0] - len(piece_refs), weight_ref, held_ref, sems
-    )
+    weights = start_weights(index_ref, weight_ref, held_ref, sems)
     copies = start_all(
         [
             pltpu.make_async_copy(qf_ref, feat_ref, own_sems.at[0]),
@@ -356,7 +333,7 @@
     )
     wait_all(pieces)
     held = [piece_vmem.at[number] for number in range(len(piece_refs))]
-    back_products(weights, held, turned_ref, held_ref, total_ref, base_ref)
+    back_products(weights, held, turned_ref, held_ref, total_ref)
     scatter_tokens(rows_ref, total_ref[...].T, 0)
     wait_all(copies)
     mixed_ref[...] = round16(rows_ref[...] * feat_ref[...])
@@ -369,7 +346,7 @@
     states = advance_states(
         mixed_ref, fades(decay_ref, 1.0), zero_states(modes), 0, tokens, True
     )
-    write_messages(message_ref, states, decay_ref, position_ref, tokens, -1)
+    write_state(state_ref, states)
     out.wait()
 
 
@@ -406,14 +383,15 @@
 
 
 def finish_kernel(
-    message_ref, local_ref, decay_ref, scale_ref, taps_ref, ahead_ref, query_ref, kf_ref, vf_ref,
-    *refs, taps,
+    position_ref, local_ref, decay_ref, scale_ref, taps_ref, ahead_ref, query_ref, kf_ref, vf_ref,
+    *refs, taps, pairs,
 ):
+    partner_ref, *message_refs = refs[:pairs]
     (
         *part_refs, _, gq_ref, gk_ref, gv_ref, projected_ref,
         total_ref, feat_ref, query_vmem, wide_ref, rows_ref, tail_ref, out_vmem, parts_vmem,
         sems, part_sems,
-    ) = refs
+    ) = refs[pairs:]
     tokens = gk_ref.shape[0]
     tail = tail_ref.shape[0]
     rim = taps - 1
@@ -435,7 +413,7 @@
             for number, ref in enumerate(part_refs)
         ]
     )
-    states = read_messages(message_ref)
+    states = incoming(position_ref, partner_ref, message_refs, decay_ref, tokens, -1)
     carried(total_ref, states, decay_ref, scale_ref, True, local_ref)
     growth = fades(decay_ref, -1.0)
     scales = scales_of(scale_ref)
@@ -512,6 +490,19 @@
     return lax.ppermute(value, axis, [(s, s ^ mask) for s in range(count)])
 
 
+def exchange_states(state, decays, tokens, direction):
+    blocks = lax.axis_size("ctx")
+    first = comes_first(lax.axis_index("ctx"), direction)
+    partner = exchange(state, "ctx", 1)
+    lead, follow = jnp.where(first, state, partner), jnp.where(first, partner, state)
+    total = lead * jnp.exp(-decays * float(tokens)) + follow
+    messages = []
+    for pair in range(1, blocks // 2):
+        faded = total * jnp.exp(-decays * float(2 * tokens * (pair - 1)))
+        messages.append(shift(faded.astype(BF16), "ctx", direction * 2 * pair))
+    return [partner] + messages
+
+
 def shards(query_in, key_in, value_in, short_taps, residues, decays, out_weight, out_grad):
     tokens, channels = query_in.shape
     taps = short_taps.shape[0]
@@ -522,7 +513,6 @@
     position = lax.axis_index("ctx")[None].astype(jnp.int32)
     tile_shape = (tokens * SUB, LANES)
     mode_shape = (modes * SUB, LANES)
-    message_shape = (blocks,) + mode_shape
     streams = (query_in, key_in, value_in)
     rim_rows = 16
 
@@ -552,15 +542,15 @@
     wide_rows = (tokens + rim) * SUB
 
     (
-        query_feat, key_feat, value_feat, local, grad_copy, messages,
+        query_feat, key_feat, value_feat, local, grad_copy, state,
         tap_tiles, scale_tiles, decay_tiles,
     ) = call(
         featurize_kernel,
         [in_hbm(tile_shape, F32)] * 4
-        + [in_hbm((tokens, channels), BF16), (message_shape, BF16)]
+        + [in_hbm((tokens, channels), BF16), (mode_shape, F32)]
         + [((3 * taps * SUB, LANES), F32), (mode_shape, F32), (mode_shape, F32)],
-        (position, narrow, taps_vmem, residues_vmem, decays_vmem, halo, out_grad),
-        [IN_SMEM] + [IN_VMEM] * 5 + [IN_HBM],
+        (narrow, taps_vmem, residues_vmem, decays_vmem, halo, out_grad),
+        [IN_VMEM] * 5 + [IN_HBM],
         [
             pltpu.VMEM((3, wide_rows, LANES), F32),
             pltpu.VMEM((4,) + tile_shape, F32),
@@ -571,7 +561,7 @@
     )
     if fans == 4:
         pieces.append(exchange(grad_copy, "ch", fans - 1))
-    arrived = lax.all_to_all(messages, "ctx", split_axis=0, concat_axis=0, tiled=True)
+    arrived = exchange_states(state, decay_tiles, tokens, 1)
 
     def weight_scratch(count):
         return [
@@ -579,28 +569,14 @@
             pltpu.SemaphoreType.DMA((count,)),
         ]
 
-    early = fans // 2
-    (base,) = call(
-        middle_kernel,
-        [((channels, tokens), F32)],
-        (order, out_weight, *pieces[:early]),
-        [IN_SMEM] + [IN_HBM] * (1 + early),
-        [
-            pltpu.VMEM((early, tokens, channels), BF16),
-            pltpu.VMEM((early, channels, tokens), BF16),
-        ]
-        + weight_scratch(early)
-        + [pltpu.SemaphoreType.DMA((early,))],
-        "middle", 6.0, 11,
-    )
+    pairs = blocks // 2
     conv_out, *partial_sums = call(
         project_kernel,
         [in_hbm(tile_shape, F32)] + [in_hbm((tokens, channels), BF16)] * fans,
         (
-            order, arrived, decay_tiles, scale_tiles, base, query_feat, local, out_weight,
-            *pieces[1:early],
+            order, position, decay_tiles, scale_tiles, query_feat, local, out_weight, *arrived,
         ),
-        [IN_SMEM] + [IN_VMEM] * 4 + [IN_HBM] * (2 + early),
+        [IN_SMEM] * 2 + [IN_VMEM] * 2 + [IN_HBM] * 3 + [IN_VMEM] * pairs,
         [
             tile,
             tile,
@@ -622,34 +598,33 @@
             jnp.stack(partial_sums), "ch", split_axis=0, concat_axis=0, tiled=True
         )
         parts = [parts[number] for number in range(fans)]
-    back_query, grad_mixed, back_messages, ahead = call(
+    back_query, grad_mixed, back_state, ahead = call(
         functools.partial(back_last_kernel, rim=rim),
-        [in_hbm(tile_shape, F32), (tile_shape, F32), (message_shape, BF16)]
+        [in_hbm(tile_shape, F32), (tile_shape, F32), (mode_shape, F32)]
         + [((4, rim * SUB, LANES), F32)],
         (
-            order, position, base, decay_tiles, out_weight, query_feat, key_feat,
-            value_feat, conv_out, *pieces[1:early], *pieces[early:],
+            order, decay_tiles, out_weight, query_feat, key_feat, value_feat, conv_out, *pieces,
         ),
-        [IN_SMEM] * 2 + [IN_VMEM] * 2 + [IN_HBM] * (4 + fans),
-        [
-            pltpu.VMEM((fans - early, tokens, channels), BF16),
-            pltpu.VMEM((fans - early, channels, tokens), BF16),
+        [IN_SMEM, IN_VMEM] + [IN_HBM] * (5 + fans),
+        [
+            pltpu.VMEM((fans, tokens, channels), BF16),
+            pltpu.VMEM((fans, channels, tokens), BF16),
             pltpu.VMEM((channels, tokens), F32),
             tile,
             tile,
             tile,
         ]
-        + weight_scratch(fans - early)
-        + [pltpu.SemaphoreType.DMA((fans - early,)), pltpu.SemaphoreType.DMA((5,))],
-        "back_last", 7.0, 13,
-    )
-    back_arrived = lax.all_to_all(back_messages, "ctx", split_axis=0, concat_axis=0, tiled=True)
+        + weight_scratch(fans)
+        + [pltpu.SemaphoreType.DMA((fans,)), pltpu.SemaphoreType.DMA((5,))],
+        "back_last", 9.0, 20,
+    )
+    back_arrived = exchange_states(back_state, decay_tiles, tokens, -1)
     ahead = shift(ahead, "ctx", -1)
     back_local, grad_query = call(
         functools.partial(back_local_kernel, taps=taps),
         [(tile_shape, F32), in_hbm((tokens, channels), BF16)],
-        (grad_mixed, decay_tiles, scale_tiles, tap_tiles, back_query, *pieces[early:]),
-        [IN_VMEM] * 4 + [IN_HBM] * (1 + fans - early),
+        (grad_mixed, decay_tiles, scale_tiles, tap_tiles, back_query, *pieces[1:]),
+        [IN_VMEM] * 4 + [IN_HBM] * fans,
         [
             pltpu.VMEM((wide_rows, LANES), F32),
             tile,
@@ -660,13 +635,13 @@
     )
     tail = 16
     grad_query, grad_key, grad_value, projected = call(
-        functools.partial(finish_kernel, taps=taps),
+        functools.partial(finish_kernel, taps=taps, pairs=pairs),
         [in_hbm((tokens, channels), BF16)] * 4,
         (
-            back_arrived, back_local, decay_tiles, scale_tiles, tap_tiles, ahead, back_query,
-            key_feat, value_feat, *parts, grad_query,
+            position, back_local, decay_tiles, scale_tiles, tap_tiles, ahead, back_query,
+            key_feat, value_feat, *back_arrived, *parts, grad_query,
         ),
-        [IN_VMEM] * 6 + [IN_HBM] * (4 + fans),
+        [IN_SMEM] + [IN_VMEM] * 5 + [IN_HBM] * 3 + [IN_VMEM] * pairs + [IN_HBM] * (1 + fans),
         [
             tile,
             pltpu.VMEM((2,) + tile_shape, F32),
@@ -680,7 +655,7 @@
             pltpu.SemaphoreType.DMA((fans,)),
         ],
         "finish", 5.0, 12,
-        {9 + fans: 0},
+        {9 + pairs + fans: 0},
     )
     return (projected, grad_query, grad_key, grad_value)
 

time: 70.6 us -> 81.6 us (1.16)
  waiting for transfers between devices: 5.8 us -> 16.1 us
  starting transfers between devices: 23.4 us -> 28.3 us
  Pallas kernels: 38 us -> 35.2 us
  local copies, waits for them, and re-layouts: 2.37 us -> 0.79 us
    ppermute x2 -> x8, starting transfers between devices: 3.64 us -> 17.3 us  [shift(): return lax.ppermute(value, axis, pairs)]
    ppermute x2 -> x8, waiting for transfers between devices: 0.01 us -> 12.8 us  [shift(): return lax.ppermute(value, axis, pairs)]
    all_to_all x2 -> x0, starting transfers between devices: 9.85 us -> none  [the longest x1 5.99 us: shards(): lax.all_to_all(messages, 'ctx', split_axis=0, concat_axis=0, tiled=True)]
    all_to_all x2 -> x0, waiting for transfers between devices: 5.72 us -> none  [the longest x1 4.43 us: shards(): lax.all_to_all(back_messages, 'ctx', split_axis=0, concat_axis=0, tiled=T...]
    ppermute x6 -> x8, waiting for transfers between devices: 0.08 us -> 3.31 us  [exchange(): return lax.ppermute(value, axis, [(s, s ^ mask) for s in range(count)])]
    pallas_call x7 -> x6, Pallas kernels: 38 us -> 35.2 us  [call(): pl.pallas_call(kernel, out_shape=[jax.ShapeDtypeStruct(*out) if own else...]
    unnamed x6, local copies, waits for them, and re-layouts: 2.37 us -> 0.79 us
    ppermute x6 -> x8, starting transfers between devices: 9.91 us -> 11 us  [exchange(): return lax.ppermute(value, axis, [(s, s ^ mask) for s in range(count)])]
  transfers between devices with their start and end apart: 10 -> 16, of which waited for: 3 -> 7; matrix products, arithmetic and copies ran while one was open for 0% -> 0% of each run, Pallas kernels for 44% -> 35%
where the time goes in v10:
time: 81.6 us; the launch traced here: 81.3 us
  Pallas kernels  35.2 us (43%)
  starting transfers between devices  28.3 us (35%)
  waiting for transfers between devices  16.1 us (20%)
    pallas_call x6, Pallas kernels, call(): pl.pallas_call(kernel, out_shape=[jax.ShapeDtypeStruct(*out) if own else...  35.2 us
    ppermute x8, starting transfers between devices, shift(): return lax.ppermute(value, axis, pairs)  17.3 us
    ppermute x8, waiting for transfers between devices, shift(): return lax.ppermute(value, axis, pairs)  12.8 us
    ppermute x8, starting transfers between devices, exchange(): return lax.ppermute(value, axis, [(s, s ^ mask) for s in range(count)])  11 us
    ppermute x8, waiting for transfers between devices, exchange(): return lax.ppermute(value, axis, [(s, s ^ mask) for s in range(count)])  3.31 us
  transfers between devices with their start and end apart: 16, of which 7 were waited for; matrix products, arithmetic and copies ran while one was open for 0% of the time, Pallas kernels for 35%

profile of v10, /device:TPU:0, one launch (start us, length us, event | category | flops | bytes accessed | tf_op | source)
XLA Modules:
  0.0 81.3 jit_solution(10417156249076722228)
XLA Ops:
  0.6 1.5 %rim.1 = (bf16[48,1024]{1,0:T(8,128)(2,1)S(1)}, bf16[3,256,1024]{2,1,0:T(8,128)(2,1)S(1)}, f32[3,7,1024]{2,1,0:T(8,128)S(1)}, f32[16,1024]{1,0:T(8,128)S(1)}, f32[16,1024]{1,0:T(8,128)S(1)}) custom-call(bf16[256,1024]{1,0:T(8,128)(2,1)} %q_ref.1, bf16[256,1024]{1,0:T(8,128)(2,1)} %k_ref.1, bf16[256,1024]{1,0:T(8,128)(2,1)} %v_ref.1, f32[3,7,1024]{2,1,0:T(8,128)} %bitcast.4, ...), custom_call_target="tpu_custom_call" | custom-call | bytes 4200000 | tf_op jit(solution)/shard_map/rim/pallas_call | solution.py:467
  2.1 2.4 %collective-permute-start = (bf16[48,1024]{1,0:T(8,128)(2,1)S(1)}, bf16[48,1024]{1,0:T(8,128)(2,1)S(1)}, u32[]{:S(2)}, u32[]{:S(2)}) collective-permute-start(bf16[48,1024]{1,0:T(8,128)(2,1)S(1)} %get-tuple-element.40), channel_id=1, source_target_pairs={{0,4},{4,8},{8,12},{12,16},{16,20},{20,24},{24,28},{1,5},{5,9},{9,... | collective-permute-start | bytes 294920 | tf_op jit(solution)/shard_map/ppermute | solution.py:485
  4.5 2.4 %collective-permute-start.6 = (bf16[256,1024]{1,0:T(8,128)(2,1)}, bf16[256,1024]{1,0:T(8,128)(2,1)S(1)}, u32[]{:S(2)}, u32[]{:S(2)}) collective-permute-start(bf16[256,1024]{1,0:T(8,128)(2,1)} %refs_0_), channel_id=1, source_target_pairs={{0,2},{1,3},{2,0},{3,1},{4,6},{5,7},{6,4},{7,5},{8,10},{9,11},{10,... | collective-permute-start | bytes 1572872 | tf_op jit(solution)/shard_map/ppermute | solution.py:490
  6.9 0.0 collective-permute-done.halo_ref
  6.9 5.8 %featurize.1 = (f32[2048,128]{1,0:T(8,128)}, f32[2048,128]{1,0:T(8,128)}, f32[2048,128]{1,0:T(8,128)}, f32[2048,128]{1,0:T(8,128)}, bf16[256,1024]{1,0:T(8,128)(...) custom-call(bf16[3,256,1024]{2,1,0:T(8,128)(2,1)S(1)} %get-tuple-elemen, ...), custom_call_target="tpu_custom_call" | custom-call | bytes 21000000 | tf_op jit(solution)/shard_map/featurize/pallas_call | solution.py:467
  12.8 1.9 %collective-permute-start.1 = (f32[128,128]{1,0:T(8,128)S(1)}, f32[128,128]{1,0:T(8,128)S(1)}, u32[]{:S(2)}, u32[]{:S(2)}) collective-permute-start(f32[128,128]{1,0:T(8,128)S(1)} %get-tuple-element.48), channel_id=1, source_target_pairs={{0,4},{4,0},{8,12},{12,8},{16,20},{20,16},{24,28},{28,24},{1,5},{5... | collective-permute-start | bytes 196616 | tf_op jit(solution)/shard_map/ppermute | solution.py:490
  14.7 1.5 %collective-permute-start.5 = (bf16[256,1024]{1,0:T(8,128)(2,1)}, bf16[256,1024]{1,0:T(8,128)(2,1)S(1)}, u32[]{:S(2)}, u32[]{:S(2)}) collective-permute-start(bf16[256,1024]{1,0:T(8,128)(2,1)} %refs_0_), channel_id=1, source_target_pairs={{0,1},{1,0},{2,3},{3,2},{4,5},{5,4},{6,7},{7,6},{8,9},{9,8},{10,11... | collective-permute-start | bytes 1572872 | tf_op jit(solution)/shard_map/ppermute | solution.py:490
  16.2 1.5 %collective-permute-start.7 = (bf16[256,1024]{1,0:T(8,128)(2,1)}, bf16[256,1024]{1,0:T(8,128)(2,1)S(1)}, u32[]{:S(2)}, u32[]{:S(2)}) collective-permute-start(bf16[256,1024]{1,0:T(8,128)(2,1)} %get-tuple-element.50), channel_id=1, source_target_pairs={{0,3},{1,2},{2,1},{3,0},{4,7},{5,6},{6,5},{7,4},{8,11},{9,10},{10,... | collective-permute-start | bytes 1572872 | tf_op jit(solution)/shard_map/ppermute | solution.py:490
  17.7 0.0 collective-permute-done.1.partner_ref
  17.7 0.1 multiply_convert_fusion.3
  17.8 6.3 %collective-permute-start.4 = (bf16[128,128]{1,0:T(8,128)(2,1)S(1)}, bf16[128,128]{1,0:T(8,128)(2,1)S(1)}, u32[]{:S(2)}, u32[]{:S(2)}) collective-permute-start(bf16[128,128]{1,0:T(8,128)(2,1)S(1)} %get-tuple-element.69), channel_id=1, source_target_pairs={{0,24},{4,28},{1,25},{5,29},{2,26},{6,30},{3,27},{7,31}} | collective-permute-start | bytes 98312 | tf_op jit(solution)/shard_map/ppermute | solution.py:485
  24.1 1.3 %collective-permute-start.3 = (bf16[128,128]{1,0:T(8,128)(2,1)S(1)}, bf16[128,128]{1,0:T(8,128)(2,1)S(1)}, u32[]{:S(2)}, u32[]{:S(2)}) collective-permute-start(bf16[128,128]{1,0:T(8,128)(2,1)S(1)} %get-tuple-element.70), channel_id=1, source_target_pairs={{0,16},{4,20},{8,24},{12,28},{1,17},{5,21},{9,25},{13,29},{2,18},{... | collective-permute-start | bytes 98312 | tf_op jit(solution)/shard_map/ppermute | solution.py:485
  25.4 0.3 collective-permute-done.4.refs_2_
  25.7 2.2 %collective-permute-start.2 = (bf16[128,128]{1,0:T(8,128)(2,1)S(1)}, bf16[128,128]{1,0:T(8,128)(2,1)S(1)}, u32[]{:S(2)}, u32[]{:S(2)}) collective-permute-start(bf16[128,128]{1,0:T(8,128)(2,1)S(1)} %get-tuple-element.71), channel_id=1, source_target_pairs={{0,8},{4,12},{8,16},{12,20},{16,24},{20,28},{1,9},{5,13},{9,17},{1... | collective-permute-start | bytes 98312 | tf_op jit(solution)/shard_map/ppermute | solution.py:485
  27.9 0.0 collective-permute-done.3.refs_1_
  27.9 1.6 %collective-permute-done.2.refs_0_ = bf16[128,128]{1,0:T(8,128)(2,1)S(1)} collective-permute-done((bf16[128,128]{1,0:T(8,128)(2,1)S(1)}, bf16[128,128]{1,0:T(8,128)(2,1)S(1)}, u32[]{:S(2)}, u32[]{:S(2)}) %collective-permute-start.2) | collective-permute-done | bytes 32800 | tf_op jit(solution)/shard_map/ppermute | solution.py:485
  29.4 6.8 %project.1 = (f32[2048,128]{1,0:T(8,128)}, bf16[256,1024]{1,0:T(8,128)(2,1)}, bf16[256,1024]{1,0:T(8,128)(2,1)}, bf16[256,1024]{1,0:T(8,128)(2,1)}, bf16[256,1024]{1,0:T(8,128)(2,1)}) custom-call(s32[4]{0:T(128)S(1)} %iota_xor_fusion.index_ref, s32[1]{0:T(128)} %bitcast.position_ref, f32[128,128]{1,0:T(8,128)S(1)} %get-tuple-element.42.decay_ref, ...), custom_call_target="tpu_custom_call" | custom-call | bytes 24500000 | tf_op jit(solution)/shard_map/project/pallas_call | solution.py:467
  36.3 1.6 %collective-permute-start.13 = (bf16[256,1024]{1,0:T(8,128)(2,1)}, bf16[256,1024]{1,0:T(8,128)(2,1)}, u32[]{:S(2)}, u32[]{:S(2)}) collective-permute-start(bf16[256,1024]{1,0:T(8,128)(2,1)} %get-tuple-element.58), channel_id=1, source_target_pairs={{0,1},{1,0},{2,3},{3,2},{4,5},{5,4},{6,7},{7,6},{8,9},{9,8},{10,11... | collective-permute-start | bytes 1572872 | tf_op jit(solution)/shard_map/ppermute | solution.py:490
  37.8 0.5 collective-permute-start.14
  38.3 0.0 collective-permute-done.6.refs_2_.refs_1_
  38.3 0.0 copy-start
  38.4 1.5 %collective-permute-start.15 = (bf16[256,1024]{1,0:T(8,128)(2,1)}, bf16[256,1024]{1,0:T(8,128)(2,1)}, u32[]{:S(2)}, u32[]{:S(2)}) collective-permute-start(bf16[256,1024]{1,0:T(8,128)(2,1)} %get-tuple-element.60), channel_id=1, source_target_pairs={{0,3},{1,2},{2,1},{3,0},{4,7},{5,6},{6,5},{7,4},{8,11},{9,10},{10,... | collective-permute-start | bytes 1572872 | tf_op jit(solution)/shard_map/ppermute | solution.py:490
  39.8 0.0 collective-permute-done.5.refs_1_.refs_0_
  39.8 0.0 copy-start.1
  39.8 2.1 %collective-permute-done.7.refs_3_.refs_2_ = bf16[256,1024]{1,0:T(8,128)(2,1)S(1)} collective-permute-done((bf16[256,1024]{1,0:T(8,128)(2,1)}, bf16[256,1024]{1,0:T(8,128)(2,1)S(1)}, u32[]{:S(2)}, u32[]{:S(2)}) %collective-permute-start.7) | collective-permute-done | bytes 524320 | tf_op jit(solution)/shard_map/ppermute | solution.py:490
  41.9 0.0 copy-start.2
  41.9 0.0 copy-done
  41.9 0.0 copy-done.1
  41.9 0.8 copy-done.2
  42.7 11.6 %back_last.1 = (f32[2048,128]{1,0:T(8,128)}, f32[2048,128]{1,0:T(8,128)S(1)}, f32[128,128]{1,0:T(8,128)S(1)}, f32[4,48,128]{2,1,0:T(8,128)S(1)}) custom-call(s32[4]{0:T(128)S(1)} %iota_xor_fusion.index_ref, f32[128,128]{1,0:T(8,128)S(1)} %get-tuple-element.42.decay_ref, bf16[1024,4096]{1,0:T(8,128)(2,1)} %weight_ref.3, ...), custom_call_target="tpu_custom_call" | custom-call | bytes 31500000 | tf_op jit(solution)/shard_map/back_last/pallas_call | solution.py:467
  54.3 0.1 collective-permute-start.9
  54.4 1.2 %collective-permute-done.9.refs_0_ = f32[128,128]{1,0:T(8,128)S(1)} collective-permute-done((f32[128,128]{1,0:T(8,128)S(1)}, f32[128,128]{1,0:T(8,128)S(1)}, u32[]{:S(2)}, u32[]{:S(2)}) %collective-permute-start.9) | collective-permute-done | bytes 65568 | tf_op jit(solution)/shard_map/ppermute | solution.py:490
  55.6 0.1 multiply_convert_fusion
  55.7 1.3 %collective-permute-start.12 = (bf16[128,128]{1,0:T(8,128)(2,1)S(1)}, bf16[128,128]{1,0:T(8,128)(2,1)S(1)}, u32[]{:S(2)}, u32[]{:S(2)}) collective-permute-start(bf16[128,128]{1,0:T(8,128)(2,1)S(1)} %get-tuple-element.66), channel_id=1, source_target_pairs={{24,0},{28,4},{25,1},{29,5},{26,2},{30,6},{27,3},{31,7}} | collective-permute-start | bytes 98312 | tf_op jit(solution)/shard_map/ppermute | solution.py:485
  57.0 1.3 %collective-permute-start.8 = (f32[4,48,128]{2,1,0:T(8,128)S(1)}, f32[4,48,128]{2,1,0:T(8,128)S(1)}, u32[]{:S(2)}, u32[]{:S(2)}) collective-permute-start(f32[4,48,128]{2,1,0:T(8,128)S(1)} %get-tuple-element.55), channel_id=1, source_target_pairs={{4,0},{8,4},{12,8},{16,12},{20,16},{24,20},{28,24},{5,1},{9,5},{13... | collective-permute-start | bytes 294920 | tf_op jit(solution)/shard_map/ppermute | solution.py:485
  58.3 5.0 %collective-permute-done.12.refs_3_ = bf16[128,128]{1,0:T(8,128)(2,1)S(1)} collective-permute-done((bf16[128,128]{1,0:T(8,128)(2,1)S(1)}, bf16[128,128]{1,0:T(8,128)(2,1)S(1)}, u32[]{:S(2)}, u32[]{:S(2)}) %collective-permute-start.12) | collective-permute-done | bytes 32800 | tf_op jit(solution)/shard_map/ppermute | solution.py:485
  63.3 1.3 %collective-permute-start.10 = (bf16[128,128]{1,0:T(8,128)(2,1)S(1)}, bf16[128,128]{1,0:T(8,128)(2,1)S(1)}, u32[]{:S(2)}, u32[]{:S(2)}) collective-permute-start(bf16[128,128]{1,0:T(8,128)(2,1)S(1)} %get-tuple-element.67), channel_id=1, source_target_pairs={{8,0},{12,4},{16,8},{20,12},{24,16},{28,20},{9,1},{13,5},{17,9},{2... | collective-permute-start | bytes 98312 | tf_op jit(solution)/shard_map/ppermute | solution.py:485
  64.6 4.5 %collective-permute-done.10.refs_1_ = bf16[128,128]{1,0:T(8,128)(2,1)S(1)} collective-permute-done((bf16[128,128]{1,0:T(8,128)(2,1)S(1)}, bf16[128,128]{1,0:T(8,128)(2,1)S(1)}, u32[]{:S(2)}, u32[]{:S(2)}) %collective-permute-start.10) | collective-permute-done | bytes 32800 | tf_op jit(solution)/shard_map/ppermute | solution.py:485
  69.1 1.3 %collective-permute-start.11 = (bf16[128,128]{1,0:T(8,128)(2,1)S(1)}, bf16[128,128]{1,0:T(8,128)(2,1)S(1)}, u32[]{:S(2)}, u32[]{:S(2)}) collective-permute-start(bf16[128,128]{1,0:T(8,128)(2,1)S(1)} %get-tuple-element.68), channel_id=1, source_target_pairs={{16,0},{20,4},{24,8},{28,12},{17,1},{21,5},{25,9},{29,13},{18,2},{... | collective-permute-start | bytes 98312 | tf_op jit(solution)/shard_map/ppermute | solution.py:485
  70.4 4.0 %back_local.1 = (f32[2048,128]{1,0:T(8,128)S(1)}, bf16[256,1024]{1,0:T(8,128)(2,1)}) custom-call(f32[2048,128]{1,0:T(8,128)S(1)} %get-tuple-element.51.signal_ref, f32[128,128]{1,0:T(8,128)S(1)} %get-tuple-element.42.decay_ref, f32[128,128]{1,0:T(8,128)S(1)} %get-tuple-element.46.scale_ref, f32[168,128]{1,0:T(8,128)S(1)} %get-tuple-element.52.taps_ref, ...), custom_call_target="tpu_custom_call" | custom-call | bytes 15750000 | tf_op jit(solution)/shard_map/back_local/pallas_call | solution.py:467
  74.4 1.4 %collective-permute-done.11.refs_2_ = bf16[128,128]{1,0:T(8,128)(2,1)S(1)} collective-permute-done((bf16[128,128]{1,0:T(8,128)(2,1)S(1)}, bf16[128,128]{1,0:T(8,128)(2,1)S(1)}, u32[]{:S(2)}, u32[]{:S(2)}) %collective-permute-start.11) | collective-permute-done | bytes 32800 | tf_op jit(solution)/shard_map/ppermute | solution.py:485
  75.8 0.0 collective-permute-done.8.ahead_ref
  75.8 0.0 collective-permute-done.13.refs_5_
  75.8 0.0 collective-permute-done.14.refs_6_
  75.8 0.0 collective-permute-done.15.refs_7_
  75.8 5.4 %finish.1 = (bf16[256,1024]{1,0:T(8,128)(2,1)}, bf16[256,1024]{1,0:T(8,128)(2,1)}, bf16[256,1024]{1,0:T(8,128)(2,1)}, bf16[256,1024]{1,0:T(8,128)(2,1)}) custom-call(s32[1]{0:T(128)} %bitcast.position_ref, f32[2048,128]{1,0:T(8,128)S(1)} %get-tuple-element.54.local_ref, ...), custom_call_target="tpu_custom_call", output_to_operand_aliasing={{0}: (17, {})} | custom-call | bytes 17500000 | tf_op jit(solution)/shard_map/finish/pallas_call | solution.py:467
  (1 shorter events, 0.0 us)
Async XLA Ops:
  2.1 4.8 %collective-permute-start = (bf16[48,1024]{1,0:T(8,128)(2,1)S(1)}, bf16[48,1024]{1,0:T(8,128)(2,1)S(1)}, u32[]{:S(2)}, u32[]{:S(2)}) collective-permute-start(bf16[48,1024]{1,0:T(8,128)(2,1)S(1)} %get-tuple-element.40), channel_id=1, source_target_pairs={{0,4},{4,8},{8,12},{12,16},{16,20},{20,24},{24,28},{1,5},{5,9},{9,... | collective-permute-start | bytes 294920 | tf_op jit(solution)/shard_map/ppermute | solution.py:485
  4.5 33.8 %collective-permute-start.6 = (bf16[256,1024]{1,0:T(8,128)(2,1)}, bf16[256,1024]{1,0:T(8,128)(2,1)S(1)}, u32[]{:S(2)}, u32[]{:S(2)}) collective-permute-start(bf16[256,1024]{1,0:T(8,128)(2,1)} %refs_0_), channel_id=1, source_target_pairs={{0,2},{1,3},{2,0},{3,1},{4,6},{5,7},{6,4},{7,5},{8,10},{9,11},{10,... | collective-permute-start | bytes 1572872 | tf_op jit(solution)/shard_map/ppermute | solution.py:490
  12.8 4.9 %collective-permute-start.1 = (f32[128,128]{1,0:T(8,128)S(1)}, f32[128,128]{1,0:T(8,128)S(1)}, u32[]{:S(2)}, u32[]{:S(2)}) collective-permute-start(f32[128,128]{1,0:T(8,128)S(1)} %get-tuple-element.48), channel_id=1, source_target_pairs={{0,4},{4,0},{8,12},{12,8},{16,20},{20,16},{24,28},{28,24},{1,5},{5... | collective-permute-start | bytes 196616 | tf_op jit(solution)/shard_map/ppermute | solution.py:490
  14.7 25.1 %collective-permute-start.5 = (bf16[256,1024]{1,0:T(8,128)(2,1)}, bf16[256,1024]{1,0:T(8,128)(2,1)S(1)}, u32[]{:S(2)}, u32[]{:S(2)}) collective-permute-start(bf16[256,1024]{1,0:T(8,128)(2,1)} %refs_0_), channel_id=1, source_target_pairs={{0,1},{1,0},{2,3},{3,2},{4,5},{5,4},{6,7},{7,6},{8,9},{9,8},{10,11... | collective-permute-start | bytes 1572872 | tf_op jit(solution)/shard_map/ppermute | solution.py:490
  16.2 25.7 %collective-permute-start.7 = (bf16[256,1024]{1,0:T(8,128)(2,1)}, bf16[256,1024]{1,0:T(8,128)(2,1)S(1)}, u32[]{:S(2)}, u32[]{:S(2)}) collective-permute-start(bf16[256,1024]{1,0:T(8,128)(2,1)} %get-tuple-element.50), channel_id=1, source_target_pairs={{0,3},{1,2},{2,1},{3,0},{4,7},{5,6},{6,5},{7,4},{8,11},{9,10},{10,... | collective-permute-start | bytes 1572872 | tf_op jit(solution)/shard_map/ppermute | solution.py:490
  17.8 7.9 %collective-permute-start.4 = (bf16[128,128]{1,0:T(8,128)(2,1)S(1)}, bf16[128,128]{1,0:T(8,128)(2,1)S(1)}, u32[]{:S(2)}, u32[]{:S(2)}) collective-permute-start(bf16[128,128]{1,0:T(8,128)(2,1)S(1)} %get-tuple-element.69), channel_id=1, source_target_pairs={{0,24},{4,28},{1,25},{5,29},{2,26},{6,30},{3,27},{7,31}} | collective-permute-start | bytes 98312 | tf_op jit(solution)/shard_map/ppermute | solution.py:485
  24.1 3.8 %collective-permute-start.3 = (bf16[128,128]{1,0:T(8,128)(2,1)S(1)}, bf16[128,128]{1,0:T(8,128)(2,1)S(1)}, u32[]{:S(2)}, u32[]{:S(2)}) collective-permute-start(bf16[128,128]{1,0:T(8,128)(2,1)S(1)} %get-tuple-element.70), channel_id=1, source_target_pairs={{0,16},{4,20},{8,24},{12,28},{1,17},{5,21},{9,25},{13,29},{2,18},{... | collective-permute-start | bytes 98312 | tf_op jit(solution)/shard_map/ppermute | solution.py:485
  25.7 3.8 %collective-permute-start.2 = (bf16[128,128]{1,0:T(8,128)(2,1)S(1)}, bf16[128,128]{1,0:T(8,128)(2,1)S(1)}, u32[]{:S(2)}, u32[]{:S(2)}) collective-permute-start(bf16[128,128]{1,0:T(8,128)(2,1)S(1)} %get-tuple-element.71), channel_id=1, source_target_pairs={{0,8},{4,12},{8,16},{12,20},{16,24},{20,28},{1,9},{5,13},{9,17},{1... | collective-permute-start | bytes 98312 | tf_op jit(solution)/shard_map/ppermute | solution.py:485
  36.3 39.5 %collective-permute-start.13 = (bf16[256,1024]{1,0:T(8,128)(2,1)}, bf16[256,1024]{1,0:T(8,128)(2,1)}, u32[]{:S(2)}, u32[]{:S(2)}) collective-permute-start(bf16[256,1024]{1,0:T(8,128)(2,1)} %get-tuple-element.58), channel_id=1, source_target_pairs={{0,1},{1,0},{2,3},{3,2},{4,5},{5,4},{6,7},{7,6},{8,9},{9,8},{10,11... | collective-permute-start | bytes 1572872 | tf_op jit(solution)/shard_map/ppermute | solution.py:490
  37.8 38.0 %collective-permute-start.14 = (bf16[256,1024]{1,0:T(8,128)(2,1)}, bf16[256,1024]{1,0:T(8,128)(2,1)}, u32[]{:S(2)}, u32[]{:S(2)}) collective-permute-start(bf16[256,1024]{1,0:T(8,128)(2,1)} %get-tuple-element.59), channel_id=1, source_target_pairs={{0,2},{1,3},{2,0},{3,1},{4,6},{5,7},{6,4},{7,5},{8,10},{9,11},{10,... | collective-permute-start | bytes 1572872 | tf_op jit(solution)/shard_map/ppermute | solution.py:490
  38.3 3.6 %copy-start = (bf16[256,1024]{1,0:T(8,128)(2,1)}, bf16[256,1024]{1,0:T(8,128)(2,1)S(1)}, u32[]{:S(2)}) copy-start(bf16[256,1024]{1,0:T(8,128)(2,1)S(1)} %collective-permute-done.6.refs_2_.refs_1_) | copy-start | bytes 1572868
  38.4 37.5 %collective-permute-start.15 = (bf16[256,1024]{1,0:T(8,128)(2,1)}, bf16[256,1024]{1,0:T(8,128)(2,1)}, u32[]{:S(2)}, u32[]{:S(2)}) collective-permute-start(bf16[256,1024]{1,0:T(8,128)(2,1)} %get-tuple-element.60), channel_id=1, source_target_pairs={{0,3},{1,2},{2,1},{3,0},{4,7},{5,6},{6,5},{7,4},{8,11},{9,10},{10,... | collective-permute-start | bytes 1572872 | tf_op jit(solution)/shard_map/ppermute | solution.py:490
  39.8 2.1 %copy-start.1 = (bf16[256,1024]{1,0:T(8,128)(2,1)}, bf16[256,1024]{1,0:T(8,128)(2,1)S(1)}, u32[]{:S(2)}) copy-start(bf16[256,1024]{1,0:T(8,128)(2,1)S(1)} %collective-permute-done.5.refs_1_.refs_0_) | copy-start | bytes 1572868
  41.9 0.8 copy-start.2
  54.3 1.3 %collective-permute-start.9 = (f32[128,128]{1,0:T(8,128)S(1)}, f32[128,128]{1,0:T(8,128)S(1)}, u32[]{:S(2)}, u32[]{:S(2)}) collective-permute-start(f32[128,128]{1,0:T(8,128)S(1)} %get-tuple-element.56), channel_id=1, source_target_pairs={{0,4},{4,0},{8,12},{12,8},{16,20},{20,16},{24,28},{28,24},{1,5},{5... | collective-permute-start | bytes 196616 | tf_op jit(solution)/shard_map/ppermute | solution.py:490
  55.7 7.6 %collective-permute-start.12 = (bf16[128,128]{1,0:T(8,128)(2,1)S(1)}, bf16[128,128]{1,0:T(8,128)(2,1)S(1)}, u32[]{:S(2)}, u32[]{:S(2)}) collective-permute-start(bf16[128,128]{1,0:T(8,128)(2,1)S(1)} %get-tuple-element.66), channel_id=1, source_target_pairs={{24,0},{28,4},{25,1},{29,5},{26,2},{30,6},{27,3},{31,7}} | collective-permute-start | bytes 98312 | tf_op jit(solution)/shard_map/ppermute | solution.py:485
  57.0 18.8 %collective-permute-start.8 = (f32[4,48,128]{2,1,0:T(8,128)S(1)}, f32[4,48,128]{2,1,0:T(8,128)S(1)}, u32[]{:S(2)}, u32[]{:S(2)}) collective-permute-start(f32[4,48,128]{2,1,0:T(8,128)S(1)} %get-tuple-element.55), channel_id=1, source_target_pairs={{4,0},{8,4},{12,8},{16,12},{20,16},{24,20},{28,24},{5,1},{9,5},{13... | collective-permute-start | bytes 294920 | tf_op jit(solution)/shard_map/ppermute | solution.py:485
  63.3 5.8 %collective-permute-start.10 = (bf16[128,128]{1,0:T(8,128)(2,1)S(1)}, bf16[128,128]{1,0:T(8,128)(2,1)S(1)}, u32[]{:S(2)}, u32[]{:S(2)}) collective-permute-start(bf16[128,128]{1,0:T(8,128)(2,1)S(1)} %get-tuple-element.67), channel_id=1, source_target_pairs={{8,0},{12,4},{16,8},{20,12},{24,16},{28,20},{9,1},{13,5},{17,9},{2... | collective-permute-start | bytes 98312 | tf_op jit(solution)/shard_map/ppermute | solution.py:485
  69.1 6.7 %collective-permute-start.11 = (bf16[128,128]{1,0:T(8,128)(2,1)S(1)}, bf16[128,128]{1,0:T(8,128)(2,1)S(1)}, u32[]{:S(2)}, u32[]{:S(2)}) collective-permute-start(bf16[128,128]{1,0:T(8,128)(2,1)S(1)} %get-tuple-element.68), channel_id=1, source_target_pairs={{16,0},{20,4},{24,8},{28,12},{17,1},{21,5},{25,9},{29,13},{18,2},{... | collective-permute-start | bytes 98312 | tf_op jit(solution)/shard_map/ppermute | solution.py:485

commit v11 on v9

--- a/solution.py
+++ b/solution.py
@@ -542,8 +542,9 @@
     halo, out_grad = lax.optimization_barrier((halo, out_grad))
     halo = shift(halo, "ctx", 1)
     if fans == 4:
-        order = lax.axis_index("ch") ^ jnp.arange(fans, dtype=jnp.int32)
-        pieces = [out_grad] + [exchange(out_grad, "ch", mask) for mask in range(1, fans - 1)]
+        masks = (0, 2, 1, 3)
+        order = lax.axis_index("ch") ^ jnp.asarray(masks, dtype=jnp.int32)
+        pieces = [out_grad, exchange(out_grad, "ch", masks[1])]
     else:
         order = jnp.arange(fans, dtype=jnp.int32)
         everyone = lax.all_gather(out_grad, "ch", axis=0, tiled=False)
@@ -570,7 +571,7 @@
         "featurize", 6.0, 10,
     )
     if fans == 4:
-        pieces.append(exchange(grad_copy, "ch", fans - 1))
+        pieces += [exchange(grad_copy, "ch", mask) for mask in masks[2:]]
     arrived = lax.all_to_all(messages, "ctx", split_axis=0, concat_axis=0, tiled=True)
 
     def weight_scratch(count):
@@ -615,7 +616,8 @@
     )
     if fans == 4:
         parts = [
-            exchange(part, "ch", mask) if mask else part for mask, part in enumerate(partial_sums)
+            exchange(part, "ch", mask) if mask else part
+            for mask, part in zip(masks, partial_sums)
         ]
     else:
         parts = lax.all_to_all(

time: 70.6 us -> 78.8 us (1.12)
  waiting for transfers between devices: 5.8 us -> 11.5 us
  starting transfers between devices: 23.4 us -> 25.2 us
    ppermute x6, waiting for transfers between devices: 0.08 us -> 6.99 us  [exchange(): return lax.ppermute(value, axis, [(s, s ^ mask) for s in range(count)])]
    all_to_all x1, starting transfers between devices: 5.99 us -> 7.49 us  [shards(): lax.all_to_all(messages, 'ctx', split_axis=0, concat_axis=0, tiled=True)]
    all_to_all x1, starting transfers between devices: 3.85 us -> 5.17 us  [shards(): lax.all_to_all(back_messages, 'ctx', split_axis=0, concat_axis=0, tiled=T...]
    all_to_all x1, waiting for transfers between devices: 1.29 us -> 0.1 us  [shards(): lax.all_to_all(messages, 'ctx', split_axis=0, concat_axis=0, tiled=True)]
    ppermute x6, starting transfers between devices: 9.91 us -> 8.95 us  [exchange(): return lax.ppermute(value, axis, [(s, s ^ mask) for s in range(count)])]
    unnamed x6 -> x8, local copies, waits for them, and re-layouts: 2.37 us -> 2.36 us
  transfers between devices with their start and end apart: 10 -> 10, of which waited for: 3 -> 3; matrix products, arithmetic and copies ran while one was open for 0% -> 1% of each run, Pallas kernels for 44% -> 40%
where the time goes in v11:
time: 78.8 us; the launch traced here: 78.4 us
  Pallas kernels  37.9 us (48%)
  starting transfers between devices  25.2 us (32%)
  waiting for transfers between devices  11.5 us (15%)
  local copies, waits for them, and re-layouts  2.36 us (3%)
    pallas_call x7, Pallas kernels, call(): pl.pallas_call(kernel, out_shape=[jax.ShapeDtypeStruct(*out) if own else...  37.9 us
    ppermute x6, starting transfers between devices, exchange(): return lax.ppermute(value, axis, [(s, s ^ mask) for s in range(count)])  8.95 us
    all_to_all x1, starting transfers between devices, shards(): lax.all_to_all(messages, 'ctx', split_axis=0, concat_axis=0, tiled=True)  7.49 us
    ppermute x6, waiting for transfers between devices, exchange(): return lax.ppermute(value, axis, [(s, s ^ mask) for s in range(count)])  6.99 us
    all_to_all x1, starting transfers between devices, shards(): lax.all_to_all(back_messages, 'ctx', split_axis=0, concat_axis=0, tiled=T...  5.17 us
    all_to_all x1, waiting for transfers between devices, shards(): lax.all_to_all(back_messages, 'ctx', split_axis=0, concat_axis=0, tiled=T...  4.4 us
    ppermute x2, starting transfers between devices, shift(): return lax.ppermute(value, axis, pairs)  3.64 us
    unnamed x8, local copies, waits for them, and re-layouts  2.36 us
  transfers between devices with their start and end apart: 10, of which 3 were waited for; matrix products, arithmetic and copies ran while one was open for 1% of the time, Pallas kernels for 40%

profile of v11, /device:TPU:0, one launch (start us, length us, event | category | flops | bytes accessed | tf_op | source)
XLA Modules:
  0.0 78.4 jit_solution(17708846965536472433)
XLA Ops:
  0.6 1.5 %rim.1 = (bf16[48,1024]{1,0:T(8,128)(2,1)S(1)}, bf16[3,256,1024]{2,1,0:T(8,128)(2,1)S(1)}, f32[3,7,1024]{2,1,0:T(8,128)S(1)}, f32[16,1024]{1,0:T(8,128)S(1)}, f32[16,1024]{1,0:T(8,128)S(1)}) custom-call(bf16[256,1024]{1,0:T(8,128)(2,1)} %q_ref.1, bf16[256,1024]{1,0:T(8,128)(2,1)} %k_ref.1, bf16[256,1024]{1,0:T(8,128)(2,1)} %v_ref.1, f32[3,7,1024]{2,1,0:T(8,128)} %bitcast.4, ...), custom_call_target="tpu_custom_call" | custom-call | bytes 4200000 | tf_op jit(solution)/shard_map/rim/pallas_call | solution.py:489
  2.1 2.4 %collective-permute-start.1 = (bf16[48,1024]{1,0:T(8,128)(2,1)S(1)}, bf16[48,1024]{1,0:T(8,128)(2,1)S(1)}, u32[]{:S(2)}, u32[]{:S(2)}) collective-permute-start(bf16[48,1024]{1,0:T(8,128)(2,1)S(1)} %get-tuple-element.41), channel_id=1, source_target_pairs={{0,4},{4,8},{8,12},{12,16},{16,20},{20,24},{24,28},{1,5},{5,9},{9,... | collective-permute-start | bytes 294920 | tf_op jit(solution)/shard_map/ppermute | solution.py:507
  4.5 2.4 %collective-permute-start = (bf16[256,1024]{1,0:T(8,128)(2,1)}, bf16[256,1024]{1,0:T(8,128)(2,1)S(1)}, u32[]{:S(2)}, u32[]{:S(2)}) collective-permute-start(bf16[256,1024]{1,0:T(8,128)(2,1)} %grad_in_ref), channel_id=1, source_target_pairs={{0,2},{1,3},{2,0},{3,1},{4,6},{5,7},{6,4},{7,5},{8,10},{9,11},{10,... | collective-permute-start | bytes 1572872 | tf_op jit(solution)/shard_map/ppermute | solution.py:512
  6.9 0.0 collective-permute-done.1.halo_ref
  6.9 6.6 %featurize.1 = (f32[2048,128]{1,0:T(8,128)}, f32[2048,128]{1,0:T(8,128)}, f32[2048,128]{1,0:T(8,128)}, f32[2048,128]{1,0:T(8,128)}, bf16[256,1024]{1,0:T(8,128)(...) custom-call(s32[1]{0:T(128)} %bitcast.position_ref, ...), custom_call_target="tpu_custom_call" | custom-call | bytes 21000000 | tf_op jit(solution)/shard_map/featurize/pallas_call | solution.py:489
  13.5 7.5 %all-to-all-start = ((bf16[8,128,128]{2,1,0:T(8,128)(2,1)}), bf16[8,128,128]{2,1,0:T(8,128)(2,1)S(1)}, u32[]{:S(2)}, u32[]{:S(2)}) async-start(bf16[8,128,128]{2,1,0:T(8,128)(2,1)} %get-tuple-element.46), calls=%async_computation | async-start | bytes 524288 | tf_op jit(solution)/shard_map/all_to_all | solution.py:575
  21.0 2.4 %collective-permute-start.3 = (bf16[256,1024]{1,0:T(8,128)(2,1)}, bf16[256,1024]{1,0:T(8,128)(2,1)S(1)}, u32[]{:S(2)}, u32[]{:S(2)}) collective-permute-start(bf16[256,1024]{1,0:T(8,128)(2,1)} %get-tuple-element.50), channel_id=1, source_target_pairs={{0,3},{1,2},{2,1},{3,0},{4,7},{5,6},{6,5},{7,4},{8,11},{9,10},{10,... | collective-permute-start | bytes 1572872 | tf_op jit(solution)/shard_map/ppermute | solution.py:512
  23.4 0.5 collective-permute-start.2
  24.0 0.7 broadcast_xor_fusion.index_ref
  24.6 0.0 collective-permute-done.refs_1_.refs_0_
  24.6 0.0 copy-start
  24.6 0.8 %copy-done = bf16[256,1024]{1,0:T(8,128)(2,1)} copy-done((bf16[256,1024]{1,0:T(8,128)(2,1)}, bf16[256,1024]{1,0:T(8,128)(2,1)S(1)}, u32[]{:S(2)}) %copy-start) | copy-done | bytes 524312
  25.4 5.2 %middle.1._.base_ref = f32[1024,256]{1,0:T(8,128)S(1)} custom-call(s32[4]{0:T(128)S(1)} %broadcast_xor_fusion.index_ref, bf16[1024,4096]{1,0:T(8,128)(2,1)} %weight_ref.5, bf16[256,1024]{1,0:T(8,128)(2,1)} %grad_in_ref, bf16[256,1024]{1,0:T(8,128)(2,1)} %copy-done), custom_call_target="tpu_custom_call" | custom-call | bytes 21000000 | tf_op jit(solution)/shard_map/middle/pallas_call | solution.py:489
  30.6 0.1 all-to-all-done.message_ref
  30.7 6.8 %project.1 = (f32[2048,128]{1,0:T(8,128)}, bf16[256,1024]{1,0:T(8,128)(2,1)}, bf16[256,1024]{1,0:T(8,128)(2,1)}, bf16[256,1024]{1,0:T(8,128)(2,1)}, bf16[256,1024]{1,0:T(8,128)(2,1)}) custom-call(s32[4]{0:T(128)S(1)} %broadcast_xor_fusion.index_ref, bf16[8,128,128]{2,1,0:T(8,128)(2,1)S(1)} %all-to-all-done.message_ref, ...), custom_call_target="tpu_custom_call" | custom-call | bytes 24500000 | tf_op jit(solution)/shard_map/project/pallas_call | solution.py:489
  37.6 1.6 %collective-permute-start.5 = (bf16[256,1024]{1,0:T(8,128)(2,1)}, bf16[256,1024]{1,0:T(8,128)(2,1)S(1)}, u32[]{:S(2)}, u32[]{:S(2)}) collective-permute-start(bf16[256,1024]{1,0:T(8,128)(2,1)} %get-tuple-element.58), channel_id=1, source_target_pairs={{0,2},{1,3},{2,0},{3,1},{4,6},{5,7},{6,4},{7,5},{8,10},{9,11},{10,... | collective-permute-start | bytes 1572872 | tf_op jit(solution)/shard_map/ppermute | solution.py:512
  39.2 1.5 %collective-permute-start.6 = (bf16[256,1024]{1,0:T(8,128)(2,1)}, bf16[256,1024]{1,0:T(8,128)(2,1)}, u32[]{:S(2)}, u32[]{:S(2)}) collective-permute-start(bf16[256,1024]{1,0:T(8,128)(2,1)} %get-tuple-element.59), channel_id=1, source_target_pairs={{0,1},{1,0},{2,3},{3,2},{4,5},{5,4},{6,7},{7,6},{8,9},{9,8},{10,11... | collective-permute-start | bytes 1572872 | tf_op jit(solution)/shard_map/ppermute | solution.py:512
  40.6 0.5 collective-permute-start.7
  41.1 0.0 collective-permute-done.3.refs_2_.refs_1_
  41.1 0.0 copy-start.1
  41.1 7.0 %collective-permute-done.2.refs_1_.refs_0_ = bf16[256,1024]{1,0:T(8,128)(2,1)S(1)} collective-permute-done((bf16[256,1024]{1,0:T(8,128)(2,1)}, bf16[256,1024]{1,0:T(8,128)(2,1)S(1)}, u32[]{:S(2)}, u32[]{:S(2)}) %collective-permute-start.2) | collective-permute-done | bytes 524320 | tf_op jit(solution)/shard_map/ppermute | solution.py:512
  48.1 0.0 copy-start.2
  48.1 0.0 copy-done.1
  48.1 0.8 %copy-done.2 = bf16[256,1024]{1,0:T(8,128)(2,1)} copy-done((bf16[256,1024]{1,0:T(8,128)(2,1)}, bf16[256,1024]{1,0:T(8,128)(2,1)S(1)}, u32[]{:S(2)}) %copy-start.2) | copy-done | bytes 524312
  48.9 8.4 %back_last.1 = (f32[2048,128]{1,0:T(8,128)}, f32[2048,128]{1,0:T(8,128)S(1)}, bf16[8,128,128]{2,1,0:T(8,128)(2,1)}, f32[4,48,128]{2,1,0:T(8,128)S(1)}) custom-call(s32[4]{0:T(128)S(1)} %broadcast_xor_fusion.index_ref, s32[1]{0:T(128)} %bitcast.position_ref, f32[1024,256]{1,0:T(8,128)S(1)} %middle.1._.base_ref, f32[128,128]{1,0:T(8,128)S(1)} %get-tuple-element.42.decay_ref, ...), custom_call_target="tpu_custom_call" | custom-call | bytes 24500000 | tf_op jit(solution)/shard_map/back_last/pallas_call | solution.py:489
  57.3 5.2 %all-to-all-start.1 = ((bf16[8,128,128]{2,1,0:T(8,128)(2,1)}), bf16[8,128,128]{2,1,0:T(8,128)(2,1)S(1)}, u32[]{:S(2)}, u32[]{:S(2)}) async-start(bf16[8,128,128]{2,1,0:T(8,128)(2,1)} %get-tuple-element.51), calls=%async_computation.1 | async-start | bytes 524288 | tf_op jit(solution)/shard_map/all_to_all | solution.py:648
  62.5 1.3 %collective-permute-start.4 = (f32[4,48,128]{2,1,0:T(8,128)S(1)}, f32[4,48,128]{2,1,0:T(8,128)S(1)}, u32[]{:S(2)}, u32[]{:S(2)}) collective-permute-start(f32[4,48,128]{2,1,0:T(8,128)S(1)} %get-tuple-element.56), channel_id=1, source_target_pairs={{4,0},{8,4},{12,8},{16,12},{20,16},{24,20},{28,24},{5,1},{9,5},{13... | collective-permute-start | bytes 294920 | tf_op jit(solution)/shard_map/ppermute | solution.py:507
  63.8 4.0 %back_local.1 = (f32[2048,128]{1,0:T(8,128)S(1)}, bf16[256,1024]{1,0:T(8,128)(2,1)}) custom-call(f32[2048,128]{1,0:T(8,128)S(1)} %get-tuple-element.52.signal_ref, f32[128,128]{1,0:T(8,128)S(1)} %get-tuple-element.42.decay_ref, f32[128,128]{1,0:T(8,128)S(1)} %get-tuple-element.47.scale_ref, f32[168,128]{1,0:T(8,128)S(1)} %get-tuple-element.53.taps_ref, ...), custom_call_target="tpu_custom_call" | custom-call | bytes 15750000 | tf_op jit(solution)/shard_map/back_local/pallas_call | solution.py:489
  67.9 0.0 collective-permute-done.4.ahead_ref
  67.9 4.4 %all-to-all-done.1.message_ref = bf16[8,128,128]{2,1,0:T(8,128)(2,1)S(1)} async-done(((bf16[8,128,128]{2,1,0:T(8,128)(2,1)}), bf16[8,128,128]{2,1,0:T(8,128)(2,1)S(1)}, u32[]{:S(2)}, u32[]{:S(2)}) %all-to-all-start.1) | async-done | bytes 262176 | tf_op jit(solution)/shard_map/all_to_all | solution.py:648
  72.3 0.0 collective-permute-done.5.refs_1_
  72.3 0.0 copy-start.3
  72.3 0.0 collective-permute-done.6.refs_2_
  72.3 0.0 collective-permute-done.7.refs_3_
  72.3 0.8 copy-done.3
  73.1 5.3 %finish.1 = (bf16[256,1024]{1,0:T(8,128)(2,1)}, bf16[256,1024]{1,0:T(8,128)(2,1)}, bf16[256,1024]{1,0:T(8,128)(2,1)}, bf16[256,1024]{1,0:T(8,128)(2,1)}) custom-call(bf16[8,128,128]{2,1,0:T(8,128)(2,1)S(1)} %all-to-all-done.1.message_ref, f32[2048,128]{1,0:T(8,128)S(1)} %get-tuple-element.55.local_ref, ...), custom_call_target="tpu_custom_call", output_to_operand_aliasing={{0}: (13, {})} | custom-call | bytes 17500000 | tf_op jit(solution)/shard_map/finish/pallas_call | solution.py:489
Async XLA Ops:
  2.1 4.8 %collective-permute-start.1 = (bf16[48,1024]{1,0:T(8,128)(2,1)S(1)}, bf16[48,1024]{1,0:T(8,128)(2,1)S(1)}, u32[]{:S(2)}, u32[]{:S(2)}) collective-permute-start(bf16[48,1024]{1,0:T(8,128)(2,1)S(1)} %get-tuple-element.41), channel_id=1, source_target_pairs={{0,4},{4,8},{8,12},{12,16},{16,20},{20,24},{24,28},{1,5},{5,9},{9,... | collective-permute-start | bytes 294920 | tf_op jit(solution)/shard_map/ppermute | solution.py:507
  4.5 20.1 %collective-permute-start = (bf16[256,1024]{1,0:T(8,128)(2,1)}, bf16[256,1024]{1,0:T(8,128)(2,1)S(1)}, u32[]{:S(2)}, u32[]{:S(2)}) collective-permute-start(bf16[256,1024]{1,0:T(8,128)(2,1)} %grad_in_ref), channel_id=1, source_target_pairs={{0,2},{1,3},{2,0},{3,1},{4,6},{5,7},{6,4},{7,5},{8,10},{9,11},{10,... | collective-permute-start | bytes 1572872 | tf_op jit(solution)/shard_map/ppermute | solution.py:512
  13.5 17.2 %all-to-all-start = ((bf16[8,128,128]{2,1,0:T(8,128)(2,1)}), bf16[8,128,128]{2,1,0:T(8,128)(2,1)S(1)}, u32[]{:S(2)}, u32[]{:S(2)}) async-start(bf16[8,128,128]{2,1,0:T(8,128)(2,1)} %get-tuple-element.46), calls=%async_computation | async-start | bytes 524288 | tf_op jit(solution)/shard_map/all_to_all | solution.py:575
  21.0 20.1 %collective-permute-start.3 = (bf16[256,1024]{1,0:T(8,128)(2,1)}, bf16[256,1024]{1,0:T(8,128)(2,1)S(1)}, u32[]{:S(2)}, u32[]{:S(2)}) collective-permute-start(bf16[256,1024]{1,0:T(8,128)(2,1)} %get-tuple-element.50), channel_id=1, source_target_pairs={{0,3},{1,2},{2,1},{3,0},{4,7},{5,6},{6,5},{7,4},{8,11},{9,10},{10,... | collective-permute-start | bytes 1572872 | tf_op jit(solution)/shard_map/ppermute | solution.py:512
  23.4 24.7 %collective-permute-start.2 = (bf16[256,1024]{1,0:T(8,128)(2,1)}, bf16[256,1024]{1,0:T(8,128)(2,1)S(1)}, u32[]{:S(2)}, u32[]{:S(2)}) collective-permute-start(bf16[256,1024]{1,0:T(8,128)(2,1)} %get-tuple-element.50), channel_id=1, source_target_pairs={{0,1},{1,0},{2,3},{3,2},{4,5},{5,4},{6,7},{7,6},{8,9},{9,8},{10,11... | collective-permute-start | bytes 1572872 | tf_op jit(solution)/shard_map/ppermute | solution.py:512
  24.6 0.8 %copy-start = (bf16[256,1024]{1,0:T(8,128)(2,1)}, bf16[256,1024]{1,0:T(8,128)(2,1)S(1)}, u32[]{:S(2)}) copy-start(bf16[256,1024]{1,0:T(8,128)(2,1)S(1)} %collective-permute-done.refs_1_.refs_0_) | copy-start | bytes 1572868
  37.6 34.7 %collective-permute-start.5 = (bf16[256,1024]{1,0:T(8,128)(2,1)}, bf16[256,1024]{1,0:T(8,128)(2,1)S(1)}, u32[]{:S(2)}, u32[]{:S(2)}) collective-permute-start(bf16[256,1024]{1,0:T(8,128)(2,1)} %get-tuple-element.58), channel_id=1, source_target_pairs={{0,2},{1,3},{2,0},{3,1},{4,6},{5,7},{6,4},{7,5},{8,10},{9,11},{10,... | collective-permute-start | bytes 1572872 | tf_op jit(solution)/shard_map/ppermute | solution.py:512
  39.2 33.1 %collective-permute-start.6 = (bf16[256,1024]{1,0:T(8,128)(2,1)}, bf16[256,1024]{1,0:T(8,128)(2,1)}, u32[]{:S(2)}, u32[]{:S(2)}) collective-permute-start(bf16[256,1024]{1,0:T(8,128)(2,1)} %get-tuple-element.59), channel_id=1, source_target_pairs={{0,1},{1,0},{2,3},{3,2},{4,5},{5,4},{6,7},{7,6},{8,9},{9,8},{10,11... | collective-permute-start | bytes 1572872 | tf_op jit(solution)/shard_map/ppermute | solution.py:512
  40.6 31.6 %collective-permute-start.7 = (bf16[256,1024]{1,0:T(8,128)(2,1)}, bf16[256,1024]{1,0:T(8,128)(2,1)}, u32[]{:S(2)}, u32[]{:S(2)}) collective-permute-start(bf16[256,1024]{1,0:T(8,128)(2,1)} %get-tuple-element.60), channel_id=1, source_target_pairs={{0,3},{1,2},{2,1},{3,0},{4,7},{5,6},{6,5},{7,4},{8,11},{9,10},{10,... | collective-permute-start | bytes 1572872 | tf_op jit(solution)/shard_map/ppermute | solution.py:512
  41.1 7.0 %copy-start.1 = (bf16[256,1024]{1,0:T(8,128)(2,1)}, bf16[256,1024]{1,0:T(8,128)(2,1)S(1)}, u32[]{:S(2)}) copy-start(bf16[256,1024]{1,0:T(8,128)(2,1)S(1)} %collective-permute-done.3.refs_2_.refs_1_) | copy-start | bytes 1572868
  48.1 0.8 %copy-start.2 = (bf16[256,1024]{1,0:T(8,128)(2,1)}, bf16[256,1024]{1,0:T(8,128)(2,1)S(1)}, u32[]{:S(2)}) copy-start(bf16[256,1024]{1,0:T(8,128)(2,1)S(1)} %collective-permute-done.2.refs_1_.refs_0_) | copy-start | bytes 1572868
  57.3 14.9 %all-to-all-start.1 = ((bf16[8,128,128]{2,1,0:T(8,128)(2,1)}), bf16[8,128,128]{2,1,0:T(8,128)(2,1)S(1)}, u32[]{:S(2)}, u32[]{:S(2)}) async-start(bf16[8,128,128]{2,1,0:T(8,128)(2,1)} %get-tuple-element.51), calls=%async_computation.1 | async-start | bytes 524288 | tf_op jit(solution)/shard_map/all_to_all | solution.py:648
  62.5 5.3 %collective-permute-start.4 = (f32[4,48,128]{2,1,0:T(8,128)S(1)}, f32[4,48,128]{2,1,0:T(8,128)S(1)}, u32[]{:S(2)}, u32[]{:S(2)}) collective-permute-start(f32[4,48,128]{2,1,0:T(8,128)S(1)} %get-tuple-element.56), channel_id=1, source_target_pairs={{4,0},{8,4},{12,8},{16,12},{20,16},{24,20},{28,24},{5,1},{9,5},{13... | collective-permute-start | bytes 294920 | tf_op jit(solution)/shard_map/ppermute | solution.py:507
  72.3 0.8 %copy-start.3 = (bf16[256,1024]{1,0:T(8,128)(2,1)}, bf16[256,1024]{1,0:T(8,128)(2,1)S(1)}, u32[]{:S(2)}) copy-start(bf16[256,1024]{1,0:T(8,128)(2,1)S(1)} %collective-permute-done.5.refs_1_) | copy-start | bytes 1572868

commit v12 on v7

--- a/solution.py
+++ b/solution.py
@@ -247,12 +247,15 @@
     index_ref, message_ref, decay_ref, scale_ref, _, qf_ref, local_ref, weight_ref, *refs
 ):
     rows_ref, feat_ref, local_vmem, gated_ref, held_ref, sent_ref, sems, out_sems = refs[-8:]
-    conv_ref, *out_refs = refs[-9 - sent_ref.shape[0] : -8]
+    conv_ref, gated_out_ref, *out_refs = refs[-10 - sent_ref.shape[0] : -8]
     parts, tokens, width = sent_ref.shape
+    offset = index_ref.shape[0] - parts
     order = list(reversed(range(parts)))
     copies = [
         pltpu.make_async_copy(
-            weight_ref.at[:, pl.ds(pl.multiple_of(index_ref[part] * width, width), width)],
+            weight_ref.at[
+                :, pl.ds(pl.multiple_of(index_ref[offset + part] * width, width), width)
+            ],
             held_ref.at[part],
             sems.at[part],
         )
@@ -276,14 +279,15 @@
         lambda group: group_rows(rows_ref, group, tokens) * group_rows(feat_ref, group, tokens),
         gated_ref,
     )
+    gated_copy = pltpu.make_async_copy(gated_ref, gated_out_ref, out_sems.at[parts])
+    gated_copy.start()
     for part in order:
         copies[part].wait()
         sent_ref[part] = jnp.dot(
             gated_ref[...], held_ref[part], preferred_element_type=F32
         ).astype(sent_ref.dtype)
         outs[part].start()
-    conv_copy.wait()
-    wait_all(outs)
+    wait_all([conv_copy, gated_copy] + outs)
 
 
 def start_weights(index_ref, first, weight_ref, held_ref, sems):
@@ -380,9 +384,13 @@
 
 
 def back_local_kernel(
-    signal_ref, decay_ref, scale_ref, taps_ref, query_ref, local_ref, gq_ref,
-    wide_ref, rows_ref, out_vmem, sem, *, taps,
+    index_ref, signal_ref, decay_ref, scale_ref, taps_ref, query_ref, gated_ref, weight_ref,
+    local_ref, gq_ref, own_ref,
+    wide_ref, rows_ref, out_vmem, gated_vmem, held_ref, own_vmem, sem, sems, *, taps,
 ):
+    gated = pltpu.make_async_copy(gated_ref, gated_vmem, sems.at[1])
+    gated.start()
+    weights = start_weights(index_ref, 0, weight_ref, held_ref, sems)
     inside = query_ref.shape[0]
     copy = pltpu.make_async_copy(query_ref, wide_ref.at[pl.ds(0, inside), :], sem)
     copy.start()
@@ -393,7 +401,13 @@
     spread_back(wide_ref, taps_ref, 0, taps, rows_ref, out_vmem)
     out = pltpu.make_async_copy(out_vmem, gq_ref, sem)
     out.start()
-    out.wait()
+    wait_all([gated, *weights])
+    own_vmem[...] = jnp.dot(
+        gated_vmem[...], held_ref[0], preferred_element_type=F32
+    ).astype(own_vmem.dtype)
+    own = pltpu.make_async_copy(own_vmem, own_ref, sems.at[0])
+    own.start()
+    wait_all([out, own])
 
 
 def finish_kernel(
@@ -584,9 +598,10 @@
         + [pltpu.SemaphoreType.DMA((early,))],
         "middle", 6.0, 11,
     )
-    conv_out, *partial_sums = call(
+    sent = fans - 1 if fans == 4 else fans
+    conv_out, gated, *partial_sums = call(
         project_kernel,
-        [in_hbm(tile_shape, F32)] + [in_hbm((tokens, channels), BF16)] * fans,
+        [in_hbm(tile_shape, F32)] + [in_hbm((tokens, channels), BF16)] * (1 + sent),
         (
             order, arrived, decay_tiles, scale_tiles, base, query_feat, local, out_weight,
             *pieces[1:early],
@@ -597,17 +612,15 @@
             tile,
             tile,
             pltpu.VMEM((tokens, channels), BF16),
-            pltpu.VMEM((fans, channels, channels), BF16),
-            pltpu.VMEM((fans, tokens, channels), BF16),
-            pltpu.SemaphoreType.DMA((fans + 2,)),
-            pltpu.SemaphoreType.DMA((fans,)),
+            pltpu.VMEM((sent, channels, channels), BF16),
+            pltpu.VMEM((sent, tokens, channels), BF16),
+            pltpu.SemaphoreType.DMA((sent + 2,)),
+            pltpu.SemaphoreType.DMA((sent + 1,)),
         ],
         "project", 7.0, 16,
     )
     if fans == 4:
-        parts = [
-            exchange(part, "ch", mask) if mask else part for mask, part in enumerate(partial_sums)
-        ]
+        parts = [exchange(part, "ch", 1 + number) for number, part in enumerate(partial_sums)]
     else:
         parts = lax.all_to_all(
             jnp.stack(partial_sums), "ch", split_axis=0, concat_axis=0, tiled=True
@@ -635,19 +648,25 @@
     )
     back_arrived = lax.all_to_all(back_messages, "ctx", split_axis=0, concat_axis=0, tiled=True)
     ahead = shift(ahead, "ctx", -1)
-    back_local, grad_query = call(
+    back_local, grad_query, own_part = call(
         functools.partial(back_local_kernel, taps=taps),
-        [(tile_shape, F32), in_hbm((tokens, channels), BF16)],
-        (grad_mixed, decay_tiles, scale_tiles, tap_tiles, back_query),
-        [IN_VMEM] * 4 + [IN_HBM],
+        [(tile_shape, F32)] + [in_hbm((tokens, channels), BF16)] * 2,
+        (order, grad_mixed, decay_tiles, scale_tiles, tap_tiles, back_query, gated, out_weight),
+        [IN_SMEM] + [IN_VMEM] * 4 + [IN_HBM] * 3,
         [
             pltpu.VMEM((wide_rows, LANES), F32),
             tile,
+            pltpu.VMEM((tokens, channels), BF16),
+            pltpu.VMEM((tokens, channels), BF16),
+            pltpu.VMEM((1, channels, channels), BF16),
             pltpu.VMEM((tokens, channels), BF16),
             pltpu.SemaphoreType.DMA,
+            pltpu.SemaphoreType.DMA((2,)),
         ],
-        "back_local", 4.5, 5,
-    )
+        "back_local", 5.0, 9,
+    )
+    if fans == 4:
+        parts = [own_part] + parts
     tail = 16
     grad_query, grad_key, grad_value, projected = call(
         functools.partial(finish_kernel, taps=taps),

time: 69.8 us -> 69.4 us (level)
  waiting for transfers between devices: 6.09 us -> 4.81 us
  Pallas kernels: 37.1 us -> 38 us
    all_to_all x1, waiting for transfers between devices: 4.43 us -> 3.15 us  [shards(): lax.all_to_all(back_messages, 'ctx', split_axis=0, concat_axis=0, tiled=T...]
    pallas_call x7, Pallas kernels: 37.1 us -> 38 us  [call(): pl.pallas_call(kernel, out_shape=[jax.ShapeDtypeStruct(*out) if own else...]
  transfers between devices with their start and end apart: 10 -> 10, of which waited for: 2 -> 2; matrix products, arithmetic and copies ran while one was open for 0% -> 0% of each run, Pallas kernels for 44% -> 45%
where the time goes in v12:
time: 69.4 us; the launch traced here: 69 us
  Pallas kernels  38 us (55%)
  starting transfers between devices  24.7 us (36%)
  waiting for transfers between devices  4.81 us (7%)
  local copies, waits for them, and re-layouts  0.78 us (1%)
  between operations  0.73 us (1%)
    pallas_call x7, Pallas kernels, call(): pl.pallas_call(kernel, out_shape=[jax.ShapeDtypeStruct(*out) if own else...  38 us
    ppermute x6, starting transfers between devices, exchange(): return lax.ppermute(value, axis, [(s, s ^ mask) for s in range(count)])  9.91 us
    all_to_all x1, starting transfers between devices, shards(): lax.all_to_all(messages, 'ctx', split_axis=0, concat_axis=0, tiled=True)  5.99 us
    all_to_all x1, starting transfers between devices, shards(): lax.all_to_all(back_messages, 'ctx', split_axis=0, concat_axis=0, tiled=T...  5.12 us
    ppermute x2, starting transfers between devices, shift(): return lax.ppermute(value, axis, pairs)  3.64 us
    all_to_all x1, waiting for transfers between devices, shards(): lax.all_to_all(back_messages, 'ctx', split_axis=0, concat_axis=0, tiled=T...  3.15 us
    ppermute x6, waiting for transfers between devices, exchange(): return lax.ppermute(value, axis, [(s, s ^ mask) for s in range(count)])  1.65 us
  transfers between devices with their start and end apart: 10, of which 2 were waited for; matrix products, arithmetic and copies ran while one was open for 0% of the time, Pallas kernels for 45%

profile of v12, /device:TPU:0, one launch (start us, length us, event | category | flops | bytes accessed | tf_op | source)
XLA Modules:
  0.0 69.0 jit_solution(5082295561932794904)
XLA Ops:
  0.6 1.5 %rim.1 = (bf16[48,1024]{1,0:T(8,128)(2,1)S(1)}, bf16[3,256,1024]{2,1,0:T(8,128)(2,1)S(1)}, f32[3,7,1024]{2,1,0:T(8,128)S(1)}, f32[16,1024]{1,0:T(8,128)S(1)}, f32[16,1024]{1,0:T(8,128)S(1)}) custom-call(bf16[256,1024]{1,0:T(8,128)(2,1)} %q_ref.1, bf16[256,1024]{1,0:T(8,128)(2,1)} %k_ref.1, bf16[256,1024]{1,0:T(8,128)(2,1)} %v_ref.1, f32[3,7,1024]{2,1,0:T(8,128)} %bitcast.4, ...), custom_call_target="tpu_custom_call" | custom-call | bytes 4200000 | tf_op jit(solution)/shard_map/rim/pallas_call | solution.py:494
  2.1 2.4 %collective-permute-start.2 = (bf16[48,1024]{1,0:T(8,128)(2,1)S(1)}, bf16[48,1024]{1,0:T(8,128)(2,1)S(1)}, u32[]{:S(2)}, u32[]{:S(2)}) collective-permute-start(bf16[48,1024]{1,0:T(8,128)(2,1)S(1)} %get-tuple-element.42), channel_id=1, source_target_pairs={{0,4},{4,8},{8,12},{12,16},{16,20},{20,24},{24,28},{1,5},{5,9},{9,... | collective-permute-start | bytes 294920 | tf_op jit(solution)/shard_map/ppermute | solution.py:512
  4.5 2.4 %collective-permute-start.1 = (bf16[256,1024]{1,0:T(8,128)(2,1)}, bf16[256,1024]{1,0:T(8,128)(2,1)S(1)}, u32[]{:S(2)}, u32[]{:S(2)}) collective-permute-start(bf16[256,1024]{1,0:T(8,128)(2,1)} %grad_in_ref), channel_id=1, source_target_pairs={{0,2},{1,3},{2,0},{3,1},{4,6},{5,7},{6,4},{7,5},{8,10},{9,11},{10,... | collective-permute-start | bytes 1572872 | tf_op jit(solution)/shard_map/ppermute | solution.py:517
  6.9 1.5 %collective-permute-start = (bf16[256,1024]{1,0:T(8,128)(2,1)}, bf16[256,1024]{1,0:T(8,128)(2,1)}, u32[]{:S(2)}, u32[]{:S(2)}) collective-permute-start(bf16[256,1024]{1,0:T(8,128)(2,1)} %grad_in_ref), channel_id=1, source_target_pairs={{0,1},{1,0},{2,3},{3,2},{4,5},{5,4},{6,7},{7,6},{8,9},{9,8},{10,11... | collective-permute-start | bytes 1572872 | tf_op jit(solution)/shard_map/ppermute | solution.py:517
  8.4 0.0 collective-permute-done.2.halo_ref
  8.4 6.6 %featurize.1 = (f32[2048,128]{1,0:T(8,128)}, f32[2048,128]{1,0:T(8,128)}, f32[2048,128]{1,0:T(8,128)}, f32[2048,128]{1,0:T(8,128)}, bf16[256,1024]{1,0:T(8,128)(...) custom-call(s32[1]{0:T(128)} %bitcast.position_ref, ...), custom_call_target="tpu_custom_call" | custom-call | bytes 21000000 | tf_op jit(solution)/shard_map/featurize/pallas_call | solution.py:494
  15.1 6.0 %all-to-all-start = ((bf16[8,128,128]{2,1,0:T(8,128)(2,1)}), bf16[8,128,128]{2,1,0:T(8,128)(2,1)S(1)}, u32[]{:S(2)}, u32[]{:S(2)}) async-start(bf16[8,128,128]{2,1,0:T(8,128)(2,1)} %get-tuple-element.47), calls=%async_computation | async-start | bytes 524288 | tf_op jit(solution)/shard_map/all_to_all | solution.py:579
  21.1 2.4 %collective-permute-start.3 = (bf16[256,1024]{1,0:T(8,128)(2,1)}, bf16[256,1024]{1,0:T(8,128)(2,1)S(1)}, u32[]{:S(2)}, u32[]{:S(2)}) collective-permute-start(bf16[256,1024]{1,0:T(8,128)(2,1)} %get-tuple-element.51), channel_id=1, source_target_pairs={{0,3},{1,2},{2,1},{3,0},{4,7},{5,6},{6,5},{7,4},{8,11},{9,10},{10,... | collective-permute-start | bytes 1572872 | tf_op jit(solution)/shard_map/ppermute | solution.py:517
  23.5 0.0 collective-permute-done.1.refs_2_.refs_1_
  23.5 0.0 copy-start
  23.5 0.0 collective-permute-done.refs_1_.refs_0_
  23.5 0.8 %copy-done = bf16[256,1024]{1,0:T(8,128)(2,1)} copy-done((bf16[256,1024]{1,0:T(8,128)(2,1)}, bf16[256,1024]{1,0:T(8,128)(2,1)S(1)}, u32[]{:S(2)}) %copy-start) | copy-done | bytes 524312
  24.3 6.7 %middle.1._.base_ref = f32[1024,256]{1,0:T(8,128)S(1)} custom-call(s32[4]{0:T(128)S(1)} %iota_xor_fusion.index_ref, bf16[1024,4096]{1,0:T(8,128)(2,1)} %weight_ref.7, bf16[256,1024]{1,0:T(8,128)(2,1)} %grad_in_ref, bf16[256,1024]{1,0:T(8,128)(2,1)} %collective-permute-done.refs_1_.refs_0_, bf16[256,1024]{1,0:T(8,128)(2,1)} %copy-done), custom_call_target="tpu_custom_call" | custom-call | bytes 21000000 | tf_op jit(solution)/shard_map/middle/pallas_call | solution.py:494
  31.1 0.0 all-to-all-done.message_ref
  31.1 6.4 %project.1 = (f32[2048,128]{1,0:T(8,128)}, bf16[256,1024]{1,0:T(8,128)(2,1)}, bf16[256,1024]{1,0:T(8,128)(2,1)}, bf16[256,1024]{1,0:T(8,128)(2,1)}, bf16[256,1024]{1,0:T(8,128)(2,1)}) custom-call(s32[4]{0:T(128)S(1)} %iota_xor_fusion.index_ref, bf16[8,128,128]{2,1,0:T(8,128)(2,1)S(1)} %all-to-all-done.message_ref, ...), custom_call_target="tpu_custom_call" | custom-call | bytes 24500000 | tf_op jit(solution)/shard_map/project/pallas_call | solution.py:494
  37.5 1.3 %collective-permute-start.5 = (bf16[256,1024]{1,0:T(8,128)(2,1)}, bf16[256,1024]{1,0:T(8,128)(2,1)}, u32[]{:S(2)}, u32[]{:S(2)}) collective-permute-start(bf16[256,1024]{1,0:T(8,128)(2,1)} %get-tuple-element.60), channel_id=1, source_target_pairs={{0,1},{1,0},{2,3},{3,2},{4,5},{5,4},{6,7},{7,6},{8,9},{9,8},{10,11... | collective-permute-start | bytes 1572872 | tf_op jit(solution)/shard_map/ppermute | solution.py:517
  38.8 1.5 %collective-permute-start.6 = (bf16[256,1024]{1,0:T(8,128)(2,1)}, bf16[256,1024]{1,0:T(8,128)(2,1)}, u32[]{:S(2)}, u32[]{:S(2)}) collective-permute-start(bf16[256,1024]{1,0:T(8,128)(2,1)} %get-tuple-element.61), channel_id=1, source_target_pairs={{0,2},{1,3},{2,0},{3,1},{4,6},{5,7},{6,4},{7,5},{8,10},{9,11},{10,... | collective-permute-start | bytes 1572872 | tf_op jit(solution)/shard_map/ppermute | solution.py:517
  40.3 0.7 %collective-permute-start.7 = (bf16[256,1024]{1,0:T(8,128)(2,1)}, bf16[256,1024]{1,0:T(8,128)(2,1)}, u32[]{:S(2)}, u32[]{:S(2)}) collective-permute-start(bf16[256,1024]{1,0:T(8,128)(2,1)} %get-tuple-element.62), channel_id=1, source_target_pairs={{0,3},{1,2},{2,1},{3,0},{4,7},{5,6},{6,5},{7,4},{8,11},{9,10},{10,... | collective-permute-start | bytes 1572872 | tf_op jit(solution)/shard_map/ppermute | solution.py:517
  41.0 0.0 collective-permute-done.3.refs_0_
  41.0 6.1 %back_last.1 = (f32[2048,128]{1,0:T(8,128)}, f32[2048,128]{1,0:T(8,128)S(1)}, bf16[8,128,128]{2,1,0:T(8,128)(2,1)}, f32[4,48,128]{2,1,0:T(8,128)S(1)}) custom-call(s32[4]{0:T(128)S(1)} %iota_xor_fusion.index_ref, s32[1]{0:T(128)} %bitcast.position_ref, f32[1024,256]{1,0:T(8,128)S(1)} %middle.1._.base_ref, f32[128,128]{1,0:T(8,128)S(1)} %get-tuple-element.43.decay_ref, ...), custom_call_target="tpu_custom_call" | custom-call | bytes 21000000 | tf_op jit(solution)/shard_map/back_last/pallas_call | solution.py:494
  47.1 5.1 %all-to-all-start.1 = ((bf16[8,128,128]{2,1,0:T(8,128)(2,1)}), bf16[8,128,128]{2,1,0:T(8,128)(2,1)S(1)}, u32[]{:S(2)}, u32[]{:S(2)}) async-start(bf16[8,128,128]{2,1,0:T(8,128)(2,1)} %get-tuple-element.52), calls=%async_computation.1 | async-start | bytes 524288 | tf_op jit(solution)/shard_map/all_to_all | solution.py:649
  52.3 1.3 %collective-permute-start.4 = (f32[4,48,128]{2,1,0:T(8,128)S(1)}, f32[4,48,128]{2,1,0:T(8,128)S(1)}, u32[]{:S(2)}, u32[]{:S(2)}) collective-permute-start(f32[4,48,128]{2,1,0:T(8,128)S(1)} %get-tuple-element.58), channel_id=1, source_target_pairs={{4,0},{8,4},{12,8},{16,12},{20,16},{24,20},{28,24},{5,1},{9,5},{13... | collective-permute-start | bytes 294920 | tf_op jit(solution)/shard_map/ppermute | solution.py:512
  53.6 5.3 %back_local.1 = (f32[2048,128]{1,0:T(8,128)S(1)}, bf16[256,1024]{1,0:T(8,128)(2,1)}, bf16[256,1024]{1,0:T(8,128)(2,1)}) custom-call(s32[4]{0:T(128)S(1)} %iota_xor_fusion.index_ref, f32[2048,128]{1,0:T(8,128)S(1)} %get-tuple-element.53.signal_ref, f32[128,128]{1,0:T(8,128)S(1)} %get-tuple-element.43.decay_ref, f32[128,128]{1,0:T(8,128)S(1)} %get-tuple-element.48.scale_ref, ...), custom_call_target="tpu_custom_call" | custom-call | bytes 17500000 | tf_op jit(solution)/shard_map/back_local/pallas_call | solution.py:494
  58.9 0.0 collective-permute-done.4.ahead_ref
  58.9 3.1 %all-to-all-done.1.message_ref = bf16[8,128,128]{2,1,0:T(8,128)(2,1)S(1)} async-done(((bf16[8,128,128]{2,1,0:T(8,128)(2,1)}), bf16[8,128,128]{2,1,0:T(8,128)(2,1)S(1)}, u32[]{:S(2)}, u32[]{:S(2)}) %all-to-all-start.1) | async-done | bytes 262176 | tf_op jit(solution)/shard_map/all_to_all | solution.py:649
  62.0 0.0 collective-permute-done.5.refs_1_
  62.0 1.6 %collective-permute-done.6.refs_2_ = bf16[256,1024]{1,0:T(8,128)(2,1)} collective-permute-done((bf16[256,1024]{1,0:T(8,128)(2,1)}, bf16[256,1024]{1,0:T(8,128)(2,1)}, u32[]{:S(2)}, u32[]{:S(2)}) %collective-permute-start.6) | collective-permute-done | bytes 524320 | tf_op jit(solution)/shard_map/ppermute | solution.py:517
  63.7 0.0 collective-permute-done.7.refs_3_
  63.7 5.3 %finish.1 = (bf16[256,1024]{1,0:T(8,128)(2,1)}, bf16[256,1024]{1,0:T(8,128)(2,1)}, bf16[256,1024]{1,0:T(8,128)(2,1)}, bf16[256,1024]{1,0:T(8,128)(2,1)}) custom-call(bf16[8,128,128]{2,1,0:T(8,128)(2,1)S(1)} %all-to-all-done.1.message_ref, f32[2048,128]{1,0:T(8,128)S(1)} %get-tuple-element.57.local_ref, ...), custom_call_target="tpu_custom_call", output_to_operand_aliasing={{0}: (13, {})} | custom-call | bytes 17500000 | tf_op jit(solution)/shard_map/finish/pallas_call | solution.py:494
  (1 shorter events, 0.0 us)
Async XLA Ops:
  2.1 6.3 %collective-permute-start.2 = (bf16[48,1024]{1,0:T(8,128)(2,1)S(1)}, bf16[48,1024]{1,0:T(8,128)(2,1)S(1)}, u32[]{:S(2)}, u32[]{:S(2)}) collective-permute-start(bf16[48,1024]{1,0:T(8,128)(2,1)S(1)} %get-tuple-element.42), channel_id=1, source_target_pairs={{0,4},{4,8},{8,12},{12,16},{16,20},{20,24},{24,28},{1,5},{5,9},{9,... | collective-permute-start | bytes 294920 | tf_op jit(solution)/shard_map/ppermute | solution.py:512
  4.5 19.0 %collective-permute-start.1 = (bf16[256,1024]{1,0:T(8,128)(2,1)}, bf16[256,1024]{1,0:T(8,128)(2,1)S(1)}, u32[]{:S(2)}, u32[]{:S(2)}) collective-permute-start(bf16[256,1024]{1,0:T(8,128)(2,1)} %grad_in_ref), channel_id=1, source_target_pairs={{0,2},{1,3},{2,0},{3,1},{4,6},{5,7},{6,4},{7,5},{8,10},{9,11},{10,... | collective-permute-start | bytes 1572872 | tf_op jit(solution)/shard_map/ppermute | solution.py:517
  6.9 16.6 %collective-permute-start = (bf16[256,1024]{1,0:T(8,128)(2,1)}, bf16[256,1024]{1,0:T(8,128)(2,1)}, u32[]{:S(2)}, u32[]{:S(2)}) collective-permute-start(bf16[256,1024]{1,0:T(8,128)(2,1)} %grad_in_ref), channel_id=1, source_target_pairs={{0,1},{1,0},{2,3},{3,2},{4,5},{5,4},{6,7},{7,6},{8,9},{9,8},{10,11... | collective-permute-start | bytes 1572872 | tf_op jit(solution)/shard_map/ppermute | solution.py:517
  15.1 16.0 %all-to-all-start = ((bf16[8,128,128]{2,1,0:T(8,128)(2,1)}), bf16[8,128,128]{2,1,0:T(8,128)(2,1)S(1)}, u32[]{:S(2)}, u32[]{:S(2)}) async-start(bf16[8,128,128]{2,1,0:T(8,128)(2,1)} %get-tuple-element.47), calls=%async_computation | async-start | bytes 524288 | tf_op jit(solution)/shard_map/all_to_all | solution.py:579
  21.1 20.0 %collective-permute-start.3 = (bf16[256,1024]{1,0:T(8,128)(2,1)}, bf16[256,1024]{1,0:T(8,128)(2,1)S(1)}, u32[]{:S(2)}, u32[]{:S(2)}) collective-permute-start(bf16[256,1024]{1,0:T(8,128)(2,1)} %get-tuple-element.51), channel_id=1, source_target_pairs={{0,3},{1,2},{2,1},{3,0},{4,7},{5,6},{6,5},{7,4},{8,11},{9,10},{10,... | collective-permute-start | bytes 1572872 | tf_op jit(solution)/shard_map/ppermute | solution.py:517
  23.5 0.8 %copy-start = (bf16[256,1024]{1,0:T(8,128)(2,1)}, bf16[256,1024]{1,0:T(8,128)(2,1)S(1)}, u32[]{:S(2)}) copy-start(bf16[256,1024]{1,0:T(8,128)(2,1)S(1)} %collective-permute-done.1.refs_2_.refs_1_) | copy-start | bytes 1572868
  37.5 24.5 %collective-permute-start.5 = (bf16[256,1024]{1,0:T(8,128)(2,1)}, bf16[256,1024]{1,0:T(8,128)(2,1)}, u32[]{:S(2)}, u32[]{:S(2)}) collective-permute-start(bf16[256,1024]{1,0:T(8,128)(2,1)} %get-tuple-element.60), channel_id=1, source_target_pairs={{0,1},{1,0},{2,3},{3,2},{4,5},{5,4},{6,7},{7,6},{8,9},{9,8},{10,11... | collective-permute-start | bytes 1572872 | tf_op jit(solution)/shard_map/ppermute | solution.py:517
  38.8 24.9 %collective-permute-start.6 = (bf16[256,1024]{1,0:T(8,128)(2,1)}, bf16[256,1024]{1,0:T(8,128)(2,1)}, u32[]{:S(2)}, u32[]{:S(2)}) collective-permute-start(bf16[256,1024]{1,0:T(8,128)(2,1)} %get-tuple-element.61), channel_id=1, source_target_pairs={{0,2},{1,3},{2,0},{3,1},{4,6},{5,7},{6,4},{7,5},{8,10},{9,11},{10,... | collective-permute-start | bytes 1572872 | tf_op jit(solution)/shard_map/ppermute | solution.py:517
  40.3 23.3 %collective-permute-start.7 = (bf16[256,1024]{1,0:T(8,128)(2,1)}, bf16[256,1024]{1,0:T(8,128)(2,1)}, u32[]{:S(2)}, u32[]{:S(2)}) collective-permute-start(bf16[256,1024]{1,0:T(8,128)(2,1)} %get-tuple-element.62), channel_id=1, source_target_pairs={{0,3},{1,2},{2,1},{3,0},{4,7},{5,6},{6,5},{7,4},{8,11},{9,10},{10,... | collective-permute-start | bytes 1572872 | tf_op jit(solution)/shard_map/ppermute | solution.py:517
  47.1 14.9 %all-to-all-start.1 = ((bf16[8,128,128]{2,1,0:T(8,128)(2,1)}), bf16[8,128,128]{2,1,0:T(8,128)(2,1)S(1)}, u32[]{:S(2)}, u32[]{:S(2)}) async-start(bf16[8,128,128]{2,1,0:T(8,128)(2,1)} %get-tuple-element.52), calls=%async_computation.1 | async-start | bytes 524288 | tf_op jit(solution)/shard_map/all_to_all | solution.py:649
  52.3 6.6 %collective-permute-start.4 = (f32[4,48,128]{2,1,0:T(8,128)S(1)}, f32[4,48,128]{2,1,0:T(8,128)S(1)}, u32[]{:S(2)}, u32[]{:S(2)}) collective-permute-start(f32[4,48,128]{2,1,0:T(8,128)S(1)} %get-tuple-element.58), channel_id=1, source_target_pairs={{4,0},{8,4},{12,8},{16,12},{20,16},{24,20},{28,24},{5,1},{9,5},{13... | collective-permute-start | bytes 294920 | tf_op jit(solution)/shard_map/ppermute | solution.py:512

commit v13 on v12

--- a/solution.py
+++ b/solution.py
@@ -167,20 +167,39 @@
         scatter_tokens(taps_ref, taps_in_ref[stream], stream * taps)
         behind = halo_ref[stream * held : (stream + 1) * held, :].astype(F32)
         scatter_tokens(wide_ref.at[stream], behind[held - rim :], 0)
-        scatter_tokens(wide_ref.at[stream], streams_ref[stream].astype(F32), rim)
-
-    def body(step, carry):
-        begin = pl.multiple_of(step * STEP * SUB, SUB)
-        rows = pl.ds(begin, STEP * SUB)
-        feats = []
+    batch = 2 * STEP
+
+    def place(number):
+        first = pl.multiple_of(number * batch, batch)
         for stream in range(3):
-            window = as_tiles(wide_ref[stream, pl.ds(begin, (STEP + rim) * SUB), :])
-            feats.append(filtered(window, taps_ref, stream, taps, STEP, True))
-            feat_ref[stream, rows, :] = as_rows(feats[-1])
-        feat_ref[3, rows, :] = as_rows(round16(feats[1] * feats[2]))
+            value = streams_ref[stream, pl.ds(first, batch), :].astype(F32)
+            scatter_tokens(wide_ref.at[stream], value, rim + first)
+
+    place(0)
+
+    def body(number, carry):
+        windows = [
+            as_tiles(
+                wide_ref[
+                    stream,
+                    pl.ds(pl.multiple_of(number * batch * SUB, SUB), (batch + rim) * SUB),
+                    :,
+                ]
+            )
+            for stream in range(3)
+        ]
+        place(jnp.minimum(number + 1, tokens // batch - 1))
+        for half in range(2):
+            rows = pl.ds(pl.multiple_of((number * 2 + half) * STEP * SUB, SUB), STEP * SUB)
+            feats = []
+            for stream in range(3):
+                window = windows[stream][half * STEP : half * STEP + STEP + rim]
+                feats.append(filtered(window, taps_ref, stream, taps, STEP, True))
+                feat_ref[stream, rows, :] = as_rows(feats[-1])
+            feat_ref[3, rows, :] = as_rows(round16(feats[1] * feats[2]))
         return carry
 
-    lax.fori_loop(0, tokens // STEP, body, 0)
+    lax.fori_loop(0, tokens // batch, body, 0)
     grad_in.wait()
     copies = start_all(
         [

time: 69.4 us -> 69 us (level)
  no operation moved by 1% of the time
where the time goes in v13:
time: 69 us; the launch traced here: 68.6 us
  Pallas kernels  37.6 us (54%)
  starting transfers between devices  24.7 us (36%)
  waiting for transfers between devices  4.81 us (7%)
  local copies, waits for them, and re-layouts  0.78 us (1%)
  between operations  0.73 us (1%)
    pallas_call x7, Pallas kernels, call(): pl.pallas_call(kernel, out_shape=[jax.ShapeDtypeStruct(*out) if own else...  37.6 us
    ppermute x6, starting transfers between devices, exchange(): return lax.ppermute(value, axis, [(s, s ^ mask) for s in range(count)])  9.91 us
    all_to_all x1, starting transfers between devices, shards(): lax.all_to_all(messages, 'ctx', split_axis=0, concat_axis=0, tiled=True)  5.99 us
    all_to_all x1, starting transfers between devices, shards(): lax.all_to_all(back_messages, 'ctx', split_axis=0, concat_axis=0, tiled=T...  5.12 us
    ppermute x2, starting transfers between devices, shift(): return lax.ppermute(value, axis, pairs)  3.64 us
    all_to_all x1, waiting for transfers between devices, shards(): lax.all_to_all(back_messages, 'ctx', split_axis=0, concat_axis=0, tiled=T...  3.15 us
    ppermute x6, waiting for transfers between devices, exchange(): return lax.ppermute(value, axis, [(s, s ^ mask) for s in range(count)])  1.65 us
  transfers between devices with their start and end apart: 10, of which 2 were waited for; matrix products, arithmetic and copies ran while one was open for 0% of the time, Pallas kernels for 45%

profile of v13, /device:TPU:0, one launch (start us, length us, event | category | flops | bytes accessed | tf_op | source)
XLA Modules:
  0.0 68.6 jit_solution(10898623448852176882)
XLA Ops:
  0.6 1.5 %rim.1 = (bf16[48,1024]{1,0:T(8,128)(2,1)S(1)}, bf16[3,256,1024]{2,1,0:T(8,128)(2,1)S(1)}, f32[3,7,1024]{2,1,0:T(8,128)S(1)}, f32[16,1024]{1,0:T(8,128)S(1)}, f32[16,1024]{1,0:T(8,128)S(1)}) custom-call(bf16[256,1024]{1,0:T(8,128)(2,1)} %q_ref.1, bf16[256,1024]{1,0:T(8,128)(2,1)} %k_ref.1, bf16[256,1024]{1,0:T(8,128)(2,1)} %v_ref.1, f32[3,7,1024]{2,1,0:T(8,128)} %bitcast.4, ...), custom_call_target="tpu_custom_call" | custom-call | bytes 4200000 | tf_op jit(solution)/shard_map/rim/pallas_call | solution.py:513
  2.1 2.4 %collective-permute-start.2 = (bf16[48,1024]{1,0:T(8,128)(2,1)S(1)}, bf16[48,1024]{1,0:T(8,128)(2,1)S(1)}, u32[]{:S(2)}, u32[]{:S(2)}) collective-permute-start(bf16[48,1024]{1,0:T(8,128)(2,1)S(1)} %get-tuple-element.42), channel_id=1, source_target_pairs={{0,4},{4,8},{8,12},{12,16},{16,20},{20,24},{24,28},{1,5},{5,9},{9,... | collective-permute-start | bytes 294920 | tf_op jit(solution)/shard_map/ppermute | solution.py:531
  4.5 2.4 %collective-permute-start.1 = (bf16[256,1024]{1,0:T(8,128)(2,1)}, bf16[256,1024]{1,0:T(8,128)(2,1)S(1)}, u32[]{:S(2)}, u32[]{:S(2)}) collective-permute-start(bf16[256,1024]{1,0:T(8,128)(2,1)} %grad_in_ref), channel_id=1, source_target_pairs={{0,2},{1,3},{2,0},{3,1},{4,6},{5,7},{6,4},{7,5},{8,10},{9,11},{10,... | collective-permute-start | bytes 1572872 | tf_op jit(solution)/shard_map/ppermute | solution.py:536
  6.9 1.5 %collective-permute-start = (bf16[256,1024]{1,0:T(8,128)(2,1)}, bf16[256,1024]{1,0:T(8,128)(2,1)}, u32[]{:S(2)}, u32[]{:S(2)}) collective-permute-start(bf16[256,1024]{1,0:T(8,128)(2,1)} %grad_in_ref), channel_id=1, source_target_pairs={{0,1},{1,0},{2,3},{3,2},{4,5},{5,4},{6,7},{7,6},{8,9},{9,8},{10,11... | collective-permute-start | bytes 1572872 | tf_op jit(solution)/shard_map/ppermute | solution.py:536
  8.4 0.0 collective-permute-done.2.halo_ref
  8.4 6.2 %featurize.1 = (f32[2048,128]{1,0:T(8,128)}, f32[2048,128]{1,0:T(8,128)}, f32[2048,128]{1,0:T(8,128)}, f32[2048,128]{1,0:T(8,128)}, bf16[256,1024]{1,0:T(8,128)(...) custom-call(s32[1]{0:T(128)} %bitcast.position_ref, ...), custom_call_target="tpu_custom_call" | custom-call | bytes 21000000 | tf_op jit(solution)/shard_map/featurize/pallas_call | solution.py:513
  14.6 6.0 %all-to-all-start = ((bf16[8,128,128]{2,1,0:T(8,128)(2,1)}), bf16[8,128,128]{2,1,0:T(8,128)(2,1)S(1)}, u32[]{:S(2)}, u32[]{:S(2)}) async-start(bf16[8,128,128]{2,1,0:T(8,128)(2,1)} %get-tuple-element.47), calls=%async_computation | async-start | bytes 524288 | tf_op jit(solution)/shard_map/all_to_all | solution.py:598
  20.6 2.4 %collective-permute-start.3 = (bf16[256,1024]{1,0:T(8,128)(2,1)}, bf16[256,1024]{1,0:T(8,128)(2,1)S(1)}, u32[]{:S(2)}, u32[]{:S(2)}) collective-permute-start(bf16[256,1024]{1,0:T(8,128)(2,1)} %get-tuple-element.51), channel_id=1, source_target_pairs={{0,3},{1,2},{2,1},{3,0},{4,7},{5,6},{6,5},{7,4},{8,11},{9,10},{10,... | collective-permute-start | bytes 1572872 | tf_op jit(solution)/shard_map/ppermute | solution.py:536
  23.1 0.0 collective-permute-done.1.refs_2_.refs_1_
  23.1 0.0 copy-start
  23.1 0.0 collective-permute-done.refs_1_.refs_0_
  23.1 0.8 %copy-done = bf16[256,1024]{1,0:T(8,128)(2,1)} copy-done((bf16[256,1024]{1,0:T(8,128)(2,1)}, bf16[256,1024]{1,0:T(8,128)(2,1)S(1)}, u32[]{:S(2)}) %copy-start) | copy-done | bytes 524312
  23.9 6.7 %middle.1._.base_ref = f32[1024,256]{1,0:T(8,128)S(1)} custom-call(s32[4]{0:T(128)S(1)} %iota_xor_fusion.index_ref, bf16[1024,4096]{1,0:T(8,128)(2,1)} %weight_ref.7, bf16[256,1024]{1,0:T(8,128)(2,1)} %grad_in_ref, bf16[256,1024]{1,0:T(8,128)(2,1)} %collective-permute-done.refs_1_.refs_0_, bf16[256,1024]{1,0:T(8,128)(2,1)} %copy-done), custom_call_target="tpu_custom_call" | custom-call | bytes 21000000 | tf_op jit(solution)/shard_map/middle/pallas_call | solution.py:513
  30.6 0.0 all-to-all-done.message_ref
  30.6 6.4 %project.1 = (f32[2048,128]{1,0:T(8,128)}, bf16[256,1024]{1,0:T(8,128)(2,1)}, bf16[256,1024]{1,0:T(8,128)(2,1)}, bf16[256,1024]{1,0:T(8,128)(2,1)}, bf16[256,1024]{1,0:T(8,128)(2,1)}) custom-call(s32[4]{0:T(128)S(1)} %iota_xor_fusion.index_ref, bf16[8,128,128]{2,1,0:T(8,128)(2,1)S(1)} %all-to-all-done.message_ref, ...), custom_call_target="tpu_custom_call" | custom-call | bytes 24500000 | tf_op jit(solution)/shard_map/project/pallas_call | solution.py:513
  37.0 1.3 %collective-permute-start.5 = (bf16[256,1024]{1,0:T(8,128)(2,1)}, bf16[256,1024]{1,0:T(8,128)(2,1)}, u32[]{:S(2)}, u32[]{:S(2)}) collective-permute-start(bf16[256,1024]{1,0:T(8,128)(2,1)} %get-tuple-element.60), channel_id=1, source_target_pairs={{0,1},{1,0},{2,3},{3,2},{4,5},{5,4},{6,7},{7,6},{8,9},{9,8},{10,11... | collective-permute-start | bytes 1572872 | tf_op jit(solution)/shard_map/ppermute | solution.py:536
  38.3 1.5 %collective-permute-start.6 = (bf16[256,1024]{1,0:T(8,128)(2,1)}, bf16[256,1024]{1,0:T(8,128)(2,1)}, u32[]{:S(2)}, u32[]{:S(2)}) collective-permute-start(bf16[256,1024]{1,0:T(8,128)(2,1)} %get-tuple-element.61), channel_id=1, source_target_pairs={{0,2},{1,3},{2,0},{3,1},{4,6},{5,7},{6,4},{7,5},{8,10},{9,11},{10,... | collective-permute-start | bytes 1572872 | tf_op jit(solution)/shard_map/ppermute | solution.py:536
  39.9 0.7 %collective-permute-start.7 = (bf16[256,1024]{1,0:T(8,128)(2,1)}, bf16[256,1024]{1,0:T(8,128)(2,1)}, u32[]{:S(2)}, u32[]{:S(2)}) collective-permute-start(bf16[256,1024]{1,0:T(8,128)(2,1)} %get-tuple-element.62), channel_id=1, source_target_pairs={{0,3},{1,2},{2,1},{3,0},{4,7},{5,6},{6,5},{7,4},{8,11},{9,10},{10,... | collective-permute-start | bytes 1572872 | tf_op jit(solution)/shard_map/ppermute | solution.py:536
  40.6 0.0 collective-permute-done.3.refs_0_
  40.6 6.1 %back_last.1 = (f32[2048,128]{1,0:T(8,128)}, f32[2048,128]{1,0:T(8,128)S(1)}, bf16[8,128,128]{2,1,0:T(8,128)(2,1)}, f32[4,48,128]{2,1,0:T(8,128)S(1)}) custom-call(s32[4]{0:T(128)S(1)} %iota_xor_fusion.index_ref, s32[1]{0:T(128)} %bitcast.position_ref, f32[1024,256]{1,0:T(8,128)S(1)} %middle.1._.base_ref, f32[128,128]{1,0:T(8,128)S(1)} %get-tuple-element.43.decay_ref, ...), custom_call_target="tpu_custom_call" | custom-call | bytes 21000000 | tf_op jit(solution)/shard_map/back_last/pallas_call | solution.py:513
  46.7 5.1 %all-to-all-start.1 = ((bf16[8,128,128]{2,1,0:T(8,128)(2,1)}), bf16[8,128,128]{2,1,0:T(8,128)(2,1)S(1)}, u32[]{:S(2)}, u32[]{:S(2)}) async-start(bf16[8,128,128]{2,1,0:T(8,128)(2,1)} %get-tuple-element.52), calls=%async_computation.1 | async-start | bytes 524288 | tf_op jit(solution)/shard_map/all_to_all | solution.py:668
  51.8 1.3 %collective-permute-start.4 = (f32[4,48,128]{2,1,0:T(8,128)S(1)}, f32[4,48,128]{2,1,0:T(8,128)S(1)}, u32[]{:S(2)}, u32[]{:S(2)}) collective-permute-start(f32[4,48,128]{2,1,0:T(8,128)S(1)} %get-tuple-element.58), channel_id=1, source_target_pairs={{4,0},{8,4},{12,8},{16,12},{20,16},{24,20},{28,24},{5,1},{9,5},{13... | collective-permute-start | bytes 294920 | tf_op jit(solution)/shard_map/ppermute | solution.py:531
  53.1 5.3 %back_local.1 = (f32[2048,128]{1,0:T(8,128)S(1)}, bf16[256,1024]{1,0:T(8,128)(2,1)}, bf16[256,1024]{1,0:T(8,128)(2,1)}) custom-call(s32[4]{0:T(128)S(1)} %iota_xor_fusion.index_ref, f32[2048,128]{1,0:T(8,128)S(1)} %get-tuple-element.53.signal_ref, f32[128,128]{1,0:T(8,128)S(1)} %get-tuple-element.43.decay_ref, f32[128,128]{1,0:T(8,128)S(1)} %get-tuple-element.48.scale_ref, ...), custom_call_target="tpu_custom_call" | custom-call | bytes 17500000 | tf_op jit(solution)/shard_map/back_local/pallas_call | solution.py:513
  58.4 0.0 collective-permute-done.4.ahead_ref
  58.4 3.1 %all-to-all-done.1.message_ref = bf16[8,128,128]{2,1,0:T(8,128)(2,1)S(1)} async-done(((bf16[8,128,128]{2,1,0:T(8,128)(2,1)}), bf16[8,128,128]{2,1,0:T(8,128)(2,1)S(1)}, u32[]{:S(2)}, u32[]{:S(2)}) %all-to-all-start.1) | async-done | bytes 262176 | tf_op jit(solution)/shard_map/all_to_all | solution.py:668
  61.6 0.0 collective-permute-done.5.refs_1_
  61.6 1.6 %collective-permute-done.6.refs_2_ = bf16[256,1024]{1,0:T(8,128)(2,1)} collective-permute-done((bf16[256,1024]{1,0:T(8,128)(2,1)}, bf16[256,1024]{1,0:T(8,128)(2,1)}, u32[]{:S(2)}, u32[]{:S(2)}) %collective-permute-start.6) | collective-permute-done | bytes 524320 | tf_op jit(solution)/shard_map/ppermute | solution.py:536
  63.2 0.0 collective-permute-done.7.refs_3_
  63.2 5.3 %finish.1 = (bf16[256,1024]{1,0:T(8,128)(2,1)}, bf16[256,1024]{1,0:T(8,128)(2,1)}, bf16[256,1024]{1,0:T(8,128)(2,1)}, bf16[256,1024]{1,0:T(8,128)(2,1)}) custom-call(bf16[8,128,128]{2,1,0:T(8,128)(2,1)S(1)} %all-to-all-done.1.message_ref, f32[2048,128]{1,0:T(8,128)S(1)} %get-tuple-element.57.local_ref, ...), custom_call_target="tpu_custom_call", output_to_operand_aliasing={{0}: (13, {})} | custom-call | bytes 17500000 | tf_op jit(solution)/shard_map/finish/pallas_call | solution.py:513
  (1 shorter events, 0.0 us)
Async XLA Ops:
  2.1 6.3 %collective-permute-start.2 = (bf16[48,1024]{1,0:T(8,128)(2,1)S(1)}, bf16[48,1024]{1,0:T(8,128)(2,1)S(1)}, u32[]{:S(2)}, u32[]{:S(2)}) collective-permute-start(bf16[48,1024]{1,0:T(8,128)(2,1)S(1)} %get-tuple-element.42), channel_id=1, source_target_pairs={{0,4},{4,8},{8,12},{12,16},{16,20},{20,24},{24,28},{1,5},{5,9},{9,... | collective-permute-start | bytes 294920 | tf_op jit(solution)/shard_map/ppermute | solution.py:531
  4.5 18.6 %collective-permute-start.1 = (bf16[256,1024]{1,0:T(8,128)(2,1)}, bf16[256,1024]{1,0:T(8,128)(2,1)S(1)}, u32[]{:S(2)}, u32[]{:S(2)}) collective-permute-start(bf16[256,1024]{1,0:T(8,128)(2,1)} %grad_in_ref), channel_id=1, source_target_pairs={{0,2},{1,3},{2,0},{3,1},{4,6},{5,7},{6,4},{7,5},{8,10},{9,11},{10,... | collective-permute-start | bytes 1572872 | tf_op jit(solution)/shard_map/ppermute | solution.py:536
  6.9 16.2 %collective-permute-start = (bf16[256,1024]{1,0:T(8,128)(2,1)}, bf16[256,1024]{1,0:T(8,128)(2,1)}, u32[]{:S(2)}, u32[]{:S(2)}) collective-permute-start(bf16[256,1024]{1,0:T(8,128)(2,1)} %grad_in_ref), channel_id=1, source_target_pairs={{0,1},{1,0},{2,3},{3,2},{4,5},{5,4},{6,7},{7,6},{8,9},{9,8},{10,11... | collective-permute-start | bytes 1572872 | tf_op jit(solution)/shard_map/ppermute | solution.py:536
  14.6 16.0 %all-to-all-start = ((bf16[8,128,128]{2,1,0:T(8,128)(2,1)}), bf16[8,128,128]{2,1,0:T(8,128)(2,1)S(1)}, u32[]{:S(2)}, u32[]{:S(2)}) async-start(bf16[8,128,128]{2,1,0:T(8,128)(2,1)} %get-tuple-element.47), calls=%async_computation | async-start | bytes 524288 | tf_op jit(solution)/shard_map/all_to_all | solution.py:598
  20.6 20.0 %collective-permute-start.3 = (bf16[256,1024]{1,0:T(8,128)(2,1)}, bf16[256,1024]{1,0:T(8,128)(2,1)S(1)}, u32[]{:S(2)}, u32[]{:S(2)}) collective-permute-start(bf16[256,1024]{1,0:T(8,128)(2,1)} %get-tuple-element.51), channel_id=1, source_target_pairs={{0,3},{1,2},{2,1},{3,0},{4,7},{5,6},{6,5},{7,4},{8,11},{9,10},{10,... | collective-permute-start | bytes 1572872 | tf_op jit(solution)/shard_map/ppermute | solution.py:536
  23.1 0.8 %copy-start = (bf16[256,1024]{1,0:T(8,128)(2,1)}, bf16[256,1024]{1,0:T(8,128)(2,1)S(1)}, u32[]{:S(2)}) copy-start(bf16[256,1024]{1,0:T(8,128)(2,1)S(1)} %collective-permute-done.1.refs_2_.refs_1_) | copy-start | bytes 1572868
  37.0 24.5 %collective-permute-start.5 = (bf16[256,1024]{1,0:T(8,128)(2,1)}, bf16[256,1024]{1,0:T(8,128)(2,1)}, u32[]{:S(2)}, u32[]{:S(2)}) collective-permute-start(bf16[256,1024]{1,0:T(8,128)(2,1)} %get-tuple-element.60), channel_id=1, source_target_pairs={{0,1},{1,0},{2,3},{3,2},{4,5},{5,4},{6,7},{7,6},{8,9},{9,8},{10,11... | collective-permute-start | bytes 1572872 | tf_op jit(solution)/shard_map/ppermute | solution.py:536
  38.3 24.9 %collective-permute-start.6 = (bf16[256,1024]{1,0:T(8,128)(2,1)}, bf16[256,1024]{1,0:T(8,128)(2,1)}, u32[]{:S(2)}, u32[]{:S(2)}) collective-permute-start(bf16[256,1024]{1,0:T(8,128)(2,1)} %get-tuple-element.61), channel_id=1, source_target_pairs={{0,2},{1,3},{2,0},{3,1},{4,6},{5,7},{6,4},{7,5},{8,10},{9,11},{10,... | collective-permute-start | bytes 1572872 | tf_op jit(solution)/shard_map/ppermute | solution.py:536
  39.9 23.3 %collective-permute-start.7 = (bf16[256,1024]{1,0:T(8,128)(2,1)}, bf16[256,1024]{1,0:T(8,128)(2,1)}, u32[]{:S(2)}, u32[]{:S(2)}) collective-permute-start(bf16[256,1024]{1,0:T(8,128)(2,1)} %get-tuple-element.62), channel_id=1, source_target_pairs={{0,3},{1,2},{2,1},{3,0},{4,7},{5,6},{6,5},{7,4},{8,11},{9,10},{10,... | collective-permute-start | bytes 1572872 | tf_op jit(solution)/shard_map/ppermute | solution.py:536
  46.7 14.9 %all-to-all-start.1 = ((bf16[8,128,128]{2,1,0:T(8,128)(2,1)}), bf16[8,128,128]{2,1,0:T(8,128)(2,1)S(1)}, u32[]{:S(2)}, u32[]{:S(2)}) async-start(bf16[8,128,128]{2,1,0:T(8,128)(2,1)} %get-tuple-element.52), calls=%async_computation.1 | async-start | bytes 524288 | tf_op jit(solution)/shard_map/all_to_all | solution.py:668
  51.8 6.6 %collective-permute-start.4 = (f32[4,48,128]{2,1,0:T(8,128)S(1)}, f32[4,48,128]{2,1,0:T(8,128)S(1)}, u32[]{:S(2)}, u32[]{:S(2)}) collective-permute-start(f32[4,48,128]{2,1,0:T(8,128)S(1)} %get-tuple-element.58), channel_id=1, source_target_pairs={{4,0},{8,4},{12,8},{16,12},{20,16},{24,20},{28,24},{5,1},{9,5},{13... | collective-permute-start | bytes 294920 | tf_op jit(solution)/shard_map/ppermute | solution.py:531

commit v14 on v13

--- a/solution.py
+++ b/solution.py
@@ -388,18 +388,32 @@
 
 
 def spread_back(wide_ref, taps_ref, stream, taps, rows_ref, out_ref):
-    tokens = out_ref.shape[0]
-
-    def body(step, carry):
-        first = pl.multiple_of(step * STEP * SUB, SUB)
-        window = as_tiles(wide_ref[pl.ds(first, (STEP + taps - 1) * SUB), :])
-        rows_ref[pl.ds(first, STEP * SUB), :] = as_rows(
-            filtered(window, taps_ref, stream, taps, STEP, False)
+    batch = 2 * STEP
+    batches = out_ref.shape[0] // batch
+
+    def bring(number):
+        first = pl.multiple_of(number * batch, batch)
+        for group in range(out_ref.shape[1] // LANES):
+            out_ref[pl.ds(first, batch), group * LANES : (group + 1) * LANES] = rows_ref[
+                pl.ds(first * SUB + group, batch, stride=SUB), :
+            ].astype(out_ref.dtype)
+
+    def filter_batch(number):
+        first = pl.multiple_of(number * batch * SUB, SUB)
+        window = as_tiles(wide_ref[pl.ds(first, (batch + taps - 1) * SUB), :])
+        rows_ref[pl.ds(first, batch * SUB), :] = as_rows(
+            filtered(window, taps_ref, stream, taps, batch, False)
         )
+
+    filter_batch(0)
+
+    def body(number, carry):
+        bring(number - 1)
+        filter_batch(number)
         return carry
 
-    lax.fori_loop(0, tokens // STEP, body, 0)
-    gather_tokens(lambda group: group_rows(rows_ref, group, tokens), out_ref)
+    lax.fori_loop(1, batches, body, 0)
+    bring(batches - 1)
 
 
 def back_local_kernel(

time: 69 us -> 68.6 us (level)
  no operation moved by 1% of the time
where the time goes in v14:
time: 68.6 us; the launch traced here: 68.2 us
  Pallas kernels  37 us (54%)
  starting transfers between devices  24.7 us (36%)
  waiting for transfers between devices  5.04 us (7%)
  local copies, waits for them, and re-layouts  0.78 us (1%)
  between operations  0.73 us (1%)
    pallas_call x7, Pallas kernels, call(): pl.pallas_call(kernel, out_shape=[jax.ShapeDtypeStruct(*out) if own else...  37 us
    ppermute x6, starting transfers between devices, exchange(): return lax.ppermute(value, axis, [(s, s ^ mask) for s in range(count)])  9.91 us
    all_to_all x1, starting transfers between devices, shards(): lax.all_to_all(messages, 'ctx', split_axis=0, concat_axis=0, tiled=True)  5.99 us
    all_to_all x1, starting transfers between devices, shards(): lax.all_to_all(back_messages, 'ctx', split_axis=0, concat_axis=0, tiled=T...  5.12 us
    ppermute x2, starting transfers between devices, shift(): return lax.ppermute(value, axis, pairs)  3.64 us
    all_to_all x1, waiting for transfers between devices, shards(): lax.all_to_all(back_messages, 'ctx', split_axis=0, concat_axis=0, tiled=T...  3.38 us
    ppermute x6, waiting for transfers between devices, exchange(): return lax.ppermute(value, axis, [(s, s ^ mask) for s in range(count)])  1.65 us
  transfers between devices with their start and end apart: 10, of which 2 were waited for; matrix products, arithmetic and copies ran while one was open for 0% of the time, Pallas kernels for 45%

profile of v14, /device:TPU:0, one launch (start us, length us, event | category | flops | bytes accessed | tf_op | source)
XLA Modules:
  0.0 68.2 jit_solution(11901709125300809323)
XLA Ops:
  0.6 1.5 %rim.1 = (bf16[48,1024]{1,0:T(8,128)(2,1)S(1)}, bf16[3,256,1024]{2,1,0:T(8,128)(2,1)S(1)}, f32[3,7,1024]{2,1,0:T(8,128)S(1)}, f32[16,1024]{1,0:T(8,128)S(1)}, f32[16,1024]{1,0:T(8,128)S(1)}) custom-call(bf16[256,1024]{1,0:T(8,128)(2,1)} %q_ref.1, bf16[256,1024]{1,0:T(8,128)(2,1)} %k_ref.1, bf16[256,1024]{1,0:T(8,128)(2,1)} %v_ref.1, f32[3,7,1024]{2,1,0:T(8,128)} %bitcast.4, ...), custom_call_target="tpu_custom_call" | custom-call | bytes 4200000 | tf_op jit(solution)/shard_map/rim/pallas_call | solution.py:527
  2.1 2.4 %collective-permute-start.2 = (bf16[48,1024]{1,0:T(8,128)(2,1)S(1)}, bf16[48,1024]{1,0:T(8,128)(2,1)S(1)}, u32[]{:S(2)}, u32[]{:S(2)}) collective-permute-start(bf16[48,1024]{1,0:T(8,128)(2,1)S(1)} %get-tuple-element.42), channel_id=1, source_target_pairs={{0,4},{4,8},{8,12},{12,16},{16,20},{20,24},{24,28},{1,5},{5,9},{9,... | collective-permute-start | bytes 294920 | tf_op jit(solution)/shard_map/ppermute | solution.py:545
  4.5 2.4 %collective-permute-start.1 = (bf16[256,1024]{1,0:T(8,128)(2,1)}, bf16[256,1024]{1,0:T(8,128)(2,1)S(1)}, u32[]{:S(2)}, u32[]{:S(2)}) collective-permute-start(bf16[256,1024]{1,0:T(8,128)(2,1)} %grad_in_ref), channel_id=1, source_target_pairs={{0,2},{1,3},{2,0},{3,1},{4,6},{5,7},{6,4},{7,5},{8,10},{9,11},{10,... | collective-permute-start | bytes 1572872 | tf_op jit(solution)/shard_map/ppermute | solution.py:550
  6.9 1.5 %collective-permute-start = (bf16[256,1024]{1,0:T(8,128)(2,1)}, bf16[256,1024]{1,0:T(8,128)(2,1)}, u32[]{:S(2)}, u32[]{:S(2)}) collective-permute-start(bf16[256,1024]{1,0:T(8,128)(2,1)} %grad_in_ref), channel_id=1, source_target_pairs={{0,1},{1,0},{2,3},{3,2},{4,5},{5,4},{6,7},{7,6},{8,9},{9,8},{10,11... | collective-permute-start | bytes 1572872 | tf_op jit(solution)/shard_map/ppermute | solution.py:550
  8.4 0.0 collective-permute-done.2.halo_ref
  8.4 6.2 %featurize.1 = (f32[2048,128]{1,0:T(8,128)}, f32[2048,128]{1,0:T(8,128)}, f32[2048,128]{1,0:T(8,128)}, f32[2048,128]{1,0:T(8,128)}, bf16[256,1024]{1,0:T(8,128)(...) custom-call(s32[1]{0:T(128)} %bitcast.position_ref, ...), custom_call_target="tpu_custom_call" | custom-call | bytes 21000000 | tf_op jit(solution)/shard_map/featurize/pallas_call | solution.py:527
  14.6 6.0 %all-to-all-start = ((bf16[8,128,128]{2,1,0:T(8,128)(2,1)}), bf16[8,128,128]{2,1,0:T(8,128)(2,1)S(1)}, u32[]{:S(2)}, u32[]{:S(2)}) async-start(bf16[8,128,128]{2,1,0:T(8,128)(2,1)} %get-tuple-element.47), calls=%async_computation | async-start | bytes 524288 | tf_op jit(solution)/shard_map/all_to_all | solution.py:612
  20.6 2.4 %collective-permute-start.3 = (bf16[256,1024]{1,0:T(8,128)(2,1)}, bf16[256,1024]{1,0:T(8,128)(2,1)S(1)}, u32[]{:S(2)}, u32[]{:S(2)}) collective-permute-start(bf16[256,1024]{1,0:T(8,128)(2,1)} %get-tuple-element.51), channel_id=1, source_target_pairs={{0,3},{1,2},{2,1},{3,0},{4,7},{5,6},{6,5},{7,4},{8,11},{9,10},{10,... | collective-permute-start | bytes 1572872 | tf_op jit(solution)/shard_map/ppermute | solution.py:550
  23.1 0.0 collective-permute-done.1.refs_2_.refs_1_
  23.1 0.0 copy-start
  23.1 0.0 collective-permute-done.refs_1_.refs_0_
  23.1 0.8 %copy-done = bf16[256,1024]{1,0:T(8,128)(2,1)} copy-done((bf16[256,1024]{1,0:T(8,128)(2,1)}, bf16[256,1024]{1,0:T(8,128)(2,1)S(1)}, u32[]{:S(2)}) %copy-start) | copy-done | bytes 524312
  23.9 6.7 %middle.1._.base_ref = f32[1024,256]{1,0:T(8,128)S(1)} custom-call(s32[4]{0:T(128)S(1)} %iota_xor_fusion.index_ref, bf16[1024,4096]{1,0:T(8,128)(2,1)} %weight_ref.7, bf16[256,1024]{1,0:T(8,128)(2,1)} %grad_in_ref, bf16[256,1024]{1,0:T(8,128)(2,1)} %collective-permute-done.refs_1_.refs_0_, bf16[256,1024]{1,0:T(8,128)(2,1)} %copy-done), custom_call_target="tpu_custom_call" | custom-call | bytes 21000000 | tf_op jit(solution)/shard_map/middle/pallas_call | solution.py:527
  30.6 0.0 all-to-all-done.message_ref
  30.6 6.4 %project.1 = (f32[2048,128]{1,0:T(8,128)}, bf16[256,1024]{1,0:T(8,128)(2,1)}, bf16[256,1024]{1,0:T(8,128)(2,1)}, bf16[256,1024]{1,0:T(8,128)(2,1)}, bf16[256,1024]{1,0:T(8,128)(2,1)}) custom-call(s32[4]{0:T(128)S(1)} %iota_xor_fusion.index_ref, bf16[8,128,128]{2,1,0:T(8,128)(2,1)S(1)} %all-to-all-done.message_ref, ...), custom_call_target="tpu_custom_call" | custom-call | bytes 24500000 | tf_op jit(solution)/shard_map/project/pallas_call | solution.py:527
  37.0 1.3 %collective-permute-start.5 = (bf16[256,1024]{1,0:T(8,128)(2,1)}, bf16[256,1024]{1,0:T(8,128)(2,1)}, u32[]{:S(2)}, u32[]{:S(2)}) collective-permute-start(bf16[256,1024]{1,0:T(8,128)(2,1)} %get-tuple-element.60), channel_id=1, source_target_pairs={{0,1},{1,0},{2,3},{3,2},{4,5},{5,4},{6,7},{7,6},{8,9},{9,8},{10,11... | collective-permute-start | bytes 1572872 | tf_op jit(solution)/shard_map/ppermute | solution.py:550
  38.3 1.5 %collective-permute-start.6 = (bf16[256,1024]{1,0:T(8,128)(2,1)}, bf16[256,1024]{1,0:T(8,128)(2,1)}, u32[]{:S(2)}, u32[]{:S(2)}) collective-permute-start(bf16[256,1024]{1,0:T(8,128)(2,1)} %get-tuple-element.61), channel_id=1, source_target_pairs={{0,2},{1,3},{2,0},{3,1},{4,6},{5,7},{6,4},{7,5},{8,10},{9,11},{10,... | collective-permute-start | bytes 1572872 | tf_op jit(solution)/shard_map/ppermute | solution.py:550
  39.9 0.7 %collective-permute-start.7 = (bf16[256,1024]{1,0:T(8,128)(2,1)}, bf16[256,1024]{1,0:T(8,128)(2,1)}, u32[]{:S(2)}, u32[]{:S(2)}) collective-permute-start(bf16[256,1024]{1,0:T(8,128)(2,1)} %get-tuple-element.62), channel_id=1, source_target_pairs={{0,3},{1,2},{2,1},{3,0},{4,7},{5,6},{6,5},{7,4},{8,11},{9,10},{10,... | collective-permute-start | bytes 1572872 | tf_op jit(solution)/shard_map/ppermute | solution.py:550
  40.6 0.0 collective-permute-done.3.refs_0_
  40.6 6.1 %back_last.1 = (f32[2048,128]{1,0:T(8,128)}, f32[2048,128]{1,0:T(8,128)S(1)}, bf16[8,128,128]{2,1,0:T(8,128)(2,1)}, f32[4,48,128]{2,1,0:T(8,128)S(1)}) custom-call(s32[4]{0:T(128)S(1)} %iota_xor_fusion.index_ref, s32[1]{0:T(128)} %bitcast.position_ref, f32[1024,256]{1,0:T(8,128)S(1)} %middle.1._.base_ref, f32[128,128]{1,0:T(8,128)S(1)} %get-tuple-element.43.decay_ref, ...), custom_call_target="tpu_custom_call" | custom-call | bytes 21000000 | tf_op jit(solution)/shard_map/back_last/pallas_call | solution.py:527
  46.7 5.1 %all-to-all-start.1 = ((bf16[8,128,128]{2,1,0:T(8,128)(2,1)}), bf16[8,128,128]{2,1,0:T(8,128)(2,1)S(1)}, u32[]{:S(2)}, u32[]{:S(2)}) async-start(bf16[8,128,128]{2,1,0:T(8,128)(2,1)} %get-tuple-element.52), calls=%async_computation.1 | async-start | bytes 524288 | tf_op jit(solution)/shard_map/all_to_all | solution.py:682
  51.8 1.3 %collective-permute-start.4 = (f32[4,48,128]{2,1,0:T(8,128)S(1)}, f32[4,48,128]{2,1,0:T(8,128)S(1)}, u32[]{:S(2)}, u32[]{:S(2)}) collective-permute-start(f32[4,48,128]{2,1,0:T(8,128)S(1)} %get-tuple-element.58), channel_id=1, source_target_pairs={{4,0},{8,4},{12,8},{16,12},{20,16},{24,20},{28,24},{5,1},{9,5},{13... | collective-permute-start | bytes 294920 | tf_op jit(solution)/shard_map/ppermute | solution.py:545
  53.1 5.1 %back_local.1 = (f32[2048,128]{1,0:T(8,128)S(1)}, bf16[256,1024]{1,0:T(8,128)(2,1)}, bf16[256,1024]{1,0:T(8,128)(2,1)}) custom-call(s32[4]{0:T(128)S(1)} %iota_xor_fusion.index_ref, f32[2048,128]{1,0:T(8,128)S(1)} %get-tuple-element.53.signal_ref, f32[128,128]{1,0:T(8,128)S(1)} %get-tuple-element.43.decay_ref, f32[128,128]{1,0:T(8,128)S(1)} %get-tuple-element.48.scale_ref, ...), custom_call_target="tpu_custom_call" | custom-call | bytes 17500000 | tf_op jit(solution)/shard_map/back_local/pallas_call | solution.py:527
  58.2 0.0 collective-permute-done.4.ahead_ref
  58.2 3.4 %all-to-all-done.1.message_ref = bf16[8,128,128]{2,1,0:T(8,128)(2,1)S(1)} async-done(((bf16[8,128,128]{2,1,0:T(8,128)(2,1)}), bf16[8,128,128]{2,1,0:T(8,128)(2,1)S(1)}, u32[]{:S(2)}, u32[]{:S(2)}) %all-to-all-start.1) | async-done | bytes 262176 | tf_op jit(solution)/shard_map/all_to_all | solution.py:682
  61.6 0.0 collective-permute-done.5.refs_1_
  61.6 1.6 %collective-permute-done.6.refs_2_ = bf16[256,1024]{1,0:T(8,128)(2,1)} collective-permute-done((bf16[256,1024]{1,0:T(8,128)(2,1)}, bf16[256,1024]{1,0:T(8,128)(2,1)}, u32[]{:S(2)}, u32[]{:S(2)}) %collective-permute-start.6) | collective-permute-done | bytes 524320 | tf_op jit(solution)/shard_map/ppermute | solution.py:550
  63.2 0.0 collective-permute-done.7.refs_3_
  63.2 5.0 %finish.1 = (bf16[256,1024]{1,0:T(8,128)(2,1)}, bf16[256,1024]{1,0:T(8,128)(2,1)}, bf16[256,1024]{1,0:T(8,128)(2,1)}, bf16[256,1024]{1,0:T(8,128)(2,1)}) custom-call(bf16[8,128,128]{2,1,0:T(8,128)(2,1)S(1)} %all-to-all-done.1.message_ref, f32[2048,128]{1,0:T(8,128)S(1)} %get-tuple-element.57.local_ref, ...), custom_call_target="tpu_custom_call", output_to_operand_aliasing={{0}: (13, {})} | custom-call | bytes 17500000 | tf_op jit(solution)/shard_map/finish/pallas_call | solution.py:527
  (1 shorter events, 0.0 us)
Async XLA Ops:
  2.1 6.3 %collective-permute-start.2 = (bf16[48,1024]{1,0:T(8,128)(2,1)S(1)}, bf16[48,1024]{1,0:T(8,128)(2,1)S(1)}, u32[]{:S(2)}, u32[]{:S(2)}) collective-permute-start(bf16[48,1024]{1,0:T(8,128)(2,1)S(1)} %get-tuple-element.42), channel_id=1, source_target_pairs={{0,4},{4,8},{8,12},{12,16},{16,20},{20,24},{24,28},{1,5},{5,9},{9,... | collective-permute-start | bytes 294920 | tf_op jit(solution)/shard_map/ppermute | solution.py:545
  4.5 18.6 %collective-permute-start.1 = (bf16[256,1024]{1,0:T(8,128)(2,1)}, bf16[256,1024]{1,0:T(8,128)(2,1)S(1)}, u32[]{:S(2)}, u32[]{:S(2)}) collective-permute-start(bf16[256,1024]{1,0:T(8,128)(2,1)} %grad_in_ref), channel_id=1, source_target_pairs={{0,2},{1,3},{2,0},{3,1},{4,6},{5,7},{6,4},{7,5},{8,10},{9,11},{10,... | collective-permute-start | bytes 1572872 | tf_op jit(solution)/shard_map/ppermute | solution.py:550
  6.9 16.2 %collective-permute-start = (bf16[256,1024]{1,0:T(8,128)(2,1)}, bf16[256,1024]{1,0:T(8,128)(2,1)}, u32[]{:S(2)}, u32[]{:S(2)}) collective-permute-start(bf16[256,1024]{1,0:T(8,128)(2,1)} %grad_in_ref), channel_id=1, source_target_pairs={{0,1},{1,0},{2,3},{3,2},{4,5},{5,4},{6,7},{7,6},{8,9},{9,8},{10,11... | collective-permute-start | bytes 1572872 | tf_op jit(solution)/shard_map/ppermute | solution.py:550
  14.6 16.0 %all-to-all-start = ((bf16[8,128,128]{2,1,0:T(8,128)(2,1)}), bf16[8,128,128]{2,1,0:T(8,128)(2,1)S(1)}, u32[]{:S(2)}, u32[]{:S(2)}) async-start(bf16[8,128,128]{2,1,0:T(8,128)(2,1)} %get-tuple-element.47), calls=%async_computation | async-start | bytes 524288 | tf_op jit(solution)/shard_map/all_to_all | solution.py:612
  20.6 20.0 %collective-permute-start.3 = (bf16[256,1024]{1,0:T(8,128)(2,1)}, bf16[256,1024]{1,0:T(8,128)(2,1)S(1)}, u32[]{:S(2)}, u32[]{:S(2)}) collective-permute-start(bf16[256,1024]{1,0:T(8,128)(2,1)} %get-tuple-element.51), channel_id=1, source_target_pairs={{0,3},{1,2},{2,1},{3,0},{4,7},{5,6},{6,5},{7,4},{8,11},{9,10},{10,... | collective-permute-start | bytes 1572872 | tf_op jit(solution)/shard_map/ppermute | solution.py:550
  23.1 0.8 %copy-start = (bf16[256,1024]{1,0:T(8,128)(2,1)}, bf16[256,1024]{1,0:T(8,128)(2,1)S(1)}, u32[]{:S(2)}) copy-start(bf16[256,1024]{1,0:T(8,128)(2,1)S(1)} %collective-permute-done.1.refs_2_.refs_1_) | copy-start | bytes 1572868
  37.0 24.5 %collective-permute-start.5 = (bf16[256,1024]{1,0:T(8,128)(2,1)}, bf16[256,1024]{1,0:T(8,128)(2,1)}, u32[]{:S(2)}, u32[]{:S(2)}) collective-permute-start(bf16[256,1024]{1,0:T(8,128)(2,1)} %get-tuple-element.60), channel_id=1, source_target_pairs={{0,1},{1,0},{2,3},{3,2},{4,5},{5,4},{6,7},{7,6},{8,9},{9,8},{10,11... | collective-permute-start | bytes 1572872 | tf_op jit(solution)/shard_map/ppermute | solution.py:550
  38.3 24.9 %collective-permute-start.6 = (bf16[256,1024]{1,0:T(8,128)(2,1)}, bf16[256,1024]{1,0:T(8,128)(2,1)}, u32[]{:S(2)}, u32[]{:S(2)}) collective-permute-start(bf16[256,1024]{1,0:T(8,128)(2,1)} %get-tuple-element.61), channel_id=1, source_target_pairs={{0,2},{1,3},{2,0},{3,1},{4,6},{5,7},{6,4},{7,5},{8,10},{9,11},{10,... | collective-permute-start | bytes 1572872 | tf_op jit(solution)/shard_map/ppermute | solution.py:550
  39.9 23.3 %collective-permute-start.7 = (bf16[256,1024]{1,0:T(8,128)(2,1)}, bf16[256,1024]{1,0:T(8,128)(2,1)}, u32[]{:S(2)}, u32[]{:S(2)}) collective-permute-start(bf16[256,1024]{1,0:T(8,128)(2,1)} %get-tuple-element.62), channel_id=1, source_target_pairs={{0,3},{1,2},{2,1},{3,0},{4,7},{5,6},{6,5},{7,4},{8,11},{9,10},{10,... | collective-permute-start | bytes 1572872 | tf_op jit(solution)/shard_map/ppermute | solution.py:550
  46.7 14.9 %all-to-all-start.1 = ((bf16[8,128,128]{2,1,0:T(8,128)(2,1)}), bf16[8,128,128]{2,1,0:T(8,128)(2,1)S(1)}, u32[]{:S(2)}, u32[]{:S(2)}) async-start(bf16[8,128,128]{2,1,0:T(8,128)(2,1)} %get-tuple-element.52), calls=%async_computation.1 | async-start | bytes 524288 | tf_op jit(solution)/shard_map/all_to_all | solution.py:682
  51.8 6.4 %collective-permute-start.4 = (f32[4,48,128]{2,1,0:T(8,128)S(1)}, f32[4,48,128]{2,1,0:T(8,128)S(1)}, u32[]{:S(2)}, u32[]{:S(2)}) collective-permute-start(f32[4,48,128]{2,1,0:T(8,128)S(1)} %get-tuple-element.58), channel_id=1, source_target_pairs={{4,0},{8,4},{12,8},{16,12},{20,16},{24,20},{28,24},{5,1},{9,5},{13... | collective-permute-start | bytes 294920 | tf_op jit(solution)/shard_map/ppermute | solution.py:545
